TPU v7x, 32 devices: a whole 2x2x4 slice. The times are simulated.
32 devices in a mesh: dp: 16 (over z, y, x), mp: 2 (over core).
Axes of the slice: x: 2, y: 2, z: 4, core: 2. Of those that a mesh axis runs over, the one named last changes fastest.
Arguments:
- text: bfloat16 [768, 40, 768], P('dp'), may hold values from -6 to 6
- cotangent: bfloat16 [768, 40, 768], P('dp'), may hold values from -6 to 6
- lengths: int32 [768], P('dp'), may hold values from 1 to 40
- box_corners: int32 [768, 4], P('dp'), may hold values from 0 to 12, as said below
- box_counts: int32 [16, 16], P('dp'), may hold values from 1 to 6, 48 in all within a row
- region_box: int32 [768], P('dp'), may hold values from 0 to 767, as said below
- patches: bfloat16 [256, 145, 1024], P('dp'), may hold values from -6 to 6
- proj_weight: bfloat16 [1024, 768], replicated, may hold values from -0.1875 to 0.1875
- proj_bias: float32 [768], replicated, may hold values from -1 to 1
- attention_in: bfloat16 [2, 3, 768, 768], P(None, None, None, 'mp'), may hold values from -0.21875 to 0.21875
- attention_bias: float32 [2, 2, 768], P(None, None, 'mp'), may hold values from -1 to 1
- attention_out: bfloat16 [2, 768, 768], P(None, 'mp'), may hold values from -0.875 to 0.875
- output_bias: float32 [3, 768], replicated, may hold values from -1 to 1
- norm_gain: float32 [3, 768], replicated, may hold values from 0.5 to 1.5
- norm_bias: float32 [3, 768], replicated, may hold values from -1 to 1
- up_weight: bfloat16 [768, 3072], P(None, 'mp'), may hold values from -0.21875 to 0.21875
- up_bias: float32 [3072], P('mp'), may hold values from -1 to 1
- down_weight: bfloat16 [3072, 768], P('mp'), may hold values from -0.15625 to 0.15625
Outputs:
- merged_text: bfloat16 [768, 40, 768], P('dp', 'mp')
- text_grad: bfloat16 [768, 40, 768], P('dp', 'mp')
- patch_grad: bfloat16 [256, 145, 1024], P(('dp', 'mp'))
- proj_weight_grad: float32 [1024, 768], P('dp', 'mp')
- proj_bias_grad: float32 [768], P('mp')
- attention_in_grad: float32 [2, 3, 768, 768], P(None, None, 'dp', 'mp')
- attention_bias_grad: float32 [2, 2, 768], P(None, None, 'mp')
- attention_out_grad: float32 [2, 768, 768], P(None, 'mp', 'dp')
- output_bias_grad: float32 [3, 768], replicated
- norm_gain_grad: float32 [3, 768], replicated
- norm_bias_grad: float32 [3, 768], replicated
- up_weight_grad: float32 [768, 3072], P('dp', 'mp')
- up_bias_grad: float32 [3072], P('mp')
- down_weight_grad: float32 [3072, 768], P('mp', 'dp')
Inputs may be any that keep to these rules, and one draw needn't show every extreme that they name: `box_counts`: each index of dp holds 16 images whose counts sum to 48. `box_corners`: first column < end column and first row < end row; ends are exclusive. `region_box`: a permutation of the 768 box numbers; box b belongs to an image of index b // 48 of dp; the 48 rows of one index of dp name boxes of exactly 16 indices, 3 boxes of each.
All inputs are finite; a program needn't handle non-finite values.
Results may differ from a plain program's by a relative error of at most 0.025.
Values may be sent and summed in bfloat16 or wider, within the bound.
No kernel may reach another device: no remote copies, remote signals or barrier semaphores. Data moves between devices by JAX's collectives and lax.ppermute only.
A program may use at most 320 MiB of HBM per device.

v0:
```python
from functools import partial

import jax
import jax.numpy as jnp
from jax import lax
from jax.sharding import PartitionSpec as P

HEAD_DIM = 64
GRID = 12


EPS = 1e-12
NEG = -1e30


def normalize(z, gain, shift):
    center = z - jnp.mean(z, axis=-1, keepdims=True)
    spread = jnp.mean(center * center, axis=-1, keepdims=True)
    return center * lax.rsqrt(spread + EPS) * gain + shift


def norm_backward(z, gain, shift, grad):
    unused, back = jax.vjp(normalize, z, gain, shift)
    return back(grad)


def product(left, right):
    return jnp.dot(left, right, preferred_element_type=jnp.float32)


def product_t(left, right):
    return lax.dot_general(
        left, right, (((0,), (0,)), ((), ())), preferred_element_type=jnp.float32
    )


def product_nt(left, right):
    return lax.dot_general(
        left, right, (((1,), (1,)), ((), ())), preferred_element_type=jnp.float32
    )


def split_sum(partial_sum):
    return lax.psum_scatter(partial_sum, "mp", scatter_dimension=1, tiled=True)


def join_tokens(piece):
    return lax.all_gather(piece, "mp", axis=1, tiled=True)


def cross_keep(corners, patch_count):
    index = jnp.arange(patch_count, dtype=jnp.int32) - 1
    grid_row = index // GRID
    grid_col = index % GRID
    inside = (grid_col[None, :] >= corners[:, 0:1]) & (grid_col[None, :] < corners[:, 1:2])
    inside = inside & (grid_row[None, :] >= corners[:, 2:3]) & (grid_row[None, :] < corners[:, 3:4])
    return inside | (index[None, :] < 0)


def attend_scores(q, k, keep):
    scores = jnp.einsum("rqhe,rkhe->rhqk", q, k, preferred_element_type=jnp.float32) * HEAD_DIM ** (
        -0.5
    )
    return jnp.where(keep[:, None, None, :], scores, NEG)


def attend_forward(q, k, v, keep):
    scores = attend_scores(q, k, keep)
    log_total = jax.scipy.special.logsumexp(scores, axis=-1)
    weights = jnp.exp(scores - log_total[..., None])
    result = jnp.einsum(
        "rhqk,rkhe->rqhe", weights.astype(jnp.bfloat16), v, preferred_element_type=jnp.float32
    )
    return (result.astype(jnp.bfloat16), log_total)


def attend_backward(q, k, v, keep, log_total, grad_out):
    weights = jnp.exp(attend_scores(q, k, keep) - log_total[..., None])
    grad_weights = jnp.einsum("rqhe,rkhe->rhqk", grad_out, v, preferred_element_type=jnp.float32)
    grad_v = jnp.einsum(
        "rhqk,rqhe->rkhe",
        weights.astype(jnp.bfloat16),
        grad_out,
        preferred_element_type=jnp.float32,
    ).astype(jnp.bfloat16)
    grad_scores = weights * (grad_weights - jnp.sum(weights * grad_weights, axis=-1, keepdims=True))
    grad_scores = (grad_scores * HEAD_DIM ** (-0.5)).astype(jnp.bfloat16)
    grad_q = jnp.einsum(
        "rhqk,rkhe->rqhe", grad_scores, k, preferred_element_type=jnp.float32
    ).astype(jnp.bfloat16)
    grad_k = jnp.einsum(
        "rhqk,rqhe->rkhe", grad_scores, q, preferred_element_type=jnp.float32
    ).astype(jnp.bfloat16)
    return (grad_q, grad_k, grad_v)


def layer_local(
    x,
    upstream,
    phrase_len,
    corners,
    patch_rows,
    attention_in,
    attention_bias,
    attention_out,
    output_bias,
    norm_gain,
    norm_bias,
    up_weight,
    up_bias,
    down_weight,
    offset,
    tokens_mine,
):
    rows, length, width = x.shape
    patch_count = patch_rows.shape[1]
    local_width = attention_in.shape[-1]
    heads_mine = local_width // HEAD_DIM
    count = rows * length

    def heads(tensor, steps):
        return tensor.reshape(rows, steps, heads_mine, HEAD_DIM)

    def mine_tokens(tensor):
        return lax.dynamic_slice_in_dim(tensor, offset, tokens_mine, 1)

    def token_sum(tensor):
        return jnp.sum(tensor.astype(jnp.float32), axis=(0, 1))

    keep_self = jnp.arange(length, dtype=jnp.int32)[None, :] < phrase_len[:, None]
    keep_cross = cross_keep(corners, patch_count)
    flat_x = x.reshape(count, width)
    flat_patch = patch_rows.reshape(rows * patch_count, width)
    self_w = attention_in[0]
    cross_w = attention_in[1]
    q = (product(flat_x, self_w[0]) + attention_bias[0, 0]).astype(jnp.bfloat16)
    k = product(flat_x, self_w[1]).astype(jnp.bfloat16)
    v = (product(flat_x, self_w[2]) + attention_bias[0, 1]).astype(jnp.bfloat16)
    attended, log_self = attend_forward(
        heads(q, length), heads(k, length), heads(v, length), keep_self
    )
    attended = attended.reshape(count, local_width)
    z_one = (
        mine_tokens(x).astype(jnp.float32)
        + split_sum(product(attended, attention_out[0]).reshape(rows, length, width))
        + output_bias[0]
    )
    after_self = normalize(z_one, norm_gain[0], norm_bias[0])
    self_low = join_tokens(after_self.astype(jnp.bfloat16)).reshape(count, width)
    q_cross = (product(self_low, cross_w[0]) + attention_bias[1, 0]).astype(jnp.bfloat16)
    k_cross = product(flat_patch, cross_w[1]).astype(jnp.bfloat16)
    v_cross = (product(flat_patch, cross_w[2]) + attention_bias[1, 1]).astype(jnp.bfloat16)
    crossed, log_cross = attend_forward(
        heads(q_cross, length), heads(k_cross, patch_count), heads(v_cross, patch_count), keep_cross
    )
    crossed = crossed.reshape(count, local_width)
    z_two = (
        after_self
        + split_sum(product(crossed, attention_out[1]).reshape(rows, length, width))
        + output_bias[1]
    )
    after_cross = normalize(z_two, norm_gain[1], norm_bias[1])
    cross_low = join_tokens(after_cross.astype(jnp.bfloat16)).reshape(count, width)
    hidden = product(cross_low, up_weight) + up_bias
    activated = jax.nn.gelu(hidden, approximate=False).astype(jnp.bfloat16)
    z_three = (
        after_cross
        + split_sum(product(activated, down_weight).reshape(rows, length, width))
        + output_bias[2]
    )
    merged_mine = normalize(z_three, norm_gain[2], norm_bias[2]).astype(jnp.bfloat16)
    grad_z3, gain_last, shift_last = norm_backward(
        z_three, norm_gain[2], norm_bias[2], mine_tokens(upstream).astype(jnp.float32)
    )
    grad_ffn = grad_z3.astype(jnp.bfloat16)
    grad_ffn_all = join_tokens(grad_ffn).reshape(count, width)
    down_grad = product_t(activated, grad_ffn_all)
    grad_act = product_nt(grad_ffn_all, down_weight)
    unused, gelu_back = jax.vjp(partial(jax.nn.gelu, approximate=False), hidden)
    grad_hidden = gelu_back(grad_act)[0].astype(jnp.bfloat16)
    up_grad = product_t(cross_low, grad_hidden)
    up_bias_grad = jnp.sum(grad_hidden.astype(jnp.float32), axis=0)
    grad_after_cross = grad_z3 + split_sum(
        product_nt(grad_hidden, up_weight).reshape(rows, length, width)
    )
    grad_z2, gain_mid, shift_mid = norm_backward(
        z_two, norm_gain[1], norm_bias[1], grad_after_cross
    )
    grad_cross_out = grad_z2.astype(jnp.bfloat16)
    grad_cross_all = join_tokens(grad_cross_out).reshape(count, width)
    cross_out_grad = product_t(crossed, grad_cross_all)
    grad_crossed = product_nt(grad_cross_all, attention_out[1]).astype(jnp.bfloat16)
    grad_qc, grad_kc, grad_vc = attend_backward(
        heads(q_cross, length),
        heads(k_cross, patch_count),
        heads(v_cross, patch_count),
        keep_cross,
        log_cross,
        heads(grad_crossed, length),
    )
    grad_qc = grad_qc.reshape(count, local_width)
    grad_kc = grad_kc.reshape(rows * patch_count, local_width)
    grad_vc = grad_vc.reshape(rows * patch_count, local_width)
    cross_in_grad = jnp.stack(
        [
            product_t(self_low, grad_qc),
            product_t(flat_patch, grad_kc),
            product_t(flat_patch, grad_vc),
        ]
    )
    cross_bias_grad = jnp.stack(
        [jnp.sum(grad_qc.astype(jnp.float32), axis=0), jnp.sum(grad_vc.astype(jnp.float32), axis=0)]
    )
    self_part = product_nt(grad_qc, cross_w[0]).reshape(rows, length, width)
    patch_part = (product_nt(grad_kc, cross_w[1]) + product_nt(grad_vc, cross_w[2])).reshape(
        rows, patch_count, width
    )
    self_mine, patch_mine = (
        lax.psum_scatter(
            self_part.astype(jnp.bfloat16), "mp", scatter_dimension=1, tiled=True
        ).astype(jnp.float32),
        lax.psum_scatter(
            patch_part.astype(jnp.bfloat16), "mp", scatter_dimension=2, tiled=True
        ).astype(jnp.float32),
    )
    row_patch_grad = patch_mine.astype(jnp.bfloat16)
    grad_z1, gain_first, shift_first = norm_backward(
        z_one, norm_gain[0], norm_bias[0], grad_z2 + self_mine
    )
    grad_self_out = grad_z1.astype(jnp.bfloat16)
    grad_self_all = join_tokens(grad_self_out).reshape(count, width)
    self_out_grad = product_t(attended, grad_self_all)
    grad_attended = product_nt(grad_self_all, attention_out[0]).astype(jnp.bfloat16)
    grad_q, grad_k, grad_v = attend_backward(
        heads(q, length),
        heads(k, length),
        heads(v, length),
        keep_self,
        log_self,
        heads(grad_attended, length),
    )
    grad_q = grad_q.reshape(count, local_width)
    grad_k = grad_k.reshape(count, local_width)
    grad_v = grad_v.reshape(count, local_width)
    self_in_grad = jnp.stack(
        [product_t(flat_x, grad_q), product_t(flat_x, grad_k), product_t(flat_x, grad_v)]
    )
    self_bias_grad = jnp.stack(
        [jnp.sum(grad_q.astype(jnp.float32), axis=0), jnp.sum(grad_v.astype(jnp.float32), axis=0)]
    )
    grad_input = (
        product_nt(grad_q, self_w[0])
        + product_nt(grad_k, self_w[1])
        + product_nt(grad_v, self_w[2])
    )
    text_grad_mine = (grad_z1 + split_sum(grad_input.reshape(rows, length, width))).astype(
        jnp.bfloat16
    )
    grads = (
        jnp.stack([self_in_grad, cross_in_grad]),
        jnp.stack([self_bias_grad, cross_bias_grad]),
        jnp.stack([self_out_grad, cross_out_grad]),
        jnp.stack([token_sum(grad_self_out), token_sum(grad_cross_out), token_sum(grad_ffn)]),
        jnp.stack([gain_first, gain_mid, gain_last]),
        jnp.stack([shift_first, shift_mid, shift_last]),
        up_grad,
        up_bias_grad,
        down_grad,
    )
    return (merged_mine, text_grad_mine, row_patch_grad, grads)


def body(
    text,
    cotangent,
    lengths,
    box_corners,
    box_counts,
    region_box,
    patches,
    proj_weight,
    proj_bias,
    attention_in,
    attention_bias,
    attention_out,
    output_bias,
    norm_gain,
    norm_bias,
    up_weight,
    up_bias,
    down_weight,
):
    rows, length, width = text.shape
    images, patch_count, vision = patches.shape
    devices = lax.axis_size("dp")
    pair = -(-rows // devices)
    slots = devices * pair
    tokens_mine = length // lax.axis_size("mp")
    offset = lax.axis_index("mp") * tokens_mine
    local_width = attention_in.shape[-1]
    order = jnp.arange(rows, dtype=jnp.int32)
    image_ids = jnp.arange(images, dtype=jnp.int32)
    target_dev = region_box // rows
    earlier = (target_dev[:, None] == target_dev[None, :]) & (order[None, :] < order[:, None])
    send_slot = target_dev * pair + jnp.sum(earlier.astype(jnp.int32), axis=1)
    slot_source = jnp.full((slots,), rows, jnp.int32).at[send_slot].set(order)
    meta = jnp.concatenate([(region_box % rows)[:, None], lengths[:, None], box_corners], axis=1)
    meta_pad = jnp.concatenate([meta, jnp.array([[rows, 1, 0, 1, 0, 1]], jnp.int32)], axis=0)
    arrived = lax.all_to_all(meta_pad[slot_source], "dp", split_axis=0, concat_axis=0, tiled=True)
    ends = jnp.cumsum(box_counts[0])
    box_image = jnp.sum((ends[None, :] <= order[:, None]).astype(jnp.int32), axis=1)
    projected = (
        product(patches.reshape(images * patch_count, vision), proj_weight) + proj_bias
    ).astype(jnp.bfloat16)
    projected = projected.reshape(images, patch_count, width)
    weights = (
        attention_in,
        attention_bias,
        attention_out,
        output_bias,
        norm_gain,
        norm_bias,
        up_weight,
        up_bias,
        down_weight,
    )
    wanted_image = jnp.concatenate([box_image, jnp.array([images], jnp.int32)], axis=0)[
        arrived[:, 0]
    ]
    projected_pad = jnp.concatenate(
        [projected, jnp.zeros((1, patch_count, width), jnp.bfloat16)], axis=0
    )
    fetched = lax.all_to_all(
        projected_pad[wanted_image], "dp", split_axis=0, concat_axis=0, tiled=True
    )
    patch_rows = fetched[send_slot]
    merged_text, text_grad, row_patch_grad, grads = layer_local(
        text, cotangent, lengths, box_corners, patch_rows, *weights, offset, tokens_mine
    )
    grad_pad = jnp.concatenate(
        [row_patch_grad, jnp.zeros((1, patch_count, local_width), jnp.bfloat16)], axis=0
    )
    returned = lax.all_to_all(grad_pad[slot_source], "dp", split_axis=0, concat_axis=0, tiled=True)
    image_onehot = (wanted_image[None, :] == image_ids[:, None]).astype(jnp.bfloat16)
    image_grad = jnp.einsum(
        "is,spd->ipd", image_onehot, returned, preferred_element_type=jnp.float32
    ).astype(jnp.bfloat16)
    weight_cols = lax.dynamic_slice_in_dim(
        proj_weight, lax.axis_index("mp") * local_width, local_width, 1
    )
    flat_grad = image_grad.reshape(images * patch_count, local_width)
    raw_part = product_nt(flat_grad, weight_cols).reshape(images, patch_count, vision)
    patch_grad = lax.psum_scatter(
        raw_part.astype(jnp.bfloat16), "mp", scatter_dimension=0, tiled=True
    )
    proj_weight_mine = product_t(patches.reshape(images * patch_count, vision), flat_grad)
    proj_bias_mine = jnp.sum(flat_grad.astype(jnp.float32), axis=0)
    (
        in_grad,
        bias_grad,
        out_grad,
        out_bias_grad,
        gain_grad,
        shift_grad,
        up_grad,
        up_bias_grad,
        down_grad,
    ) = grads
    summed = (
        lax.psum_scatter(in_grad, "dp", scatter_dimension=2, tiled=True),
        lax.psum_scatter(out_grad, "dp", scatter_dimension=2, tiled=True),
        lax.psum_scatter(up_grad, "dp", scatter_dimension=0, tiled=True),
        lax.psum_scatter(down_grad, "dp", scatter_dimension=1, tiled=True),
        lax.psum_scatter(proj_weight_mine, "dp", scatter_dimension=0, tiled=True),
    )
    small = lax.psum((bias_grad, up_bias_grad, proj_bias_mine), "dp")
    shared = lax.psum((out_bias_grad, gain_grad, shift_grad), ("dp", "mp"))
    return (
        merged_text,
        text_grad,
        patch_grad,
        summed[4],
        small[2],
        summed[0],
        small[0],
        summed[1],
        shared[0],
        shared[1],
        shared[2],
        summed[2],
        small[1],
        summed[3],
    )


def solution(mesh):
    placed = (
        P("dp", None, None),
        P("dp", None, None),
        P("dp"),
        P("dp", None),
        P("dp", None),
        P("dp"),
        P("dp", None, None),
        P(),
        P(),
        P(None, None, None, "mp"),
        P(None, None, "mp"),
        P(None, "mp", None),
        P(),
        P(),
        P(),
        P(None, "mp"),
        P("mp"),
        P("mp", None),
    )
    return jax.shard_map(
        body,
        mesh=mesh,
        in_specs=placed,
        out_specs=(
            P("dp", "mp", None),
            P("dp", "mp", None),
            P(("dp", "mp"), None, None),
            P("dp", "mp"),
            P("mp"),
            P(None, None, "dp", "mp"),
            P(None, None, "mp"),
            P(None, "mp", "dp"),
            P(),
            P(),
            P(),
            P("dp", "mp"),
            P("mp"),
            P("mp", "dp"),
        ),
        check_vma=False,
    )
```

profile of v0, /device:TPU:0, one launch (start us, length us, event | category | flops | bytes accessed | tf_op | source)
XLA Modules:
  0.0 2043.4 jit_solution(15591238528609804390)
XLA Ops:
  11.1 8.3 all-to-all-start
  21.2 7.2 copy.243
  51.4 9.2 gather_fusion.2
  60.7 6.9 all-to-all-start.1
  126.8 11.3 reduce-scatter.16.cloned.1.call-done
  144.5 13.0 all-gather.6.cloned.1.call-done
  171.4 105.9 %all-to-all-done.1 = bf16[48,145,768]{2,1,0:T(8,128)(2,1)} async-done(((bf16[48,145,768]{2,1,0:T(8,128)(2,1)}), bf16[48,145,768]{2,1,0:T(8,128)(2,1)}, u32[]{:S(2)}, u32[]{:S(2)}) %all-to-all-start.1) | async-done | bytes 10690592 | tf_op jit(solution)/shard_map/all_to_all | solution.py:333
  277.3 11.3 gather_fusion.3
  288.6 10.5 reshape.489
  299.1 11.0 convolution_convert_fusion
  310.1 8.6 add_convert_fusion.2
  318.7 16.9 reshape.580
  335.7 16.1 copy.253
  351.8 16.9 reshape.579
  368.7 16.5 copy.254
  385.2 12.0 fusion.9
  397.3 6.9 exponential_reduce_fusion
  404.3 8.9 convert_bitcast_fusion.6
  429.4 58.0 %reduce-scatter.18.cloned.1.call-done = f32[48,20,768]{2,0,1:T(8,128)} async-done(((f32[48,40,768]{2,0,1:T(8,128)}), f32[48,20,768]{2,0,1:T(8,128)}) %reduce-scatter.18.cloned.1.call-update) | async-done | bytes 2949136 | tf_op jit(solution)/shard_map/reduce_scatter | solution.py:44
  494.5 13.2 all-gather.8.cloned.1.call-done
  510.7 31.1 %multiply_convert_fusion.1 = (bf16[1920,1536]{1,0:T(8,128)(2,1)S(1)}, f32[1920,1536]{1,0:T(8,128)}, f32[1920,1536]{1,0:T(8,128)}) fusion(f32[1536]{0:T(1024)S(1)} %copy-done.82, bf16[1920,768]{1,0:T(8,128)(2,1)S(1)} %bitcast.214, bf16[768,1536]{1,0:T(8,128)(2,1)S(1)} %copy-done.78), kind=kOutput, calls=%fused_computation.17 | convolution fusion | flops 4724490240 | bytes 34805760 | tf_op jit(solution)/shard_map/dot_general | solution.py:28
  555.0 11.4 reduce-scatter.20.cloned.1.call-done
  577.2 13.2 all-gather.10.cloned.1.call-done
  593.4 16.8 convert_reduce_fusion.1
  610.1 6.8 fusion.191
  621.3 15.2 reduce-scatter.22.cloned.1.call-done
  636.6 7.3 multiply_reduce_fusion.2
  649.1 13.0 all-gather.12.cloned.1.call-done
  675.0 11.2 fusion.79
  686.2 79.2 %convert_reduce_fusion.2 = (f32[6,64]{1,0:T(8,128)}, bf16[48,40,6,64]{3,1,2,0:T(8,128)(2,1)}) fusion(bf16[48,145,6,64]{1,3,2,0:T(8,128)(2,1)} %copy.253, f32[48,6,40,145]{3,2,1,0:T(8,128)} %fusion.79, f32[48,6,40,145]{3,2,1,0:T(8,128)} %get-tuple-element.147, f32[48,6,40]{2,1,0:T(8,128)S(1)} %copy-done.36, pred[48,145]{1,0:T(8,128)(4,1)S(1)} %copy-done.42), kind=kOutput, calls=%fused_computation.43 | convolution fusion | flops 234408720 | bytes 20237616 | tf_op jit(solution)/shard_map/rhqk,rkhe->rqhe/dot_general | solution.py:88
  770.1 6.1 dot_general.176
  781.7 80.7 %convert_bitcast_fusion.1 = bf16[48,145,6,64]{1,3,2,0:T(8,128)(2,1)} fusion(f32[48,6,40,145]{3,2,1,0:T(8,128)} %fusion.79, f32[48,6,40,145]{3,2,1,0:T(8,128)} %get-tuple-element.147, f32[48,6,40]{2,1,0:T(8,128)S(1)} %copy-done.36, pred[48,145]{1,0:T(8,128)(4,1)S(1)} %copy-done.42, bf16[48,40,6,64]{3,2,1,0:T(8,128)(2,1)} %reshape.492), kind=kOutput, calls=%fused_computation.37 | convolution fusion | flops 234869904 | bytes 20236080 | tf_op jit(solution)/shard_map/rhqk,rqhe->rkhe/dot_general | solution.py:91
  862.4 12.9 copy.280
  875.3 15.2 reshape.506
  890.5 11.3 convert_reduce_fusion
  901.8 13.0 copy.282
  914.8 15.2 reshape.507
  940.7 13.4 fusion.101
  954.1 18.5 add_convert_fusion
  972.6 10.6 convert_element_type.226
  983.2 26.1 %copy.310 = bf16[48,145,768]{1,0,2:T(8,128)(2,1)} copy(bf16[48,145,768]{2,1,0:T(8,128)(2,1)} %convert_element_type.226) | data formatting | bytes 21381120
  1009.3 28.9 %reshape.573 = bf16[768,6960]{1,0:T(8,128)(2,1)} reshape(bf16[768,48,145]{2,1,0:T(8,128)(2,1)} %bitcast.205) | data formatting | bytes 21381120
  1043.1 6.4 reshape.509
  1055.6 6.1 reshape.510
  1071.5 9.5 convolution_bitcast_fusion.2
  1114.0 7.6 fusion.76
  1121.5 14.4 convert_bitcast_fusion.3
  1146.6 15.4 convert_reduce_fusion.4
  1198.8 13.6 copy.289
  1226.6 29.0 %reshape.574 = bf16[384,48,145]{2,1,0:T(8,128)(2,1)} reshape(bf16[384,6960]{1,0:T(8,128)(2,1)} %reduce-scatter.34.cloned.1.call-done) | data formatting | bytes 10690560
  1255.6 12.5 copy.311
  1273.8 7.2 gather_fusion.4
  1281.0 6.9 all-to-all-start.2
  1288.1 129.7 %all-to-all-done.2 = bf16[48,145,384]{2,1,0:T(8,128)(2,1)} async-done(((bf16[48,145,384]{2,1,0:T(8,128)(2,1)}), bf16[48,145,384]{2,1,0:T(8,128)(2,1)}, u32[]{:S(2)}, u32[]{:S(2)}) %all-to-all-start.2) | async-done | bytes 5345312 | tf_op jit(solution)/shard_map/all_to_all | solution.py:343
  1427.2 9.9 fusion.193
  1437.2 9.7 fusion.192
  1447.0 6.3 convolution_bitcast_fusion
  1458.3 73.6 %all-reduce.4 = (f32[3,768]{1,0:T(4,128)}, f32[3,768]{1,0:T(4,128)}, f32[3,768]{1,0:T(4,128)}) all-reduce(f32[3,768]{1,0:T(4,128)S(1)} %pad_maximum_fusion.2, f32[3,768]{1,0:T(4,128)S(1)} %pad_maximum_fusion.3, f32[3,768]{1,0:T(4,128)S(1)} %pad_maximum_fusion.4), channel_id=1, replica_groups=mesh['dp'=16,'mp'=2] {'dp','mp'}, use_global_device_ids=true, to_apply=%region_43.44 | all-reduce | flops 6912 | bytes 55296 | tf_op jit(solution)/shard_map/psum | solution.py:377
  1532.1 57.5 %all-reduce.9.cloned.1.call-done = (f32[2,3,768,384]{3,0,1,2:T(2,128)}, f32[2,384,768]{1,0,2:T(2,128)}) async-done(((f32[2,3,768,384]{3,0,1,2:T(2,128)}, f32[2,384,768]{1,0,2:T(2,128)}), (f32[2,3,768,384]{3,0,1,2:T(2,128)}, f32[2,384,768]{1,0,2:T(2,128)})) %all-reduce.9.cloned.1.call-update) | async-done | bytes 9437200
  1593.1 11.7 reduce-scatter.26.cloned.1.call-done
  1609.0 77.4 %all-reduce.5 = (f32[384]{0:T(512)}, f32[2,2,384]{2,1,0:T(2,128)}, f32[1536]{0:T(1024)}) all-reduce(f32[384]{0:T(512)S(1)} %get-tuple-element.149, f32[2,2,384]{2,1,0:T(2,128)S(1)} %pad_maximum_fusion.5, f32[1536]{0:T(1024)S(1)} %copy-done.66), channel_id=1, replica_groups=mesh['dp'=16,'mp'=2] {'dp'}, use_global_device_ids=true, to_apply=%region_32.33 | all-reduce | flops 3456 | bytes 27648 | tf_op jit(solution)/shard_map/psum | solution.py:376
  1690.8 74.3 %reduce-scatter.32.cloned.1.call-done = f32[1536,48]{0,1:T(8,128)} async-done(((f32[1536,768]{0,1:T(8,128)}), f32[1536,48]{0,1:T(8,128)}) %reduce-scatter.32.cloned.1.call-update) | async-done | bytes 294928 | tf_op jit(solution)/shard_map/reduce_scatter | solution.py:373
  1765.1 142.8 %reduce-scatter.30.cloned.1.call-done = f32[48,1536]{1,0:T(8,128)} async-done(((f32[768,1536]{1,0:T(8,128)}), f32[48,1536]{1,0:T(8,128)}) %reduce-scatter.30.cloned.1.call-update) | async-done | bytes 294928 | tf_op jit(solution)/shard_map/reduce_scatter | solution.py:372
  1907.9 128.7 %reduce-scatter.36.cloned.1.call-done = f32[64,384]{1,0:T(8,128)} async-done(((f32[1024,384]{1,0:T(8,128)}), f32[64,384]{1,0:T(8,128)}) %reduce-scatter.36.cloned.1.call-update) | async-done | bytes 98320
  (379 shorter events, 351.0 us)
Async XLA Ops:
  7.2 25.9 %copy-start = (bf16[48,40,768]{2,1,0:T(8,128)(2,1)S(1)}, bf16[48,40,768]{2,1,0:T(8,128)(2,1)}, u32[]{:S(2)}) copy-start(bf16[48,40,768]{2,1,0:T(8,128)(2,1)} %param.20) | copy-start | bytes 8847364
  9.0 19.4 copy-start.71
  11.1 39.4 %all-to-all-start = ((s32[16,3,6]{2,1,0:T(4,128)}), s32[16,3,6]{2,1,0:T(4,128)S(1)}, u32[]{:S(2)}, u32[]{:S(2)}) async-start(s32[16,3,6]{2,1,0:T(4,128)} %reshape.570), calls=%async_computation.1 | async-start | bytes 65536 | tf_op jit(solution)/shard_map/all_to_all | solution.py:309
  51.4 9.3 copy-start.74
  60.7 216.6 %all-to-all-start.1 = ((bf16[48,145,768]{2,1,0:T(8,128)(2,1)}), bf16[48,145,768]{2,1,0:T(8,128)(2,1)}, u32[]{:S(2)}, u32[]{:S(2)}) async-start(bf16[48,145,768]{2,1,0:T(8,128)(2,1)} %gather_fusion.2), calls=%async_computation.2 | async-start | bytes 22413312 | tf_op jit(solution)/shard_map/all_to_all | solution.py:333
  67.7 70.5 %reduce-scatter.16.cloned.1.call-start = ((), (), s32[]{:S(2)}) async-start(), calls=%async_computation.14 | async-start | bytes 8847360 | tf_op jit(solution)/shard_map/reduce_scatter | solution.py:44
  87.2 5.7 copy-start.73
  92.9 7.7 copy-start.52
  122.8 34.8 %all-gather.6.cloned.1.call-start = ((), (), s32[]{:S(2)}) async-start(), calls=%async_computation.15 | async-start | bytes 4423680 | tf_op jit(solution)/shard_map/all_gather | solution.py:48
  124.7 362.7 %copy-start.49 = (f32[768]{0:T(1024)}, f32[768]{0:T(1024)S(1)}, u32[]{:S(2)}) copy-start(f32[768]{0:T(1024)S(1)} %get-tuple-element.96) | copy-start | bytes 9220
  141.1 346.4 %copy-start.37 = (f32[48,20]{0,1:T(8,128)}, f32[48,20]{0,1:T(8,128)S(1)}, u32[]{:S(2)}) copy-start(f32[48,20]{0,1:T(8,128)S(1)} %broadcast_multiply_fusion.2) | copy-start | bytes 11524
  142.5 345.0 %copy-start.39 = (f32[48,20]{0,1:T(8,128)}, f32[48,20]{0,1:T(8,128)S(1)}, u32[]{:S(2)}) copy-start(f32[48,20]{0,1:T(8,128)S(1)} %fusion.137) | copy-start | bytes 11524
  144.3 343.1 %reduce-scatter.18.cloned.1.call-start = ((), (), s32[]{:S(2)}) async-start(), calls=%async_computation.16 | async-start | bytes 8847360 | tf_op jit(solution)/shard_map/reduce_scatter | solution.py:44
  144.5 259.7 %copy-start.41 = (pred[48,145]{1,0:T(8,128)(4,1)}, pred[48,145]{1,0:T(8,128)(4,1)S(1)}, u32[]{:S(2)}) copy-start(pred[48,145]{1,0:T(8,128)(4,1)S(1)} %and_or_fusion) | copy-start | bytes 20884
  299.1 11.0 copy-start.15
  404.3 8.9 copy-start.35
  429.4 78.4 %all-gather.8.cloned.1.call-start = ((), (), s32[]{:S(2)}) async-start(), calls=%async_computation.17 | async-start | bytes 4423680 | tf_op jit(solution)/shard_map/all_gather | solution.py:48
  491.7 19.0 copy-start.45
  494.5 16.2 copy-start.82
  494.5 72.0 %reduce-scatter.20.cloned.1.call-start = ((), (), s32[]{:S(2)}) async-start(), calls=%async_computation.18 | async-start | bytes 8847360 | tf_op jit(solution)/shard_map/reduce_scatter | solution.py:44
  510.7 31.2 %copy-start.22 = (bf16[48,40,768]{2,1,0:T(8,128)(2,1)}, bf16[48,40,768]{2,1,0:T(8,128)(2,1)S(1)}, u32[]{:S(2)}) copy-start(bf16[48,40,768]{2,1,0:T(8,128)(2,1)S(1)} %copy.257) | copy-start | bytes 8847364
  510.7 31.2 %copy-start.76 = (bf16[1536,768]{1,0:T(8,128)(2,1)S(1)}, bf16[1536,768]{1,0:T(8,128)(2,1)}, u32[]{:S(2)}) copy-start(bf16[1536,768]{1,0:T(8,128)(2,1)} %param.37) | copy-start | bytes 7077892
  541.9 4.8 copy-start.85
  551.2 15.3 copy-start.60
  551.2 39.2 %all-gather.10.cloned.1.call-start = ((), (), s32[]{:S(2)}) async-start(), calls=%async_computation.19 | async-start | bytes 4423680 | tf_op jit(solution)/shard_map/all_gather | solution.py:48
  577.1 59.4 %reduce-scatter.22.cloned.1.call-start = ((), (), s32[]{:S(2)}) async-start(), calls=%async_computation.20 | async-start | bytes 8847360 | tf_op jit(solution)/shard_map/reduce_scatter | solution.py:44
  593.3 16.8 copy-start.23
  593.3 16.8 copy-start.79
  621.3 15.3 copy-start.59
  621.3 40.8 %all-gather.12.cloned.1.call-start = ((), (), s32[]{:S(2)}) async-start(), calls=%async_computation.21 | async-start | bytes 4423680 | tf_op jit(solution)/shard_map/all_gather | solution.py:48
  636.6 7.3 copy-start.46
  636.6 7.4 copy-start.4
  648.8 281.2 %reduce-scatter.24.cloned.1.call-start = ((), (), s32[]{:S(2)}) async-start(), calls=%async_computation.22 | async-start | bytes 4423680 | tf_op jit(solution)/shard_map/reduce_scatter | solution.py:219
  675.0 11.2 copy-start.36
  675.0 11.2 copy-start.42
  781.7 309.8 %all-gather.14.cloned.1.call-start = ((), (), s32[]{:S(2)}) async-start(), calls=%async_computation.23 | async-start | bytes 4423680 | tf_op jit(solution)/shard_map/all_gather | solution.py:48
  914.8 15.2 copy-start.38
  914.8 15.3 copy-start.40
  914.8 15.3 copy-start.50
  930.1 4.9 copy-start.7
  930.1 5.3 copy-start.18
  940.6 286.0 %reduce-scatter.34.cloned.1.call-start = ((), (), s32[]{:S(2)}) async-start(), calls=%async_computation.28 | async-start | bytes 16220160
  1038.2 551.4 %all-reduce.9.cloned.1.call-start = ((), (), s32[]{:S(2)}) async-start(), calls=%async_computation.30 | async-start | bytes 18874368
  1067.6 13.4 slice-start
  1067.6 13.4 slice-start.2
  1071.5 9.5 slice-start.1
  1071.5 9.5 slice-start.3
  1071.5 9.5 slice-start.4
  1113.9 7.6 copy-start.34
  1113.9 7.6 copy-start.53
  1212.4 392.4 %reduce-scatter.26.cloned.1.call-start = ((), (), s32[]{:S(2)}) async-start(), calls=%async_computation.24 | async-start | bytes 8847360 | tf_op jit(solution)/shard_map/reduce_scatter | solution.py:44
  1281.0 136.9 %copy-start.75 = (s32[48]{0:T(128)S(1)}, s32[48]{0:T(128)}, u32[]{:S(2)}) copy-start(s32[48]{0:T(128)} %copy-done.74) | copy-start | bytes 580
  1281.0 136.9 %all-to-all-start.2 = ((bf16[48,145,384]{2,1,0:T(8,128)(2,1)}), bf16[48,145,384]{2,1,0:T(8,128)(2,1)}, u32[]{:S(2)}, u32[]{:S(2)}) async-start(bf16[48,145,384]{2,1,0:T(8,128)(2,1)} %gather_fusion.4), calls=%async_computation.8 | async-start | bytes 11206656 | tf_op jit(solution)/shard_map/all_to_all | solution.py:343
  1287.8 398.6 %reduce-scatter.28.cloned.1.call-start = ((), (), s32[]{:S(2)}) async-start(), calls=%async_computation.25 | async-start | bytes 7471104 | tf_op jit(solution)/shard_map/reduce_scatter | solution.py:353
  1417.8 4.8 copy-start.81
  1427.2 338.0 %reduce-scatter.32.cloned.1.call-start = ((), (), s32[]{:S(2)}) async-start(), calls=%async_computation.27 | async-start | bytes 5013504 | tf_op jit(solution)/shard_map/reduce_scatter | solution.py:373
  1437.2 470.8 %reduce-scatter.30.cloned.1.call-start = ((), (), s32[]{:S(2)}) async-start(), calls=%async_computation.26 | async-start | bytes 5013504 | tf_op jit(solution)/shard_map/reduce_scatter | solution.py:372
  1446.9 589.8 %reduce-scatter.36.cloned.1.call-start = ((), (), s32[]{:S(2)}) async-start(), calls=%async_computation.29 | async-start | bytes 1671168
  1453.3 4.8 copy-start.72
  1453.3 4.9 copy-start.58
  1453.3 4.9 copy-start.57
  1453.3 4.9 copy-start.64
  1453.4 151.5 %copy-start.48 = (f32[48,20]{0,1:T(8,128)S(1)}, f32[48,20]{0,1:T(8,128)}, u32[]{:S(2)}) copy-start(f32[48,20]{0,1:T(8,128)} %copy-done.47) | copy-start | bytes 11524
  1593.1 15.8 copy-start.66
  (47 other events, 141.0 us)
Sparse Core Ops, SparseCore 0:
  122.9 15.1 reduce-scatter.15
  144.4 13.0 all-gather.5
  429.5 57.9 reduce-scatter.17
  494.6 13.0 all-gather.7
  551.3 15.0 reduce-scatter.19
  577.3 13.0 all-gather.9
  621.4 15.1 reduce-scatter.21
  649.0 13.0 all-gather.11
  781.8 11.7 reduce-scatter.23
  940.7 12.9 all-gather.13
  1038.3 20.5 reduce-scatter.33
  1212.6 376.9 all-reduce.8
  1591.9 12.8 reduce-scatter.25
  1607.1 14.1 reduce-scatter.27
  1626.9 138.2 reduce-scatter.31
  1771.6 136.3 reduce-scatter.29
  1913.1 123.4 reduce-scatter.35
where the time goes:
time: 2060 us; the launch traced here: 2040 us
  waiting for transfers between devices  799 us (39%)
  local copies, waits for them, and re-layouts  509 us (25%)
  matrix products  481 us (23%)
  blocking collectives  151 us (7%)
  other arithmetic  63.4 us (3%)
  starting transfers between devices  23.8 us (1%)
    unnamed x20, waiting for transfers between devices  187 us
    reduce_scatter x1, waiting for transfers between devices, body(): lax.psum_scatter(up_grad, 'dp', scatter_dimension=0, tiled=True)  143 us
    unnamed x195, local copies, waits for them, and re-layouts  136 us
    all_to_all x1, waiting for transfers between devices, body(): lax.all_to_all(grad_pad[slot_source], 'dp', split_axis=0, concat_axis=0,...  130 us
    reduce_scatter x5, waiting for transfers between devices, split_sum(): return lax.psum_scatter(partial_sum, 'mp', scatter_dimension=1, tiled=True)  108 us
    all_to_all x1, waiting for transfers between devices, body(): lax.all_to_all(projected_pad[wanted_image], 'dp', split_axis=0, concat_ax...  106 us
    reshape x10, local copies, waits for them, and re-layouts, heads(): return tensor.reshape(rows, steps, heads_mine, HEAD_DIM)  101 us
    dot_general x2, matrix products, attend_backward(): jnp.einsum('rhqk,rqhe->rkhe', grad_scores, q, preferred_element_type=jnp....  95 us
  transfers between devices with their start and end apart: 20, of which 15 were waited for; matrix products, arithmetic and copies ran while one was open for 31% of the time, Pallas kernels for 0%

commit v1 on v0

v1 whole, which is shorter than its diff:
```python
import math
from functools import partial

import jax
import jax.numpy as jnp
from jax import lax
from jax.experimental import pallas as pl
from jax.experimental.pallas import tpu as pltpu
from jax.sharding import PartitionSpec as P

HEAD_DIM = 64
GRID = 12
EPS = 1e-12
NEG = -1e30
SCALE = HEAD_DIM ** (-0.5)

F32 = jnp.float32
BF16 = jnp.bfloat16

GROUP = 4 * HEAD_DIM
BAND = 32
BANDS = 5
LANES = 128
TILE = 256
PAIRED = 2
VMEM_LIMIT = 58 << 20


def dot(left, right):
    return lax.dot_general(left, right, (((1,), (0,)), ((), ())), preferred_element_type=F32)


def dot_nt(left, right):
    return lax.dot_general(left, right, (((1,), (1,)), ((), ())), preferred_element_type=F32)


def dot_tn(left, right):
    return lax.dot_general(left, right, (((0,), (0,)), ((), ())), preferred_element_type=F32)


def rows_spec(block, offset):
    rank = len(block)
    return pl.BlockSpec(block, lambda s, *_: (s + offset,) + (0,) * (rank - 1))


def whole_spec(shape):
    rank = len(shape)
    return pl.BlockSpec(shape, lambda s, *_: (0,) * rank, pipeline_mode=pl.Buffered(1))


ANY = pl.BlockSpec(memory_space=pl.ANY)


def run(body, steps, scalars, ins, outs, scratch, flops, after=()):
    ns, ni, no = len(scalars), len(ins), len(outs)

    def kernel(*refs):
        rest = refs[ns + ni + len(after) :]
        body(refs[:ns], refs[ns : ns + ni], rest[:no], rest[no:])

    moved = sum(math.prod(a.shape) * a.dtype.itemsize for a, _ in ins)
    ins = list(ins) + [(array, ANY) for array in after]
    moved += sum(math.prod(shape) * jnp.dtype(dtype).itemsize for shape, dtype, _ in outs)
    return pl.pallas_call(
        kernel,
        grid_spec=pltpu.PrefetchScalarGridSpec(
            num_scalar_prefetch=ns,
            grid=(steps,),
            in_specs=[spec for _, spec in ins],
            out_specs=[spec for _, _, spec in outs],
            scratch_shapes=scratch,
        ),
        out_shape=[jax.ShapeDtypeStruct(shape, dtype) for shape, dtype, _ in outs],
        compiler_params=pltpu.CompilerParams(
            dimension_semantics=("arbitrary",), vmem_limit_bytes=VMEM_LIMIT
        ),
        cost_estimate=pl.CostEstimate(flops=flops, bytes_accessed=moved, transcendentals=0),
    )(*scalars, *[array for array, _ in ins])


class Loads:
    def __init__(self, steps, sems, pairs):
        self.steps = steps
        self.copies = [
            pltpu.make_async_copy(source, target, sems.at[at])
            for at, (source, target) in enumerate(pairs)
        ]

    def first(self, action):
        if self.steps == 1:
            action()
        else:
            pl.when(pl.program_id(0) == 0)(action)

    def start(self):
        self.first(lambda: [copy.start() for copy in self.copies] and None)

    def wait(self, *which):
        self.first(lambda: [self.copies[at].wait() for at in which] and None)


def side_by_side(own, mate, target, width):
    return [(own, target.at[:, pl.ds(0, width)]), (mate, target.at[:, pl.ds(width, width)])]


def one_above(own, mate, target, height):
    return [(own, target.at[pl.ds(0, height)]), (mate, target.at[pl.ds(height, height)])]


def moments(z):
    center = z - jnp.mean(z, axis=-1, keepdims=True)
    rstd = lax.rsqrt(jnp.mean(center * center, axis=-1, keepdims=True) + EPS)
    return center * rstd, rstd


def norm_grad(unit, rstd, gain, grad):
    inner = grad * gain
    return rstd * (
        inner
        - jnp.mean(inner, axis=-1, keepdims=True)
        - unit * jnp.mean(inner * unit, axis=-1, keepdims=True)
    )


def fold(block):
    return jnp.sum(block.reshape(block.shape[0] // 8, 8, block.shape[1]), axis=0)


def gelu(u):
    z = jnp.abs(u) * (0.5**0.5)
    bell = jnp.exp(u * u * -0.5)
    t = 1.0 / (1.0 + 0.3275911 * z)
    poly = t * (
        0.5 * 0.254829592
        + t
        * (
            0.5 * -0.284496736
            + t * (0.5 * 1.421413741 + t * (0.5 * -1.453152027 + t * (0.5 * 1.061405429)))
        )
    )
    tail = poly * bell
    phi = jnp.where(u >= 0.0, 1.0 - tail, tail)
    return u * phi, phi + u * (bell * (1.0 / math.sqrt(2.0 * math.pi)))


def spread_heads(block, lane_head):
    parts = [jnp.where(lane_head == h, block, 0.0) for h in range(GROUP // HEAD_DIM)]
    return jnp.concatenate(parts, axis=0).astype(BF16)


def gather_heads(block, lane_head, tokens):
    total = jnp.where(lane_head == 0, block[0:tokens], 0.0)
    for h in range(1, GROUP // HEAD_DIM):
        total = jnp.where(lane_head == h, block[h * tokens : (h + 1) * tokens], total)
    return total


def lane_heads():
    return lax.broadcasted_iota(jnp.int32, (1, GROUP), 1) // HEAD_DIM


def attend(items):
    scores = [dot_nt(qm, kb) for qm, kb, vb, keep in items]
    weights = []
    for score, (qm, kb, vb, keep) in zip(scores, items):
        score = jnp.where(keep, score, NEG)
        top = jnp.max(score, axis=1, keepdims=True)
        weight = jnp.exp(score - top)
        weight = weight * (1.0 / jnp.sum(weight, axis=1, keepdims=True))
        weights.append(weight.astype(BF16))
    return [dot(weight, vb) for weight, (qm, kb, vb, keep) in zip(weights, items)]


def attend_grad(items):
    scores = [dot_nt(kb, qm) for qm, kb, vb, dom, keep in items]
    grads = [dot_nt(vb, dom) for qm, kb, vb, dom, keep in items]
    middle = []
    for score, grad, (qm, kb, vb, dom, keep) in zip(scores, grads, items):
        score = jnp.where(keep, score, NEG)
        top = jnp.max(score, axis=0, keepdims=True)
        weight = jnp.exp(score - top)
        weight = weight * (1.0 / jnp.sum(weight, axis=0, keepdims=True))
        inner = jnp.sum(weight * grad, axis=0, keepdims=True)
        grad_score = weight * (grad - inner)
        middle.append(
            (weight.astype(BF16), grad_score.astype(BF16), jnp.transpose(grad_score).astype(BF16))
        )
    results = []
    for (weight, grad_score, turned), (qm, kb, vb, dom, keep) in zip(middle, items):
        results.append((dot(turned, kb), dot(grad_score, qm), dot(weight, dom)))
    return results


def box_keep(corners, slot, shape, axis):
    index = lax.broadcasted_iota(jnp.int32, shape, axis) - 1
    grid_row = (index * 2731) >> 15
    grid_col = index - grid_row * GRID
    inside = (grid_col >= corners[slot * 4]) & (grid_col < corners[slot * 4 + 1])
    inside = inside & (grid_row >= corners[slot * 4 + 2]) & (grid_row < corners[slot * 4 + 3])
    return (inside & (index >= 0)) | (index < 0)


def band_loop(total, body, part=None):
    @pl.loop(0, total // (BAND * BANDS))
    def _(step):
        sums = []
        for band in range(BANDS):
            start = pl.multiple_of(step * (BAND * BANDS) + band * BAND, BAND)
            folded = body(pl.ds(start, BAND))
            if folded is not None:
                sums.append(folded)
        for terms in zip(*sums):
            at = terms[0][0]
            part[at] += sum(value for _, value in terms[1:]) + terms[0][1]


def by_columns(left, weight, finish, transposed=False):
    count = weight.shape[0] if transposed else weight.shape[1]
    for start in range(0, count, GROUP):
        cols = slice(start, start + GROUP)
        value = dot_nt(left, weight[cols, :]) if transposed else dot(left, weight[:, cols])
        finish(cols, value)


def both_halves(own, mate, at):
    return jnp.concatenate([own[at[0], at[1] : at[1] + 1], mate[at[0], at[1] : at[1] + 1]], axis=1)


def row_pairs(source, where, first, count, length, finish):
    for at in range(0, count, 2):
        both = [source[where[first + at + n]].astype(F32) for n in range(2)]
        finish(slice(at * length, (at + 2) * length), jnp.concatenate(both, axis=0))


def split_lanes(target, rows, start, value):
    for lane in range(0, value.shape[1], LANES):
        target[(start + lane) // LANES, rows, :] = value[:, lane : lane + LANES]


def join_lanes(source, rows):
    return jnp.concatenate([source[lane, rows, :] for lane in range(source.shape[0])], axis=1)


def fetch_kernel(count, scalars, ins, outs, scratch):
    (source,) = scalars
    (sems,) = scratch
    copies = [
        pltpu.make_async_copy(table.at[source[at]], out.at[at], sems.at[which * count + at])
        for which, (table, out) in enumerate(zip(ins, outs))
        for at in range(count)
    ]
    for copy in copies:
        copy.start()
    for copy in copies:
        copy.wait()


def project_kernel(images, own_images, patch_pad, patch_count, local, scalars, ins, outs, scratch):
    (core,) = scalars
    patches, proj_weight, proj_bias, ain, ain_mate, bias_own, bias_mate = ins
    proj, keys, values = outs
    taken, raw, w1, w2, sems, weight_sems = scratch
    loads = Loads(
        1,
        weight_sems,
        side_by_side(ain.at[1, 1], ain_mate.at[1, 1], w1, local)
        + side_by_side(ain.at[1, 2], ain_mate.at[1, 2], w2, local),
    )
    parts, span = taken.shape[0], taken.shape[1]
    arrivals = Loads(
        1, sems, [(patches.at[pl.ds(n * span, span)], taken.at[n]) for n in range(parts)]
    )
    arrivals.start()
    loads.start()
    rows = span * images
    width = raw.shape[0] * LANES
    for n in range(parts):
        arrivals.wait(n)
        flat = taken[n].reshape(rows, taken.shape[3])
        for start in range(0, width, GROUP):
            cols = slice(start, start + GROUP)
            split_lanes(
                raw,
                slice(n * rows, (n + 1) * rows),
                start,
                dot(flat, proj_weight[:, cols]) + proj_bias[:, cols],
            )
    loads.wait(0, 1, 2, 3)
    bias = both_halves(bias_own, bias_mate, (1, 1))
    first = core[0] * own_images
    rest = jnp.zeros((patch_pad - patch_count, width), F32)

    @pl.loop(0, images // 2)
    def _(step):
        both = []
        for at in range(2):
            which = lax.rem(step * 2 + at + first, images)
            own = jnp.concatenate(
                [
                    raw[lane, pl.ds(which, patch_count, stride=images), :]
                    for lane in range(raw.shape[0])
                ],
                axis=1,
            )
            both.append(jnp.concatenate([own, rest], axis=0))
        low = jnp.concatenate(both, axis=0).astype(BF16)
        pair = pl.ds(step * 2, 2)
        proj[pair] = low.reshape(2, patch_pad, width)
        for start in range(0, width, GROUP):
            cols = slice(start, start + GROUP)
            keys[pair, :, cols] = (
                dot(low, w1[:, cols]).astype(BF16).reshape(2, patch_pad, GROUP)
            )
            values[pair, :, cols] = (
                (dot(low, w2[:, cols]) + bias[:, cols]).astype(BF16).reshape(2, patch_pad, GROUP)
            )


def self_kernel(steps, rows, local, length, scalars, ins, outs, scratch):
    lens, where = scalars
    x_in, ain, ain_mate, aout, aout_mate, bias_own, bias_mate, out_bias, gain, shift = ins
    x_out, z_one, q_out, k_out, v_out, att_own, att_mate, low_out, cross_q = outs
    wq, wk, wv, wo, wc, qs, ks, vs, acc, low, sems = scratch
    total = rows * length
    loads = Loads(
        steps,
        sems,
        side_by_side(ain.at[0, 0], ain_mate.at[0, 0], wq, local)
        + side_by_side(ain.at[0, 1], ain_mate.at[0, 1], wk, local)
        + side_by_side(ain.at[0, 2], ain_mate.at[0, 2], wv, local)
        + one_above(aout.at[0], aout_mate.at[0], wo, local)
        + side_by_side(ain.at[1, 0], ain_mate.at[1, 0], wc, local),
    )
    loads.start()
    bias_q = both_halves(bias_own, bias_mate, (0, 0))
    bias_v = both_halves(bias_own, bias_mate, (0, 1))
    bias_c = both_halves(bias_own, bias_mate, (1, 0))

    def put(at, both):
        x_out[at] = both.astype(BF16)

    base = pl.program_id(0) * rows
    row_pairs(x_in, where, base, rows, length, put)
    xb = x_out[...]

    def keep_q(cols, value):
        value = (value + bias_q[:, cols]).astype(BF16)
        q_out[:, cols] = value
        qs[:, cols] = value.astype(F32) * SCALE

    def keep_k(cols, value):
        value = value.astype(BF16)
        k_out[:, cols] = value
        ks[:, cols] = value.astype(F32)

    def keep_v(cols, value):
        value = (value + bias_v[:, cols]).astype(BF16)
        v_out[:, cols] = value
        vs[:, cols] = value.astype(F32)

    loads.wait(0, 1)
    by_columns(xb, wq, keep_q)
    loads.wait(2, 3)
    by_columns(xb, wk, keep_k)
    loads.wait(4, 5)
    by_columns(xb, wv, keep_v)
    lane_head = lane_heads()
    key_index = lax.broadcasted_iota(jnp.int32, (1, length), 1)

    @pl.loop(0, rows // PAIRED)
    def _(step):
        items, places = [], []
        for row in range(PAIRED):
            row = step * PAIRED + row
            at = pl.ds(pl.multiple_of(row * length, 8), length)
            keep = key_index < lens[base + row]
            for g in range(qs.shape[1] // GROUP):
                lanes = slice(g * GROUP, (g + 1) * GROUP)
                items.append(
                    (
                        spread_heads(qs[at, lanes], lane_head),
                        ks[at, lanes].astype(BF16),
                        vs[at, lanes].astype(BF16),
                        keep,
                    )
                )
                places.append((at, lanes))
        for (at, lanes), result in zip(places, attend(items)):
            acc[at, lanes] = gather_heads(result, lane_head, length)

    def cast(at):
        value = acc[at].astype(BF16)
        low[at] = value
        att_own[at] = value[:, :local]
        att_mate[at] = value[:, local:]

    def to_acc(cols, value):
        acc[:, cols] = value

    band_loop(total, cast)
    loads.wait(6, 7)
    by_columns(low[...], wo, to_acc)

    def norm(at):
        z = x_out[at].astype(F32) + acc[at] + out_bias[0:1]
        z_one[at] = z
        unit, _ = moments(z)
        h = (unit * gain[0:1] + shift[0:1]).astype(BF16)
        low[at] = h
        low_out[at] = h

    band_loop(total, norm)
    loads.wait(8, 9)

    def to_query(cols, value):
        cross_q[:, cols] = (value + bias_c[:, cols]).astype(BF16)

    by_columns(low[...], wc, to_query)


def cross_kernel(rows, length, scalars, ins, outs, scratch):
    image, corners = scalars
    queries, keys, values = ins
    (att,) = outs
    qs, acc = scratch
    patch_pad = keys.shape[1]
    lane_head = lane_heads()
    base = pl.program_id(0) * rows

    def spread(at):
        qs[at] = queries[at].astype(F32) * SCALE

    band_loop(rows * length, spread)

    @pl.loop(0, rows // PAIRED)
    def _(step):
        items, places = [], []
        for row in range(PAIRED):
            row = step * PAIRED + row
            at = pl.ds(pl.multiple_of(row * length, 8), length)
            which = image[base + row]
            keep = box_keep(corners, base + row, (1, patch_pad), 1)
            for g in range(qs.shape[1] // GROUP):
                lanes = slice(g * GROUP, (g + 1) * GROUP)
                items.append(
                    (
                        spread_heads(qs[at, lanes], lane_head),
                        keys[which, :, lanes],
                        values[which, :, lanes],
                        keep,
                    )
                )
                places.append((at, lanes))
        for (at, lanes), result in zip(places, attend(items)):
            acc[at, lanes] = gather_heads(result, lane_head, length)

    def cast(at):
        att[at] = acc[at].astype(BF16)

    band_loop(rows * length, cast)


def feed_kernel(steps, rows, local, hidden, length, scalars, ins, outs, scratch):
    (where,) = scalars
    grad_in, att, z_one, aout, aout_mate, up, up_mate, down, down_mate = ins[:9]
    out_bias, gains, shift, up_bias, up_bias_mate = ins[9:]
    merged, low_out, df_out, do_out, dz_out, a_own, a_mate = outs[:7]
    g_out, du_out = outs[7:9], outs[9:11]
    da_out, sums, up_sums = outs[11:]
    wo, wu0, wu1, wd0, wd1, acc, kept, unit_two, rstd_two, low, upstream, slope, part, up_part, sems = (
        scratch
    )
    total = rows * length
    loads = Loads(
        steps,
        sems,
        one_above(aout.at[1], aout_mate.at[1], wo, local)
        + [(up, wu0), (down, wd0), (up_mate, wu1), (down_mate, wd1)],
    )
    loads.start()
    part[...] = jnp.zeros_like(part)

    def put(at, both):
        upstream[at] = both.astype(BF16)

    base = pl.program_id(0) * rows
    row_pairs(grad_in, where, base, rows, length, put)

    def to_acc(cols, value):
        acc[:, cols] = value

    a_own[...] = att[:, :local]
    a_mate[...] = att[:, local:]
    loads.wait(0, 1)
    by_columns(att[...], wo, to_acc)

    def norm_two(at):
        unit, _ = moments(z_one[at])
        h_one = unit * gains[0:1] + shift[0:1]
        unit, rstd = moments(h_one + acc[at] + out_bias[1:2])
        h_two = unit * gains[1:2] + shift[1:2]
        unit_two[at] = unit
        rstd_two[at] = rstd
        kept[at] = h_two
        h_low = h_two.astype(BF16)
        low[at] = h_low
        low_out[at] = h_low

    band_loop(total, norm_two)
    acc[...] = jnp.zeros_like(acc)
    loads.wait(2, 3, 4, 5)

    @pl.loop(0, hidden // TILE)
    def _(step):
        cols = pl.ds(pl.multiple_of(step * TILE, TILE), TILE)
        units = [dot(low[...], wu[:, cols]) for wu in (wu0, wu1)]
        for half, (wd, biases) in enumerate(((wd0, up_bias), (wd1, up_bias_mate))):
            bias = biases[:, cols]
            for start in range(0, total, BAND):
                at = slice(start, start + BAND)
                active, sloped = gelu(units[half][at] + bias)
                g_out[half][at, cols] = active.astype(BF16)
                slope[half, at, cols] = sloped
            acc[...] += dot(g_out[half][:, cols], wd[cols, :])

    def norm_three(at):
        unit, rstd = moments(kept[at] + acc[at] + out_bias[2:3])
        gain = gains[2:3]
        unit_three = unit * gain + shift[2:3]
        grad = upstream[at].astype(F32)
        dz = norm_grad(unit, rstd, gain, grad)
        kept[at] = dz
        acc[at] = unit_three
        dz_low = dz.astype(BF16)
        low[at] = dz_low
        df_out[at] = dz_low
        return (
            (0, fold(dz_low.astype(F32))),
            (1, fold(grad * unit)),
            (2, fold(grad)),
        )

    band_loop(total, norm_three, part)

    for row in range(rows):
        merged[where[base + row]] = acc[row * length : (row + 1) * length].astype(BF16)
    acc[...] = jnp.zeros_like(acc)

    @pl.loop(0, hidden // TILE)
    def _(step):
        cols = pl.ds(pl.multiple_of(step * TILE, TILE), TILE)
        grads = [dot_nt(low[...], wd[cols, :]) for wd in (wd0, wd1)]
        for half, wu in enumerate((wu0, wu1)):
            folded = 0.0
            for start in range(0, total, BAND):
                at = slice(start, start + BAND)
                du = (grads[half][at] * slope[half, at, cols]).astype(BF16)
                du_out[half][at, cols] = du
                folded = folded + fold(du.astype(F32))
            up_part[half, :, cols] = folded
            acc[...] += dot_nt(du_out[half][:, cols], wu[:, cols])

    def norm_two_back(at):
        grad = kept[at] + acc[at]
        unit = unit_two[at]
        dz = norm_grad(unit, rstd_two[at], gains[1:2], grad)
        dz_out[at] = dz
        dz_low = dz.astype(BF16)
        low[at] = dz_low
        do_out[at] = dz_low
        return (
            (3, fold(dz_low.astype(F32))),
            (4, fold(grad * unit)),
            (5, fold(grad)),
        )

    band_loop(total, norm_two_back, part)

    def to_grad(cols, value):
        da_out[:, cols] = value.astype(BF16)

    by_columns(low[...], wo, to_grad, transposed=True)
    for at in range(8):
        sums[0, at : at + 1] = jnp.sum(part[at], axis=0, keepdims=True)
    for half in range(2):
        up_sums[0, half : half + 1] = jnp.sum(up_part[half], axis=0, keepdims=True)


def cross_grad_kernel(steps, rows, length, scalars, ins, outs, scratch):
    image, corners = scalars
    queries, grads, keys, values = ins
    own, mate, grad_queries = outs
    qs, gs, acc, dk, dv = scratch
    patch_pad = keys.shape[1]

    def clear():
        @pl.loop(0, dk.shape[0])
        def _(at):
            dk[at] = jnp.zeros(dk.shape[1:], F32)
            dv[at] = jnp.zeros(dv.shape[1:], F32)

    pl.when(pl.program_id(0) == 0)(clear)

    def spread(at):
        qs[at] = queries[at].astype(F32) * SCALE
        gs[at] = grads[at].astype(F32)

    band_loop(rows * length, spread)
    lane_head = lane_heads()
    base = pl.program_id(0) * rows

    @pl.loop(0, rows // PAIRED)
    def _(step):
        items, places = [], []
        for row in range(PAIRED):
            row = step * PAIRED + row
            at = pl.ds(pl.multiple_of(row * length, 8), length)
            which = image[base + row]
            keep = box_keep(corners, base + row, (patch_pad, 1), 0)
            for g in range(qs.shape[1] // GROUP):
                lanes = slice(g * GROUP, (g + 1) * GROUP)
                items.append(
                    (
                        spread_heads(qs[at, lanes], lane_head),
                        keys[which, :, lanes],
                        values[which, :, lanes],
                        spread_heads(gs[at, lanes], lane_head),
                        keep,
                    )
                )
                places.append((at, which, lanes))
        for (at, which, lanes), (grad_q, grad_k, grad_v) in zip(places, attend_grad(items)):
            acc[at, lanes] = gather_heads(grad_q, lane_head, length) * SCALE
            dk[which, :, lanes] += grad_k
            dv[which, :, lanes] += grad_v

    def cast(at):
        grad_queries[at] = acc[at].astype(BF16)

    band_loop(rows * length, cast)

    @pl.when(pl.program_id(0) == steps - 1)
    def _():
        half = own.shape[1]

        @pl.loop(0, half)
        def _(at):
            own[0, at] = dk[at].astype(BF16)
            own[1, at] = dv[at].astype(BF16)
            mate[0, at] = dk[half + at].astype(BF16)
            mate[1, at] = dv[half + at].astype(BF16)


def image_kernel(images, patch_count, local, scalars, ins, outs, scratch):
    (core,) = scalars
    piece, piece_mate, patches, proj_weight, ain, ain_mate = ins
    kv_own, kv_mate, patch_grad, weight_grad, sums = outs
    narrow, wide, taken, w1, w2, part, sems, weight_sems = scratch
    parts, span = taken.shape[0], taken.shape[1]
    loads = Loads(
        1,
        weight_sems,
        side_by_side(ain.at[1, 1], ain_mate.at[1, 1], w1, local)
        + side_by_side(ain.at[1, 2], ain_mate.at[1, 2], w2, local),
    )
    arrivals = Loads(
        1, sems, [(patches.at[pl.ds(n * span, span)], taken.at[n]) for n in range(parts)]
    )
    loads.start()
    arrivals.start()
    part[...] = jnp.zeros_like(part)
    own_images, patch_pad = piece.shape[1], piece.shape[2]
    width = w1.shape[0]

    slab = 80

    @pl.loop(0, wide.shape[1] // slab)
    def _(step):
        at = pl.ds(pl.multiple_of(step * slab, slab), slab)
        for lane in range(wide.shape[0]):
            wide[lane, at] = jnp.zeros((slab, LANES), F32)

    loads.wait(0, 1, 2, 3)
    first = core[0] * own_images

    @pl.loop(0, own_images // 2)
    def _(step):
        pair = pl.ds(step * 2, 2)
        halves = []
        for half in (slice(0, local), slice(local, width)):
            swapped = slice(width - half.stop, width - half.start)
            both = piece[:, pair, :, half].astype(F32) + piece_mate[:, pair, :, swapped].astype(F32)
            both = both.astype(BF16)
            halves.append([both[at].reshape(2 * patch_pad, local) for at in range(2)])
        (dk_own, dv_own), (dk_mate, dv_mate) = halves
        rows = pl.ds(pl.multiple_of(step * 2 * patch_pad, 2 * patch_pad), 2 * patch_pad)
        kv_own[rows, :local] = dk_own
        kv_own[rows, local:] = dv_own
        kv_mate[rows, :local] = dk_mate
        kv_mate[rows, local:] = dv_mate
        dk = jnp.concatenate([dk_own, dk_mate], axis=1)
        dv = jnp.concatenate([dv_own, dv_mate], axis=1)
        part[1] += fold(dv.astype(F32))
        for start in range(0, width, GROUP):
            cols = slice(start, start + GROUP)
            grad = dot_nt(dk, w1[cols, :]) + dot_nt(dv, w2[cols, :])
            grad = grad.astype(BF16).astype(F32)
            part[0, :, cols] += fold(grad)
            for at in range(2):
                one = grad[at * patch_pad : at * patch_pad + patch_count]
                which = step * 2 + at
                spot = pl.ds(which, patch_count, stride=own_images)
                split_lanes(narrow, spot, start, one)
                split_lanes(wide, pl.ds(which + first, patch_count, stride=images), start, one)

    for n in range(parts):
        arrivals.wait(n)
        few = slice(n * span * own_images, (n + 1) * span * own_images)
        some = join_lanes(narrow, few).astype(BF16)
        for start in range(0, proj_weight.shape[0], GROUP):
            cols = slice(start, start + GROUP)
            back = dot_nt(some, proj_weight[cols, :]).astype(BF16)
            patch_grad[n * span : (n + 1) * span, :, cols] = back.reshape(span, own_images, GROUP)
        flat = taken[n].reshape(span * images, taken.shape[3])
        grad = join_lanes(wide, slice(n * span * images, (n + 1) * span * images)).astype(BF16)
        product = dot_tn(flat, grad)
        if n == 0:
            weight_grad[...] = product
        else:
            weight_grad[...] += product
    for at in range(2):
        sums[at : at + 1] = jnp.sum(part[at], axis=0, keepdims=True)


def self_grad_kernel(steps, rows, local, length, scalars, ins, outs, scratch):
    lens, where = scalars
    dq2, z_one, dz_two, q_in, k_in, v_in, ain, ain_mate, aout, aout_mate, gain = ins
    text_grad, do_out, dq2_own, dq2_mate, qkv_own, qkv_mate, sums = outs
    wc, wo, wq, wk, wv, acc, kept, low, low_k, low_v, qs, ks, vs, part, sems = scratch
    total = rows * length
    loads = Loads(
        steps,
        sems,
        side_by_side(ain.at[1, 0], ain_mate.at[1, 0], wc, local)
        + one_above(aout.at[0], aout_mate.at[0], wo, local)
        + side_by_side(ain.at[0, 0], ain_mate.at[0, 0], wq, local)
        + side_by_side(ain.at[0, 1], ain_mate.at[0, 1], wk, local)
        + side_by_side(ain.at[0, 2], ain_mate.at[0, 2], wv, local),
    )
    loads.start()
    part[...] = jnp.zeros_like(part)

    def to_acc(cols, value):
        acc[:, cols] = value

    loads.wait(0, 1)
    by_columns(dq2[...], wc, to_acc, transposed=True)

    def norm_back(at):
        unit, rstd = moments(z_one[at])
        grad = dz_two[at] + acc[at]
        dz = norm_grad(unit, rstd, gain[0:1], grad)
        kept[at] = dz
        dz_low = dz.astype(BF16)
        low[at] = dz_low
        do_out[at] = dz_low
        qs[at] = q_in[at].astype(F32) * SCALE
        ks[at] = k_in[at].astype(F32)
        vs[at] = v_in[at].astype(F32)
        query = dq2[at]
        dq2_own[at] = query[:, :local]
        dq2_mate[at] = query[:, local:]
        return (
            (0, fold(dz_low.astype(F32))),
            (1, fold(grad * unit)),
            (2, fold(grad)),
            (5, fold(query.astype(F32))),
        )

    band_loop(total, norm_back, part)
    loads.wait(2, 3)
    by_columns(low[...], wo, to_acc, transposed=True)
    lane_head = lane_heads()
    key_index = lax.broadcasted_iota(jnp.int32, (length, 1), 0)
    base = pl.program_id(0) * rows

    @pl.loop(0, rows // PAIRED)
    def _(step):
        items, places = [], []
        for row in range(PAIRED):
            row = step * PAIRED + row
            at = pl.ds(pl.multiple_of(row * length, 8), length)
            keep = key_index < lens[base + row]
            for g in range(qs.shape[1] // GROUP):
                lanes = slice(g * GROUP, (g + 1) * GROUP)
                items.append(
                    (
                        spread_heads(qs[at, lanes], lane_head),
                        ks[at, lanes].astype(BF16),
                        vs[at, lanes].astype(BF16),
                        spread_heads(acc[at, lanes], lane_head),
                        keep,
                    )
                )
                places.append((at, lanes))
        for (at, lanes), (grad_q, grad_k, grad_v) in zip(places, attend_grad(items)):
            qs[at, lanes] = gather_heads(grad_q, lane_head, length) * SCALE
            ks[at, lanes] = grad_k
            vs[at, lanes] = grad_v

    def cast(at):
        sums = []
        for slot, (source, target) in enumerate(((qs, low), (ks, low_k), (vs, low_v))):
            value = source[at].astype(BF16)
            target[at] = value
            qkv_own[at, slot * local : (slot + 1) * local] = value[:, :local]
            qkv_mate[at, slot * local : (slot + 1) * local] = value[:, local:]
            if slot != 1:
                sums.append((3 + slot // 2, fold(value.astype(F32))))
        return sums

    band_loop(total, cast, part)
    loads.wait(4, 5, 6, 7, 8, 9)
    for start in range(0, kept.shape[1], GROUP):
        cols = slice(start, start + GROUP)
        acc[:, cols] = (
            kept[:, cols]
            + dot_nt(low[...], wq[cols, :])
            + dot_nt(low_k[...], wk[cols, :])
            + dot_nt(low_v[...], wv[cols, :])
        )

    for row in range(rows):
        text_grad[where[base + row]] = acc[row * length : (row + 1) * length].astype(BF16)
    for at in range(8):
        sums[0, at : at + 1] = jnp.sum(part[at], axis=0, keepdims=True)


def pack_kernel(local, hidden, scalars, ins, outs, scratch):
    (core,) = scalars
    feed, up, self_, image = ins
    feed_sum = jnp.sum(feed[...], axis=0)
    self_sum = jnp.sum(self_[...], axis=0)
    up_sum = jnp.sum(up[...], axis=0)
    common = [(0, 0), (1, 3), (1, 0), (0, 1), (1, 4), (1, 1), (0, 2), (1, 5), (1, 2)]
    even = core[0] == 0
    for out, mine in zip(outs, (True, False)):
        out[...] = jnp.zeros_like(out)
        at = 0
        for which, row in common:
            source = feed_sum if which else self_sum
            for half in range(2):
                out[at : at + 1] = source[row : row + 1, half * local : (half + 1) * local]
                at += 1
        lanes = slice(0, local) if mine else slice(local, 2 * local)
        for row in (3, 4, 5):
            out[at : at + 1] = self_sum[row : row + 1, lanes]
            at += 1
        out[at : at + 1] = image[1:2, lanes]
        at += 1
        half = 0 if mine else 1
        for start in range(0, hidden, local):
            out[at : at + 1] = up_sum[half : half + 1, start : start + local]
            at += 1
        low, high = image[0:1, :local], image[0:1, local:]
        out[at : at + 1] = jnp.where(even == mine, low, high)


def halve_kernel(rows, length, scalars, ins, outs, scratch):
    core, where = scalars
    (tall,) = scratch

    def put(at, both):
        split_lanes(tall, at, 0, both)

    row_pairs(ins[0], where, 0, rows, length, put)
    half = length // 2
    for out, first in zip(outs, (core[0] * half, (1 - core[0]) * half)):
        for token in range(half):
            out[token] = join_lanes(
                tall, pl.ds(first + token, rows, stride=length)
            ).astype(BF16)


def place_kernel(scalars, ins, outs, scratch):
    own, mate, place = ins
    (out,) = outs
    count, slots = out.shape[1], own.shape[1]
    index = lax.broadcasted_iota(jnp.int32, (count, slots), 1)
    from_own = jnp.where(place[...] == index, 1.0, 0.0).astype(BF16)
    from_mate = jnp.where(place[...] == index + slots, 1.0, 0.0).astype(BF16)
    for token in range(out.shape[0]):
        out[token] = (dot(from_own, own[token]) + dot(from_mate, mate[token])).astype(BF16)


def body(
    text,
    cotangent,
    lengths,
    box_corners,
    box_counts,
    region_box,
    patches,
    proj_weight,
    proj_bias,
    attention_in,
    attention_bias,
    attention_out,
    output_bias,
    norm_gain,
    norm_bias,
    up_weight,
    up_bias,
    down_weight,
):
    rows, length, width = text.shape
    images, patch_count, vision = patches.shape
    local = attention_in.shape[-1]
    hidden = up_weight.shape[-1]
    devices = lax.axis_size("dp")
    me, core = lax.axis_index("dp"), lax.axis_index("mp")
    pair = -(-rows // devices)
    each, odd = pair // 2, pair % 2
    deep = each + odd
    slots = devices * each + devices // 2 * odd
    patch_pad = -(-patch_count // 16) * 16
    own_images = images // 2
    step_rows = 12 if slots % 12 == 0 else 8
    steps = slots // step_rows
    tokens = step_rows * length
    all_tokens = slots * length
    full = slots * 2 == rows
    core_scalar = core.astype(jnp.int32).reshape(1)

    def mate(value):
        return lax.ppermute(value, "mp", [(0, 1), (1, 0)])

    def tie(*values):
        return lax.optimization_barrier(values)

    def exchange(value):
        return lax.all_to_all(value, "dp", split_axis=0, concat_axis=0, tiled=True)

    ain_mate = mate(attention_in)
    bias_mate = mate(attention_bias)
    aout_mate = mate(attention_out)
    up_bias_own = up_bias.reshape(1, hidden)
    up_bias_mate = mate(up_bias_own)
    up_mate = mate(up_weight)
    down_mate = mate(down_weight)

    number = jnp.arange(rows, dtype=jnp.int32)
    target = region_box // rows
    earlier = (target[:, None] == target[None, :]) & (number[None, :] < number[:, None])
    nth = jnp.sum(earlier.astype(jnp.int32), axis=1)
    even_part = nth < 2 * each
    row_core = jnp.where(even_part, nth // max(each, 1), (target ^ me) & 1)
    depth = jnp.where(even_part, nth % max(each, 1), each)
    spot = jnp.arange(devices * deep, dtype=jnp.int32)
    hit = (spot[:, None] == (target * deep + depth)[None, :]) & (row_core == core)[None, :]
    source = jnp.sum(jnp.where(hit, number[None, :], 0), axis=1)
    slot = jnp.where(even_part, target * each + depth, devices * each + (target >> 1))
    place = jnp.where(row_core == core, slot, slot + slots)[:, None]
    order = jnp.arange(slots, dtype=jnp.int32)
    late = order - devices * each
    where = jnp.where(
        late < 0,
        order // max(each, 1) * deep + order % max(each, 1),
        (2 * late + ((me & 1) ^ core)) * deep + each,
    )
    meta = jnp.concatenate(
        [(region_box % rows)[:, None], lengths[:, None], box_corners], axis=1
    )
    meta_out = jnp.sum(jnp.where(hit[:, :, None], meta[None], 0), axis=1)
    if not full:
        empty = jnp.array([0, 1, 0, 1, 0, 1], jnp.int32)
        meta_out = jnp.where(jnp.any(hit, axis=1)[:, None], meta_out, empty[None])
    arrived = exchange(meta_out)[where]
    ends = jnp.cumsum(box_counts[0])
    image = jnp.sum((ends[None, :] <= arrived[:, 0:1]).astype(jnp.int32), axis=1)
    image = (image + own_images * core) % images
    lens = arrived[:, 1]
    corners = arrived[:, 2:].reshape(-1)

    block_shape = (devices * deep, length, width)
    if full:
        x_out, upstream_out = run(
            partial(fetch_kernel, devices * deep),
            1,
            [source],
            [(text, ANY), (cotangent, ANY)],
            [(block_shape, BF16, whole_spec(block_shape))] * 2,
            [pltpu.SemaphoreType.DMA((2 * devices * deep,))],
            0,
        )
    else:
        valid = jnp.any(hit, axis=1)[:, None, None]
        x_out = jnp.where(valid, text[source], 0)
        upstream_out = jnp.where(valid, cotangent[source], 0)
    x_in = exchange(x_out)

    patches, aout_mate, image, corners, lens = tie(patches, aout_mate, image, corners, lens)
    by_patch = jnp.transpose(patches, (1, 0, 2))
    parts = next(n for n in (5, 4, 3, 2, 1) if patch_count % n == 0)
    weight_scratch = pltpu.VMEM((width, width), BF16)

    def slabs(count):
        return pltpu.VMEM((width // LANES, count, LANES), F32)

    patch_scratch = pltpu.VMEM((parts, patch_count // parts, images, vision), BF16)
    image_shape = (images, patch_pad, width)
    proj, keys, values = run(
        partial(project_kernel, images, own_images, patch_pad, patch_count, local),
        1,
        [core_scalar],
        [
            (by_patch, ANY),
            (proj_weight, whole_spec(proj_weight.shape)),
            (proj_bias.reshape(1, width), whole_spec((1, width))),
            (attention_in, ANY),
            (ain_mate, ANY),
            (attention_bias, whole_spec(attention_bias.shape)),
            (bias_mate, whole_spec(bias_mate.shape)),
        ],
        [(image_shape, BF16, whole_spec(image_shape))] * 3,
        [
            patch_scratch,
            slabs(patch_count * images),
            weight_scratch,
            weight_scratch,
            pltpu.SemaphoreType.DMA((parts,)),
            pltpu.SemaphoreType.DMA((4,)),
        ],
        2 * images * patch_pad * width * (vision + 2 * width),
    )

    upstream_out, proj, keys, values = tie(upstream_out, proj, keys, values)
    upstream_in = exchange(upstream_out)

    def token_in(value):
        return (value, rows_spec((tokens, value.shape[1]), 0))

    def token_out(cols, dtype):
        return ((all_tokens, cols), dtype, rows_spec((tokens, cols), 0))

    block_out = (block_shape, BF16, whole_spec(block_shape))

    def f32_tokens(cols):
        return pltpu.VMEM((tokens, cols), F32)

    def low_tokens(cols):
        return pltpu.VMEM((tokens, cols), BF16)

    def whole(value):
        return (value, whole_spec(value.shape))

    attention_flops = 4 * 4 * all_tokens * width * 64

    x, z_one, q_self, k_self, v_self, att_own, att_mate, self_low, queries = run(
        partial(self_kernel, steps, step_rows, local, length),
        steps,
        [lens, where],
        [
            whole(x_in),
            (attention_in, ANY),
            (ain_mate, ANY),
            (attention_out, ANY),
            (aout_mate, ANY),
            whole(attention_bias),
            whole(bias_mate),
            whole(output_bias),
            whole(norm_gain),
            whole(norm_bias),
        ],
        [token_out(width, BF16), token_out(width, F32)]
        + [token_out(width, BF16)] * 3
        + [token_out(local, BF16)] * 2
        + [token_out(width, BF16)] * 2,
        [weight_scratch] * 5
        + [f32_tokens(width)] * 4
        + [low_tokens(width), pltpu.SemaphoreType.DMA((10,))],
        2 * all_tokens * width * width * 5 + attention_flops,
    )

    (attended,) = run(
        partial(cross_kernel, step_rows, length),
        steps,
        [image, corners],
        [token_in(queries), whole(keys), whole(values)],
        [token_out(width, BF16)],
        [f32_tokens(width)] * 2,
        attention_flops * 4,
    )

    result = run(
        partial(feed_kernel, steps, step_rows, local, hidden, length),
        steps,
        [where],
        [
            whole(upstream_in),
            token_in(attended),
            token_in(z_one),
            (attention_out, ANY),
            (aout_mate, ANY),
            (up_weight, ANY),
            (up_mate, ANY),
            (down_weight, ANY),
            (down_mate, ANY),
            whole(output_bias),
            whole(norm_gain),
            whole(norm_bias),
            whole(up_bias_own),
            whole(up_bias_mate),
        ],
        [block_out]
        + [token_out(width, BF16)] * 3
        + [token_out(width, F32)]
        + [token_out(local, BF16)] * 2
        + [token_out(hidden, BF16)] * 4
        + [
            token_out(width, BF16),
            ((steps, 8, width), F32, rows_spec((1, 8, width), 0)),
            ((steps, 2, hidden), F32, rows_spec((1, 2, hidden), 0)),
        ],
        [weight_scratch]
        + [pltpu.VMEM((width, hidden), BF16)] * 2
        + [pltpu.VMEM((hidden, width), BF16)] * 2
        + [f32_tokens(width)] * 3
        + [f32_tokens(1), low_tokens(width), low_tokens(width)]
        + [pltpu.VMEM((2, tokens, hidden), F32)]
        + [pltpu.VMEM((8, 8, width), F32), pltpu.VMEM((2, 8, hidden), F32)]
        + [pltpu.SemaphoreType.DMA((6,))],
        2 * all_tokens * width * (2 * width + 8 * hidden),
    )
    merged_out, cross_low, grad_ffn, grad_cross, dz_two, a_own, a_mate = result[:7]
    g_own, g_mate, du_own, du_mate, grad_att, feed_sums, up_sums = result[7:]

    bits = devices.bit_length() - 1

    def partner_bits(value, mask):
        return lax.ppermute(value, "dp", [(d, d ^ mask) for d in range(devices)])

    def opened(value):
        return value.reshape((2,) * bits + (value.shape[0] // devices, value.shape[1]))

    def swap(value, axis, bit):
        mine = (me >> bit) & 1
        away = lax.dynamic_index_in_dim(value, 1 - mine, axis, keepdims=False)
        stay = lax.dynamic_index_in_dim(value, mine, axis, keepdims=False)
        return stay, partner_bits(away, 1 << bit)

    def first_swaps(by_x, by_y):
        return swap(opened(by_x), bits - 1, 0) + swap(opened(by_y), bits - 2, 1)

    def second_swaps(stay_x, got_x, stay_y, got_y):
        return swap(add(stay_x, got_x), bits - 2, 1) + swap(add(stay_y, got_y), bits - 2, 0)

    def add(stay, got):
        return (stay.astype(F32) + got.astype(F32)).astype(BF16)

    def last_parts(stay_x, got_x, stay_y, got_y):
        parts = [add(stay_x, got_x), add(stay_y, got_y)]
        return jnp.concatenate(
            [part.reshape((devices // 4,) + part.shape[-2:]) for part in parts], axis=2
        )

    def last_sum(both, first_width):
        groups = [[low + 4 * n for n in range(devices // 4)] for low in range(4)]
        both = lax.all_to_all(
            both, "dp", split_axis=0, concat_axis=0, axis_index_groups=groups, tiled=True
        )
        total = jnp.sum(both.astype(F32), axis=0)
        return total[:, :first_width], total[:, first_width:]

    def low_tn(left, right):
        return dot_tn(left, right).astype(BF16)

    merged_in = exchange(merged_out)
    up_away, down_away = low_tn(cross_low, du_mate), low_tn(grad_ffn, g_mate)
    grad_att, queries, up_away, down_away = tie(grad_att, queries, up_away, down_away)
    up_got, down_got = mate(up_away), mate(down_away)

    half_shape = (2, own_images, patch_pad, width)
    image_acc = pltpu.VMEM(image_shape, F32)
    piece, piece_out, grad_queries = run(
        partial(cross_grad_kernel, steps, step_rows, length),
        steps,
        [image, corners],
        [token_in(queries), token_in(grad_att), whole(keys), whole(values)],
        [(half_shape, BF16, whole_spec(half_shape))] * 2 + [token_out(width, BF16)],
        [f32_tokens(width)] * 3 + [image_acc] * 2,
        attention_flops * 12,
    )
    piece_mate = mate(piece_out)

    up_part = (dot_tn(cross_low, du_own) + up_got.astype(F32)).astype(BF16)
    down_part = (dot_tn(grad_ffn, g_own) + down_got.astype(F32)).astype(BF16)
    grad_queries, up_part, down_part = tie(grad_queries, up_part, down_part)
    feed_stage = first_swaps(up_part, down_part)

    result = run(
        partial(self_grad_kernel, steps, step_rows, local, length),
        steps,
        [lens, where],
        [
            token_in(grad_queries),
            token_in(z_one),
            token_in(dz_two),
            token_in(q_self),
            token_in(k_self),
            token_in(v_self),
            (attention_in, ANY),
            (ain_mate, ANY),
            (attention_out, ANY),
            (aout_mate, ANY),
            whole(norm_gain),
        ],
        [block_out]
        + [token_out(width, BF16)]
        + [token_out(local, BF16)] * 2
        + [token_out(3 * local, BF16)] * 2
        + [((steps, 8, width), F32, rows_spec((1, 8, width), 0))],
        [weight_scratch] * 5
        + [f32_tokens(width)] * 2
        + [low_tokens(width)] * 3
        + [f32_tokens(width)] * 3
        + [pltpu.VMEM((8, 8, width), F32), pltpu.SemaphoreType.DMA((10,))],
        2 * all_tokens * width * width * 5 + attention_flops * 2,
    )
    text_out, grad_self, dq_own, dq_mate, qkv_own, qkv_mate, self_sums = result
    text_in = exchange(text_out)

    self_away = jnp.concatenate(
        [
            low_tn(x, qkv_mate),
            low_tn(grad_self, att_mate),
            low_tn(grad_cross, a_mate),
            low_tn(self_low, dq_mate),
        ],
        axis=1,
    )
    self_got = mate(self_away)
    feed_stage = tie(self_away, *feed_stage)[1:]
    feed_stage = second_swaps(*feed_stage)
    self_own = jnp.concatenate(
        [
            dot_tn(x, qkv_own),
            dot_tn(grad_self, att_own),
            dot_tn(grad_cross, a_own),
            dot_tn(self_low, dq_own),
        ],
        axis=1,
    )
    self_part = (self_own + self_got.astype(F32)).astype(BF16)
    half_width = self_part.shape[1] // 2
    self_stage = first_swaps(self_part[:, :half_width], self_part[:, half_width:])
    feed_parts = last_parts(*feed_stage)
    piece, piece_mate, self_part, feed_parts = tie(piece, piece_mate, self_part, feed_parts)

    flat_images = own_images * patch_pad
    patch_grad_shape = (patch_count, own_images, vision)
    kv_own, kv_mate, patch_grad, proj_weight_sum, image_sums = run(
        partial(image_kernel, images, patch_count, local),
        1,
        [core_scalar],
        [
            whole(piece),
            whole(piece_mate),
            (by_patch, ANY),
            whole(proj_weight),
            (attention_in, ANY),
            (ain_mate, ANY),
        ],
        [
            ((flat_images, width), BF16, whole_spec((flat_images, width))),
            ((flat_images, width), BF16, whole_spec((flat_images, width))),
            (patch_grad_shape, BF16, whole_spec(patch_grad_shape)),
            ((vision, width), F32, whole_spec((vision, width))),
            ((8, width), F32, whole_spec((8, width))),
        ],
        [
            slabs(patch_count * own_images),
            slabs(patch_count * images),
            patch_scratch,
            weight_scratch,
            weight_scratch,
            pltpu.VMEM((2, 8, width), F32),
            pltpu.SemaphoreType.DMA((parts,)),
            pltpu.SemaphoreType.DMA((4,)),
        ],
        2 * flat_images * width * (2 * width + 2 * vision),
    )

    up_grad, down_grad = last_sum(feed_parts, hidden)
    self_stage = second_swaps(*self_stage)
    kv_low = proj[:own_images].reshape(flat_images, width)
    kv_away = low_tn(kv_low, kv_mate)
    kv_got = mate(kv_away)
    proj_away = lax.dynamic_slice_in_dim(proj_weight_sum, (1 - core) * local, local, 1)
    proj_got = mate(proj_away.astype(BF16))
    kv_part = (dot_tn(kv_low, kv_own) + kv_got.astype(F32)).astype(BF16)
    proj_own = lax.dynamic_slice_in_dim(proj_weight_sum, core * local, local, 1)
    proj_part = (proj_own + proj_got.astype(F32)).astype(BF16)
    proj_part = proj_part.reshape(width, vision * local // width)
    image_stage = first_swaps(kv_part, proj_part)
    self_one, self_two = last_sum(last_parts(*self_stage), half_width)
    image_stage = second_swaps(*image_stage)
    kv_grad, proj_grad = last_sum(last_parts(*image_stage), width)
    proj_grad = proj_grad.reshape(vision // devices, local)

    lines = 23 + hidden // local
    packed_shape = (-(-lines // 8) * 8, local)
    small, small_out = run(
        partial(pack_kernel, local, hidden),
        1,
        [core_scalar],
        [whole(feed_sums), whole(up_sums), whole(self_sums), whole(image_sums)],
        [(packed_shape, F32, whole_spec(packed_shape))] * 2,
        [],
        0,
        [up_grad, kv_part, proj_part],
    )
    small = small + mate(small_out)
    for bit in range(bits):
        small = small + partner_bits(small, 1 << bit)
    common = small[:18].reshape(3, 3, width)
    bias_grad = small[18:22].reshape(2, 2, local)
    up_bias_grad = small[22 : 22 + hidden // local].reshape(hidden)
    proj_bias_grad = small[22 + hidden // local]

    ready = [self_one[:, at * local : (at + 1) * local] for at in range(3)]
    out_self, out_cross, query_cross = [
        self_two[:, at * local : (at + 1) * local] for at in range(3)
    ]
    in_grad = jnp.stack(
        ready + [query_cross, kv_grad[:, :local], kv_grad[:, local:]]
    ).reshape(2, 3, width // devices, local)
    out_grad = jnp.stack([out_self.T, out_cross.T])

    def tokens_out(value, after, after_place):
        shape = (length // 2, slots, width)
        own, away = run(
            partial(halve_kernel, slots, length),
            1,
            [core_scalar, where],
            [whole(value)],
            [(shape, BF16, whole_spec(shape))] * 2,
            [slabs(all_tokens)],
            0,
            after,
        )
        shape = (length // 2, rows, width)
        (out,) = run(
            place_kernel,
            1,
            [],
            [whole(own), whole(mate(away)), whole(place)],
            [(shape, BF16, whole_spec(shape))],
            [],
            0,
            after_place,
        )
        return jnp.transpose(out, (1, 0, 2))

    return (
        tokens_out(merged_in, [self_part], [kv_part]),
        tokens_out(text_in, [kv_away], [kv_part, proj_part]),
        jnp.transpose(patch_grad, (1, 0, 2)),
        proj_grad,
        proj_bias_grad,
        in_grad,
        bias_grad,
        out_grad,
        common[0],
        common[1],
        common[2],
        up_grad,
        up_bias_grad,
        down_grad.T,
    )


def solution(mesh):
    placed = (
        P("dp", None, None),
        P("dp", None, None),
        P("dp"),
        P("dp", None),
        P("dp", None),
        P("dp"),
        P("dp", None, None),
        P(),
        P(),
        P(None, None, None, "mp"),
        P(None, None, "mp"),
        P(None, "mp", None),
        P(),
        P(),
        P(),
        P(None, "mp"),
        P("mp"),
        P("mp", None),
    )
    return jax.shard_map(
        body,
        mesh=mesh,
        in_specs=placed,
        out_specs=(
            P("dp", "mp", None),
            P("dp", "mp", None),
            P(("dp", "mp"), None, None),
            P("dp", "mp"),
            P("mp"),
            P(None, None, "dp", "mp"),
            P(None, None, "mp"),
            P(None, "mp", "dp"),
            P(),
            P(),
            P(),
            P("dp", "mp"),
            P("mp"),
            P("mp", "dp"),
        ),
        check_vma=False,
    )
```

time: 2060 us -> 470 us (0.23)
  waiting for transfers between devices: 799 us -> 63.4 us
  local copies, waits for them, and re-layouts: 509 us -> 32.6 us
  matrix products: 481 us -> 43.4 us
  Pallas kernels: 0 us -> 217 us
  blocking collectives: 151 us -> 0 us
  starting transfers between devices: 23.8 us -> 77 us
  other arithmetic: 63.4 us -> 27.5 us
    dot_general x46 -> x14, matrix products: 481 us -> 43.4 us  [dot_tn(): lax.dot_general(left, right, (((0,), (0,)), ((), ())), preferred_element_...]
    reduce_scatter x9 -> x0, waiting for transfers between devices: 325 us -> none  [the longest x1 143 us: body(): lax.psum_scatter(up_grad, 'dp', scatter_dimension=0, tiled=True)]
    pallas_call x0 -> x13, Pallas kernels: none -> 217 us  [run(): pl.pallas_call(kernel, grid_spec=pltpu.PrefetchScalarGridSpec(num_scalar_...]
    all_to_all x3 -> x8, waiting for transfers between devices: 236 us -> 29.9 us  [the longest x5 17.5 us: exchange(): return lax.all_to_all(value, 'dp', split_axis=0, concat_axis=0, tiled=True)]
    reshape x24 -> x7, local copies, waits for them, and re-layouts: 200 us -> 4.66 us  [the longest x1 1.51 us: body(): proj_part = proj_part.reshape(width, vision * local // width)]
    unnamed x20 -> x0, waiting for transfers between devices: 187 us -> none
    psum x2 -> x0, blocking collectives: 151 us -> none  [the longest x1 77.4 us: body(): small = lax.psum((bias_grad, up_bias_grad, proj_bias_mine), 'dp')]
    unnamed x195 -> x83, local copies, waits for them, and re-layouts: 136 us -> 7.77 us
  transfers between devices with their start and end apart: 20 -> 39, of which waited for: 15 -> 12; matrix products, arithmetic and copies ran while one was open for 31% -> 18% of each run, Pallas kernels for 0% -> 35%
where the time goes in v1:
time: 470 us; the launch traced here: 463 us
  Pallas kernels  217 us (46%)
  starting transfers between devices  77 us (16%)
  waiting for transfers between devices  63.4 us (13%)
  matrix products  43.4 us (9%)
  local copies, waits for them, and re-layouts  32.6 us (7%)
  other arithmetic  27.5 us (6%)
    pallas_call x13, Pallas kernels, run(): pl.pallas_call(kernel, grid_spec=pltpu.PrefetchScalarGridSpec(num_scalar_...  217 us
    dot_general x14, matrix products, dot_tn(): lax.dot_general(left, right, (((0,), (0,)), ((), ())), preferred_element_...  43.4 us
    all_to_all x5, starting transfers between devices, exchange(): return lax.all_to_all(value, 'dp', split_axis=0, concat_axis=0, tiled=True)  38.5 us
    ppermute x16, waiting for transfers between devices, partner_bits(): return lax.ppermute(value, 'dp', [(d, d ^ mask) for d in range(devices)])  33.1 us
    ppermute x16, starting transfers between devices, partner_bits(): return lax.ppermute(value, 'dp', [(d, d ^ mask) for d in range(devices)])  22.2 us
    all_to_all x5, waiting for transfers between devices, exchange(): return lax.all_to_all(value, 'dp', split_axis=0, concat_axis=0, tiled=True)  17.5 us
    all_to_all x3, starting transfers between devices, last_sum(): lax.all_to_all(both, 'dp', split_axis=0, concat_axis=0, axis_index_groups...  13.3 us
    all_to_all x3, waiting for transfers between devices, last_sum(): lax.all_to_all(both, 'dp', split_axis=0, concat_axis=0, axis_index_groups...  12.4 us
  transfers between devices with their start and end apart: 39, of which 12 were waited for; matrix products, arithmetic and copies ran while one was open for 18% of the time, Pallas kernels for 35%

profile of v1, /device:TPU:0, one launch (start us, length us, event | category | flops | bytes accessed | tf_op | source)
XLA Modules:
  0.0 463.0 jit_solution(13513499196122036711)
XLA Ops:
  3.6 7.9 %all-to-all-start = ((s32[16,2,6]{2,1,0:T(2,128)}), s32[16,2,6]{2,1,0:T(2,128)S(1)}, u32[]{:S(2)}, u32[]{:S(2)}) async-start(s32[16,2,6]{2,1,0:T(2,128)} %bitcast.4), calls=%async_computation | async-start | bytes 32768 | tf_op jit(solution)/shard_map/all_to_all | solution.py:942
  12.1 5.5 %shard_map.281 = (bf16[32,40,768]{2,1,0:T(8,128)(2,1)}, bf16[32,40,768]{2,1,0:T(8,128)(2,1)}) custom-call(s32[32]{0:T(128)} %select_reduce_fusion.1.refs_0_, bf16[48,40,768]{2,1,0:T(8,128)(2,1)} %refs_1_.1, bf16[48,40,768]{2,1,0:T(8,128)(2,1)} %refs_2_.2), custom_call_target="tpu_custom_call" | custom-call | bytes 9830400 | tf_op jit(solution)/shard_map/pallas_call | solution.py:64
  18.8 5.8 %all-to-all-start.2 = ((bf16[32,40,768]{2,1,0:T(8,128)(2,1)}), bf16[32,40,768]{2,1,0:T(8,128)(2,1)S(1)}, u32[]{:S(2)}, u32[]{:S(2)}) async-start(bf16[32,40,768]{2,1,0:T(8,128)(2,1)} %get-tuple-element.96), calls=%async_computation.2 | async-start | bytes 3932160 | tf_op jit(solution)/shard_map/all_to_all | solution.py:942
  29.3 21.5 %shard_map.282 = (bf16[16,160,768]{2,1,0:T(8,128)(2,1)}, bf16[16,160,768]{2,1,0:T(8,128)(2,1)}, bf16[16,160,768]{2,1,0:T(8,128)(2,1)}) custom-call(s32[1]{0:T(128)} %bitcast.refs_0_, bf16[145,16,1024]{2,1,0:T(8,128)(2,1)} %bitcast.168, bf16[1024,768]{1,0:T(8,128)(2,1)} %refs_4_.5, f32[1,768]{1,0:T(1,128)} %reshape.219.refs_3_, ...), custom_call_target="tpu_custom_call" | custom-call | flops 10066329600 | bytes 25213952 | tf_op jit(solution)/shard_map/pallas_call | solution.py:64
  50.8 14.9 %all-to-all-done.2.refs_2_ = bf16[32,40,768]{2,1,0:T(8,128)(2,1)S(1)} async-done(((bf16[32,40,768]{2,1,0:T(8,128)(2,1)}), bf16[32,40,768]{2,1,0:T(8,128)(2,1)S(1)}, u32[]{:S(2)}, u32[]{:S(2)}) %all-to-all-start.2) | async-done | bytes 1966112 | tf_op jit(solution)/shard_map/all_to_all | solution.py:942
  67.0 9.7 %all-to-all-start.1 = ((bf16[32,40,768]{2,1,0:T(8,128)(2,1)}), bf16[32,40,768]{2,1,0:T(8,128)(2,1)}, u32[]{:S(2)}, u32[]{:S(2)}) async-start(bf16[32,40,768]{2,1,0:T(8,128)(2,1)} %get-tuple-element.92), calls=%async_computation.1 | async-start | bytes 3932160 | tf_op jit(solution)/shard_map/all_to_all | solution.py:942
  78.0 23.8 %shard_map.283 = (bf16[960,768]{1,0:T(8,128)(2,1)}, f32[960,768]{1,0:T(8,128)}, bf16[960,768]{1,0:T(8,128)(2,1)}, bf16[960,768]{1,0:T(8,128)(2,1)}, bf16[960,768...) custom-call(s32[24]{0:T(128)} %get-tuple-element.95.refs_0_, ...), custom_call_target="tpu_custom_call" | custom-call | flops 6417285120 | bytes 24714240 | tf_op jit(solution)/shard_map/pallas_call | solution.py:64
  101.8 13.9 %shard_map.284.refs_2_ = bf16[960,768]{1,0:T(8,128)(2,1)} custom-call(s32[24]{0:T(128)} %and_select_fusion.refs_0_, s32[96]{0:T(128)} %reshape.218.refs_1_, bf16[960,768]{1,0:T(8,128)(2,1)} %get-tuple-element.108.refs_2_, bf16[16,160,768]{2,1,0:T(8,128)(2,1)} %get-tuple-element.99.refs_3_.refs_4_, bf16[16,160,768]{2,1,0:T(8,128)(2,1)} %get-tuple-element.100.refs_4_.refs_5_), custom_call_target="tpu_custom_call" | custom-call | flops 3019898880 | bytes 10813440 | tf_op jit(solution)/shard_map/pallas_call | solution.py:64
  115.7 1.4 all-to-all-done.1.refs_1_
  117.1 55.9 %shard_map.285 = (bf16[32,40,768]{2,1,0:T(8,128)(2,1)}, bf16[960,768]{1,0:T(8,128)(2,1)}, bf16[960,768]{1,0:T(8,128)(2,1)}, bf16[960,768]{1,0:T(8,128)(2,1)}, f3...) custom-call(s32[24]{0:T(128)} %compare_select_fusion.4.refs_1_.refs_, ...), custom_call_target="tpu_custom_call" | custom-call | flops 20384317440 | bytes 42384384 | tf_op jit(solution)/shard_map/pallas_call | solution.py:64
  173.0 6.5 %convolution_convert_fusion.2 = bf16[768,1536]{1,0:T(8,128)(2,1)} fusion(bf16[960,768]{1,0:T(8,128)(2,1)} %get-tuple-element.104, bf16[960,1536]{1,0:T(8,128)(2,1)} %get-tuple-element.105), kind=kOutput, calls=%fused_computation.8 | convolution fusion | flops 2266103808 | bytes 6782976 | tf_op jit(solution)/shard_map/dot_general | solution.py:38
  179.5 3.9 convolution_convert_fusion.1
  184.7 2.9 slice.90
  187.6 9.3 %all-to-all-start.3 = ((bf16[32,40,768]{2,1,0:T(8,128)(2,1)}), bf16[32,40,768]{2,1,0:T(8,128)(2,1)S(1)}, u32[]{:S(2)}, u32[]{:S(2)}) async-start(bf16[32,40,768]{2,1,0:T(8,128)(2,1)} %get-tuple-element.102), calls=%async_computation.3 | async-start | bytes 3932160 | tf_op jit(solution)/shard_map/all_to_all | solution.py:942
  196.9 26.1 %shard_map.286 = (bf16[2,8,160,768]{3,2,1,0:T(8,128)(2,1)}, bf16[2,8,160,768]{3,2,1,0:T(8,128)(2,1)}, bf16[960,768]{1,0:T(8,128)(2,1)}) custom-call(s32[24]{0:T(128)} %and_select_fusion.refs_0_, s32[96]{0:T(128)} %reshape.218.refs_1_, bf16[960,768]{1,0:T(8,128)(2,1)} %get-tuple-element.108.refs_2_, bf16[960,768]{1,0:T(8,128)(2,1)} %get-tuple-element.109.refs_3_, ...), custom_call_target="tpu_custom_call" | custom-call | flops 9059696640 | bytes 20152320 | tf_op jit(solution)/shard_map/pallas_call | solution.py:64
  224.1 2.0 fusion.30
  226.8 4.4 add_convert_fusion.1
  231.2 4.2 add_convert_fusion
  236.7 2.0 collective-permute-start.10
  239.8 1.5 collective-permute-start.11
  241.3 30.3 %shard_map.287 = (bf16[32,40,768]{2,1,0:T(8,128)(2,1)}, bf16[960,768]{1,0:T(8,128)(2,1)}, bf16[960,384]{1,0:T(8,128)(2,1)}, bf16[960,384]{1,0:T(8,128)(2,1)}, bf...) custom-call(s32[24]{0:T(128)} %get-tuple-element.95.refs_0_, ...), custom_call_target="tpu_custom_call" | custom-call | flops 7172259840 | bytes 30630912 | tf_op jit(solution)/shard_map/pallas_call | solution.py:64
  271.7 2.7 convolution_convert_fusion.6
  276.5 2.3 convolution_convert_fusion
  278.7 2.0 pad_maximum_fusion
  281.6 4.0 fusion.28
  285.6 2.0 fusion.29
  288.6 1.6 add_convert_fusion.4
  290.9 1.6 add_convert_fusion.3
  292.6 2.0 fusion.31
  294.7 10.8 %collective-permute-done.12 = bf16[2,2,48,1536]{3,2,1,0:T(8,128)(2,1)S(1)} collective-permute-done((bf16[2,2,48,1536]{3,2,1,0:T(8,128)(2,1)S(1)}, bf16[2,2,48,1536]{3,2,1,0:T(8,128)(2,1)S(1)}, u32[]{:S(2)}, u32[]{:S(2)}) %collective-permute-start.12) | collective-permute-done | bytes 589856 | tf_op jit(solution)/shard_map/ppermute | solution.py:1141
  305.6 1.8 collective-permute-done.13
  308.9 5.8 %all-to-all-start.4 = ((bf16[32,40,768]{2,1,0:T(8,128)(2,1)}), bf16[32,40,768]{2,1,0:T(8,128)(2,1)}, u32[]{:S(2)}, u32[]{:S(2)}) async-start(bf16[32,40,768]{2,1,0:T(8,128)(2,1)} %get-tuple-element.148), calls=%async_computation.4 | async-start | bytes 3932160 | tf_op jit(solution)/shard_map/all_to_all | solution.py:942
  316.7 3.8 fusion.refs_3_
  320.5 24.1 %shard_map.289 = (bf16[1280,768]{1,0:T(8,128)(2,1)}, bf16[1280,768]{1,0:T(8,128)(2,1)}, bf16[145,8,1024]{2,1,0:T(8,128)(2,1)}, f32[1024,768]{1,0:T(8,128)}, f32[8,768]{1,0:T(8,128)}) custom-call(s32[1]{0:T(128)} %bitcast.refs_0_, bf16[2,8,160,768]{3,2,1,0:T(8,128)(2,1)} %get-tuple-element.144.refs_1_, ...), custom_call_target="tpu_custom_call" | custom-call | flops 7046430720 | bytes 30744576 | tf_op jit(solution)/shard_map/pallas_call | solution.py:64
  344.6 1.5 dynamic-slice_convert_fusion
  346.2 1.5 fusion.25
  347.7 2.2 dynamic-slice_bitcast_fusion.5
  349.9 2.0 collective-permute-start.27
  352.9 1.5 collective-permute-start.29
  354.3 4.0 shard_map.288
  358.3 4.3 convolution_convert_fusion.3.refs_3_
  363.2 4.8 %all-to-all-start.6 = ((bf16[4,48,3072]{2,1,0:T(8,128)(2,1)}), bf16[4,48,3072]{2,1,0:T(8,128)(2,1)}, u32[]{:S(2)}, u32[]{:S(2)}) async-start(bf16[4,48,3072]{2,1,0:T(8,128)(2,1)} %pad_maximum_fusion.1), calls=%async_computation.6 | async-start | bytes 2359296 | tf_op jit(solution)/shard_map/all_to_all | solution.py:1169
  367.9 4.0 shard_map.291
  371.9 1.8 add_convert_fusion.5
  374.4 1.5 reshape.226.refs_4_.refs_7_
  376.7 1.6 fusion.2
  378.4 1.4 collective-permute-start.28
  379.8 1.4 fusion.1
  381.3 6.6 %collective-permute-done.20 = bf16[2,2,2,48,512]{4,3,2,1,0:T(8,128)(2,1)S(1)} collective-permute-done((bf16[2,2,2,48,512]{4,3,2,1,0:T(8,128)(2,1)S(1)}, bf16[2,2,2,48,512]{4,3,2,1,0:T(8,128)(2,1)S(1)}, u32[]{:S(2)}, u32[]{:S(2)}) %collective-permute-start.20) | collective-permute-done | bytes 393248 | tf_op jit(solution)/shard_map/ppermute | solution.py:1141
  389.3 1.5 collective-permute-start.21
  390.8 3.1 add_convert_fusion.2.refs_3_.refs_6_
  395.4 3.4 shard_map.290
  398.8 3.4 shard_map.292
  402.4 1.5 convert_reduce_fusion
  404.7 1.5 shard_map.293
  408.5 1.5 collective-permute-start.23
  411.0 5.1 %all-to-all-start.7 = ((bf16[4,48,2304]{2,1,0:T(8,128)(2,1)}), bf16[4,48,2304]{2,1,0:T(8,128)(2,1)S(1)}, u32[]{:S(2)}, u32[]{:S(2)}) async-start(bf16[4,48,2304]{2,1,0:T(8,128)(2,1)} %pad_maximum_fusion.2), calls=%async_computation.7 | async-start | bytes 1769472 | tf_op jit(solution)/shard_map/all_to_all | solution.py:1169
  419.1 2.4 collective-permute-done.24
  421.5 1.8 collective-permute-start.25
  424.5 7.2 %collective-permute-done.25 = f32[32,384]{1,0:T(8,128)S(1)} collective-permute-done((f32[32,384]{1,0:T(8,128)S(1)}, f32[32,384]{1,0:T(8,128)S(1)}, u32[]{:S(2)}, u32[]{:S(2)}) %collective-permute-start.25) | collective-permute-done | bytes 49184 | tf_op jit(solution)/shard_map/ppermute | solution.py:1141
  431.7 4.7 %collective-permute-start.26 = (f32[32,384]{1,0:T(8,128)S(1)}, f32[32,384]{1,0:T(8,128)S(1)}, u32[]{:S(2)}, u32[]{:S(2)}) collective-permute-start(f32[32,384]{1,0:T(8,128)S(1)} %add.248), channel_id=1, source_target_pairs={{0,16},{2,18},{4,20},{6,22},{8,24},{10,26},{12,28},{14,30},{16,0},... | collective-permute-start | bytes 147464 | tf_op jit(solution)/shard_map/ppermute | solution.py:1141
  437.4 3.1 collective-permute-done.26
  445.1 3.5 all-to-all-start.5
  449.4 12.4 %all-to-all-done.5 = bf16[4,48,1280]{2,1,0:T(8,128)(2,1)S(1)} async-done(((bf16[4,48,1280]{2,1,0:T(8,128)(2,1)}), bf16[4,48,1280]{2,1,0:T(8,128)(2,1)S(1)}, u32[]{:S(2)}, u32[]{:S(2)}) %all-to-all-start.5) | async-done | bytes 491552 | tf_op jit(solution)/shard_map/all_to_all | solution.py:1169
  (204 shorter events, 47.5 us)
Async XLA Ops:
  0.6 28.0 %collective-permute-start.1 = (bf16[2,3,768,384]{3,2,1,0:T(8,128)(2,1)}, bf16[2,3,768,384]{3,2,1,0:T(8,128)(2,1)}, u32[]{:S(2)}, u32[]{:S(2)}) collective-permute-start(bf16[2,3,768,384]{3,2,1,0:T(8,128)(2,1)} %refs_5_.3), channel_id=1, source_target_pairs={{0,1},{1,0},{2,3},{3,2},{4,5},{5,4},{6,7},{7,6},{8,9},{9,8},{10,11... | collective-permute-start | bytes 10616840 | tf_op jit(solution)/shard_map/ppermute | solution.py:936
  3.6 15.2 %all-to-all-start = ((s32[16,2,6]{2,1,0:T(2,128)}), s32[16,2,6]{2,1,0:T(2,128)S(1)}, u32[]{:S(2)}, u32[]{:S(2)}) async-start(s32[16,2,6]{2,1,0:T(2,128)} %bitcast.4), calls=%async_computation | async-start | bytes 32768 | tf_op jit(solution)/shard_map/all_to_all | solution.py:942
  18.8 5.9 %copy-start.17 = (bf16[2,384,768]{2,1,0:T(8,128)(2,1)S(1)}, bf16[2,384,768]{2,1,0:T(8,128)(2,1)}, u32[]{:S(2)}) copy-start(bf16[2,384,768]{2,1,0:T(8,128)(2,1)} %refs_10_.5) | copy-start | bytes 3538948
  18.8 5.9 %copy-start.18 = (f32[2,2,384]{2,1,0:T(2,128)S(1)}, f32[2,2,384]{2,1,0:T(2,128)}, u32[]{:S(2)}) copy-start(f32[2,2,384]{2,1,0:T(2,128)} %refs_7_.1) | copy-start | bytes 18436
  18.8 6.4 %copy-start.15 = (f32[768]{0:T(1024)S(1)}, f32[768]{0:T(1024)}, u32[]{:S(2)}) copy-start(f32[768]{0:T(1024)} %param.26) | copy-start | bytes 9220
  18.8 7.0 %copy-start.16 = (s32[1,16]{1,0:T(1,128)S(1)}, s32[1,16]{1,0:T(1,128)}, u32[]{:S(2)}) copy-start(s32[1,16]{1,0:T(1,128)} %param.22) | copy-start | bytes 196
  18.8 46.9 %all-to-all-start.2 = ((bf16[32,40,768]{2,1,0:T(8,128)(2,1)}), bf16[32,40,768]{2,1,0:T(8,128)(2,1)S(1)}, u32[]{:S(2)}, u32[]{:S(2)}) async-start(bf16[32,40,768]{2,1,0:T(8,128)(2,1)} %get-tuple-element.96), calls=%async_computation.2 | async-start | bytes 3932160 | tf_op jit(solution)/shard_map/all_to_all | solution.py:942
  24.7 4.0 collective-permute-start
  24.8 3.9 collective-permute-start.2
  50.8 26.5 %copy-start.13 = (f32[1536]{0:T(1024)S(1)}, f32[1536]{0:T(1024)}, u32[]{:S(2)}) copy-start(f32[1536]{0:T(1024)} %param.34) | copy-start | bytes 18436
  67.0 50.1 %all-to-all-start.1 = ((bf16[32,40,768]{2,1,0:T(8,128)(2,1)}), bf16[32,40,768]{2,1,0:T(8,128)(2,1)}, u32[]{:S(2)}, u32[]{:S(2)}) async-start(bf16[32,40,768]{2,1,0:T(8,128)(2,1)} %get-tuple-element.92), calls=%async_computation.1 | async-start | bytes 3932160 | tf_op jit(solution)/shard_map/all_to_all | solution.py:942
  76.7 39.0 %collective-permute-start.3 = (bf16[768,1536]{1,0:T(8,128)(2,1)}, bf16[768,1536]{1,0:T(8,128)(2,1)}, u32[]{:S(2)}, u32[]{:S(2)}) collective-permute-start(bf16[768,1536]{1,0:T(8,128)(2,1)} %refs_6_.3), channel_id=1, source_target_pairs={{0,1},{1,0},{2,3},{3,2},{4,5},{5,4},{6,7},{7,6},{8,9},{9,8},{10,11... | collective-permute-start | bytes 7077896 | tf_op jit(solution)/shard_map/ppermute | solution.py:936
  76.8 38.9 %collective-permute-start.4 = (bf16[1536,768]{1,0:T(8,128)(2,1)}, bf16[1536,768]{1,0:T(8,128)(2,1)}, u32[]{:S(2)}, u32[]{:S(2)}) collective-permute-start(bf16[1536,768]{1,0:T(8,128)(2,1)} %refs_8_.2), channel_id=1, source_target_pairs={{0,1},{1,0},{2,3},{3,2},{4,5},{5,4},{6,7},{7,6},{8,9},{9,8},{10,11... | collective-permute-start | bytes 7077896 | tf_op jit(solution)/shard_map/ppermute | solution.py:936
  77.3 24.5 %copy-start.14 = (f32[1,1536]{1,0:T(1,128)}, f32[1,1536]{1,0:T(1,128)S(1)}, u32[]{:S(2)}) copy-start(f32[1,1536]{1,0:T(1,128)S(1)} %reshape.220.refs_13_) | copy-start | bytes 18436
  77.3 38.4 %collective-permute-start.5 = (f32[1,1536]{1,0:T(1,128)S(1)}, f32[1,1536]{1,0:T(1,128)S(1)}, u32[]{:S(2)}, u32[]{:S(2)}) collective-permute-start(f32[1,1536]{1,0:T(1,128)S(1)} %reshape.220.refs_13_), channel_id=1, source_target_pairs={{0,1},{1,0},{2,3},{3,2},{4,5},{5,4},{6,7},{7,6},{8,9},{9,8},{10,11... | collective-permute-start | bytes 18440 | tf_op jit(solution)/shard_map/ppermute | solution.py:936
  173.0 6.5 %copy-start.24 = (bf16[960,1536]{1,0:T(8,128)(2,1)S(1)}, bf16[960,1536]{1,0:T(8,128)(2,1)}, u32[]{:S(2)}) copy-start(bf16[960,1536]{1,0:T(8,128)(2,1)} %get-tuple-element.107) | copy-start | bytes 8847364
  173.0 6.5 %copy-start.28 = (bf16[960,768]{1,0:T(8,128)(2,1)S(1)}, bf16[960,768]{1,0:T(8,128)(2,1)}, u32[]{:S(2)}) copy-start(bf16[960,768]{1,0:T(8,128)(2,1)} %get-tuple-element.106) | copy-start | bytes 4423684
  183.5 42.7 %collective-permute-start.7 = (bf16[768,1536]{1,0:T(8,128)(2,1)}, bf16[768,1536]{1,0:T(8,128)(2,1)}, u32[]{:S(2)}, u32[]{:S(2)}) collective-permute-start(bf16[768,1536]{1,0:T(8,128)(2,1)} %convolution_convert_fusion.2), channel_id=1, source_target_pairs={{0,1},{1,0},{2,3},{3,2},{4,5},{5,4},{6,7},{7,6},{8,9},{9,8},{10,11... | collective-permute-start | bytes 7077896 | tf_op jit(solution)/shard_map/ppermute | solution.py:936
  183.5 47.7 %collective-permute-start.8 = (bf16[768,1536]{1,0:T(8,128)(2,1)}, bf16[768,1536]{1,0:T(8,128)(2,1)}, u32[]{:S(2)}, u32[]{:S(2)}) collective-permute-start(bf16[768,1536]{1,0:T(8,128)(2,1)} %convolution_convert_fusion.1), channel_id=1, source_target_pairs={{0,1},{1,0},{2,3},{3,2},{4,5},{5,4},{6,7},{7,6},{8,9},{9,8},{10,11... | collective-permute-start | bytes 7077896 | tf_op jit(solution)/shard_map/ppermute | solution.py:936
  187.6 120.0 %all-to-all-start.3 = ((bf16[32,40,768]{2,1,0:T(8,128)(2,1)}), bf16[32,40,768]{2,1,0:T(8,128)(2,1)S(1)}, u32[]{:S(2)}, u32[]{:S(2)}) async-start(bf16[32,40,768]{2,1,0:T(8,128)(2,1)} %get-tuple-element.102), calls=%async_computation.3 | async-start | bytes 3932160 | tf_op jit(solution)/shard_map/all_to_all | solution.py:942
  196.9 26.1 %copy-start.22 = (bf16[960,768]{1,0:T(8,128)(2,1)S(1)}, bf16[960,768]{1,0:T(8,128)(2,1)}, u32[]{:S(2)}) copy-start(bf16[960,768]{1,0:T(8,128)(2,1)} %get-tuple-element.126) | copy-start | bytes 4423684
  196.9 26.1 %copy-start.32 = (bf16[960,384]{1,0:T(8,128)(2,1)S(1)}, bf16[960,384]{1,0:T(8,128)(2,1)}, u32[]{:S(2)}) copy-start(bf16[960,384]{1,0:T(8,128)(2,1)} %get-tuple-element.132) | copy-start | bytes 2211844
  223.0 97.5 %collective-permute-start.6 = (bf16[2,8,160,768]{3,2,1,0:T(8,128)(2,1)}, bf16[2,8,160,768]{3,2,1,0:T(8,128)(2,1)}, u32[]{:S(2)}, u32[]{:S(2)}) collective-permute-start(bf16[2,8,160,768]{3,2,1,0:T(8,128)(2,1)} %get-tuple-element.111), channel_id=1, source_target_pairs={{0,1},{1,0},{2,3},{3,2},{4,5},{5,4},{6,7},{7,6},{8,9},{9,8},{10,11... | collective-permute-start | bytes 11796488 | tf_op jit(solution)/shard_map/ppermute | solution.py:936
  224.1 2.7 copy-start.38
  226.8 4.4 copy-start.29
  226.8 4.4 copy-start.37
  236.7 50.9 %collective-permute-start.10 = (bf16[2,2,2,48,1536]{4,3,2,1,0:T(8,128)(2,1)}, bf16[2,2,2,48,1536]{4,3,2,1,0:T(8,128)(2,1)S(1)}, u32[]{:S(2)}, u32[]{:S(2)}) collective-permute-start(bf16[2,2,2,48,1536]{4,3,2,1,0:T(8,128)(2,1)} %get-tuple-element.168), channel_id=1, source_target_pairs={{0,2},{2,0},{4,6},{6,4},{8,10},{10,8},{12,14},{14,12},{16,18},{18,... | collective-permute-start | bytes 3538952 | tf_op jit(solution)/shard_map/ppermute | solution.py:1141
  239.8 47.8 %collective-permute-start.11 = (bf16[2,2,2,48,1536]{4,3,2,1,0:T(8,128)(2,1)}, bf16[2,2,2,48,1536]{4,3,2,1,0:T(8,128)(2,1)}, u32[]{:S(2)}, u32[]{:S(2)}) collective-permute-start(bf16[2,2,2,48,1536]{4,3,2,1,0:T(8,128)(2,1)} %get-tuple-element.166), channel_id=1, source_target_pairs={{0,4},{2,6},{4,0},{6,2},{8,12},{10,14},{12,8},{14,10},{16,20},{18,... | collective-permute-start | bytes 3538952 | tf_op jit(solution)/shard_map/ppermute | solution.py:1141
  271.7 2.7 copy-start.21
  271.7 2.7 copy-start.33
  278.7 2.8 copy-start.31
  280.7 35.1 %collective-permute-start.9 = (bf16[768,2304]{1,0:T(8,128)(2,1)}, bf16[768,2304]{1,0:T(8,128)(2,1)}, u32[]{:S(2)}, u32[]{:S(2)}) collective-permute-start(bf16[768,2304]{1,0:T(8,128)(2,1)} %pad_maximum_fusion), channel_id=1, source_target_pairs={{0,1},{1,0},{2,3},{3,2},{4,5},{5,4},{6,7},{7,6},{8,9},{9,8},{10,11... | collective-permute-start | bytes 10616840 | tf_op jit(solution)/shard_map/ppermute | solution.py:936
  281.6 4.0 copy-start.23
  281.6 4.0 copy-start.25
  290.2 15.2 %collective-permute-start.12 = (bf16[2,2,48,1536]{3,2,1,0:T(8,128)(2,1)S(1)}, bf16[2,2,48,1536]{3,2,1,0:T(8,128)(2,1)S(1)}, u32[]{:S(2)}, u32[]{:S(2)}) collective-permute-start(bf16[2,2,48,1536]{3,2,1,0:T(8,128)(2,1)S(1)} %dynamic-slice_bitcast_fusion.8), channel_id=1, source_target_pairs={{0,4},{2,6},{4,0},{6,2},{8,12},{10,14},{12,8},{14,10},{16,20},{18,... | collective-permute-start | bytes 1769480 | tf_op jit(solution)/shard_map/ppermute | solution.py:1141
  292.5 15.0 %collective-permute-start.13 = (bf16[2,2,48,1536]{3,2,1,0:T(8,128)(2,1)S(1)}, bf16[2,2,48,1536]{3,2,1,0:T(8,128)(2,1)S(1)}, u32[]{:S(2)}, u32[]{:S(2)}) collective-permute-start(bf16[2,2,48,1536]{3,2,1,0:T(8,128)(2,1)S(1)} %dynamic-slice_bitcast_fusion.7), channel_id=1, source_target_pairs={{0,2},{2,0},{4,6},{6,4},{8,10},{10,8},{12,14},{14,12},{16,18},{18,... | collective-permute-start | bytes 1769480 | tf_op jit(solution)/shard_map/ppermute | solution.py:1141
  308.9 54.3 %all-to-all-start.4 = ((bf16[32,40,768]{2,1,0:T(8,128)(2,1)}), bf16[32,40,768]{2,1,0:T(8,128)(2,1)}, u32[]{:S(2)}, u32[]{:S(2)}) async-start(bf16[32,40,768]{2,1,0:T(8,128)(2,1)} %get-tuple-element.148), calls=%async_computation.4 | async-start | bytes 3932160 | tf_op jit(solution)/shard_map/all_to_all | solution.py:942
  320.5 25.7 %copy-start = (bf16[768,2304]{1,0:T(8,128)(2,1)}, bf16[768,2304]{1,0:T(8,128)(2,1)S(1)}, u32[]{:S(2)}) copy-start(bf16[768,2304]{1,0:T(8,128)(2,1)S(1)} %fusion.refs_3_) | copy-start | bytes 10616836
  346.1 25.8 %collective-permute-start.17 = (bf16[1024,384]{1,0:T(8,128)(2,1)S(1)}, bf16[1024,384]{1,0:T(8,128)(2,1)}, u32[]{:S(2)}, u32[]{:S(2)}) collective-permute-start(bf16[1024,384]{1,0:T(8,128)(2,1)S(1)} %dynamic-slice_convert_fusion), channel_id=1, source_target_pairs={{0,1},{1,0},{2,3},{3,2},{4,5},{5,4},{6,7},{7,6},{8,9},{9,8},{10,11... | collective-permute-start | bytes 2359304 | tf_op jit(solution)/shard_map/ppermute | solution.py:936
  349.9 26.0 %collective-permute-start.27 = (bf16[2,2,2,48,1152]{4,3,2,1,0:T(8,128)(2,1)}, bf16[2,2,2,48,1152]{4,3,2,1,0:T(8,128)(2,1)}, u32[]{:S(2)}, u32[]{:S(2)}) collective-permute-start(bf16[2,2,2,48,1152]{4,3,2,1,0:T(8,128)(2,1)} %dynamic-slice_bitcast_fusion.5), channel_id=1, source_target_pairs={{0,2},{2,0},{4,6},{6,4},{8,10},{10,8},{12,14},{14,12},{16,18},{18,... | collective-permute-start | bytes 2654216 | tf_op jit(solution)/shard_map/ppermute | solution.py:1141
  352.9 5.5 %copy-start.6 = (bf16[8,160,768]{2,1,0:T(8,128)(2,1)S(1)}, bf16[8,160,768]{2,1,0:T(8,128)(2,1)}, u32[]{:S(2)}) copy-start(bf16[8,160,768]{2,1,0:T(8,128)(2,1)} %slice.90) | copy-start | bytes 5898244
  352.9 25.5 %collective-permute-start.29 = (bf16[2,2,2,48,1152]{4,3,2,1,0:T(8,128)(2,1)}, bf16[2,2,2,48,1152]{4,3,2,1,0:T(8,128)(2,1)}, u32[]{:S(2)}, u32[]{:S(2)}) collective-permute-start(bf16[2,2,2,48,1152]{4,3,2,1,0:T(8,128)(2,1)} %dynamic-slice_bitcast_fusion.4), channel_id=1, source_target_pairs={{0,4},{2,6},{4,0},{6,2},{8,12},{10,14},{12,8},{14,10},{16,20},{18,... | collective-permute-start | bytes 2654216 | tf_op jit(solution)/shard_map/ppermute | solution.py:1141
  358.3 36.5 %collective-permute-start.14 = (bf16[20,24,768]{2,1,0:T(8,128)(2,1)}, bf16[20,24,768]{2,1,0:T(8,128)(2,1)}, u32[]{:S(2)}, u32[]{:S(2)}) collective-permute-start(bf16[20,24,768]{2,1,0:T(8,128)(2,1)} %get-tuple-element.142), channel_id=1, source_target_pairs={{0,1},{1,0},{2,3},{3,2},{4,5},{5,4},{6,7},{7,6},{8,9},{9,8},{10,11... | collective-permute-start | bytes 2211848 | tf_op jit(solution)/shard_map/ppermute | solution.py:936
  362.6 26.6 %collective-permute-start.15 = (bf16[768,768]{1,0:T(8,128)(2,1)}, bf16[768,768]{1,0:T(8,128)(2,1)}, u32[]{:S(2)}, u32[]{:S(2)}) collective-permute-start(bf16[768,768]{1,0:T(8,128)(2,1)} %convolution_convert_fusion.3.refs_3_), channel_id=1, source_target_pairs={{0,1},{1,0},{2,3},{3,2},{4,5},{5,4},{6,7},{7,6},{8,9},{9,8},{10,11... | collective-permute-start | bytes 3538952 | tf_op jit(solution)/shard_map/ppermute | solution.py:936
  363.2 39.2 %all-to-all-start.6 = ((bf16[4,48,3072]{2,1,0:T(8,128)(2,1)}), bf16[4,48,3072]{2,1,0:T(8,128)(2,1)}, u32[]{:S(2)}, u32[]{:S(2)}) async-start(bf16[4,48,3072]{2,1,0:T(8,128)(2,1)} %pad_maximum_fusion.1), calls=%async_computation.6 | async-start | bytes 2359296 | tf_op jit(solution)/shard_map/all_to_all | solution.py:1169
  371.9 26.9 %collective-permute-start.16 = (bf16[20,24,768]{2,1,0:T(8,128)(2,1)}, bf16[20,24,768]{2,1,0:T(8,128)(2,1)}, u32[]{:S(2)}, u32[]{:S(2)}) collective-permute-start(bf16[20,24,768]{2,1,0:T(8,128)(2,1)} %get-tuple-element.150), channel_id=1, source_target_pairs={{0,1},{1,0},{2,3},{3,2},{4,5},{5,4},{6,7},{7,6},{8,9},{9,8},{10,11... | collective-permute-start | bytes 2211848 | tf_op jit(solution)/shard_map/ppermute | solution.py:936
  374.4 4.0 copy-start.4
  375.9 12.0 %collective-permute-start.20 = (bf16[2,2,2,48,512]{4,3,2,1,0:T(8,128)(2,1)S(1)}, bf16[2,2,2,48,512]{4,3,2,1,0:T(8,128)(2,1)S(1)}, u32[]{:S(2)}, u32[]{:S(2)}) collective-permute-start(bf16[2,2,2,48,512]{4,3,2,1,0:T(8,128)(2,1)S(1)} %dynamic-slice_bitcast_fusion.11), channel_id=1, source_target_pairs={{0,4},{2,6},{4,0},{6,2},{8,12},{10,14},{12,8},{14,10},{16,20},{18,... | collective-permute-start | bytes 1179656 | tf_op jit(solution)/shard_map/ppermute | solution.py:1141
  378.4 10.1 %copy-start.5 = (bf16[2,2,2,2,48,512]{5,4,3,2,1,0:T(8,128)(2,1)S(1)}, bf16[2,2,2,2,48,512]{5,4,3,2,1,0:T(8,128)(2,1)}, u32[]{:S(2)}) copy-start(bf16[2,2,2,2,48,512]{5,4,3,2,1,0:T(8,128)(2,1)} %copy-done.4) | copy-start | bytes 2359300
  378.4 12.4 %copy-start.7 = (bf16[8,160,768]{2,1,0:T(8,128)(2,1)S(1)}, bf16[8,160,768]{2,1,0:T(8,128)(2,1)}, u32[]{:S(2)}) copy-start(bf16[8,160,768]{2,1,0:T(8,128)(2,1)} %slice.90) | copy-start | bytes 5898244
  378.4 12.3 %copy-start.34 = (bf16[1280,768]{1,0:T(8,128)(2,1)S(1)}, bf16[1280,768]{1,0:T(8,128)(2,1)}, u32[]{:S(2)}) copy-start(bf16[1280,768]{1,0:T(8,128)(2,1)} %get-tuple-element.146) | copy-start | bytes 5898244
  378.4 23.8 %collective-permute-start.28 = (bf16[2,2,48,1152]{3,2,1,0:T(8,128)(2,1)S(1)}, bf16[2,2,48,1152]{3,2,1,0:T(8,128)(2,1)S(1)}, u32[]{:S(2)}, u32[]{:S(2)}) collective-permute-start(bf16[2,2,48,1152]{3,2,1,0:T(8,128)(2,1)S(1)} %dynamic-slice_bitcast_fusion.10), channel_id=1, source_target_pairs={{0,4},{2,6},{4,0},{6,2},{8,12},{10,14},{12,8},{14,10},{16,20},{18,... | collective-permute-start | bytes 1327112 | tf_op jit(solution)/shard_map/ppermute | solution.py:1141
  387.9 18.4 %collective-permute-start.30 = (bf16[2,2,48,1152]{3,2,1,0:T(8,128)(2,1)S(1)}, bf16[2,2,48,1152]{3,2,1,0:T(8,128)(2,1)}, u32[]{:S(2)}, u32[]{:S(2)}) collective-permute-start(bf16[2,2,48,1152]{3,2,1,0:T(8,128)(2,1)S(1)} %dynamic-slice_bitcast_fusion.9), channel_id=1, source_target_pairs={{0,2},{2,0},{4,6},{6,4},{8,10},{10,8},{12,14},{14,12},{16,18},{18,... | collective-permute-start | bytes 1327112 | tf_op jit(solution)/shard_map/ppermute | solution.py:1141
  389.3 28.8 %collective-permute-start.21 = (bf16[2,2,48,512]{3,2,1,0:T(8,128)(2,1)}, bf16[2,2,48,512]{3,2,1,0:T(8,128)(2,1)}, u32[]{:S(2)}, u32[]{:S(2)}) collective-permute-start(bf16[2,2,48,512]{3,2,1,0:T(8,128)(2,1)} %dynamic-slice_bitcast_fusion.13), channel_id=1, source_target_pairs={{0,2},{2,0},{4,6},{6,4},{8,10},{10,8},{12,14},{14,12},{16,18},{18,... | collective-permute-start | bytes 589832 | tf_op jit(solution)/shard_map/ppermute | solution.py:1141
  394.8 28.5 %collective-permute-start.18 = (bf16[2,2,2,48,768]{4,3,2,1,0:T(8,128)(2,1)}, bf16[2,2,2,48,768]{4,3,2,1,0:T(8,128)(2,1)}, u32[]{:S(2)}, u32[]{:S(2)}) collective-permute-start(bf16[2,2,2,48,768]{4,3,2,1,0:T(8,128)(2,1)} %dynamic-slice_bitcast_fusion.6), channel_id=1, source_target_pairs={{0,2},{2,0},{4,6},{6,4},{8,10},{10,8},{12,14},{14,12},{16,18},{18,... | collective-permute-start | bytes 1769480 | tf_op jit(solution)/shard_map/ppermute | solution.py:1141
  406.2 1.4 collective-permute-start.22
  408.5 8.8 %collective-permute-start.23 = (f32[32,384]{1,0:T(8,128)S(1)}, f32[32,384]{1,0:T(8,128)S(1)}, u32[]{:S(2)}, u32[]{:S(2)}) collective-permute-start(f32[32,384]{1,0:T(8,128)S(1)} %add.245), channel_id=1, source_target_pairs={{0,2},{2,0},{4,6},{6,4},{8,10},{10,8},{12,14},{14,12},{16,18},{18,... | collective-permute-start | bytes 147464 | tf_op jit(solution)/shard_map/ppermute | solution.py:1141
  410.0 13.3 %copy-start.2 = (bf16[768,768]{1,0:T(8,128)(2,1)S(1)}, bf16[768,768]{1,0:T(8,128)(2,1)}, u32[]{:S(2)}) copy-start(bf16[768,768]{1,0:T(8,128)(2,1)} %copy-done.1) | copy-start | bytes 3538948
  411.0 34.1 %all-to-all-start.7 = ((bf16[4,48,2304]{2,1,0:T(8,128)(2,1)}), bf16[4,48,2304]{2,1,0:T(8,128)(2,1)S(1)}, u32[]{:S(2)}, u32[]{:S(2)}) async-start(bf16[4,48,2304]{2,1,0:T(8,128)(2,1)} %pad_maximum_fusion.2), calls=%async_computation.7 | async-start | bytes 1769472 | tf_op jit(solution)/shard_map/all_to_all | solution.py:1169
  417.3 4.2 collective-permute-start.24
  421.5 10.2 %collective-permute-start.25 = (f32[32,384]{1,0:T(8,128)S(1)}, f32[32,384]{1,0:T(8,128)S(1)}, u32[]{:S(2)}, u32[]{:S(2)}) collective-permute-start(f32[32,384]{1,0:T(8,128)S(1)} %add.247), channel_id=1, source_target_pairs={{0,8},{2,10},{4,12},{6,14},{8,0},{10,2},{12,4},{14,6},{16,24},{18,... | collective-permute-start | bytes 147464 | tf_op jit(solution)/shard_map/ppermute | solution.py:1141
  431.7 8.8 %collective-permute-start.26 = (f32[32,384]{1,0:T(8,128)S(1)}, f32[32,384]{1,0:T(8,128)S(1)}, u32[]{:S(2)}, u32[]{:S(2)}) collective-permute-start(f32[32,384]{1,0:T(8,128)S(1)} %add.248), channel_id=1, source_target_pairs={{0,16},{2,18},{4,20},{6,22},{8,24},{10,26},{12,28},{14,30},{16,0},... | collective-permute-start | bytes 147464 | tf_op jit(solution)/shard_map/ppermute | solution.py:1141
  436.4 7.8 %collective-permute-start.19 = (bf16[2,2,48,768]{3,2,1,0:T(8,128)(2,1)S(1)}, bf16[2,2,48,768]{3,2,1,0:T(8,128)(2,1)S(1)}, u32[]{:S(2)}, u32[]{:S(2)}) collective-permute-start(bf16[2,2,48,768]{3,2,1,0:T(8,128)(2,1)S(1)} %dynamic-slice_bitcast_fusion.12), channel_id=1, source_target_pairs={{0,4},{2,6},{4,0},{6,2},{8,12},{10,14},{12,8},{14,10},{16,20},{18,... | collective-permute-start | bytes 884744 | tf_op jit(solution)/shard_map/ppermute | solution.py:1141
  445.1 16.7 %all-to-all-start.5 = ((bf16[4,48,1280]{2,1,0:T(8,128)(2,1)}), bf16[4,48,1280]{2,1,0:T(8,128)(2,1)S(1)}, u32[]{:S(2)}, u32[]{:S(2)}) async-start(bf16[4,48,1280]{2,1,0:T(8,128)(2,1)} %pad_maximum_fusion.3), calls=%async_computation.5 | async-start | bytes 983040 | tf_op jit(solution)/shard_map/all_to_all | solution.py:1169
  (14 other events, 20.8 us)

commit v2 on v1

--- a/solution.py
+++ b/solution.py
@@ -22,7 +22,7 @@
 BANDS = 5
 LANES = 128
 TILE = 256
-PAIRED = 2
+PAIRED = 4
 VMEM_LIMIT = 58 << 20
 
 
@@ -127,9 +127,8 @@
 
 
 def gelu(u):
-    z = jnp.abs(u) * (0.5**0.5)
-    bell = jnp.exp(u * u * -0.5)
-    t = 1.0 / (1.0 + 0.3275911 * z)
+    bell = jnp.exp2(u * u * (-0.5 / math.log(2.0)))
+    t = 1.0 / (1.0 + (0.3275911 * 0.5**0.5) * jnp.abs(u))
     poly = t * (
         0.5 * 0.254829592
         + t
@@ -305,7 +304,11 @@
             both.append(jnp.concatenate([own, rest], axis=0))
         low = jnp.concatenate(both, axis=0).astype(BF16)
         pair = pl.ds(step * 2, 2)
-        proj[pair] = low.reshape(2, patch_pad, width)
+
+        @pl.when(step < own_images // 2)
+        def _():
+            proj[pair] = low.reshape(2, patch_pad, width)
+
         for start in range(0, width, GROUP):
             cols = slice(start, start + GROUP)
             keys[pair, :, cols] = (
@@ -319,7 +322,7 @@
 def self_kernel(steps, rows, local, length, scalars, ins, outs, scratch):
     lens, where = scalars
     x_in, ain, ain_mate, aout, aout_mate, bias_own, bias_mate, out_bias, gain, shift = ins
-    x_out, z_one, q_out, k_out, v_out, att_own, att_mate, low_out, cross_q = outs
+    x_out, unit_one, q_out, k_out, v_out, att_own, att_mate, low_out, cross_q, rstd_one = outs
     wq, wk, wv, wo, wc, qs, ks, vs, acc, low, sems = scratch
     total = rows * length
     loads = Loads(
@@ -403,8 +406,9 @@
 
     def norm(at):
         z = x_out[at].astype(F32) + acc[at] + out_bias[0:1]
-        z_one[at] = z
-        unit, _ = moments(z)
+        unit, rstd = moments(z)
+        unit_one[at] = unit
+        rstd_one[at] = rstd
         h = (unit * gain[0:1] + shift[0:1]).astype(BF16)
         low[at] = h
         low_out[at] = h
@@ -462,20 +466,29 @@
 
 def feed_kernel(steps, rows, local, hidden, length, scalars, ins, outs, scratch):
     (where,) = scalars
-    grad_in, att, z_one, aout, aout_mate, up, up_mate, down, down_mate = ins[:9]
+    grad_in, att, unit_one, aout, aout_mate, up, up_mate, down, down_mate = ins[:9]
     out_bias, gains, shift, up_bias, up_bias_mate = ins[9:]
     merged, low_out, df_out, do_out, dz_out, a_own, a_mate = outs[:7]
     g_out, du_out = outs[7:9], outs[9:11]
     da_out, sums, up_sums = outs[11:]
-    wo, wu0, wu1, wd0, wd1, acc, kept, unit_two, rstd_two, low, upstream, slope, part, up_part, sems = (
-        scratch
-    )
+    wo, wu, wd, acc, kept, unit_two, rstd_two, low, upstream, even, odd, slope = scratch[:12]
+    part, up_part, sems = scratch[12:]
+    tiles = hidden // TILE
     total = rows * length
     loads = Loads(
         steps,
         sems,
         one_above(aout.at[1], aout_mate.at[1], wo, local)
-        + [(up, wu0), (down, wd0), (up_mate, wu1), (down_mate, wd1)],
+        + [
+            (source.at[:, pl.ds(t * TILE, TILE)], wu.at[t, :, pl.ds(half * TILE, TILE)])
+            for t in range(tiles)
+            for half, source in enumerate((up, up_mate))
+        ]
+        + [
+            (source.at[pl.ds(t * TILE, TILE)], wd.at[t, pl.ds(half * TILE, TILE)])
+            for t in range(tiles)
+            for half, source in enumerate((down, down_mate))
+        ],
     )
     loads.start()
     part[...] = jnp.zeros_like(part)
@@ -495,8 +508,7 @@
     by_columns(att[...], wo, to_acc)
 
     def norm_two(at):
-        unit, _ = moments(z_one[at])
-        h_one = unit * gains[0:1] + shift[0:1]
+        h_one = unit_one[at] * gains[0:1] + shift[0:1]
         unit, rstd = moments(h_one + acc[at] + out_bias[1:2])
         h_two = unit * gains[1:2] + shift[1:2]
         unit_two[at] = unit
@@ -508,20 +520,36 @@
 
     band_loop(total, norm_two)
     acc[...] = jnp.zeros_like(acc)
-    loads.wait(2, 3, 4, 5)
-
-    @pl.loop(0, hidden // TILE)
-    def _(step):
-        cols = pl.ds(pl.multiple_of(step * TILE, TILE), TILE)
-        units = [dot(low[...], wu[:, cols]) for wu in (wu0, wu1)]
-        for half, (wd, biases) in enumerate(((wd0, up_bias), (wd1, up_bias_mate))):
-            bias = biases[:, cols]
+    loads.wait(*range(2, 2 + 4 * tiles))
+    biases = (up_bias, up_bias_mate)
+
+    def activate(units, t):
+        cols = pl.ds(pl.multiple_of(t * TILE, TILE), TILE)
+        for half in range(2):
+            lanes = slice(half * TILE, (half + 1) * TILE)
+            bias = biases[half][:, cols]
             for start in range(0, total, BAND):
                 at = slice(start, start + BAND)
-                active, sloped = gelu(units[half][at] + bias)
+                active, sloped = gelu(units[at, lanes] + bias)
                 g_out[half][at, cols] = active.astype(BF16)
-                slope[half, at, cols] = sloped
-            acc[...] += dot(g_out[half][:, cols], wd[cols, :])
+                slope[t, at, lanes] = sloped
+
+    def add_down(t):
+        cols = pl.ds(pl.multiple_of(t * TILE, TILE), TILE)
+        both = jnp.concatenate([g_out[0][:, cols], g_out[1][:, cols]], axis=1)
+        acc[...] += dot(both, wd[t])
+
+    even[...] = dot(low[...], wu[0])
+
+    @pl.loop(0, tiles // 2)
+    def _(step):
+        first = 2 * step
+        odd[...] = dot(low[...], wu[first + 1])
+        activate(even, first)
+        add_down(first)
+        even[...] = dot(low[...], wu[jnp.minimum(first + 2, tiles - 1)])
+        activate(odd, first + 1)
+        add_down(first + 1)
 
     def norm_three(at):
         unit, rstd = moments(kept[at] + acc[at] + out_bias[2:3])
@@ -546,19 +574,21 @@
         merged[where[base + row]] = acc[row * length : (row + 1) * length].astype(BF16)
     acc[...] = jnp.zeros_like(acc)
 
-    @pl.loop(0, hidden // TILE)
-    def _(step):
-        cols = pl.ds(pl.multiple_of(step * TILE, TILE), TILE)
-        grads = [dot_nt(low[...], wd[cols, :]) for wd in (wd0, wd1)]
-        for half, wu in enumerate((wu0, wu1)):
+    @pl.loop(0, tiles)
+    def _(t):
+        cols = pl.ds(pl.multiple_of(t * TILE, TILE), TILE)
+        grads = dot_nt(low[...], wd[t])
+        for half in range(2):
+            lanes = slice(half * TILE, (half + 1) * TILE)
             folded = 0.0
             for start in range(0, total, BAND):
                 at = slice(start, start + BAND)
-                du = (grads[half][at] * slope[half, at, cols]).astype(BF16)
+                du = (grads[at, lanes] * slope[t, at, lanes]).astype(BF16)
                 du_out[half][at, cols] = du
                 folded = folded + fold(du.astype(F32))
             up_part[half, :, cols] = folded
-            acc[...] += dot_nt(du_out[half][:, cols], wu[:, cols])
+        both = jnp.concatenate([du_out[0][:, cols], du_out[1][:, cols]], axis=1)
+        acc[...] += dot_nt(both, wu[t])
 
     def norm_two_back(at):
         grad = kept[at] + acc[at]
@@ -734,7 +764,7 @@
 
 def self_grad_kernel(steps, rows, local, length, scalars, ins, outs, scratch):
     lens, where = scalars
-    dq2, z_one, dz_two, q_in, k_in, v_in, ain, ain_mate, aout, aout_mate, gain = ins
+    dq2, unit_one, rstd_one, dz_two, q_in, k_in, v_in, ain, ain_mate, aout, aout_mate, gain = ins
     text_grad, do_out, dq2_own, dq2_mate, qkv_own, qkv_mate, sums = outs
     wc, wo, wq, wk, wv, acc, kept, low, low_k, low_v, qs, ks, vs, part, sems = scratch
     total = rows * length
@@ -757,9 +787,9 @@
     by_columns(dq2[...], wc, to_acc, transposed=True)
 
     def norm_back(at):
-        unit, rstd = moments(z_one[at])
+        unit = unit_one[at]
         grad = dz_two[at] + acc[at]
-        dz = norm_grad(unit, rstd, gain[0:1], grad)
+        dz = norm_grad(unit, rstd_one[at], gain[0:1], grad)
         kept[at] = dz
         dz_low = dz.astype(BF16)
         low[at] = dz_low
@@ -1022,7 +1052,8 @@
             (attention_bias, whole_spec(attention_bias.shape)),
             (bias_mate, whole_spec(bias_mate.shape)),
         ],
-        [(image_shape, BF16, whole_spec(image_shape))] * 3,
+        [((own_images,) + image_shape[1:], BF16, whole_spec((own_images,) + image_shape[1:]))]
+        + [(image_shape, BF16, whole_spec(image_shape))] * 2,
         [
             patch_scratch,
             slabs(patch_count * images),
@@ -1056,7 +1087,7 @@
 
     attention_flops = 4 * 4 * all_tokens * width * 64
 
-    x, z_one, q_self, k_self, v_self, att_own, att_mate, self_low, queries = run(
+    x, unit_one, q_self, k_self, v_self, att_own, att_mate, self_low, queries, rstd_one = run(
         partial(self_kernel, steps, step_rows, local, length),
         steps,
         [lens, where],
@@ -1075,7 +1106,8 @@
         [token_out(width, BF16), token_out(width, F32)]
         + [token_out(width, BF16)] * 3
         + [token_out(local, BF16)] * 2
-        + [token_out(width, BF16)] * 2,
+        + [token_out(width, BF16)] * 2
+        + [token_out(1, F32)],
         [weight_scratch] * 5
         + [f32_tokens(width)] * 4
         + [low_tokens(width), pltpu.SemaphoreType.DMA((10,))],
@@ -1099,7 +1131,7 @@
         [
             whole(upstream_in),
             token_in(attended),
-            token_in(z_one),
+            token_in(unit_one),
             (attention_out, ANY),
             (aout_mate, ANY),
             (up_weight, ANY),
@@ -1123,13 +1155,16 @@
             ((steps, 2, hidden), F32, rows_spec((1, 2, hidden), 0)),
         ],
         [weight_scratch]
-        + [pltpu.VMEM((width, hidden), BF16)] * 2
-        + [pltpu.VMEM((hidden, width), BF16)] * 2
+        + [
+            pltpu.VMEM((hidden // TILE, width, 2 * TILE), BF16),
+            pltpu.VMEM((hidden // TILE, 2 * TILE, width), BF16),
+        ]
         + [f32_tokens(width)] * 3
         + [f32_tokens(1), low_tokens(width), low_tokens(width)]
-        + [pltpu.VMEM((2, tokens, hidden), F32)]
+        + [f32_tokens(2 * TILE)] * 2
+        + [pltpu.VMEM((hidden // TILE, tokens, 2 * TILE), F32)]
         + [pltpu.VMEM((8, 8, width), F32), pltpu.VMEM((2, 8, hidden), F32)]
-        + [pltpu.SemaphoreType.DMA((6,))],
+        + [pltpu.SemaphoreType.DMA((2 + 4 * hidden // TILE,))],
         2 * all_tokens * width * (2 * width + 8 * hidden),
     )
     merged_out, cross_low, grad_ffn, grad_cross, dz_two, a_own, a_mate = result[:7]
@@ -1204,7 +1239,8 @@
         [lens, where],
         [
             token_in(grad_queries),
-            token_in(z_one),
+            token_in(unit_one),
+            token_in(rstd_one),
             token_in(dz_two),
             token_in(q_self),
             token_in(k_self),
@@ -1293,7 +1329,7 @@
 
     up_grad, down_grad = last_sum(feed_parts, hidden)
     self_stage = second_swaps(*self_stage)
-    kv_low = proj[:own_images].reshape(flat_images, width)
+    kv_low = proj.reshape(flat_images, width)
     kv_away = low_tn(kv_low, kv_mate)
     kv_got = mate(kv_away)
     proj_away = lax.dynamic_slice_in_dim(proj_weight_sum, (1 - core) * local, local, 1)

time: 470 us -> 458 us (0.974)
  waiting for transfers between devices: 63.4 us -> 57.2 us
  local copies, waits for them, and re-layouts: 32.6 us -> 27.8 us
    ppermute x16, waiting for transfers between devices: 33.1 us -> 25.4 us  [partner_bits(): return lax.ppermute(value, 'dp', [(d, d ^ mask) for d in range(devices)])]
    pallas_call x13, Pallas kernels: 217 us -> 213 us  [run(): pl.pallas_call(kernel, grid_spec=pltpu.PrefetchScalarGridSpec(num_scalar_...]
  transfers between devices with their start and end apart: 39 -> 39, of which waited for: 12 -> 12; matrix products, arithmetic and copies ran while one was open for 18% -> 18% of each run, Pallas kernels for 35% -> 34%
where the time goes in v2:
time: 458 us; the launch traced here: 452 us
  Pallas kernels  213 us (47%)
  starting transfers between devices  80.5 us (18%)
  waiting for transfers between devices  57.2 us (12%)
  matrix products  44.1 us (10%)
  local copies, waits for them, and re-layouts  27.8 us (6%)
  other arithmetic  27.7 us (6%)
    pallas_call x13, Pallas kernels, run(): pl.pallas_call(kernel, grid_spec=pltpu.PrefetchScalarGridSpec(num_scalar_...  213 us
    dot_general x14, matrix products, dot_tn(): lax.dot_general(left, right, (((0,), (0,)), ((), ())), preferred_element_...  44.1 us
    all_to_all x5, starting transfers between devices, exchange(): return lax.all_to_all(value, 'dp', split_axis=0, concat_axis=0, tiled=True)  38.5 us
    ppermute x16, waiting for transfers between devices, partner_bits(): return lax.ppermute(value, 'dp', [(d, d ^ mask) for d in range(devices)])  25.4 us
    ppermute x16, starting transfers between devices, partner_bits(): return lax.ppermute(value, 'dp', [(d, d ^ mask) for d in range(devices)])  24.3 us
    all_to_all x5, waiting for transfers between devices, exchange(): return lax.all_to_all(value, 'dp', split_axis=0, concat_axis=0, tiled=True)  19 us
    all_to_all x3, starting transfers between devices, last_sum(): lax.all_to_all(both, 'dp', split_axis=0, concat_axis=0, axis_index_groups...  14.7 us
    all_to_all x3, waiting for transfers between devices, last_sum(): lax.all_to_all(both, 'dp', split_axis=0, concat_axis=0, axis_index_groups...  12.4 us
  transfers between devices with their start and end apart: 39, of which 12 were waited for; matrix products, arithmetic and copies ran while one was open for 18% of the time, Pallas kernels for 34%

profile of v2, /device:TPU:0, one launch (start us, length us, event | category | flops | bytes accessed | tf_op | source)
XLA Modules:
  0.0 451.8 jit_solution(4200947246403043945)
XLA Ops:
  3.6 7.9 %all-to-all-start = ((s32[16,2,6]{2,1,0:T(2,128)}), s32[16,2,6]{2,1,0:T(2,128)S(1)}, u32[]{:S(2)}, u32[]{:S(2)}) async-start(s32[16,2,6]{2,1,0:T(2,128)} %bitcast.4), calls=%async_computation | async-start | bytes 32768 | tf_op jit(solution)/shard_map/all_to_all | solution.py:972
  12.1 5.5 %shard_map.281 = (bf16[32,40,768]{2,1,0:T(8,128)(2,1)}, bf16[32,40,768]{2,1,0:T(8,128)(2,1)}) custom-call(s32[32]{0:T(128)} %select_reduce_fusion.1.refs_0_, bf16[48,40,768]{2,1,0:T(8,128)(2,1)} %refs_1_.1, bf16[48,40,768]{2,1,0:T(8,128)(2,1)} %refs_2_.2), custom_call_target="tpu_custom_call" | custom-call | bytes 9830400 | tf_op jit(solution)/shard_map/pallas_call | solution.py:64
  18.8 5.9 %all-to-all-start.2 = ((bf16[32,40,768]{2,1,0:T(8,128)(2,1)}), bf16[32,40,768]{2,1,0:T(8,128)(2,1)S(1)}, u32[]{:S(2)}, u32[]{:S(2)}) async-start(bf16[32,40,768]{2,1,0:T(8,128)(2,1)} %get-tuple-element.97), calls=%async_computation.2 | async-start | bytes 3932160 | tf_op jit(solution)/shard_map/all_to_all | solution.py:972
  29.3 22.8 %shard_map.282 = (bf16[8,160,768]{2,1,0:T(8,128)(2,1)}, bf16[16,160,768]{2,1,0:T(8,128)(2,1)}, bf16[16,160,768]{2,1,0:T(8,128)(2,1)}) custom-call(s32[1]{0:T(128)} %bitcast.refs_0_, bf16[145,16,1024]{2,1,0:T(8,128)(2,1)} %bitcast.168, bf16[1024,768]{1,0:T(8,128)(2,1)} %refs_4_.5, f32[1,768]{1,0:T(1,128)} %reshape.219.refs_3_, ...), custom_call_target="tpu_custom_call" | custom-call | flops 10066329600 | bytes 23247872 | tf_op jit(solution)/shard_map/pallas_call | solution.py:64
  52.1 13.5 %all-to-all-done.2.refs_2_ = bf16[32,40,768]{2,1,0:T(8,128)(2,1)S(1)} async-done(((bf16[32,40,768]{2,1,0:T(8,128)(2,1)}), bf16[32,40,768]{2,1,0:T(8,128)(2,1)S(1)}, u32[]{:S(2)}, u32[]{:S(2)}) %all-to-all-start.2) | async-done | bytes 1966112 | tf_op jit(solution)/shard_map/all_to_all | solution.py:972
  65.6 1.3 copy-done.7
  66.9 9.8 %all-to-all-start.1 = ((bf16[32,40,768]{2,1,0:T(8,128)(2,1)}), bf16[32,40,768]{2,1,0:T(8,128)(2,1)}, u32[]{:S(2)}, u32[]{:S(2)}) async-start(bf16[32,40,768]{2,1,0:T(8,128)(2,1)} %get-tuple-element.93), calls=%async_computation.1 | async-start | bytes 3932160 | tf_op jit(solution)/shard_map/all_to_all | solution.py:972
  77.9 22.1 %shard_map.283 = (bf16[960,768]{1,0:T(8,128)(2,1)}, f32[960,768]{1,0:T(8,128)}, bf16[960,768]{1,0:T(8,128)(2,1)}, bf16[960,768]{1,0:T(8,128)(2,1)}, bf16[960,768...) custom-call(s32[24]{0:T(128)} %get-tuple-element.96.refs_0_, ...), custom_call_target="tpu_custom_call" | custom-call | flops 6417285120 | bytes 24718080 | tf_op jit(solution)/shard_map/pallas_call | solution.py:64
  100.0 12.5 %shard_map.284.refs_2_ = bf16[960,768]{1,0:T(8,128)(2,1)} custom-call(s32[24]{0:T(128)} %and_select_fusion.refs_0_, s32[96]{0:T(128)} %reshape.218.refs_1_, bf16[960,768]{1,0:T(8,128)(2,1)} %get-tuple-element.109.refs_2_, bf16[16,160,768]{2,1,0:T(8,128)(2,1)} %get-tuple-element.100.refs_3_.refs_4_, bf16[16,160,768]{2,1,0:T(8,128)(2,1)} %get-tuple-element.101.refs_4_.refs_5_), custom_call_target="tpu_custom_call" | custom-call | flops 3019898880 | bytes 10813440 | tf_op jit(solution)/shard_map/pallas_call | solution.py:64
  112.5 4.4 all-to-all-done.1.refs_1_
  116.9 56.9 %shard_map.285 = (bf16[32,40,768]{2,1,0:T(8,128)(2,1)}, bf16[960,768]{1,0:T(8,128)(2,1)}, bf16[960,768]{1,0:T(8,128)(2,1)}, bf16[960,768]{1,0:T(8,128)(2,1)}, f3...) custom-call(s32[24]{0:T(128)} %compare_select_fusion.4.refs_1_.refs_, ...), custom_call_target="tpu_custom_call" | custom-call | flops 20384317440 | bytes 42384384 | tf_op jit(solution)/shard_map/pallas_call | solution.py:64
  173.8 6.5 %convolution_convert_fusion.1 = bf16[768,1536]{1,0:T(8,128)(2,1)} fusion(bf16[960,768]{1,0:T(8,128)(2,1)} %get-tuple-element.107, bf16[960,1536]{1,0:T(8,128)(2,1)} %get-tuple-element.108), kind=kOutput, calls=%fused_computation.7 | convolution fusion | flops 2266103808 | bytes 6782976 | tf_op jit(solution)/shard_map/dot_general | solution.py:38
  180.3 4.0 convolution_convert_fusion.2
  185.4 24.7 %shard_map.286 = (bf16[2,8,160,768]{3,2,1,0:T(8,128)(2,1)}, bf16[2,8,160,768]{3,2,1,0:T(8,128)(2,1)}, bf16[960,768]{1,0:T(8,128)(2,1)}) custom-call(s32[24]{0:T(128)} %and_select_fusion.refs_0_, s32[96]{0:T(128)} %reshape.218.refs_1_, bf16[960,768]{1,0:T(8,128)(2,1)} %get-tuple-element.109.refs_2_, bf16[960,768]{1,0:T(8,128)(2,1)} %get-tuple-element.110.refs_3_, ...), custom_call_target="tpu_custom_call" | custom-call | flops 9059696640 | bytes 20152320 | tf_op jit(solution)/shard_map/pallas_call | solution.py:64
  210.2 9.2 %all-to-all-start.3 = ((bf16[32,40,768]{2,1,0:T(8,128)(2,1)}), bf16[32,40,768]{2,1,0:T(8,128)(2,1)S(1)}, u32[]{:S(2)}, u32[]{:S(2)}) async-start(bf16[32,40,768]{2,1,0:T(8,128)(2,1)} %get-tuple-element.103), calls=%async_computation.3 | async-start | bytes 3932160 | tf_op jit(solution)/shard_map/all_to_all | solution.py:972
  219.4 2.5 convolution_convert_fusion.5
  222.0 2.1 fusion.30
  224.7 4.4 add_convert_fusion
  229.1 4.2 add_convert_fusion.1
  233.3 1.2 dynamic-slice_bitcast_fusion.2
  234.5 1.9 collective-permute-start.10
  236.5 1.2 dynamic-slice_bitcast_fusion
  237.7 1.5 collective-permute-start.11
  239.1 27.8 %shard_map.287 = (bf16[32,40,768]{2,1,0:T(8,128)(2,1)}, bf16[960,768]{1,0:T(8,128)(2,1)}, bf16[960,384]{1,0:T(8,128)(2,1)}, bf16[960,384]{1,0:T(8,128)(2,1)}, bf...) custom-call(s32[24]{0:T(128)} %get-tuple-element.96.refs_0_, ...), custom_call_target="tpu_custom_call" | custom-call | flops 7172259840 | bytes 30634752 | tf_op jit(solution)/shard_map/pallas_call | solution.py:64
  266.9 4.5 convolution_convert_fusion
  274.0 2.0 pad_maximum_fusion
  277.3 4.0 fusion.28
  281.3 2.0 fusion.29
  284.3 1.6 add_convert_fusion.4
  286.6 1.6 add_convert_fusion.3
  288.4 2.0 fusion.31
  290.5 10.2 %collective-permute-done.12 = bf16[2,2,48,1536]{3,2,1,0:T(8,128)(2,1)S(1)} collective-permute-done((bf16[2,2,48,1536]{3,2,1,0:T(8,128)(2,1)S(1)}, bf16[2,2,48,1536]{3,2,1,0:T(8,128)(2,1)S(1)}, u32[]{:S(2)}, u32[]{:S(2)}) %collective-permute-start.12) | collective-permute-done | bytes 589856 | tf_op jit(solution)/shard_map/ppermute | solution.py:1176
  300.8 1.8 collective-permute-done.13
  302.8 1.3 copy-done.3
  304.0 5.8 %all-to-all-start.4 = ((bf16[32,40,768]{2,1,0:T(8,128)(2,1)}), bf16[32,40,768]{2,1,0:T(8,128)(2,1)}, u32[]{:S(2)}, u32[]{:S(2)}) async-start(bf16[32,40,768]{2,1,0:T(8,128)(2,1)} %get-tuple-element.150), calls=%async_computation.4 | async-start | bytes 3932160 | tf_op jit(solution)/shard_map/all_to_all | solution.py:972
  311.9 3.8 fusion.refs_3_
  315.7 24.1 %shard_map.289 = (bf16[1280,768]{1,0:T(8,128)(2,1)}, bf16[1280,768]{1,0:T(8,128)(2,1)}, bf16[145,8,1024]{2,1,0:T(8,128)(2,1)}, f32[1024,768]{1,0:T(8,128)}, f32[8,768]{1,0:T(8,128)}) custom-call(s32[1]{0:T(128)} %bitcast.refs_0_, bf16[2,8,160,768]{3,2,1,0:T(8,128)(2,1)} %get-tuple-element.146.refs_1_, ...), custom_call_target="tpu_custom_call" | custom-call | flops 7046430720 | bytes 30744576 | tf_op jit(solution)/shard_map/pallas_call | solution.py:64
  339.8 1.5 dynamic-slice_convert_fusion
  342.7 2.0 collective-permute-start.27
  345.7 1.5 collective-permute-start.29
  347.2 2.8 convolution_convert_fusion.3.refs_3_
  349.9 4.0 shard_map.288
  354.4 4.8 %all-to-all-start.6 = ((bf16[4,48,3072]{2,1,0:T(8,128)(2,1)}), bf16[4,48,3072]{2,1,0:T(8,128)(2,1)}, u32[]{:S(2)}, u32[]{:S(2)}) async-start(bf16[4,48,3072]{2,1,0:T(8,128)(2,1)} %pad_maximum_fusion.1), calls=%async_computation.6 | async-start | bytes 2359296 | tf_op jit(solution)/shard_map/all_to_all | solution.py:1204
  359.2 4.0 shard_map.291
  363.2 1.8 add_convert_fusion.5
  365.7 1.5 reshape.226.refs_4_.refs_7_
  368.2 2.1 collective-permute-start.20
  370.3 1.6 fusion.2
  372.2 1.5 fusion.1
  375.5 3.1 add_convert_fusion.2.refs_3_.refs_6_
  383.1 3.4 shard_map.290
  386.5 3.4 shard_map.292
  390.1 1.5 convert_reduce_fusion
  392.5 1.5 shard_map.293
  398.2 6.5 %all-to-all-start.7 = ((bf16[4,48,2304]{2,1,0:T(8,128)(2,1)}), bf16[4,48,2304]{2,1,0:T(8,128)(2,1)S(1)}, u32[]{:S(2)}, u32[]{:S(2)}) async-start(bf16[4,48,2304]{2,1,0:T(8,128)(2,1)} %pad_maximum_fusion.2), calls=%async_computation.7 | async-start | bytes 1769472 | tf_op jit(solution)/shard_map/all_to_all | solution.py:1204
  404.7 1.4 collective-permute-start.24
  407.1 1.7 collective-permute-done.24
  408.9 3.2 collective-permute-start.25
  412.1 1.2 fusion.3
  413.3 7.0 %collective-permute-done.25 = f32[32,384]{1,0:T(8,128)S(1)} collective-permute-done((f32[32,384]{1,0:T(8,128)S(1)}, f32[32,384]{1,0:T(8,128)S(1)}, u32[]{:S(2)}, u32[]{:S(2)}) %collective-permute-start.25) | collective-permute-done | bytes 49184 | tf_op jit(solution)/shard_map/ppermute | solution.py:1176
  420.3 4.7 %collective-permute-start.26 = (f32[32,384]{1,0:T(8,128)S(1)}, f32[32,384]{1,0:T(8,128)S(1)}, u32[]{:S(2)}, u32[]{:S(2)}) collective-permute-start(f32[32,384]{1,0:T(8,128)S(1)} %add.248), channel_id=1, source_target_pairs={{0,16},{2,18},{4,20},{6,22},{8,24},{10,26},{12,28},{14,30},{16,0},... | collective-permute-start | bytes 147464 | tf_op jit(solution)/shard_map/ppermute | solution.py:1176
  426.1 3.1 collective-permute-done.26
  433.7 3.5 all-to-all-start.5
  438.0 12.4 %all-to-all-done.5 = bf16[4,48,1280]{2,1,0:T(8,128)(2,1)S(1)} async-done(((bf16[4,48,1280]{2,1,0:T(8,128)(2,1)}), bf16[4,48,1280]{2,1,0:T(8,128)(2,1)S(1)}, u32[]{:S(2)}, u32[]{:S(2)}) %all-to-all-start.5) | async-done | bytes 491552 | tf_op jit(solution)/shard_map/all_to_all | solution.py:1204
  (207 shorter events, 45.1 us)
Async XLA Ops:
  0.6 28.1 %collective-permute-start.1 = (bf16[2,3,768,384]{3,2,1,0:T(8,128)(2,1)}, bf16[2,3,768,384]{3,2,1,0:T(8,128)(2,1)}, u32[]{:S(2)}, u32[]{:S(2)}) collective-permute-start(bf16[2,3,768,384]{3,2,1,0:T(8,128)(2,1)} %refs_5_.3), channel_id=1, source_target_pairs={{0,1},{1,0},{2,3},{3,2},{4,5},{5,4},{6,7},{7,6},{8,9},{9,8},{10,11... | collective-permute-start | bytes 10616840 | tf_op jit(solution)/shard_map/ppermute | solution.py:966
  3.6 15.2 %all-to-all-start = ((s32[16,2,6]{2,1,0:T(2,128)}), s32[16,2,6]{2,1,0:T(2,128)S(1)}, u32[]{:S(2)}, u32[]{:S(2)}) async-start(s32[16,2,6]{2,1,0:T(2,128)} %bitcast.4), calls=%async_computation | async-start | bytes 32768 | tf_op jit(solution)/shard_map/all_to_all | solution.py:972
  18.8 5.9 %copy-start.16 = (bf16[2,384,768]{2,1,0:T(8,128)(2,1)S(1)}, bf16[2,384,768]{2,1,0:T(8,128)(2,1)}, u32[]{:S(2)}) copy-start(bf16[2,384,768]{2,1,0:T(8,128)(2,1)} %refs_11_.5) | copy-start | bytes 3538948
  18.8 6.0 %copy-start.17 = (f32[2,2,384]{2,1,0:T(2,128)S(1)}, f32[2,2,384]{2,1,0:T(2,128)}, u32[]{:S(2)}) copy-start(f32[2,2,384]{2,1,0:T(2,128)} %refs_7_.1) | copy-start | bytes 18436
  18.8 6.5 %copy-start.15 = (s32[1,16]{1,0:T(1,128)S(1)}, s32[1,16]{1,0:T(1,128)}, u32[]{:S(2)}) copy-start(s32[1,16]{1,0:T(1,128)} %param.22) | copy-start | bytes 196
  18.8 6.7 %copy-start.14 = (f32[768]{0:T(1024)S(1)}, f32[768]{0:T(1024)}, u32[]{:S(2)}) copy-start(f32[768]{0:T(1024)} %param.26) | copy-start | bytes 9220
  18.8 46.8 %all-to-all-start.2 = ((bf16[32,40,768]{2,1,0:T(8,128)(2,1)}), bf16[32,40,768]{2,1,0:T(8,128)(2,1)S(1)}, u32[]{:S(2)}, u32[]{:S(2)}) async-start(bf16[32,40,768]{2,1,0:T(8,128)(2,1)} %get-tuple-element.97), calls=%async_computation.2 | async-start | bytes 3932160 | tf_op jit(solution)/shard_map/all_to_all | solution.py:972
  24.7 4.0 collective-permute-start
  24.8 3.9 collective-permute-start.2
  52.1 25.1 %copy-start.12 = (f32[1536]{0:T(1024)S(1)}, f32[1536]{0:T(1024)}, u32[]{:S(2)}) copy-start(f32[1536]{0:T(1024)} %param.34) | copy-start | bytes 18436
  66.9 50.0 %all-to-all-start.1 = ((bf16[32,40,768]{2,1,0:T(8,128)(2,1)}), bf16[32,40,768]{2,1,0:T(8,128)(2,1)}, u32[]{:S(2)}, u32[]{:S(2)}) async-start(bf16[32,40,768]{2,1,0:T(8,128)(2,1)} %get-tuple-element.93), calls=%async_computation.1 | async-start | bytes 3932160 | tf_op jit(solution)/shard_map/all_to_all | solution.py:972
  76.6 35.9 %collective-permute-start.3 = (bf16[768,1536]{1,0:T(8,128)(2,1)}, bf16[768,1536]{1,0:T(8,128)(2,1)}, u32[]{:S(2)}, u32[]{:S(2)}) collective-permute-start(bf16[768,1536]{1,0:T(8,128)(2,1)} %refs_6_.3), channel_id=1, source_target_pairs={{0,1},{1,0},{2,3},{3,2},{4,5},{5,4},{6,7},{7,6},{8,9},{9,8},{10,11... | collective-permute-start | bytes 7077896 | tf_op jit(solution)/shard_map/ppermute | solution.py:966
  76.7 35.8 %collective-permute-start.4 = (bf16[1536,768]{1,0:T(8,128)(2,1)}, bf16[1536,768]{1,0:T(8,128)(2,1)}, u32[]{:S(2)}, u32[]{:S(2)}) collective-permute-start(bf16[1536,768]{1,0:T(8,128)(2,1)} %refs_8_.1), channel_id=1, source_target_pairs={{0,1},{1,0},{2,3},{3,2},{4,5},{5,4},{6,7},{7,6},{8,9},{9,8},{10,11... | collective-permute-start | bytes 7077896 | tf_op jit(solution)/shard_map/ppermute | solution.py:966
  77.2 22.8 %copy-start.13 = (f32[1,1536]{1,0:T(1,128)}, f32[1,1536]{1,0:T(1,128)S(1)}, u32[]{:S(2)}) copy-start(f32[1,1536]{1,0:T(1,128)S(1)} %reshape.220.refs_13_) | copy-start | bytes 18436
  77.2 35.3 %collective-permute-start.5 = (f32[1,1536]{1,0:T(1,128)S(1)}, f32[1,1536]{1,0:T(1,128)S(1)}, u32[]{:S(2)}, u32[]{:S(2)}) collective-permute-start(f32[1,1536]{1,0:T(1,128)S(1)} %reshape.220.refs_13_), channel_id=1, source_target_pairs={{0,1},{1,0},{2,3},{3,2},{4,5},{5,4},{6,7},{7,6},{8,9},{9,8},{10,11... | collective-permute-start | bytes 18440 | tf_op jit(solution)/shard_map/ppermute | solution.py:966
  112.5 4.4 copy-start.19
  173.8 6.5 %copy-start.25 = (bf16[960,1536]{1,0:T(8,128)(2,1)S(1)}, bf16[960,1536]{1,0:T(8,128)(2,1)}, u32[]{:S(2)}) copy-start(bf16[960,1536]{1,0:T(8,128)(2,1)} %get-tuple-element.106) | copy-start | bytes 8847364
  173.8 6.5 %copy-start.29 = (bf16[960,768]{1,0:T(8,128)(2,1)S(1)}, bf16[960,768]{1,0:T(8,128)(2,1)}, u32[]{:S(2)}) copy-start(bf16[960,768]{1,0:T(8,128)(2,1)} %get-tuple-element.105) | copy-start | bytes 4423684
  184.2 39.9 %collective-permute-start.8 = (bf16[768,1536]{1,0:T(8,128)(2,1)}, bf16[768,1536]{1,0:T(8,128)(2,1)}, u32[]{:S(2)}, u32[]{:S(2)}) collective-permute-start(bf16[768,1536]{1,0:T(8,128)(2,1)} %convolution_convert_fusion.1), channel_id=1, source_target_pairs={{0,1},{1,0},{2,3},{3,2},{4,5},{5,4},{6,7},{7,6},{8,9},{9,8},{10,11... | collective-permute-start | bytes 7077896 | tf_op jit(solution)/shard_map/ppermute | solution.py:966
  184.2 44.8 %collective-permute-start.7 = (bf16[768,1536]{1,0:T(8,128)(2,1)}, bf16[768,1536]{1,0:T(8,128)(2,1)}, u32[]{:S(2)}, u32[]{:S(2)}) collective-permute-start(bf16[768,1536]{1,0:T(8,128)(2,1)} %convolution_convert_fusion.2), channel_id=1, source_target_pairs={{0,1},{1,0},{2,3},{3,2},{4,5},{5,4},{6,7},{7,6},{8,9},{9,8},{10,11... | collective-permute-start | bytes 7077896 | tf_op jit(solution)/shard_map/ppermute | solution.py:966
  210.2 105.5 %collective-permute-start.6 = (bf16[2,8,160,768]{3,2,1,0:T(8,128)(2,1)}, bf16[2,8,160,768]{3,2,1,0:T(8,128)(2,1)}, u32[]{:S(2)}, u32[]{:S(2)}) collective-permute-start(bf16[2,8,160,768]{3,2,1,0:T(8,128)(2,1)} %get-tuple-element.112), channel_id=1, source_target_pairs={{0,1},{1,0},{2,3},{3,2},{4,5},{5,4},{6,7},{7,6},{8,9},{9,8},{10,11... | collective-permute-start | bytes 11796488 | tf_op jit(solution)/shard_map/ppermute | solution.py:966
  210.2 9.2 %copy-start.34 = (bf16[960,384]{1,0:T(8,128)(2,1)S(1)}, bf16[960,384]{1,0:T(8,128)(2,1)}, u32[]{:S(2)}) copy-start(bf16[960,384]{1,0:T(8,128)(2,1)} %get-tuple-element.134) | copy-start | bytes 2211844
  210.2 92.6 %all-to-all-start.3 = ((bf16[32,40,768]{2,1,0:T(8,128)(2,1)}), bf16[32,40,768]{2,1,0:T(8,128)(2,1)S(1)}, u32[]{:S(2)}, u32[]{:S(2)}) async-start(bf16[32,40,768]{2,1,0:T(8,128)(2,1)} %get-tuple-element.103), calls=%async_computation.3 | async-start | bytes 3932160 | tf_op jit(solution)/shard_map/all_to_all | solution.py:972
  224.7 4.4 copy-start.30
  224.7 4.4 copy-start.39
  234.5 48.8 %collective-permute-start.10 = (bf16[2,2,2,48,1536]{4,3,2,1,0:T(8,128)(2,1)}, bf16[2,2,2,48,1536]{4,3,2,1,0:T(8,128)(2,1)S(1)}, u32[]{:S(2)}, u32[]{:S(2)}) collective-permute-start(bf16[2,2,2,48,1536]{4,3,2,1,0:T(8,128)(2,1)} %get-tuple-element.170), channel_id=1, source_target_pairs={{0,2},{2,0},{4,6},{6,4},{8,10},{10,8},{12,14},{14,12},{16,18},{18,... | collective-permute-start | bytes 3538952 | tf_op jit(solution)/shard_map/ppermute | solution.py:1176
  237.7 45.7 %collective-permute-start.11 = (bf16[2,2,2,48,1536]{4,3,2,1,0:T(8,128)(2,1)}, bf16[2,2,2,48,1536]{4,3,2,1,0:T(8,128)(2,1)}, u32[]{:S(2)}, u32[]{:S(2)}) collective-permute-start(bf16[2,2,2,48,1536]{4,3,2,1,0:T(8,128)(2,1)} %get-tuple-element.168), channel_id=1, source_target_pairs={{0,4},{2,6},{4,0},{6,2},{8,12},{10,14},{12,8},{14,10},{16,20},{18,... | collective-permute-start | bytes 3538952 | tf_op jit(solution)/shard_map/ppermute | solution.py:1176
  266.9 4.5 copy-start.24
  266.9 4.5 copy-start.33
  276.0 35.1 %collective-permute-start.9 = (bf16[768,2304]{1,0:T(8,128)(2,1)}, bf16[768,2304]{1,0:T(8,128)(2,1)}, u32[]{:S(2)}, u32[]{:S(2)}) collective-permute-start(bf16[768,2304]{1,0:T(8,128)(2,1)} %pad_maximum_fusion), channel_id=1, source_target_pairs={{0,1},{1,0},{2,3},{3,2},{4,5},{5,4},{6,7},{7,6},{8,9},{9,8},{10,11... | collective-permute-start | bytes 10616840 | tf_op jit(solution)/shard_map/ppermute | solution.py:966
  277.3 4.0 copy-start.26
  286.0 14.7 %collective-permute-start.12 = (bf16[2,2,48,1536]{3,2,1,0:T(8,128)(2,1)S(1)}, bf16[2,2,48,1536]{3,2,1,0:T(8,128)(2,1)S(1)}, u32[]{:S(2)}, u32[]{:S(2)}) collective-permute-start(bf16[2,2,48,1536]{3,2,1,0:T(8,128)(2,1)S(1)} %dynamic-slice_bitcast_fusion.8), channel_id=1, source_target_pairs={{0,4},{2,6},{4,0},{6,2},{8,12},{10,14},{12,8},{14,10},{16,20},{18,... | collective-permute-start | bytes 1769480 | tf_op jit(solution)/shard_map/ppermute | solution.py:1176
  288.2 14.4 %collective-permute-start.13 = (bf16[2,2,48,1536]{3,2,1,0:T(8,128)(2,1)S(1)}, bf16[2,2,48,1536]{3,2,1,0:T(8,128)(2,1)S(1)}, u32[]{:S(2)}, u32[]{:S(2)}) collective-permute-start(bf16[2,2,48,1536]{3,2,1,0:T(8,128)(2,1)S(1)} %dynamic-slice_bitcast_fusion.7), channel_id=1, source_target_pairs={{0,2},{2,0},{4,6},{6,4},{8,10},{10,8},{12,14},{14,12},{16,18},{18,... | collective-permute-start | bytes 1769480 | tf_op jit(solution)/shard_map/ppermute | solution.py:1176
  304.0 50.4 %all-to-all-start.4 = ((bf16[32,40,768]{2,1,0:T(8,128)(2,1)}), bf16[32,40,768]{2,1,0:T(8,128)(2,1)}, u32[]{:S(2)}, u32[]{:S(2)}) async-start(bf16[32,40,768]{2,1,0:T(8,128)(2,1)} %get-tuple-element.150), calls=%async_computation.4 | async-start | bytes 3932160 | tf_op jit(solution)/shard_map/all_to_all | solution.py:972
  315.7 25.7 %copy-start = (bf16[768,2304]{1,0:T(8,128)(2,1)}, bf16[768,2304]{1,0:T(8,128)(2,1)S(1)}, u32[]{:S(2)}) copy-start(bf16[768,2304]{1,0:T(8,128)(2,1)S(1)} %fusion.refs_3_) | copy-start | bytes 10616836
  341.3 21.9 %collective-permute-start.17 = (bf16[1024,384]{1,0:T(8,128)(2,1)S(1)}, bf16[1024,384]{1,0:T(8,128)(2,1)}, u32[]{:S(2)}, u32[]{:S(2)}) collective-permute-start(bf16[1024,384]{1,0:T(8,128)(2,1)S(1)} %dynamic-slice_convert_fusion), channel_id=1, source_target_pairs={{0,1},{1,0},{2,3},{3,2},{4,5},{5,4},{6,7},{7,6},{8,9},{9,8},{10,11... | collective-permute-start | bytes 2359304 | tf_op jit(solution)/shard_map/ppermute | solution.py:966
  341.4 5.8 %copy-start.37 = (bf16[1280,768]{1,0:T(8,128)(2,1)S(1)}, bf16[1280,768]{1,0:T(8,128)(2,1)}, u32[]{:S(2)}) copy-start(bf16[1280,768]{1,0:T(8,128)(2,1)} %get-tuple-element.149) | copy-start | bytes 5898244
  341.7 8.2 %copy-start.4 = (bf16[768,1152]{1,0:T(8,128)(2,1)}, bf16[768,1152]{1,0:T(8,128)(2,1)S(1)}, u32[]{:S(2)}) copy-start(bf16[768,1152]{1,0:T(8,128)(2,1)S(1)} %get-tuple-element.166) | copy-start | bytes 5308420
  341.7 5.5 %copy-start.20 = (bf16[8,160,768]{2,1,0:T(8,128)(2,1)S(1)}, bf16[8,160,768]{2,1,0:T(8,128)(2,1)}, u32[]{:S(2)}) copy-start(bf16[8,160,768]{2,1,0:T(8,128)(2,1)} %get-tuple-element.145) | copy-start | bytes 5898244
  342.7 25.5 %collective-permute-start.27 = (bf16[2,2,2,48,1152]{4,3,2,1,0:T(8,128)(2,1)}, bf16[2,2,2,48,1152]{4,3,2,1,0:T(8,128)(2,1)}, u32[]{:S(2)}, u32[]{:S(2)}) collective-permute-start(bf16[2,2,2,48,1152]{4,3,2,1,0:T(8,128)(2,1)} %dynamic-slice_bitcast_fusion.5), channel_id=1, source_target_pairs={{0,2},{2,0},{4,6},{6,4},{8,10},{10,8},{12,14},{14,12},{16,18},{18,... | collective-permute-start | bytes 2654216 | tf_op jit(solution)/shard_map/ppermute | solution.py:1176
  345.7 26.4 %collective-permute-start.29 = (bf16[2,2,2,48,1152]{4,3,2,1,0:T(8,128)(2,1)}, bf16[2,2,2,48,1152]{4,3,2,1,0:T(8,128)(2,1)}, u32[]{:S(2)}, u32[]{:S(2)}) collective-permute-start(bf16[2,2,2,48,1152]{4,3,2,1,0:T(8,128)(2,1)} %dynamic-slice_bitcast_fusion.4), channel_id=1, source_target_pairs={{0,4},{2,6},{4,0},{6,2},{8,12},{10,14},{12,8},{14,10},{16,20},{18,... | collective-permute-start | bytes 2654216 | tf_op jit(solution)/shard_map/ppermute | solution.py:1176
  349.9 24.6 %collective-permute-start.15 = (bf16[768,768]{1,0:T(8,128)(2,1)}, bf16[768,768]{1,0:T(8,128)(2,1)}, u32[]{:S(2)}, u32[]{:S(2)}) collective-permute-start(bf16[768,768]{1,0:T(8,128)(2,1)} %convolution_convert_fusion.3.refs_3_), channel_id=1, source_target_pairs={{0,1},{1,0},{2,3},{3,2},{4,5},{5,4},{6,7},{7,6},{8,9},{9,8},{10,11... | collective-permute-start | bytes 3538952 | tf_op jit(solution)/shard_map/ppermute | solution.py:966
  353.9 28.1 %collective-permute-start.14 = (bf16[20,24,768]{2,1,0:T(8,128)(2,1)}, bf16[20,24,768]{2,1,0:T(8,128)(2,1)}, u32[]{:S(2)}, u32[]{:S(2)}) collective-permute-start(bf16[20,24,768]{2,1,0:T(8,128)(2,1)} %get-tuple-element.144), channel_id=1, source_target_pairs={{0,1},{1,0},{2,3},{3,2},{4,5},{5,4},{6,7},{7,6},{8,9},{9,8},{10,11... | collective-permute-start | bytes 2211848 | tf_op jit(solution)/shard_map/ppermute | solution.py:966
  354.4 35.7 %all-to-all-start.6 = ((bf16[4,48,3072]{2,1,0:T(8,128)(2,1)}), bf16[4,48,3072]{2,1,0:T(8,128)(2,1)}, u32[]{:S(2)}, u32[]{:S(2)}) async-start(bf16[4,48,3072]{2,1,0:T(8,128)(2,1)} %pad_maximum_fusion.1), calls=%async_computation.6 | async-start | bytes 2359296 | tf_op jit(solution)/shard_map/all_to_all | solution.py:1204
  363.2 23.3 %collective-permute-start.16 = (bf16[20,24,768]{2,1,0:T(8,128)(2,1)}, bf16[20,24,768]{2,1,0:T(8,128)(2,1)}, u32[]{:S(2)}, u32[]{:S(2)}) collective-permute-start(bf16[20,24,768]{2,1,0:T(8,128)(2,1)} %get-tuple-element.152), channel_id=1, source_target_pairs={{0,1},{1,0},{2,3},{3,2},{4,5},{5,4},{6,7},{7,6},{8,9},{9,8},{10,11... | collective-permute-start | bytes 2211848 | tf_op jit(solution)/shard_map/ppermute | solution.py:966
  365.7 6.3 %copy-start.5 = (bf16[2,2,2,2,48,512]{5,4,3,2,1,0:T(8,128)(2,1)}, bf16[2,2,2,2,48,512]{5,4,3,2,1,0:T(8,128)(2,1)S(1)}, u32[]{:S(2)}) copy-start(bf16[2,2,2,2,48,512]{5,4,3,2,1,0:T(8,128)(2,1)S(1)} %reshape_reshape.3) | copy-start | bytes 2359300
  368.2 12.1 %collective-permute-start.20 = (bf16[2,2,2,48,512]{4,3,2,1,0:T(8,128)(2,1)S(1)}, bf16[2,2,2,48,512]{4,3,2,1,0:T(8,128)(2,1)S(1)}, u32[]{:S(2)}, u32[]{:S(2)}) collective-permute-start(bf16[2,2,2,48,512]{4,3,2,1,0:T(8,128)(2,1)S(1)} %dynamic-slice_bitcast_fusion.11), channel_id=1, source_target_pairs={{0,4},{2,6},{4,0},{6,2},{8,12},{10,14},{12,8},{14,10},{16,20},{18,... | collective-permute-start | bytes 1179656 | tf_op jit(solution)/shard_map/ppermute | solution.py:1176
  372.0 3.5 copy-start.36
  372.1 3.4 copy-start.21
  372.1 17.9 %collective-permute-start.28 = (bf16[2,2,48,1152]{3,2,1,0:T(8,128)(2,1)S(1)}, bf16[2,2,48,1152]{3,2,1,0:T(8,128)(2,1)S(1)}, u32[]{:S(2)}, u32[]{:S(2)}) collective-permute-start(bf16[2,2,48,1152]{3,2,1,0:T(8,128)(2,1)S(1)} %dynamic-slice_bitcast_fusion.10), channel_id=1, source_target_pairs={{0,4},{2,6},{4,0},{6,2},{8,12},{10,14},{12,8},{14,10},{16,20},{18,... | collective-permute-start | bytes 1327112 | tf_op jit(solution)/shard_map/ppermute | solution.py:1176
  374.5 19.5 %collective-permute-start.30 = (bf16[2,2,48,1152]{3,2,1,0:T(8,128)(2,1)}, bf16[2,2,48,1152]{3,2,1,0:T(8,128)(2,1)}, u32[]{:S(2)}, u32[]{:S(2)}) collective-permute-start(bf16[2,2,48,1152]{3,2,1,0:T(8,128)(2,1)} %dynamic-slice_bitcast_fusion.9), channel_id=1, source_target_pairs={{0,2},{2,0},{4,6},{6,4},{8,10},{10,8},{12,14},{14,12},{16,18},{18,... | collective-permute-start | bytes 1327112 | tf_op jit(solution)/shard_map/ppermute | solution.py:1176
  375.5 5.7 %copy-start.6 = (bf16[2,2,2,2,48,512]{5,4,3,2,1,0:T(8,128)(2,1)S(1)}, bf16[2,2,2,2,48,512]{5,4,3,2,1,0:T(8,128)(2,1)}, u32[]{:S(2)}) copy-start(bf16[2,2,2,2,48,512]{5,4,3,2,1,0:T(8,128)(2,1)} %copy-done.5) | copy-start | bytes 2359300
  378.6 4.5 copy-start.1
  380.2 31.9 %collective-permute-start.18 = (bf16[2,2,2,48,768]{4,3,2,1,0:T(8,128)(2,1)}, bf16[2,2,2,48,768]{4,3,2,1,0:T(8,128)(2,1)}, u32[]{:S(2)}, u32[]{:S(2)}) collective-permute-start(bf16[2,2,2,48,768]{4,3,2,1,0:T(8,128)(2,1)} %dynamic-slice_bitcast_fusion.6), channel_id=1, source_target_pairs={{0,2},{2,0},{4,6},{6,4},{8,10},{10,8},{12,14},{14,12},{16,18},{18,... | collective-permute-start | bytes 1769480 | tf_op jit(solution)/shard_map/ppermute | solution.py:1176
  382.0 24.1 %collective-permute-start.21 = (bf16[2,2,48,512]{3,2,1,0:T(8,128)(2,1)}, bf16[2,2,48,512]{3,2,1,0:T(8,128)(2,1)}, u32[]{:S(2)}, u32[]{:S(2)}) collective-permute-start(bf16[2,2,48,512]{3,2,1,0:T(8,128)(2,1)} %dynamic-slice_bitcast_fusion.13), channel_id=1, source_target_pairs={{0,2},{2,0},{4,6},{6,4},{8,10},{10,8},{12,14},{14,12},{16,18},{18,... | collective-permute-start | bytes 589832 | tf_op jit(solution)/shard_map/ppermute | solution.py:1176
  394.0 1.4 collective-permute-start.22
  396.2 8.5 %collective-permute-start.23 = (f32[32,384]{1,0:T(8,128)S(1)}, f32[32,384]{1,0:T(8,128)S(1)}, u32[]{:S(2)}, u32[]{:S(2)}) collective-permute-start(f32[32,384]{1,0:T(8,128)S(1)} %add.245), channel_id=1, source_target_pairs={{0,2},{2,0},{4,6},{6,4},{8,10},{10,8},{12,14},{14,12},{16,18},{18,... | collective-permute-start | bytes 147464 | tf_op jit(solution)/shard_map/ppermute | solution.py:1176
  398.2 13.9 %copy-start.2 = (bf16[768,768]{1,0:T(8,128)(2,1)S(1)}, bf16[768,768]{1,0:T(8,128)(2,1)}, u32[]{:S(2)}) copy-start(bf16[768,768]{1,0:T(8,128)(2,1)} %copy-done.1) | copy-start | bytes 3538948
  398.2 35.4 %all-to-all-start.7 = ((bf16[4,48,2304]{2,1,0:T(8,128)(2,1)}), bf16[4,48,2304]{2,1,0:T(8,128)(2,1)S(1)}, u32[]{:S(2)}, u32[]{:S(2)}) async-start(bf16[4,48,2304]{2,1,0:T(8,128)(2,1)} %pad_maximum_fusion.2), calls=%async_computation.7 | async-start | bytes 1769472 | tf_op jit(solution)/shard_map/all_to_all | solution.py:1204
  404.7 4.2 collective-permute-start.24
  408.9 11.4 %collective-permute-start.25 = (f32[32,384]{1,0:T(8,128)S(1)}, f32[32,384]{1,0:T(8,128)S(1)}, u32[]{:S(2)}, u32[]{:S(2)}) collective-permute-start(f32[32,384]{1,0:T(8,128)S(1)} %add.247), channel_id=1, source_target_pairs={{0,8},{2,10},{4,12},{6,14},{8,0},{10,2},{12,4},{14,6},{16,24},{18,... | collective-permute-start | bytes 147464 | tf_op jit(solution)/shard_map/ppermute | solution.py:1176
  420.3 8.8 %collective-permute-start.26 = (f32[32,384]{1,0:T(8,128)S(1)}, f32[32,384]{1,0:T(8,128)S(1)}, u32[]{:S(2)}, u32[]{:S(2)}) collective-permute-start(f32[32,384]{1,0:T(8,128)S(1)} %add.248), channel_id=1, source_target_pairs={{0,16},{2,18},{4,20},{6,22},{8,24},{10,26},{12,28},{14,30},{16,0},... | collective-permute-start | bytes 147464 | tf_op jit(solution)/shard_map/ppermute | solution.py:1176
  425.0 7.8 %collective-permute-start.19 = (bf16[2,2,48,768]{3,2,1,0:T(8,128)(2,1)S(1)}, bf16[2,2,48,768]{3,2,1,0:T(8,128)(2,1)S(1)}, u32[]{:S(2)}, u32[]{:S(2)}) collective-permute-start(bf16[2,2,48,768]{3,2,1,0:T(8,128)(2,1)S(1)} %dynamic-slice_bitcast_fusion.12), channel_id=1, source_target_pairs={{0,4},{2,6},{4,0},{6,2},{8,12},{10,14},{12,8},{14,10},{16,20},{18,... | collective-permute-start | bytes 884744 | tf_op jit(solution)/shard_map/ppermute | solution.py:1176
  433.7 16.7 %all-to-all-start.5 = ((bf16[4,48,1280]{2,1,0:T(8,128)(2,1)}), bf16[4,48,1280]{2,1,0:T(8,128)(2,1)S(1)}, u32[]{:S(2)}, u32[]{:S(2)}) async-start(bf16[4,48,1280]{2,1,0:T(8,128)(2,1)} %pad_maximum_fusion.3), calls=%async_computation.5 | async-start | bytes 983040 | tf_op jit(solution)/shard_map/all_to_all | solution.py:1204
  (16 other events, 30.1 us)

commit v3 on v2

--- a/solution.py
+++ b/solution.py
@@ -74,7 +74,9 @@
         compiler_params=pltpu.CompilerParams(
             dimension_semantics=("arbitrary",), vmem_limit_bytes=VMEM_LIMIT
         ),
-        cost_estimate=pl.CostEstimate(flops=flops, bytes_accessed=moved, transcendentals=0),
+        cost_estimate=pl.CostEstimate(
+            flops=flops, bytes_accessed=moved, transcendentals=0
+        ),
     )(*scalars, *[array for array, _ in ins])
 
 
@@ -289,11 +291,13 @@
     first = core[0] * own_images
     rest = jnp.zeros((patch_pad - patch_count, width), F32)
 
-    @pl.loop(0, images // 2)
+    group = 4
+
+    @pl.loop(0, images // group)
     def _(step):
         both = []
-        for at in range(2):
-            which = lax.rem(step * 2 + at + first, images)
+        for at in range(group):
+            which = lax.rem(step * group + at + first, images)
             own = jnp.concatenate(
                 [
                     raw[lane, pl.ds(which, patch_count, stride=images), :]
@@ -303,19 +307,18 @@
             )
             both.append(jnp.concatenate([own, rest], axis=0))
         low = jnp.concatenate(both, axis=0).astype(BF16)
-        pair = pl.ds(step * 2, 2)
-
-        @pl.when(step < own_images // 2)
+        some = pl.ds(step * group, group)
+
+        @pl.when(step < own_images // group)
         def _():
-            proj[pair] = low.reshape(2, patch_pad, width)
-
+            proj[some] = low.reshape(group, patch_pad, width)
+
+        shape = (group, patch_pad, GROUP)
         for start in range(0, width, GROUP):
             cols = slice(start, start + GROUP)
-            keys[pair, :, cols] = (
-                dot(low, w1[:, cols]).astype(BF16).reshape(2, patch_pad, GROUP)
-            )
-            values[pair, :, cols] = (
-                (dot(low, w2[:, cols]) + bias[:, cols]).astype(BF16).reshape(2, patch_pad, GROUP)
+            keys[some, :, cols] = dot(low, w1[:, cols]).astype(BF16).reshape(shape)
+            values[some, :, cols] = (
+                (dot(low, w2[:, cols]) + bias[:, cols]).astype(BF16).reshape(shape)
             )
 
 
@@ -524,7 +527,7 @@
     biases = (up_bias, up_bias_mate)
 
     def activate(units, t):
-        cols = pl.ds(pl.multiple_of(t * TILE, TILE), TILE)
+        cols = slice(t * TILE, (t + 1) * TILE)
         for half in range(2):
             lanes = slice(half * TILE, (half + 1) * TILE)
             bias = biases[half][:, cols]
@@ -535,21 +538,17 @@
                 slope[t, at, lanes] = sloped
 
     def add_down(t):
-        cols = pl.ds(pl.multiple_of(t * TILE, TILE), TILE)
+        cols = slice(t * TILE, (t + 1) * TILE)
         both = jnp.concatenate([g_out[0][:, cols], g_out[1][:, cols]], axis=1)
         acc[...] += dot(both, wd[t])
 
+    units = (even, odd)
     even[...] = dot(low[...], wu[0])
-
-    @pl.loop(0, tiles // 2)
-    def _(step):
-        first = 2 * step
-        odd[...] = dot(low[...], wu[first + 1])
-        activate(even, first)
-        add_down(first)
-        even[...] = dot(low[...], wu[jnp.minimum(first + 2, tiles - 1)])
-        activate(odd, first + 1)
-        add_down(first + 1)
+    for t in range(tiles):
+        if t + 1 < tiles:
+            units[(t + 1) % 2][...] = dot(low[...], wu[t + 1])
+        activate(units[t % 2], t)
+        add_down(t)
 
     def norm_three(at):
         unit, rstd = moments(kept[at] + acc[at] + out_bias[2:3])
@@ -574,9 +573,8 @@
         merged[where[base + row]] = acc[row * length : (row + 1) * length].astype(BF16)
     acc[...] = jnp.zeros_like(acc)
 
-    @pl.loop(0, tiles)
-    def _(t):
-        cols = pl.ds(pl.multiple_of(t * TILE, TILE), TILE)
+    for t in range(tiles):
+        cols = slice(t * TILE, (t + 1) * TILE)
         grads = dot_nt(low[...], wd[t])
         for half in range(2):
             lanes = slice(half * TILE, (half + 1) * TILE)
@@ -864,6 +862,19 @@
         text_grad[where[base + row]] = acc[row * length : (row + 1) * length].astype(BF16)
     for at in range(8):
         sums[0, at : at + 1] = jnp.sum(part[at], axis=0, keepdims=True)
+
+
+def join_kernel(scalars, ins, outs, scratch):
+    stay_x, got_x, stay_y, got_y = ins
+    (out,) = outs
+    for start, stay, got in ((0, stay_x, got_x), (stay_x.shape[1], stay_y, got_y)):
+        for at in range(0, out.shape[0], 96):
+            rows = slice(at, at + 96)
+            out[rows, start : start + stay.shape[1]] = add_low(stay[rows], got[rows])
+
+
+def add_low(left, right):
+    return (left.astype(F32) + right.astype(F32)).astype(BF16)
 
 
 def pack_kernel(local, hidden, scalars, ins, outs, scratch):
@@ -1191,13 +1202,23 @@
         return swap(add(stay_x, got_x), bits - 2, 1) + swap(add(stay_y, got_y), bits - 2, 0)
 
     def add(stay, got):
-        return (stay.astype(F32) + got.astype(F32)).astype(BF16)
-
-    def last_parts(stay_x, got_x, stay_y, got_y):
-        parts = [add(stay_x, got_x), add(stay_y, got_y)]
-        return jnp.concatenate(
-            [part.reshape((devices // 4,) + part.shape[-2:]) for part in parts], axis=2
+        return add_low(stay, got)
+
+    def last_parts(values, after):
+        count = values[0].size // values[0].shape[-1]
+        shape = (count, values[0].shape[-1] + values[2].shape[-1])
+        values = [value.reshape(count, value.shape[-1]) for value in values]
+        (joined,) = run(
+            join_kernel,
+            1,
+            [],
+            [whole(value) for value in values],
+            [(shape, BF16, whole_spec(shape))],
+            [],
+            0,
+            after,
         )
+        return joined.reshape(devices // 4, count // (devices // 4), shape[1])
 
     def last_sum(both, first_width):
         groups = [[low + 4 * n for n in range(devices // 4)] for low in range(4)]
@@ -1290,8 +1311,6 @@
     self_part = (self_own + self_got.astype(F32)).astype(BF16)
     half_width = self_part.shape[1] // 2
     self_stage = first_swaps(self_part[:, :half_width], self_part[:, half_width:])
-    feed_parts = last_parts(*feed_stage)
-    piece, piece_mate, self_part, feed_parts = tie(piece, piece_mate, self_part, feed_parts)
 
     flat_images = own_images * patch_pad
     patch_grad_shape = (patch_count, own_images, vision)
@@ -1327,7 +1346,7 @@
         2 * flat_images * width * (2 * width + 2 * vision),
     )
 
-    up_grad, down_grad = last_sum(feed_parts, hidden)
+    up_grad, down_grad = last_sum(last_parts(feed_stage, [kv_own]), hidden)
     self_stage = second_swaps(*self_stage)
     kv_low = proj.reshape(flat_images, width)
     kv_away = low_tn(kv_low, kv_mate)
@@ -1339,9 +1358,9 @@
     proj_part = (proj_own + proj_got.astype(F32)).astype(BF16)
     proj_part = proj_part.reshape(width, vision * local // width)
     image_stage = first_swaps(kv_part, proj_part)
-    self_one, self_two = last_sum(last_parts(*self_stage), half_width)
+    self_one, self_two = last_sum(last_parts(self_stage, []), half_width)
     image_stage = second_swaps(*image_stage)
-    kv_grad, proj_grad = last_sum(last_parts(*image_stage), width)
+    kv_grad, proj_grad = last_sum(last_parts(image_stage, []), width)
     proj_grad = proj_grad.reshape(vision // devices, local)
 
     lines = 23 + hidden // local
@@ -1400,7 +1419,7 @@
 
     return (
         tokens_out(merged_in, [self_part], [kv_part]),
-        tokens_out(text_in, [kv_away], [kv_part, proj_part]),
+        tokens_out(text_in, [kv_own], [kv_part, proj_part]),
         jnp.transpose(patch_grad, (1, 0, 2)),
         proj_grad,
         proj_bias_grad,

time: 458 us -> 488 us (1.066)
  waiting for transfers between devices: 57.2 us -> 83.8 us
  Pallas kernels: 213 us -> 225 us
  starting transfers between devices: 80.5 us -> 71.5 us
  local copies, waits for them, and re-layouts: 27.8 us -> 35.6 us
  other arithmetic: 27.7 us -> 20.2 us
    ppermute x16, waiting for transfers between devices: 25.4 us -> 51.5 us  [partner_bits(): return lax.ppermute(value, 'dp', [(d, d ^ mask) for d in range(devices)])]
    pallas_call x13 -> x16, Pallas kernels: 213 us -> 225 us  [run(): pl.pallas_call(kernel, grid_spec=pltpu.PrefetchScalarGridSpec(num_scalar_...]
    ppermute x16, starting transfers between devices: 24.3 us -> 16.5 us  [partner_bits(): return lax.ppermute(value, 'dp', [(d, d ^ mask) for d in range(devices)])]
    unnamed x87 -> x95, local copies, waits for them, and re-layouts: 7.62 us -> 11.9 us
    convert_element_type x12 -> x5, other arithmetic: 10.2 us -> 7.09 us  [add_low(): return (left.astype(F32) + right.astype(F32)).astype(BF16)]
  transfers between devices with their start and end apart: 39 -> 39, of which waited for: 12 -> 11; matrix products, arithmetic and copies ran while one was open for 18% -> 17% of each run, Pallas kernels for 34% -> 33%
where the time goes in v3:
time: 488 us; the launch traced here: 485 us
  Pallas kernels  225 us (46%)
  waiting for transfers between devices  83.8 us (17%)
  starting transfers between devices  71.5 us (15%)
  matrix products  47.8 us (10%)
  local copies, waits for them, and re-layouts  35.6 us (7%)
  other arithmetic  20.2 us (4%)
    pallas_call x16, Pallas kernels, run(): pl.pallas_call(kernel, grid_spec=pltpu.PrefetchScalarGridSpec(num_scalar_...  225 us
    ppermute x16, waiting for transfers between devices, partner_bits(): return lax.ppermute(value, 'dp', [(d, d ^ mask) for d in range(devices)])  51.5 us
    dot_general x14, matrix products, dot_tn(): lax.dot_general(left, right, (((0,), (0,)), ((), ())), preferred_element_...  47.8 us
    all_to_all x5, starting transfers between devices, exchange(): return lax.all_to_all(value, 'dp', split_axis=0, concat_axis=0, tiled=True)  37.3 us
    all_to_all x5, waiting for transfers between devices, exchange(): return lax.all_to_all(value, 'dp', split_axis=0, concat_axis=0, tiled=True)  19.7 us
    ppermute x16, starting transfers between devices, partner_bits(): return lax.ppermute(value, 'dp', [(d, d ^ mask) for d in range(devices)])  16.5 us
    all_to_all x3, starting transfers between devices, last_sum(): lax.all_to_all(both, 'dp', split_axis=0, concat_axis=0, axis_index_groups...  14.8 us
    unnamed x95, local copies, waits for them, and re-layouts  11.9 us
  transfers between devices with their start and end apart: 39, of which 11 were waited for; matrix products, arithmetic and copies ran while one was open for 17% of the time, Pallas kernels for 33%

profile of v3, /device:TPU:0, one launch (start us, length us, event | category | flops | bytes accessed | tf_op | source)
XLA Modules:
  0.0 485.3 jit_solution(4484672906342016625)
XLA Ops:
  3.6 7.9 %all-to-all-start = ((s32[16,2,6]{2,1,0:T(2,128)}), s32[16,2,6]{2,1,0:T(2,128)S(1)}, u32[]{:S(2)}, u32[]{:S(2)}) async-start(s32[16,2,6]{2,1,0:T(2,128)} %bitcast.4), calls=%async_computation | async-start | bytes 32768 | tf_op jit(solution)/shard_map/all_to_all | solution.py:983
  12.1 5.5 %shard_map.281 = (bf16[32,40,768]{2,1,0:T(8,128)(2,1)}, bf16[32,40,768]{2,1,0:T(8,128)(2,1)}) custom-call(s32[32]{0:T(128)} %select_reduce_fusion.1.refs_0_, bf16[48,40,768]{2,1,0:T(8,128)(2,1)} %refs_1_.1, bf16[48,40,768]{2,1,0:T(8,128)(2,1)} %refs_2_.2), custom_call_target="tpu_custom_call" | custom-call | bytes 9830400 | tf_op jit(solution)/shard_map/pallas_call | solution.py:64
  18.8 5.8 %all-to-all-start.2 = ((bf16[32,40,768]{2,1,0:T(8,128)(2,1)}), bf16[32,40,768]{2,1,0:T(8,128)(2,1)S(1)}, u32[]{:S(2)}, u32[]{:S(2)}) async-start(bf16[32,40,768]{2,1,0:T(8,128)(2,1)} %get-tuple-element.93), calls=%async_computation.2 | async-start | bytes 3932160 | tf_op jit(solution)/shard_map/all_to_all | solution.py:983
  29.3 22.2 %shard_map.282 = (bf16[8,160,768]{2,1,0:T(8,128)(2,1)}, bf16[16,160,768]{2,1,0:T(8,128)(2,1)}, bf16[16,160,768]{2,1,0:T(8,128)(2,1)}) custom-call(s32[1]{0:T(128)} %bitcast.refs_0_, bf16[145,16,1024]{2,1,0:T(8,128)(2,1)} %bitcast.181, bf16[1024,768]{1,0:T(8,128)(2,1)} %refs_4_.5, f32[1,768]{1,0:T(1,128)} %reshape.240.refs_3_, ...), custom_call_target="tpu_custom_call" | custom-call | flops 10066329600 | bytes 23247872 | tf_op jit(solution)/shard_map/pallas_call | solution.py:64
  51.4 14.1 %all-to-all-done.2.refs_2_ = bf16[32,40,768]{2,1,0:T(8,128)(2,1)S(1)} async-done(((bf16[32,40,768]{2,1,0:T(8,128)(2,1)}), bf16[32,40,768]{2,1,0:T(8,128)(2,1)S(1)}, u32[]{:S(2)}, u32[]{:S(2)}) %all-to-all-start.2) | async-done | bytes 1966112 | tf_op jit(solution)/shard_map/all_to_all | solution.py:983
  65.5 1.3 copy-done.8
  66.8 9.7 %all-to-all-start.1 = ((bf16[32,40,768]{2,1,0:T(8,128)(2,1)}), bf16[32,40,768]{2,1,0:T(8,128)(2,1)}, u32[]{:S(2)}, u32[]{:S(2)}) async-start(bf16[32,40,768]{2,1,0:T(8,128)(2,1)} %get-tuple-element.89), calls=%async_computation.1 | async-start | bytes 3932160 | tf_op jit(solution)/shard_map/all_to_all | solution.py:983
  77.8 22.1 %shard_map.283 = (bf16[960,768]{1,0:T(8,128)(2,1)}, f32[960,768]{1,0:T(8,128)}, bf16[960,768]{1,0:T(8,128)(2,1)}, bf16[960,768]{1,0:T(8,128)(2,1)}, bf16[960,768...) custom-call(s32[24]{0:T(128)} %get-tuple-element.92.refs_0_, ...), custom_call_target="tpu_custom_call" | custom-call | flops 6417285120 | bytes 24718080 | tf_op jit(solution)/shard_map/pallas_call | solution.py:64
  100.0 12.5 %shard_map.284.refs_2_ = bf16[960,768]{1,0:T(8,128)(2,1)} custom-call(s32[24]{0:T(128)} %and_select_fusion.refs_0_, s32[96]{0:T(128)} %reshape.239.refs_1_, bf16[960,768]{1,0:T(8,128)(2,1)} %get-tuple-element.106.refs_2_, bf16[16,160,768]{2,1,0:T(8,128)(2,1)} %get-tuple-element.96.refs_3_.refs_4_, bf16[16,160,768]{2,1,0:T(8,128)(2,1)} %get-tuple-element.97.refs_4_.refs_5_), custom_call_target="tpu_custom_call" | custom-call | flops 3019898880 | bytes 10813440 | tf_op jit(solution)/shard_map/pallas_call | solution.py:64
  112.5 4.4 all-to-all-done.1.refs_1_
  116.8 63.2 %shard_map.285 = (bf16[32,40,768]{2,1,0:T(8,128)(2,1)}, bf16[960,768]{1,0:T(8,128)(2,1)}, bf16[960,768]{1,0:T(8,128)(2,1)}, bf16[960,768]{1,0:T(8,128)(2,1)}, f3...) custom-call(s32[24]{0:T(128)} %compare_select_fusion.4.refs_1_.refs_, ...), custom_call_target="tpu_custom_call" | custom-call | flops 20384317440 | bytes 42384384 | tf_op jit(solution)/shard_map/pallas_call | solution.py:64
  180.1 6.5 %convolution_convert_fusion.1 = bf16[768,1536]{1,0:T(8,128)(2,1)} fusion(bf16[960,768]{1,0:T(8,128)(2,1)} %get-tuple-element.104, bf16[960,1536]{1,0:T(8,128)(2,1)} %get-tuple-element.105), kind=kOutput, calls=%fused_computation.7 | convolution fusion | flops 2266103808 | bytes 6782976 | tf_op jit(solution)/shard_map/dot_general | solution.py:38
  186.6 4.0 convolution_convert_fusion.2
  191.1 24.3 %shard_map.286 = (bf16[2,8,160,768]{3,2,1,0:T(8,128)(2,1)}, bf16[2,8,160,768]{3,2,1,0:T(8,128)(2,1)}, bf16[960,768]{1,0:T(8,128)(2,1)}) custom-call(s32[24]{0:T(128)} %and_select_fusion.refs_0_, s32[96]{0:T(128)} %reshape.239.refs_1_, bf16[960,768]{1,0:T(8,128)(2,1)} %get-tuple-element.106.refs_2_, bf16[960,768]{1,0:T(8,128)(2,1)} %get-tuple-element.107.refs_3_, ...), custom_call_target="tpu_custom_call" | custom-call | flops 9059696640 | bytes 20152320 | tf_op jit(solution)/shard_map/pallas_call | solution.py:64
  215.4 9.2 %all-to-all-start.3 = ((bf16[32,40,768]{2,1,0:T(8,128)(2,1)}), bf16[32,40,768]{2,1,0:T(8,128)(2,1)S(1)}, u32[]{:S(2)}, u32[]{:S(2)}) async-start(bf16[32,40,768]{2,1,0:T(8,128)(2,1)} %get-tuple-element.99), calls=%async_computation.3 | async-start | bytes 3932160 | tf_op jit(solution)/shard_map/all_to_all | solution.py:983
  224.6 3.0 convolution_convert_fusion.5
  227.6 2.1 fusion.24
  230.3 4.4 add_convert_fusion
  234.7 4.2 add_convert_fusion.1
  240.2 1.9 collective-permute-start.18
  243.4 1.5 collective-permute-start.19
  244.8 28.0 %shard_map.287 = (bf16[32,40,768]{2,1,0:T(8,128)(2,1)}, bf16[960,768]{1,0:T(8,128)(2,1)}, bf16[960,384]{1,0:T(8,128)(2,1)}, bf16[960,384]{1,0:T(8,128)(2,1)}, bf...) custom-call(s32[24]{0:T(128)} %get-tuple-element.92.refs_0_, ...), custom_call_target="tpu_custom_call" | custom-call | flops 7172259840 | bytes 30634752 | tf_op jit(solution)/shard_map/pallas_call | solution.py:64
  272.9 2.7 convolution_convert_fusion.6
  277.7 2.3 convolution_convert_fusion
  280.0 2.0 pad_maximum_fusion
  283.5 2.0 fusion.23
  285.5 2.0 add_convert_fusion.2
  290.0 23.2 %shard_map.289 = (bf16[1280,768]{1,0:T(8,128)(2,1)}, bf16[1280,768]{1,0:T(8,128)(2,1)}, bf16[145,8,1024]{2,1,0:T(8,128)(2,1)}, f32[1024,768]{1,0:T(8,128)}, f32[8,768]{1,0:T(8,128)}) custom-call(s32[1]{0:T(128)} %bitcast.refs_0_, bf16[2,8,160,768]{3,2,1,0:T(8,128)(2,1)} %get-tuple-element.133.refs_1_, ...), custom_call_target="tpu_custom_call" | custom-call | flops 7046430720 | bytes 30744576 | tf_op jit(solution)/shard_map/pallas_call | solution.py:64
  313.2 1.5 dynamic-slice_convert_fusion
  314.9 5.0 %convolution_convert_fusion.3 = bf16[768,768]{1,0:T(8,128)(2,1)} fusion(bf16[1280,768]{1,0:T(8,128)(2,1)} %bitcast.184, bf16[1280,768]{1,0:T(8,128)(2,1)} %get-tuple-element.136), kind=kOutput, calls=%fused_computation.20 | convolution fusion | flops 1510539264 | bytes 5111808 | tf_op jit(solution)/shard_map/dot_general | solution.py:38
  321.3 2.9 shard_map.294
  324.2 5.2 %all-to-all-start.6 = ((bf16[4,48,3072]{2,1,0:T(8,128)(2,1)}), bf16[4,48,3072]{2,1,0:T(8,128)(2,1)}, u32[]{:S(2)}, u32[]{:S(2)}) async-start(bf16[4,48,3072]{2,1,0:T(8,128)(2,1)} %bitcast.158), calls=%async_computation.6 | async-start | bytes 2359296 | tf_op jit(solution)/shard_map/all_to_all | solution.py:1225
  329.4 3.7 fusion.25
  333.1 4.0 fusion.22
  339.6 1.5 collective-permute-start.16
  341.1 3.0 add_convert_fusion.4.refs_3_.refs_6_
  346.0 1.5 collective-permute-start.14
  347.5 11.1 %all-to-all-done.6 = bf16[4,48,3072]{2,1,0:T(8,128)(2,1)} async-done(((bf16[4,48,3072]{2,1,0:T(8,128)(2,1)}), bf16[4,48,3072]{2,1,0:T(8,128)(2,1)}, u32[]{:S(2)}, u32[]{:S(2)}) %all-to-all-start.6) | async-done | bytes 1179680 | tf_op jit(solution)/shard_map/all_to_all | solution.py:1225
  358.6 4.7 all-to-all-start.4
  363.3 4.0 fusion.refs_3_
  367.6 1.5 copy-done
  369.4 1.8 collective-permute-start.29
  373.0 1.5 collective-permute-start.17
  378.0 2.6 collective-permute-done.17
  380.6 31.2 %collective-permute-done.15 = bf16[2,2,48,768]{3,2,1,0:T(8,128)(2,1)S(1)} collective-permute-done((bf16[2,2,48,768]{3,2,1,0:T(8,128)(2,1)S(1)}, bf16[2,2,48,768]{3,2,1,0:T(8,128)(2,1)S(1)}, u32[]{:S(2)}, u32[]{:S(2)}) %collective-permute-start.15) | collective-permute-done | bytes 294944 | tf_op jit(solution)/shard_map/ppermute | solution.py:1187
  412.5 2.1 shard_map.293
  414.6 1.4 fusion.1
  416.8 1.5 collective-permute-start.30
  418.3 4.6 all-to-all-start.5
  422.9 1.4 fusion.2
  425.8 1.5 reshape.243.refs_4_.refs_7_
  427.3 1.5 convert_reduce_fusion
  428.8 7.9 %collective-permute-done.28 = bf16[2,2,48,1152]{3,2,1,0:T(8,128)(2,1)S(1)} collective-permute-done((bf16[2,2,48,1152]{3,2,1,0:T(8,128)(2,1)S(1)}, bf16[2,2,48,1152]{3,2,1,0:T(8,128)(2,1)S(1)}, u32[]{:S(2)}, u32[]{:S(2)}) %collective-permute-start.28) | collective-permute-done | bytes 442400 | tf_op jit(solution)/shard_map/ppermute | solution.py:1187
  437.4 2.5 shard_map.296
  439.9 5.0 %all-to-all-start.7 = ((bf16[4,48,2304]{2,1,0:T(8,128)(2,1)}), bf16[4,48,2304]{2,1,0:T(8,128)(2,1)S(1)}, u32[]{:S(2)}, u32[]{:S(2)}) async-start(bf16[4,48,2304]{2,1,0:T(8,128)(2,1)} %bitcast.159), calls=%async_computation.7 | async-start | bytes 1769472 | tf_op jit(solution)/shard_map/all_to_all | solution.py:1225
  445.8 1.5 shard_map.295
  447.3 1.4 collective-permute-done.22
  449.9 4.0 shard_map.288
  454.3 3.8 collective-permute-done.24
  458.1 2.1 collective-permute-start.25
  460.2 5.7 %collective-permute-done.25 = f32[32,384]{1,0:T(8,128)S(1)} collective-permute-done((f32[32,384]{1,0:T(8,128)S(1)}, f32[32,384]{1,0:T(8,128)S(1)}, u32[]{:S(2)}, u32[]{:S(2)}) %collective-permute-start.25) | collective-permute-done | bytes 49184 | tf_op jit(solution)/shard_map/ppermute | solution.py:1187
  466.0 4.0 shard_map.291
  475.5 3.4 shard_map.290
  480.6 3.4 shard_map.292
  (215 shorter events, 46.5 us)
Async XLA Ops:
  0.6 28.0 %collective-permute-start.1 = (bf16[2,3,768,384]{3,2,1,0:T(8,128)(2,1)}, bf16[2,3,768,384]{3,2,1,0:T(8,128)(2,1)}, u32[]{:S(2)}, u32[]{:S(2)}) collective-permute-start(bf16[2,3,768,384]{3,2,1,0:T(8,128)(2,1)} %refs_5_.3), channel_id=1, source_target_pairs={{0,1},{1,0},{2,3},{3,2},{4,5},{5,4},{6,7},{7,6},{8,9},{9,8},{10,11... | collective-permute-start | bytes 10616840 | tf_op jit(solution)/shard_map/ppermute | solution.py:977
  3.6 15.2 %all-to-all-start = ((s32[16,2,6]{2,1,0:T(2,128)}), s32[16,2,6]{2,1,0:T(2,128)S(1)}, u32[]{:S(2)}, u32[]{:S(2)}) async-start(s32[16,2,6]{2,1,0:T(2,128)} %bitcast.4), calls=%async_computation | async-start | bytes 32768 | tf_op jit(solution)/shard_map/all_to_all | solution.py:983
  18.8 5.8 %copy-start.24 = (bf16[2,384,768]{2,1,0:T(8,128)(2,1)S(1)}, bf16[2,384,768]{2,1,0:T(8,128)(2,1)}, u32[]{:S(2)}) copy-start(bf16[2,384,768]{2,1,0:T(8,128)(2,1)} %refs_11_.5) | copy-start | bytes 3538948
  18.8 5.9 %copy-start.25 = (f32[2,2,384]{2,1,0:T(2,128)S(1)}, f32[2,2,384]{2,1,0:T(2,128)}, u32[]{:S(2)}) copy-start(f32[2,2,384]{2,1,0:T(2,128)} %refs_7_.1) | copy-start | bytes 18436
  18.8 6.4 %copy-start.23 = (s32[1,16]{1,0:T(1,128)S(1)}, s32[1,16]{1,0:T(1,128)}, u32[]{:S(2)}) copy-start(s32[1,16]{1,0:T(1,128)} %param.22) | copy-start | bytes 196
  18.8 6.7 %copy-start.22 = (f32[768]{0:T(1024)S(1)}, f32[768]{0:T(1024)}, u32[]{:S(2)}) copy-start(f32[768]{0:T(1024)} %param.26) | copy-start | bytes 9220
  18.8 46.7 %all-to-all-start.2 = ((bf16[32,40,768]{2,1,0:T(8,128)(2,1)}), bf16[32,40,768]{2,1,0:T(8,128)(2,1)S(1)}, u32[]{:S(2)}, u32[]{:S(2)}) async-start(bf16[32,40,768]{2,1,0:T(8,128)(2,1)} %get-tuple-element.93), calls=%async_computation.2 | async-start | bytes 3932160 | tf_op jit(solution)/shard_map/all_to_all | solution.py:983
  24.7 4.0 collective-permute-start
  24.8 3.9 collective-permute-start.2
  51.4 25.7 %copy-start.20 = (f32[1536]{0:T(1024)S(1)}, f32[1536]{0:T(1024)}, u32[]{:S(2)}) copy-start(f32[1536]{0:T(1024)} %param.34) | copy-start | bytes 18436
  66.8 50.0 %all-to-all-start.1 = ((bf16[32,40,768]{2,1,0:T(8,128)(2,1)}), bf16[32,40,768]{2,1,0:T(8,128)(2,1)}, u32[]{:S(2)}, u32[]{:S(2)}) async-start(bf16[32,40,768]{2,1,0:T(8,128)(2,1)} %get-tuple-element.89), calls=%async_computation.1 | async-start | bytes 3932160 | tf_op jit(solution)/shard_map/all_to_all | solution.py:983
  76.6 35.9 %collective-permute-start.3 = (bf16[768,1536]{1,0:T(8,128)(2,1)}, bf16[768,1536]{1,0:T(8,128)(2,1)}, u32[]{:S(2)}, u32[]{:S(2)}) collective-permute-start(bf16[768,1536]{1,0:T(8,128)(2,1)} %refs_6_.3), channel_id=1, source_target_pairs={{0,1},{1,0},{2,3},{3,2},{4,5},{5,4},{6,7},{7,6},{8,9},{9,8},{10,11... | collective-permute-start | bytes 7077896 | tf_op jit(solution)/shard_map/ppermute | solution.py:977
  76.7 35.8 %collective-permute-start.4 = (bf16[1536,768]{1,0:T(8,128)(2,1)}, bf16[1536,768]{1,0:T(8,128)(2,1)}, u32[]{:S(2)}, u32[]{:S(2)}) collective-permute-start(bf16[1536,768]{1,0:T(8,128)(2,1)} %refs_8_.1), channel_id=1, source_target_pairs={{0,1},{1,0},{2,3},{3,2},{4,5},{5,4},{6,7},{7,6},{8,9},{9,8},{10,11... | collective-permute-start | bytes 7077896 | tf_op jit(solution)/shard_map/ppermute | solution.py:977
  77.2 22.8 %copy-start.21 = (f32[1,1536]{1,0:T(1,128)}, f32[1,1536]{1,0:T(1,128)S(1)}, u32[]{:S(2)}) copy-start(f32[1,1536]{1,0:T(1,128)S(1)} %reshape.241.refs_13_) | copy-start | bytes 18436
  77.2 35.3 %collective-permute-start.5 = (f32[1,1536]{1,0:T(1,128)S(1)}, f32[1,1536]{1,0:T(1,128)S(1)}, u32[]{:S(2)}, u32[]{:S(2)}) collective-permute-start(f32[1,1536]{1,0:T(1,128)S(1)} %reshape.241.refs_13_), channel_id=1, source_target_pairs={{0,1},{1,0},{2,3},{3,2},{4,5},{5,4},{6,7},{7,6},{8,9},{9,8},{10,11... | collective-permute-start | bytes 18440 | tf_op jit(solution)/shard_map/ppermute | solution.py:977
  112.4 4.4 copy-start.27
  180.1 6.5 %copy-start.32 = (bf16[960,1536]{1,0:T(8,128)(2,1)S(1)}, bf16[960,1536]{1,0:T(8,128)(2,1)}, u32[]{:S(2)}) copy-start(bf16[960,1536]{1,0:T(8,128)(2,1)} %get-tuple-element.103) | copy-start | bytes 8847364
  180.1 6.5 %copy-start.35 = (bf16[960,768]{1,0:T(8,128)(2,1)S(1)}, bf16[960,768]{1,0:T(8,128)(2,1)}, u32[]{:S(2)}) copy-start(bf16[960,768]{1,0:T(8,128)(2,1)} %get-tuple-element.102) | copy-start | bytes 4423684
  190.5 39.1 %collective-permute-start.7 = (bf16[768,1536]{1,0:T(8,128)(2,1)}, bf16[768,1536]{1,0:T(8,128)(2,1)}, u32[]{:S(2)}, u32[]{:S(2)}) collective-permute-start(bf16[768,1536]{1,0:T(8,128)(2,1)} %convolution_convert_fusion.1), channel_id=1, source_target_pairs={{0,1},{1,0},{2,3},{3,2},{4,5},{5,4},{6,7},{7,6},{8,9},{9,8},{10,11... | collective-permute-start | bytes 7077896 | tf_op jit(solution)/shard_map/ppermute | solution.py:977
  190.5 44.1 %collective-permute-start.6 = (bf16[768,1536]{1,0:T(8,128)(2,1)}, bf16[768,1536]{1,0:T(8,128)(2,1)}, u32[]{:S(2)}, u32[]{:S(2)}) collective-permute-start(bf16[768,1536]{1,0:T(8,128)(2,1)} %convolution_convert_fusion.2), channel_id=1, source_target_pairs={{0,1},{1,0},{2,3},{3,2},{4,5},{5,4},{6,7},{7,6},{8,9},{9,8},{10,11... | collective-permute-start | bytes 7077896 | tf_op jit(solution)/shard_map/ppermute | solution.py:977
  215.4 74.7 %collective-permute-start.10 = (bf16[2,8,160,768]{3,2,1,0:T(8,128)(2,1)}, bf16[2,8,160,768]{3,2,1,0:T(8,128)(2,1)}, u32[]{:S(2)}, u32[]{:S(2)}) collective-permute-start(bf16[2,8,160,768]{3,2,1,0:T(8,128)(2,1)} %get-tuple-element.134), channel_id=1, source_target_pairs={{0,1},{1,0},{2,3},{3,2},{4,5},{5,4},{6,7},{7,6},{8,9},{9,8},{10,11... | collective-permute-start | bytes 11796488 | tf_op jit(solution)/shard_map/ppermute | solution.py:977
  215.4 9.2 %copy-start.30 = (bf16[960,768]{1,0:T(8,128)(2,1)S(1)}, bf16[960,768]{1,0:T(8,128)(2,1)}, u32[]{:S(2)}) copy-start(bf16[960,768]{1,0:T(8,128)(2,1)} %get-tuple-element.122) | copy-start | bytes 4423684
  215.4 108.8 %all-to-all-start.3 = ((bf16[32,40,768]{2,1,0:T(8,128)(2,1)}), bf16[32,40,768]{2,1,0:T(8,128)(2,1)S(1)}, u32[]{:S(2)}, u32[]{:S(2)}) async-start(bf16[32,40,768]{2,1,0:T(8,128)(2,1)} %get-tuple-element.99), calls=%async_computation.3 | async-start | bytes 3932160 | tf_op jit(solution)/shard_map/all_to_all | solution.py:983
  224.6 3.0 copy-start.34
  230.3 4.4 copy-start.36
  230.3 4.4 copy-start.43
  240.2 45.4 %collective-permute-start.18 = (bf16[2,2,2,48,1536]{4,3,1,0,2:T(8,128)(2,1)}, bf16[2,2,2,48,1536]{4,3,1,0,2:T(8,128)(2,1)S(1)}, u32[]{:S(2)}, u32[]{:S(2)}) collective-permute-start(bf16[2,2,2,48,1536]{4,3,1,0,2:T(8,128)(2,1)} %bitcast.147), channel_id=1, source_target_pairs={{0,2},{2,0},{4,6},{6,4},{8,10},{10,8},{12,14},{14,12},{16,18},{18,... | collective-permute-start | bytes 3538952 | tf_op jit(solution)/shard_map/ppermute | solution.py:1187
  243.4 42.2 %collective-permute-start.19 = (bf16[2,2,2,48,1536]{4,3,1,0,2:T(8,128)(2,1)}, bf16[2,2,2,48,1536]{4,3,1,0,2:T(8,128)(2,1)}, u32[]{:S(2)}, u32[]{:S(2)}) collective-permute-start(bf16[2,2,2,48,1536]{4,3,1,0,2:T(8,128)(2,1)} %bitcast.145), channel_id=1, source_target_pairs={{0,4},{2,6},{4,0},{6,2},{8,12},{10,14},{12,8},{14,10},{16,20},{18,... | collective-permute-start | bytes 3538952 | tf_op jit(solution)/shard_map/ppermute | solution.py:1187
  272.9 2.7 copy-start.29
  272.9 2.7 copy-start.39
  281.9 81.4 %collective-permute-start.8 = (bf16[768,2304]{1,0:T(8,128)(2,1)}, bf16[768,2304]{1,0:T(8,128)(2,1)}, u32[]{:S(2)}, u32[]{:S(2)}) collective-permute-start(bf16[768,2304]{1,0:T(8,128)(2,1)} %pad_maximum_fusion), channel_id=1, source_target_pairs={{0,1},{1,0},{2,3},{3,2},{4,5},{5,4},{6,7},{7,6},{8,9},{9,8},{10,11... | collective-permute-start | bytes 10616840 | tf_op jit(solution)/shard_map/ppermute | solution.py:977
  288.4 31.8 %collective-permute-start.21 = (bf16[2,2,48,1536]{3,2,1,0:T(8,128)(2,1)S(1)}, bf16[2,2,48,1536]{3,2,1,0:T(8,128)(2,1)S(1)}, u32[]{:S(2)}, u32[]{:S(2)}) collective-permute-start(bf16[2,2,48,1536]{3,2,1,0:T(8,128)(2,1)S(1)} %get-tuple-element.168), channel_id=1, source_target_pairs={{0,2},{2,0},{4,6},{6,4},{8,10},{10,8},{12,14},{14,12},{16,18},{18,... | collective-permute-start | bytes 1769480 | tf_op jit(solution)/shard_map/ppermute | solution.py:1187
  289.9 30.3 %collective-permute-start.20 = (bf16[2,2,48,1536]{3,2,1,0:T(8,128)(2,1)S(1)}, bf16[2,2,48,1536]{3,2,1,0:T(8,128)(2,1)S(1)}, u32[]{:S(2)}, u32[]{:S(2)}) collective-permute-start(bf16[2,2,48,1536]{3,2,1,0:T(8,128)(2,1)S(1)} %get-tuple-element.170), channel_id=1, source_target_pairs={{0,4},{2,6},{4,0},{6,2},{8,12},{10,14},{12,8},{14,10},{16,20},{18,... | collective-permute-start | bytes 1769480 | tf_op jit(solution)/shard_map/ppermute | solution.py:1187
  314.7 22.4 %collective-permute-start.13 = (bf16[1024,384]{1,0:T(8,128)(2,1)S(1)}, bf16[1024,384]{1,0:T(8,128)(2,1)S(1)}, u32[]{:S(2)}, u32[]{:S(2)}) collective-permute-start(bf16[1024,384]{1,0:T(8,128)(2,1)S(1)} %dynamic-slice_convert_fusion), channel_id=1, source_target_pairs={{0,1},{1,0},{2,3},{3,2},{4,5},{5,4},{6,7},{7,6},{8,9},{9,8},{10,11... | collective-permute-start | bytes 2359304 | tf_op jit(solution)/shard_map/ppermute | solution.py:977
  319.9 21.2 %collective-permute-start.11 = (bf16[768,768]{1,0:T(8,128)(2,1)}, bf16[768,768]{1,0:T(8,128)(2,1)}, u32[]{:S(2)}, u32[]{:S(2)}) collective-permute-start(bf16[768,768]{1,0:T(8,128)(2,1)} %convolution_convert_fusion.3), channel_id=1, source_target_pairs={{0,1},{1,0},{2,3},{3,2},{4,5},{5,4},{6,7},{7,6},{8,9},{9,8},{10,11... | collective-permute-start | bytes 3538952 | tf_op jit(solution)/shard_map/ppermute | solution.py:977
  324.2 8.9 %copy-start.3 = (bf16[32,40,768]{2,1,0:T(8,128)(2,1)}, bf16[32,40,768]{2,1,0:T(8,128)(2,1)S(1)}, u32[]{:S(2)}) copy-start(bf16[32,40,768]{2,1,0:T(8,128)(2,1)S(1)} %all-to-all-done.3.refs_2_) | copy-start | bytes 5898244
  324.2 34.4 %all-to-all-start.6 = ((bf16[4,48,3072]{2,1,0:T(8,128)(2,1)}), bf16[4,48,3072]{2,1,0:T(8,128)(2,1)}, u32[]{:S(2)}, u32[]{:S(2)}) async-start(bf16[4,48,3072]{2,1,0:T(8,128)(2,1)} %bitcast.158), calls=%async_computation.6 | async-start | bytes 2359296 | tf_op jit(solution)/shard_map/all_to_all | solution.py:1225
  329.3 3.8 copy-start.38
  329.4 3.7 copy-start.42
  333.1 4.0 copy-start.9
  337.4 3.7 copy-start.4
  338.0 3.1 copy-start.28
  339.6 31.5 %collective-permute-start.16 = (bf16[2,2,2,48,512]{4,3,1,0,2:T(8,128)(2,1)}, bf16[2,2,2,48,512]{4,3,1,0,2:T(8,128)(2,1)}, u32[]{:S(2)}, u32[]{:S(2)}) collective-permute-start(bf16[2,2,2,48,512]{4,3,1,0,2:T(8,128)(2,1)} %bitcast.151), channel_id=1, source_target_pairs={{0,4},{2,6},{4,0},{6,2},{8,12},{10,14},{12,8},{14,10},{16,20},{18,... | collective-permute-start | bytes 1179656 | tf_op jit(solution)/shard_map/ppermute | solution.py:1187
  346.0 28.4 %collective-permute-start.14 = (bf16[2,2,2,48,768]{4,3,2,1,0:T(8,128)(2,1)}, bf16[2,2,2,48,768]{4,3,2,1,0:T(8,128)(2,1)}, u32[]{:S(2)}, u32[]{:S(2)}) collective-permute-start(bf16[2,2,2,48,768]{4,3,2,1,0:T(8,128)(2,1)} %dynamic-slice_bitcast_fusion.2), channel_id=1, source_target_pairs={{0,2},{2,0},{4,6},{6,4},{8,10},{10,8},{12,14},{14,12},{16,18},{18,... | collective-permute-start | bytes 1769480 | tf_op jit(solution)/shard_map/ppermute | solution.py:1187
  358.6 4.7 copy-start.7
  358.6 59.7 %all-to-all-start.4 = ((bf16[32,40,768]{2,1,0:T(8,128)(2,1)}), bf16[32,40,768]{2,1,0:T(8,128)(2,1)}, u32[]{:S(2)}, u32[]{:S(2)}) async-start(bf16[32,40,768]{2,1,0:T(8,128)(2,1)} %get-tuple-element.137), calls=%async_computation.4 | async-start | bytes 3932160 | tf_op jit(solution)/shard_map/all_to_all | solution.py:983
  369.3 5.2 %copy-start.2 = (bf16[768,768]{1,0:T(8,128)(2,1)S(1)}, bf16[768,768]{1,0:T(8,128)(2,1)}, u32[]{:S(2)}) copy-start(bf16[768,768]{1,0:T(8,128)(2,1)} %copy-done.1) | copy-start | bytes 3538948
  369.4 45.2 %collective-permute-start.29 = (bf16[2,2,2,48,1152]{4,3,1,0,2:T(8,128)(2,1)S(1)}, bf16[2,2,2,48,1152]{4,3,1,0,2:T(8,128)(2,1)}, u32[]{:S(2)}, u32[]{:S(2)}) collective-permute-start(bf16[2,2,2,48,1152]{4,3,1,0,2:T(8,128)(2,1)S(1)} %bitcast.169), channel_id=1, source_target_pairs={{0,4},{2,6},{4,0},{6,2},{8,12},{10,14},{12,8},{14,10},{16,20},{18,... | collective-permute-start | bytes 2654216 | tf_op jit(solution)/shard_map/ppermute | solution.py:1187
  373.0 7.6 %collective-permute-start.17 = (bf16[2,2,48,512]{3,2,1,0:T(8,128)(2,1)S(1)}, bf16[2,2,48,512]{3,2,1,0:T(8,128)(2,1)S(1)}, u32[]{:S(2)}, u32[]{:S(2)}) collective-permute-start(bf16[2,2,48,512]{3,2,1,0:T(8,128)(2,1)S(1)} %get-tuple-element.184), channel_id=1, source_target_pairs={{0,2},{2,0},{4,6},{6,4},{8,10},{10,8},{12,14},{14,12},{16,18},{18,... | collective-permute-start | bytes 589832 | tf_op jit(solution)/shard_map/ppermute | solution.py:1187
  376.4 35.4 %collective-permute-start.15 = (bf16[2,2,48,768]{3,2,1,0:T(8,128)(2,1)S(1)}, bf16[2,2,48,768]{3,2,1,0:T(8,128)(2,1)S(1)}, u32[]{:S(2)}, u32[]{:S(2)}) collective-permute-start(bf16[2,2,48,768]{3,2,1,0:T(8,128)(2,1)S(1)} %get-tuple-element.180), channel_id=1, source_target_pairs={{0,4},{2,6},{4,0},{6,2},{8,12},{10,14},{12,8},{14,10},{16,20},{18,... | collective-permute-start | bytes 884744 | tf_op jit(solution)/shard_map/ppermute | solution.py:1187
  377.4 45.5 %collective-permute-start.27 = (bf16[2,2,2,48,1152]{4,3,1,0,2:T(8,128)(2,1)S(1)}, bf16[2,2,2,48,1152]{4,3,1,0,2:T(8,128)(2,1)}, u32[]{:S(2)}, u32[]{:S(2)}) collective-permute-start(bf16[2,2,2,48,1152]{4,3,1,0,2:T(8,128)(2,1)S(1)} %bitcast.170), channel_id=1, source_target_pairs={{0,2},{2,0},{4,6},{6,4},{8,10},{10,8},{12,14},{14,12},{16,18},{18,... | collective-permute-start | bytes 2654216 | tf_op jit(solution)/shard_map/ppermute | solution.py:1187
  380.6 31.2 %copy-start.18 = (bf16[2,2,48,512]{3,2,1,0:T(8,128)(2,1)}, bf16[2,2,48,512]{3,2,1,0:T(8,128)(2,1)S(1)}, u32[]{:S(2)}) copy-start(bf16[2,2,48,512]{3,2,1,0:T(8,128)(2,1)S(1)} %collective-permute-done.17) | copy-start | bytes 589828
  416.8 12.0 %collective-permute-start.30 = (bf16[2,2,48,1152]{3,2,1,0:T(8,128)(2,1)S(1)}, bf16[2,2,48,1152]{3,2,1,0:T(8,128)(2,1)}, u32[]{:S(2)}, u32[]{:S(2)}) collective-permute-start(bf16[2,2,48,1152]{3,2,1,0:T(8,128)(2,1)S(1)} %get-tuple-element.172), channel_id=1, source_target_pairs={{0,2},{2,0},{4,6},{6,4},{8,10},{10,8},{12,14},{14,12},{16,18},{18,... | collective-permute-start | bytes 1327112 | tf_op jit(solution)/shard_map/ppermute | solution.py:1187
  418.3 21.7 %all-to-all-start.5 = ((bf16[4,48,1280]{2,1,0:T(8,128)(2,1)}), bf16[4,48,1280]{2,1,0:T(8,128)(2,1)S(1)}, u32[]{:S(2)}, u32[]{:S(2)}) async-start(bf16[4,48,1280]{2,1,0:T(8,128)(2,1)} %bitcast.24), calls=%async_computation.5 | async-start | bytes 983040 | tf_op jit(solution)/shard_map/all_to_all | solution.py:1225
  422.9 2.8 copy-start.6
  425.2 11.5 %collective-permute-start.28 = (bf16[2,2,48,1152]{3,2,1,0:T(8,128)(2,1)S(1)}, bf16[2,2,48,1152]{3,2,1,0:T(8,128)(2,1)S(1)}, u32[]{:S(2)}, u32[]{:S(2)}) collective-permute-start(bf16[2,2,48,1152]{3,2,1,0:T(8,128)(2,1)S(1)} %get-tuple-element.174), channel_id=1, source_target_pairs={{0,4},{2,6},{4,0},{6,2},{8,12},{10,14},{12,8},{14,10},{16,20},{18,... | collective-permute-start | bytes 1327112 | tf_op jit(solution)/shard_map/ppermute | solution.py:1187
  439.9 44.1 %all-to-all-start.7 = ((bf16[4,48,2304]{2,1,0:T(8,128)(2,1)}), bf16[4,48,2304]{2,1,0:T(8,128)(2,1)S(1)}, u32[]{:S(2)}, u32[]{:S(2)}) async-start(bf16[4,48,2304]{2,1,0:T(8,128)(2,1)} %bitcast.159), calls=%async_computation.7 | async-start | bytes 1769472 | tf_op jit(solution)/shard_map/all_to_all | solution.py:1225
  447.3 1.4 collective-permute-start.22
  449.6 4.3 collective-permute-start.23
  453.8 20.8 %collective-permute-start.9 = (bf16[20,24,768]{2,1,0:T(8,128)(2,1)}, bf16[20,24,768]{2,1,0:T(8,128)(2,1)S(1)}, u32[]{:S(2)}, u32[]{:S(2)}) collective-permute-start(bf16[20,24,768]{2,1,0:T(8,128)(2,1)} %get-tuple-element.131), channel_id=1, source_target_pairs={{0,1},{1,0},{2,3},{3,2},{4,5},{5,4},{6,7},{7,6},{8,9},{9,8},{10,11... | collective-permute-start | bytes 2211848 | tf_op jit(solution)/shard_map/ppermute | solution.py:977
  453.9 4.2 collective-permute-start.24
  458.1 7.8 %collective-permute-start.25 = (f32[32,384]{1,0:T(8,128)S(1)}, f32[32,384]{1,0:T(8,128)S(1)}, u32[]{:S(2)}, u32[]{:S(2)}) collective-permute-start(f32[32,384]{1,0:T(8,128)S(1)} %add.225), channel_id=1, source_target_pairs={{0,8},{2,10},{4,12},{6,14},{8,0},{10,2},{12,4},{14,6},{16,24},{18,... | collective-permute-start | bytes 147464 | tf_op jit(solution)/shard_map/ppermute | solution.py:1187
  465.9 5.1 %collective-permute-start.26 = (f32[32,384]{1,0:T(8,128)S(1)}, f32[32,384]{1,0:T(8,128)S(1)}, u32[]{:S(2)}, u32[]{:S(2)}) collective-permute-start(f32[32,384]{1,0:T(8,128)S(1)} %add.226), channel_id=1, source_target_pairs={{0,16},{2,18},{4,20},{6,22},{8,24},{10,26},{12,28},{14,30},{16,0},... | collective-permute-start | bytes 147464 | tf_op jit(solution)/shard_map/ppermute | solution.py:1187
  470.0 9.7 %collective-permute-start.12 = (bf16[20,24,768]{2,1,0:T(8,128)(2,1)}, bf16[20,24,768]{2,1,0:T(8,128)(2,1)S(1)}, u32[]{:S(2)}, u32[]{:S(2)}) collective-permute-start(bf16[20,24,768]{2,1,0:T(8,128)(2,1)} %get-tuple-element.139), channel_id=1, source_target_pairs={{0,1},{1,0},{2,3},{3,2},{4,5},{5,4},{6,7},{7,6},{8,9},{9,8},{10,11... | collective-permute-start | bytes 2211848 | tf_op jit(solution)/shard_map/ppermute | solution.py:977
  (20 other events, 28.5 us)

commit v4 on v3

--- a/solution.py
+++ b/solution.py
@@ -51,7 +51,7 @@
 ANY = pl.BlockSpec(memory_space=pl.ANY)
 
 
-def run(body, steps, scalars, ins, outs, scratch, flops, after=()):
+def run(body, steps, scalars, ins, outs, scratch, flops, after=(), light=False):
     ns, ni, no = len(scalars), len(ins), len(outs)
 
     def kernel(*refs):
@@ -75,7 +75,9 @@
             dimension_semantics=("arbitrary",), vmem_limit_bytes=VMEM_LIMIT
         ),
         cost_estimate=pl.CostEstimate(
-            flops=flops, bytes_accessed=moved, transcendentals=0
+            flops=0 if light else flops,
+            bytes_accessed=0 if light else moved,
+            transcendentals=0,
         ),
     )(*scalars, *[array for array, _ in ins])
 
@@ -865,12 +867,13 @@
 
 
 def join_kernel(scalars, ins, outs, scratch):
-    stay_x, got_x, stay_y, got_y = ins
     (out,) = outs
-    for start, stay, got in ((0, stay_x, got_x), (stay_x.shape[1], stay_y, got_y)):
+    start = 0
+    for stay, got in zip(ins[::2], ins[1::2]):
         for at in range(0, out.shape[0], 96):
             rows = slice(at, at + 96)
             out[rows, start : start + stay.shape[1]] = add_low(stay[rows], got[rows])
+        start += stay.shape[1]
 
 
 def add_low(left, right):
@@ -1206,7 +1209,7 @@
 
     def last_parts(values, after):
         count = values[0].size // values[0].shape[-1]
-        shape = (count, values[0].shape[-1] + values[2].shape[-1])
+        shape = (count, sum(value.shape[-1] for value in values[::2]))
         values = [value.reshape(count, value.shape[-1]) for value in values]
         (joined,) = run(
             join_kernel,
@@ -1220,13 +1223,14 @@
         )
         return joined.reshape(devices // 4, count // (devices // 4), shape[1])
 
-    def last_sum(both, first_width):
+    def last_sum(both, *widths):
         groups = [[low + 4 * n for n in range(devices // 4)] for low in range(4)]
         both = lax.all_to_all(
             both, "dp", split_axis=0, concat_axis=0, axis_index_groups=groups, tiled=True
         )
         total = jnp.sum(both.astype(F32), axis=0)
-        return total[:, :first_width], total[:, first_width:]
+        ends = [sum(widths[:n]) for n in range(len(widths) + 1)]
+        return [total[:, start:stop] for start, stop in zip(ends, ends[1:])]
 
     def low_tn(left, right):
         return dot_tn(left, right).astype(BF16)
@@ -1287,6 +1291,35 @@
     text_out, grad_self, dq_own, dq_mate, qkv_own, qkv_mate, self_sums = result
     text_in = exchange(text_out)
 
+    token_shape = (length // 2, slots, width)
+    final_shape = (length // 2, rows, width)
+
+    def halves(value, after):
+        own, away = run(
+            partial(halve_kernel, slots, length),
+            1,
+            [core_scalar, where],
+            [whole(value)],
+            [(token_shape, BF16, whole_spec(token_shape))] * 2,
+            [slabs(all_tokens)],
+            0,
+            after,
+        )
+        return own, mate(away)
+
+    def placed(own, got, after):
+        (out,) = run(
+            place_kernel,
+            1,
+            [],
+            [whole(own), whole(got), whole(place)],
+            [(final_shape, BF16, whole_spec(final_shape))],
+            [],
+            0,
+            after,
+        )
+        return out
+
     self_away = jnp.concatenate(
         [
             low_tn(x, qkv_mate),
@@ -1311,6 +1344,7 @@
     self_part = (self_own + self_got.astype(F32)).astype(BF16)
     half_width = self_part.shape[1] // 2
     self_stage = first_swaps(self_part[:, :half_width], self_part[:, half_width:])
+    merged_own, merged_got = halves(merged_in, [self_part])
 
     flat_images = own_images * patch_pad
     patch_grad_shape = (patch_count, own_images, vision)
@@ -1344,9 +1378,10 @@
             pltpu.SemaphoreType.DMA((4,)),
         ],
         2 * flat_images * width * (2 * width + 2 * vision),
-    )
-
-    up_grad, down_grad = last_sum(last_parts(feed_stage, [kv_own]), hidden)
+        [self_part],
+    )
+
+    self_got_x, self_got_y = self_stage[1], self_stage[3]
     self_stage = second_swaps(*self_stage)
     kv_low = proj.reshape(flat_images, width)
     kv_away = low_tn(kv_low, kv_mate)
@@ -1358,10 +1393,11 @@
     proj_part = (proj_own + proj_got.astype(F32)).astype(BF16)
     proj_part = proj_part.reshape(width, vision * local // width)
     image_stage = first_swaps(kv_part, proj_part)
-    self_one, self_two = last_sum(last_parts(self_stage, []), half_width)
     image_stage = second_swaps(*image_stage)
-    kv_grad, proj_grad = last_sum(last_parts(image_stage, []), width)
-    proj_grad = proj_grad.reshape(vision // devices, local)
+    text_own, text_got = halves(text_in, [kv_own])
+    up_grad, down_grad = last_sum(last_parts(feed_stage, [text_own]), hidden, hidden)
+    merged_final = placed(merged_own, merged_got, [kv_part])
+    text_final = placed(text_own, text_got, [kv_part, proj_part])
 
     lines = 23 + hidden // local
     packed_shape = (-(-lines // 8) * 8, local)
@@ -1373,11 +1409,19 @@
         [(packed_shape, F32, whole_spec(packed_shape))] * 2,
         [],
         0,
-        [up_grad, kv_part, proj_part],
+        [kv_part, proj_part, self_got_x, self_got_y],
     )
     small = small + mate(small_out)
     for bit in range(bits):
         small = small + partner_bits(small, 1 << bit)
+    self_one, self_two, kv_grad, proj_grad = last_sum(
+        last_parts(self_stage + image_stage, [merged_final, text_final, small, up_grad]),
+        half_width,
+        half_width,
+        width,
+        vision * local // width,
+    )
+    proj_grad = proj_grad.reshape(vision // devices, local)
     common = small[:18].reshape(3, 3, width)
     bias_grad = small[18:22].reshape(2, 2, local)
     up_bias_grad = small[22 : 22 + hidden // local].reshape(hidden)
@@ -1392,34 +1436,9 @@
     ).reshape(2, 3, width // devices, local)
     out_grad = jnp.stack([out_self.T, out_cross.T])
 
-    def tokens_out(value, after, after_place):
-        shape = (length // 2, slots, width)
-        own, away = run(
-            partial(halve_kernel, slots, length),
-            1,
-            [core_scalar, where],
-            [whole(value)],
-            [(shape, BF16, whole_spec(shape))] * 2,
-            [slabs(all_tokens)],
-            0,
-            after,
-        )
-        shape = (length // 2, rows, width)
-        (out,) = run(
-            place_kernel,
-            1,
-            [],
-            [whole(own), whole(mate(away)), whole(place)],
-            [(shape, BF16, whole_spec(shape))],
-            [],
-            0,
-            after_place,
-        )
-        return jnp.transpose(out, (1, 0, 2))
-
     return (
-        tokens_out(merged_in, [self_part], [kv_part]),
-        tokens_out(text_in, [kv_own], [kv_part, proj_part]),
+        jnp.transpose(merged_final, (1, 0, 2)),
+        jnp.transpose(text_final, (1, 0, 2)),
         jnp.transpose(patch_grad, (1, 0, 2)),
         proj_grad,
         proj_bias_grad,

time: 488 us -> 478 us (0.980)
  waiting for transfers between devices: 83.8 us -> 75.6 us
    ppermute x16, waiting for transfers between devices: 51.5 us -> 29.7 us  [partner_bits(): return lax.ppermute(value, 'dp', [(d, d ^ mask) for d in range(devices)])]
    all_to_all x3 -> x2, waiting for transfers between devices: 11.1 us -> 25.6 us  [last_sum(): lax.all_to_all(both, 'dp', split_axis=0, concat_axis=0, axis_index_groups...]
    all_to_all x3 -> x2, starting transfers between devices: 14.8 us -> 8.43 us  [last_sum(): lax.all_to_all(both, 'dp', split_axis=0, concat_axis=0, axis_index_groups...]
    unnamed x95 -> x97, local copies, waits for them, and re-layouts: 11.9 us -> 7.29 us
    pallas_call x16 -> x15, Pallas kernels: 225 us -> 223 us  [run(): pl.pallas_call(kernel, grid_spec=pltpu.PrefetchScalarGridSpec(num_scalar_...]
  transfers between devices with their start and end apart: 39 -> 38, of which waited for: 11 -> 12; matrix products, arithmetic and copies ran while one was open for 17% -> 18% of each run, Pallas kernels for 33% -> 33%
where the time goes in v4:
time: 478 us; the launch traced here: 475 us
  Pallas kernels  223 us (47%)
  waiting for transfers between devices  75.6 us (16%)
  starting transfers between devices  70.6 us (15%)
  matrix products  47.4 us (10%)
  local copies, waits for them, and re-layouts  35.5 us (7%)
  other arithmetic  21.6 us (5%)
    pallas_call x15, Pallas kernels, run(): pl.pallas_call(kernel, grid_spec=pltpu.PrefetchScalarGridSpec(num_scalar_...  223 us
    dot_general x14, matrix products, dot_tn(): lax.dot_general(left, right, (((0,), (0,)), ((), ())), preferred_element_...  47.4 us
    all_to_all x5, starting transfers between devices, exchange(): return lax.all_to_all(value, 'dp', split_axis=0, concat_axis=0, tiled=True)  39.3 us
    ppermute x16, waiting for transfers between devices, partner_bits(): return lax.ppermute(value, 'dp', [(d, d ^ mask) for d in range(devices)])  29.7 us
    all_to_all x2, waiting for transfers between devices, last_sum(): lax.all_to_all(both, 'dp', split_axis=0, concat_axis=0, axis_index_groups...  25.6 us
    ppermute x16, starting transfers between devices, partner_bits(): return lax.ppermute(value, 'dp', [(d, d ^ mask) for d in range(devices)])  19.7 us
    all_to_all x5, waiting for transfers between devices, exchange(): return lax.all_to_all(value, 'dp', split_axis=0, concat_axis=0, tiled=True)  19.7 us
  transfers between devices with their start and end apart: 38, of which 12 were waited for; matrix products, arithmetic and copies ran while one was open for 18% of the time, Pallas kernels for 33%

profile of v4, /device:TPU:0, one launch (start us, length us, event | category | flops | bytes accessed | tf_op | source)
XLA Modules:
  0.0 475.2 jit_solution(1673631321339891972)
XLA Ops:
  3.6 7.9 %all-to-all-start = ((s32[16,2,6]{2,1,0:T(2,128)}), s32[16,2,6]{2,1,0:T(2,128)S(1)}, u32[]{:S(2)}, u32[]{:S(2)}) async-start(s32[16,2,6]{2,1,0:T(2,128)} %bitcast.4), calls=%async_computation | async-start | bytes 32768 | tf_op jit(solution)/shard_map/all_to_all | solution.py:986
  12.1 5.5 %shard_map.281 = (bf16[32,40,768]{2,1,0:T(8,128)(2,1)}, bf16[32,40,768]{2,1,0:T(8,128)(2,1)}) custom-call(s32[32]{0:T(128)} %select_reduce_fusion.1.refs_0_, bf16[48,40,768]{2,1,0:T(8,128)(2,1)} %refs_1_.1, bf16[48,40,768]{2,1,0:T(8,128)(2,1)} %refs_2_.2), custom_call_target="tpu_custom_call" | custom-call | bytes 9830400 | tf_op jit(solution)/shard_map/pallas_call | solution.py:64
  18.8 5.9 %all-to-all-start.2 = ((bf16[32,40,768]{2,1,0:T(8,128)(2,1)}), bf16[32,40,768]{2,1,0:T(8,128)(2,1)S(1)}, u32[]{:S(2)}, u32[]{:S(2)}) async-start(bf16[32,40,768]{2,1,0:T(8,128)(2,1)} %get-tuple-element.93), calls=%async_computation.2 | async-start | bytes 3932160 | tf_op jit(solution)/shard_map/all_to_all | solution.py:986
  29.4 22.2 %shard_map.282 = (bf16[8,160,768]{2,1,0:T(8,128)(2,1)}, bf16[16,160,768]{2,1,0:T(8,128)(2,1)}, bf16[16,160,768]{2,1,0:T(8,128)(2,1)}) custom-call(s32[1]{0:T(128)} %bitcast.refs_0_, bf16[145,16,1024]{2,1,0:T(8,128)(2,1)} %bitcast.182, bf16[1024,768]{1,0:T(8,128)(2,1)} %refs_4_.5, f32[1,768]{1,0:T(1,128)} %reshape.237.refs_3_, ...), custom_call_target="tpu_custom_call" | custom-call | flops 10066329600 | bytes 23247872 | tf_op jit(solution)/shard_map/pallas_call | solution.py:64
  51.6 14.0 %all-to-all-done.2.refs_2_ = bf16[32,40,768]{2,1,0:T(8,128)(2,1)S(1)} async-done(((bf16[32,40,768]{2,1,0:T(8,128)(2,1)}), bf16[32,40,768]{2,1,0:T(8,128)(2,1)S(1)}, u32[]{:S(2)}, u32[]{:S(2)}) %all-to-all-start.2) | async-done | bytes 1966112 | tf_op jit(solution)/shard_map/all_to_all | solution.py:986
  66.8 9.6 %all-to-all-start.1 = ((bf16[32,40,768]{2,1,0:T(8,128)(2,1)}), bf16[32,40,768]{2,1,0:T(8,128)(2,1)}, u32[]{:S(2)}, u32[]{:S(2)}) async-start(bf16[32,40,768]{2,1,0:T(8,128)(2,1)} %get-tuple-element.89), calls=%async_computation.1 | async-start | bytes 3932160 | tf_op jit(solution)/shard_map/all_to_all | solution.py:986
  77.7 22.1 %shard_map.283 = (bf16[960,768]{1,0:T(8,128)(2,1)}, f32[960,768]{1,0:T(8,128)}, bf16[960,768]{1,0:T(8,128)(2,1)}, bf16[960,768]{1,0:T(8,128)(2,1)}, bf16[960,768...) custom-call(s32[24]{0:T(128)} %get-tuple-element.92.refs_0_, ...), custom_call_target="tpu_custom_call" | custom-call | flops 6417285120 | bytes 24718080 | tf_op jit(solution)/shard_map/pallas_call | solution.py:64
  99.8 12.5 %shard_map.284.refs_2_ = bf16[960,768]{1,0:T(8,128)(2,1)} custom-call(s32[24]{0:T(128)} %and_select_fusion.refs_0_, s32[96]{0:T(128)} %reshape.236.refs_1_, bf16[960,768]{1,0:T(8,128)(2,1)} %get-tuple-element.106.refs_2_, bf16[16,160,768]{2,1,0:T(8,128)(2,1)} %get-tuple-element.96.refs_3_.refs_4_, bf16[16,160,768]{2,1,0:T(8,128)(2,1)} %get-tuple-element.97.refs_4_.refs_5_), custom_call_target="tpu_custom_call" | custom-call | flops 3019898880 | bytes 10813440 | tf_op jit(solution)/shard_map/pallas_call | solution.py:64
  112.3 4.5 all-to-all-done.1.refs_1_
  116.8 62.0 %shard_map.285 = (bf16[32,40,768]{2,1,0:T(8,128)(2,1)}, bf16[960,768]{1,0:T(8,128)(2,1)}, bf16[960,768]{1,0:T(8,128)(2,1)}, bf16[960,768]{1,0:T(8,128)(2,1)}, f3...) custom-call(s32[24]{0:T(128)} %compare_select_fusion.4.refs_1_.refs_, ...), custom_call_target="tpu_custom_call" | custom-call | flops 20384317440 | bytes 42384384 | tf_op jit(solution)/shard_map/pallas_call | solution.py:64
  178.8 6.5 %convolution_convert_fusion.1 = bf16[768,1536]{1,0:T(8,128)(2,1)} fusion(bf16[960,768]{1,0:T(8,128)(2,1)} %get-tuple-element.104, bf16[960,1536]{1,0:T(8,128)(2,1)} %get-tuple-element.105), kind=kOutput, calls=%fused_computation.7 | convolution fusion | flops 2266103808 | bytes 6782976 | tf_op jit(solution)/shard_map/dot_general | solution.py:38
  185.3 4.0 convolution_convert_fusion.2
  189.8 9.2 %all-to-all-start.3 = ((bf16[32,40,768]{2,1,0:T(8,128)(2,1)}), bf16[32,40,768]{2,1,0:T(8,128)(2,1)S(1)}, u32[]{:S(2)}, u32[]{:S(2)}) async-start(bf16[32,40,768]{2,1,0:T(8,128)(2,1)} %get-tuple-element.99), calls=%async_computation.3 | async-start | bytes 3932160 | tf_op jit(solution)/shard_map/all_to_all | solution.py:986
  199.0 2.4 convolution_convert_fusion.5
  201.4 24.5 %shard_map.286 = (bf16[2,8,160,768]{3,2,1,0:T(8,128)(2,1)}, bf16[2,8,160,768]{3,2,1,0:T(8,128)(2,1)}, bf16[960,768]{1,0:T(8,128)(2,1)}) custom-call(s32[24]{0:T(128)} %and_select_fusion.refs_0_, s32[96]{0:T(128)} %reshape.236.refs_1_, bf16[960,768]{1,0:T(8,128)(2,1)} %get-tuple-element.106.refs_2_, bf16[960,768]{1,0:T(8,128)(2,1)} %get-tuple-element.107.refs_3_, ...), custom_call_target="tpu_custom_call" | custom-call | flops 9059696640 | bytes 20152320 | tf_op jit(solution)/shard_map/pallas_call | solution.py:64
  226.0 6.2 %add_convert_fusion = bf16[768,1536]{1,0:T(8,128)(2,1)} fusion(bf16[768,1536]{1,0:T(8,128)(2,1)} %collective-permute-done.7, bf16[960,768]{1,0:T(8,128)(2,1)S(1)} %copy-done.38, bf16[960,1536]{1,0:T(8,128)(2,1)} %get-tuple-element.111), kind=kOutput, calls=%fused_computation.3 | convolution fusion | flops 2268463104 | bytes 9142272 | tf_op jit(solution)/shard_map/dot_general | solution.py:38
  232.2 5.3 %add_convert_fusion.1 = bf16[768,1536]{1,0:T(8,128)(2,1)} fusion(bf16[768,1536]{1,0:T(8,128)(2,1)} %collective-permute-done.6, bf16[960,768]{1,0:T(8,128)(2,1)S(1)} %copy-done.37, bf16[960,1536]{1,0:T(8,128)(2,1)S(1)} %copy-done.45), kind=kOutput, calls=%fused_computation.4 | convolution fusion | flops 2268463104 | bytes 9142272 | tf_op jit(solution)/shard_map/dot_general | solution.py:38
  237.5 28.3 %shard_map.287 = (bf16[32,40,768]{2,1,0:T(8,128)(2,1)}, bf16[960,768]{1,0:T(8,128)(2,1)}, bf16[960,384]{1,0:T(8,128)(2,1)}, bf16[960,384]{1,0:T(8,128)(2,1)}, bf...) custom-call(s32[24]{0:T(128)} %get-tuple-element.92.refs_0_, ...), custom_call_target="tpu_custom_call" | custom-call | flops 7172259840 | bytes 30634752 | tf_op jit(solution)/shard_map/pallas_call | solution.py:64
  265.8 4.0 convolution_convert_fusion
  272.4 1.9 pad_maximum_fusion
  275.6 1.9 constant_dynamic-slice_fusion.4
  277.5 2.0 collective-permute-start.27
  279.8 1.6 collective-permute-start.28
  281.4 2.0 fusion.24
  285.0 2.0 fusion.23
  287.0 2.0 fusion.25
  289.2 4.1 fusion.22
  293.3 12.3 %collective-permute-done.27 = bf16[2,2,2,48,1536]{4,3,1,0,2:T(8,128)(2,1)S(1)} collective-permute-done((bf16[2,2,2,48,1536]{4,3,1,0,2:T(8,128)(2,1)S(1)}, bf16[2,2,2,48,1536]{4,3,1,0,2:T(8,128)(2,1)S(1)}, u32[]{:S(2)}, u32[]{:S(2)}) %collective-permute-start.27) | collective-permute-done | bytes 1179680 | tf_op jit(solution)/shard_map/ppermute | solution.py:1190
  305.6 1.9 collective-permute-done.28
  307.5 2.2 add_convert_fusion.2
  311.0 6.8 %all-to-all-start.4 = ((bf16[32,40,768]{2,1,0:T(8,128)(2,1)}), bf16[32,40,768]{2,1,0:T(8,128)(2,1)}, u32[]{:S(2)}, u32[]{:S(2)}) async-start(bf16[32,40,768]{2,1,0:T(8,128)(2,1)} %get-tuple-element.137), calls=%async_computation.4 | async-start | bytes 3932160 | tf_op jit(solution)/shard_map/all_to_all | solution.py:986
  317.7 2.5 dynamic-slice_bitcast_fusion.2
  320.2 1.9 collective-permute-start.30
  323.2 1.5 collective-permute-start.29
  324.7 5.3 %fusion.refs_3_.refs_7_ = bf16[768,2304]{1,0:T(8,128)(2,1)} fusion(f32[768,384]{1,0:T(8,128)} %fusion.25, f32[768,384]{1,0:T(8,128)} %fusion.24, f32[768,384]{1,0:T(8,128)} %fusion.23, f32[768,1152]{1,0:T(8,128)S(1)} %copy-done.6, bf16[768,2304]{1,0:T(8,128)(2,1)} %collective-permute-done.8), kind=kLoop, calls=%fused_computation.2 | loop fusion | flops 10616832 | bytes 14155776 | tf_op jit(solution)/shard_map/convert_element_type | solution.py:1344
  330.0 23.2 %shard_map.289 = (bf16[1280,768]{1,0:T(8,128)(2,1)}, bf16[1280,768]{1,0:T(8,128)(2,1)}, bf16[145,8,1024]{2,1,0:T(8,128)(2,1)}, f32[1024,768]{1,0:T(8,128)}, f32[8,768]{1,0:T(8,128)}) custom-call(s32[1]{0:T(128)} %bitcast.refs_0_, bf16[2,8,160,768]{3,2,1,0:T(8,128)(2,1)} %get-tuple-element.133.refs_1_, ...), custom_call_target="tpu_custom_call" | custom-call | flops 7046430720 | bytes 30744576 | tf_op jit(solution)/shard_map/pallas_call | solution.py:64
  353.2 2.4 dynamic-slice_convert_fusion
  358.7 2.8 convolution_convert_fusion.3
  361.4 4.1 shard_map.288
  366.5 4.0 shard_map.291
  371.3 2.9 shard_map.294
  374.2 4.8 %all-to-all-start.5 = ((bf16[4,48,3072]{2,1,0:T(8,128)(2,1)}), bf16[4,48,3072]{2,1,0:T(8,128)(2,1)}, u32[]{:S(2)}, u32[]{:S(2)}) async-start(bf16[4,48,3072]{2,1,0:T(8,128)(2,1)} %bitcast.162), calls=%async_computation.5 | async-start | bytes 2359296 | tf_op jit(solution)/shard_map/all_to_all | solution.py:1228
  379.1 1.8 add_convert_fusion.5
  380.9 1.5 reshape.240.refs_4_.refs_6_
  382.4 1.5 reshape_reshape.3
  386.8 6.1 %collective-permute-done.14.refs_7_ = bf16[2,2,2,48,1152]{4,3,2,1,0:T(8,128)(2,1)} collective-permute-done((bf16[2,2,2,48,1152]{4,3,2,1,0:T(8,128)(2,1)}, bf16[2,2,2,48,1152]{4,3,2,1,0:T(8,128)(2,1)}, u32[]{:S(2)}, u32[]{:S(2)}) %collective-permute-start.14) | collective-permute-done | bytes 884768 | tf_op jit(solution)/shard_map/ppermute | solution.py:1190
  392.9 1.4 fusion.2
  394.3 4.1 add_convert_fusion.4.refs_3_.refs_5_
  398.4 1.6 shard_map.293
  403.0 1.5 collective-permute-start.18
  404.5 2.4 collective-permute-done.23
  408.3 2.7 collective-permute-done.24
  411.1 1.5 collective-permute-start.25
  413.8 1.5 collective-permute-done.25
  415.3 2.6 collective-permute-start.26
  419.2 3.4 shard_map.292.refs_9_
  422.6 2.1 collective-permute-start.21
  424.7 3.4 shard_map.290.refs_8_
  429.7 1.5 collective-permute-start.19
  431.2 1.5 convert_reduce_fusion.1
  433.6 2.8 collective-permute-done.19
  437.1 3.1 shard_map.295
  440.2 3.7 all-to-all-start.6
  447.6 25.6 %all-to-all-done.6 = bf16[4,48,3584]{2,1,0:T(8,128)(2,1)S(1)} async-done(((bf16[4,48,3584]{2,1,0:T(8,128)(2,1)}), bf16[4,48,3584]{2,1,0:T(8,128)(2,1)S(1)}, u32[]{:S(2)}, u32[]{:S(2)}) %all-to-all-start.6) | async-done | bytes 1376288 | tf_op jit(solution)/shard_map/all_to_all | solution.py:1228
  (212 shorter events, 43.9 us)
Async XLA Ops:
  0.6 28.1 %collective-permute-start.1 = (bf16[2,3,768,384]{3,2,1,0:T(8,128)(2,1)}, bf16[2,3,768,384]{3,2,1,0:T(8,128)(2,1)}, u32[]{:S(2)}, u32[]{:S(2)}) collective-permute-start(bf16[2,3,768,384]{3,2,1,0:T(8,128)(2,1)} %refs_5_.3), channel_id=1, source_target_pairs={{0,1},{1,0},{2,3},{3,2},{4,5},{5,4},{6,7},{7,6},{8,9},{9,8},{10,11... | collective-permute-start | bytes 10616840 | tf_op jit(solution)/shard_map/ppermute | solution.py:980
  3.6 15.2 %all-to-all-start = ((s32[16,2,6]{2,1,0:T(2,128)}), s32[16,2,6]{2,1,0:T(2,128)S(1)}, u32[]{:S(2)}, u32[]{:S(2)}) async-start(s32[16,2,6]{2,1,0:T(2,128)} %bitcast.4), calls=%async_computation | async-start | bytes 32768 | tf_op jit(solution)/shard_map/all_to_all | solution.py:986
  18.8 6.0 %copy-start.21 = (f32[2,2,384]{2,1,0:T(2,128)S(1)}, f32[2,2,384]{2,1,0:T(2,128)}, u32[]{:S(2)}) copy-start(f32[2,2,384]{2,1,0:T(2,128)} %refs_7_.1) | copy-start | bytes 18436
  18.8 6.5 %copy-start.20 = (s32[1,16]{1,0:T(1,128)S(1)}, s32[1,16]{1,0:T(1,128)}, u32[]{:S(2)}) copy-start(s32[1,16]{1,0:T(1,128)} %param.22) | copy-start | bytes 196
  18.8 6.8 %copy-start.19 = (f32[768]{0:T(1024)S(1)}, f32[768]{0:T(1024)}, u32[]{:S(2)}) copy-start(f32[768]{0:T(1024)} %param.26) | copy-start | bytes 9220
  18.8 46.7 %all-to-all-start.2 = ((bf16[32,40,768]{2,1,0:T(8,128)(2,1)}), bf16[32,40,768]{2,1,0:T(8,128)(2,1)S(1)}, u32[]{:S(2)}, u32[]{:S(2)}) async-start(bf16[32,40,768]{2,1,0:T(8,128)(2,1)} %get-tuple-element.93), calls=%async_computation.2 | async-start | bytes 3932160 | tf_op jit(solution)/shard_map/all_to_all | solution.py:986
  24.8 4.0 collective-permute-start
  24.9 3.9 collective-permute-start.2
  51.5 25.5 %copy-start.17 = (f32[1536]{0:T(1024)S(1)}, f32[1536]{0:T(1024)}, u32[]{:S(2)}) copy-start(f32[1536]{0:T(1024)} %param.34) | copy-start | bytes 18436
  66.8 49.9 %all-to-all-start.1 = ((bf16[32,40,768]{2,1,0:T(8,128)(2,1)}), bf16[32,40,768]{2,1,0:T(8,128)(2,1)}, u32[]{:S(2)}, u32[]{:S(2)}) async-start(bf16[32,40,768]{2,1,0:T(8,128)(2,1)} %get-tuple-element.89), calls=%async_computation.1 | async-start | bytes 3932160 | tf_op jit(solution)/shard_map/all_to_all | solution.py:986
  76.4 35.9 %collective-permute-start.3 = (bf16[768,1536]{1,0:T(8,128)(2,1)}, bf16[768,1536]{1,0:T(8,128)(2,1)}, u32[]{:S(2)}, u32[]{:S(2)}) collective-permute-start(bf16[768,1536]{1,0:T(8,128)(2,1)} %refs_6_.3), channel_id=1, source_target_pairs={{0,1},{1,0},{2,3},{3,2},{4,5},{5,4},{6,7},{7,6},{8,9},{9,8},{10,11... | collective-permute-start | bytes 7077896 | tf_op jit(solution)/shard_map/ppermute | solution.py:980
  76.5 35.8 %collective-permute-start.4 = (bf16[1536,768]{1,0:T(8,128)(2,1)}, bf16[1536,768]{1,0:T(8,128)(2,1)}, u32[]{:S(2)}, u32[]{:S(2)}) collective-permute-start(bf16[1536,768]{1,0:T(8,128)(2,1)} %refs_8_.1), channel_id=1, source_target_pairs={{0,1},{1,0},{2,3},{3,2},{4,5},{5,4},{6,7},{7,6},{8,9},{9,8},{10,11... | collective-permute-start | bytes 7077896 | tf_op jit(solution)/shard_map/ppermute | solution.py:980
  77.0 22.8 %copy-start.18 = (f32[1,1536]{1,0:T(1,128)}, f32[1,1536]{1,0:T(1,128)S(1)}, u32[]{:S(2)}) copy-start(f32[1,1536]{1,0:T(1,128)S(1)} %reshape.238.refs_13_) | copy-start | bytes 18436
  77.0 35.3 %collective-permute-start.5 = (f32[1,1536]{1,0:T(1,128)S(1)}, f32[1,1536]{1,0:T(1,128)S(1)}, u32[]{:S(2)}, u32[]{:S(2)}) collective-permute-start(f32[1,1536]{1,0:T(1,128)S(1)} %reshape.238.refs_13_), channel_id=1, source_target_pairs={{0,1},{1,0},{2,3},{3,2},{4,5},{5,4},{6,7},{7,6},{8,9},{9,8},{10,11... | collective-permute-start | bytes 18440 | tf_op jit(solution)/shard_map/ppermute | solution.py:980
  112.3 4.5 copy-start.23
  178.8 6.5 %copy-start.32 = (bf16[960,1536]{1,0:T(8,128)(2,1)S(1)}, bf16[960,1536]{1,0:T(8,128)(2,1)}, u32[]{:S(2)}) copy-start(bf16[960,1536]{1,0:T(8,128)(2,1)} %get-tuple-element.103) | copy-start | bytes 8847364
  178.8 6.5 %copy-start.36 = (bf16[960,768]{1,0:T(8,128)(2,1)S(1)}, bf16[960,768]{1,0:T(8,128)(2,1)}, u32[]{:S(2)}) copy-start(bf16[960,768]{1,0:T(8,128)(2,1)} %get-tuple-element.102) | copy-start | bytes 4423684
  189.3 36.6 %collective-permute-start.7 = (bf16[768,1536]{1,0:T(8,128)(2,1)}, bf16[768,1536]{1,0:T(8,128)(2,1)}, u32[]{:S(2)}, u32[]{:S(2)}) collective-permute-start(bf16[768,1536]{1,0:T(8,128)(2,1)} %convolution_convert_fusion.1), channel_id=1, source_target_pairs={{0,1},{1,0},{2,3},{3,2},{4,5},{5,4},{6,7},{7,6},{8,9},{9,8},{10,11... | collective-permute-start | bytes 7077896 | tf_op jit(solution)/shard_map/ppermute | solution.py:980
  189.3 42.9 %collective-permute-start.6 = (bf16[768,1536]{1,0:T(8,128)(2,1)}, bf16[768,1536]{1,0:T(8,128)(2,1)}, u32[]{:S(2)}, u32[]{:S(2)}) collective-permute-start(bf16[768,1536]{1,0:T(8,128)(2,1)} %convolution_convert_fusion.2), channel_id=1, source_target_pairs={{0,1},{1,0},{2,3},{3,2},{4,5},{5,4},{6,7},{7,6},{8,9},{9,8},{10,11... | collective-permute-start | bytes 7077896 | tf_op jit(solution)/shard_map/ppermute | solution.py:980
  189.8 9.2 %copy-start.41 = (bf16[960,384]{1,0:T(8,128)(2,1)S(1)}, bf16[960,384]{1,0:T(8,128)(2,1)}, u32[]{:S(2)}) copy-start(bf16[960,384]{1,0:T(8,128)(2,1)} %get-tuple-element.128) | copy-start | bytes 2211844
  189.8 119.9 %all-to-all-start.3 = ((bf16[32,40,768]{2,1,0:T(8,128)(2,1)}), bf16[32,40,768]{2,1,0:T(8,128)(2,1)S(1)}, u32[]{:S(2)}, u32[]{:S(2)}) async-start(bf16[32,40,768]{2,1,0:T(8,128)(2,1)} %get-tuple-element.99), calls=%async_computation.3 | async-start | bytes 3932160 | tf_op jit(solution)/shard_map/all_to_all | solution.py:986
  201.4 24.5 %copy-start.38 = (bf16[960,768]{1,0:T(8,128)(2,1)S(1)}, bf16[960,768]{1,0:T(8,128)(2,1)}, u32[]{:S(2)}) copy-start(bf16[960,768]{1,0:T(8,128)(2,1)} %get-tuple-element.104) | copy-start | bytes 4423684
  225.9 6.2 %copy-start.37 = (bf16[960,768]{1,0:T(8,128)(2,1)S(1)}, bf16[960,768]{1,0:T(8,128)(2,1)}, u32[]{:S(2)}) copy-start(bf16[960,768]{1,0:T(8,128)(2,1)} %get-tuple-element.102) | copy-start | bytes 4423684
  225.9 6.2 %copy-start.45 = (bf16[960,1536]{1,0:T(8,128)(2,1)S(1)}, bf16[960,1536]{1,0:T(8,128)(2,1)}, u32[]{:S(2)}) copy-start(bf16[960,1536]{1,0:T(8,128)(2,1)} %get-tuple-element.109) | copy-start | bytes 8847364
  237.5 28.3 %copy-start.43 = (bf16[960,768]{1,0:T(8,128)(2,1)S(1)}, bf16[960,768]{1,0:T(8,128)(2,1)}, u32[]{:S(2)}) copy-start(bf16[960,768]{1,0:T(8,128)(2,1)} %get-tuple-element.100) | copy-start | bytes 4423684
  265.8 4.0 copy-start.30
  265.8 4.0 copy-start.40
  274.4 50.4 %collective-permute-start.8 = (bf16[768,2304]{1,0:T(8,128)(2,1)}, bf16[768,2304]{1,0:T(8,128)(2,1)}, u32[]{:S(2)}, u32[]{:S(2)}) collective-permute-start(bf16[768,2304]{1,0:T(8,128)(2,1)} %pad_maximum_fusion), channel_id=1, source_target_pairs={{0,1},{1,0},{2,3},{3,2},{4,5},{5,4},{6,7},{7,6},{8,9},{9,8},{10,11... | collective-permute-start | bytes 10616840 | tf_op jit(solution)/shard_map/ppermute | solution.py:980
  275.0 55.0 %collective-permute-start.10 = (bf16[2,8,160,768]{3,2,1,0:T(8,128)(2,1)}, bf16[2,8,160,768]{3,2,1,0:T(8,128)(2,1)}, u32[]{:S(2)}, u32[]{:S(2)}) collective-permute-start(bf16[2,8,160,768]{3,2,1,0:T(8,128)(2,1)} %get-tuple-element.134), channel_id=1, source_target_pairs={{0,1},{1,0},{2,3},{3,2},{4,5},{5,4},{6,7},{7,6},{8,9},{9,8},{10,11... | collective-permute-start | bytes 11796488 | tf_op jit(solution)/shard_map/ppermute | solution.py:980
  277.5 28.1 %collective-permute-start.27 = (bf16[2,2,2,48,1536]{4,3,1,0,2:T(8,128)(2,1)S(1)}, bf16[2,2,2,48,1536]{4,3,1,0,2:T(8,128)(2,1)S(1)}, u32[]{:S(2)}, u32[]{:S(2)}) collective-permute-start(bf16[2,2,2,48,1536]{4,3,1,0,2:T(8,128)(2,1)S(1)} %bitcast.170), channel_id=1, source_target_pairs={{0,2},{2,0},{4,6},{6,4},{8,10},{10,8},{12,14},{14,12},{16,18},{18,... | collective-permute-start | bytes 3538952 | tf_op jit(solution)/shard_map/ppermute | solution.py:1190
  279.8 27.7 %collective-permute-start.28 = (bf16[2,2,2,48,1536]{4,3,1,0,2:T(8,128)(2,1)S(1)}, bf16[2,2,2,48,1536]{4,3,1,0,2:T(8,128)(2,1)S(1)}, u32[]{:S(2)}, u32[]{:S(2)}) collective-permute-start(bf16[2,2,2,48,1536]{4,3,1,0,2:T(8,128)(2,1)S(1)} %bitcast.171), channel_id=1, source_target_pairs={{0,4},{2,6},{4,0},{6,2},{8,12},{10,14},{12,8},{14,10},{16,20},{18,... | collective-permute-start | bytes 3538952 | tf_op jit(solution)/shard_map/ppermute | solution.py:1190
  311.0 55.5 %all-to-all-start.4 = ((bf16[32,40,768]{2,1,0:T(8,128)(2,1)}), bf16[32,40,768]{2,1,0:T(8,128)(2,1)}, u32[]{:S(2)}, u32[]{:S(2)}) async-start(bf16[32,40,768]{2,1,0:T(8,128)(2,1)} %get-tuple-element.137), calls=%async_computation.4 | async-start | bytes 3932160 | tf_op jit(solution)/shard_map/all_to_all | solution.py:986
  317.7 4.4 copy-start.5
  317.7 7.0 %copy-start.6 = (f32[768,1152]{1,0:T(8,128)S(1)}, f32[768,1152]{1,0:T(8,128)}, u32[]{:S(2)}) copy-start(f32[768,1152]{1,0:T(8,128)} %fusion.22) | copy-start | bytes 10616836
  320.2 50.3 %collective-permute-start.30 = (bf16[2,2,48,1536]{3,2,1,0:T(8,128)(2,1)}, bf16[2,2,48,1536]{3,2,1,0:T(8,128)(2,1)}, u32[]{:S(2)}, u32[]{:S(2)}) collective-permute-start(bf16[2,2,48,1536]{3,2,1,0:T(8,128)(2,1)} %get-tuple-element.164), channel_id=1, source_target_pairs={{0,2},{2,0},{4,6},{6,4},{8,10},{10,8},{12,14},{14,12},{16,18},{18,... | collective-permute-start | bytes 1769480 | tf_op jit(solution)/shard_map/ppermute | solution.py:1190
  323.2 47.8 %collective-permute-start.29 = (bf16[2,2,48,1536]{3,2,1,0:T(8,128)(2,1)}, bf16[2,2,48,1536]{3,2,1,0:T(8,128)(2,1)}, u32[]{:S(2)}, u32[]{:S(2)}) collective-permute-start(bf16[2,2,48,1536]{3,2,1,0:T(8,128)(2,1)} %get-tuple-element.166), channel_id=1, source_target_pairs={{0,4},{2,6},{4,0},{6,2},{8,12},{10,14},{12,8},{14,10},{16,20},{18,... | collective-permute-start | bytes 1769480 | tf_op jit(solution)/shard_map/ppermute | solution.py:1190
  330.0 25.6 %copy-start = (bf16[768,2304]{1,0:T(8,128)(2,1)S(1)}, bf16[768,2304]{1,0:T(8,128)(2,1)}, u32[]{:S(2)}) copy-start(bf16[768,2304]{1,0:T(8,128)(2,1)} %fusion.refs_3_.refs_7_) | copy-start | bytes 10616836
  355.6 3.1 copy-start.26
  355.6 23.4 %collective-permute-start.13 = (bf16[1024,384]{1,0:T(8,128)(2,1)}, bf16[1024,384]{1,0:T(8,128)(2,1)}, u32[]{:S(2)}, u32[]{:S(2)}) collective-permute-start(bf16[1024,384]{1,0:T(8,128)(2,1)} %dynamic-slice_convert_fusion), channel_id=1, source_target_pairs={{0,1},{1,0},{2,3},{3,2},{4,5},{5,4},{6,7},{7,6},{8,9},{9,8},{10,11... | collective-permute-start | bytes 2359304 | tf_op jit(solution)/shard_map/ppermute | solution.py:980
  355.9 5.6 %copy-start.3 = (bf16[768,1152]{1,0:T(8,128)(2,1)}, bf16[768,1152]{1,0:T(8,128)(2,1)S(1)}, u32[]{:S(2)}) copy-start(bf16[768,1152]{1,0:T(8,128)(2,1)S(1)} %get-tuple-element.158) | copy-start | bytes 5308420
  356.9 29.1 %collective-permute-start.16 = (bf16[2,2,2,48,1152]{4,3,2,1,0:T(8,128)(2,1)}, bf16[2,2,2,48,1152]{4,3,2,1,0:T(8,128)(2,1)S(1)}, u32[]{:S(2)}, u32[]{:S(2)}) collective-permute-start(bf16[2,2,2,48,1152]{4,3,2,1,0:T(8,128)(2,1)} %dynamic-slice_bitcast_fusion), channel_id=1, source_target_pairs={{0,4},{2,6},{4,0},{6,2},{8,12},{10,14},{12,8},{14,10},{16,20},{18,... | collective-permute-start | bytes 2654216 | tf_op jit(solution)/shard_map/ppermute | solution.py:1190
  361.4 32.8 %collective-permute-start.11 = (bf16[768,768]{1,0:T(8,128)(2,1)}, bf16[768,768]{1,0:T(8,128)(2,1)}, u32[]{:S(2)}, u32[]{:S(2)}) collective-permute-start(bf16[768,768]{1,0:T(8,128)(2,1)} %convolution_convert_fusion.3), channel_id=1, source_target_pairs={{0,1},{1,0},{2,3},{3,2},{4,5},{5,4},{6,7},{7,6},{8,9},{9,8},{10,11... | collective-permute-start | bytes 3538952 | tf_op jit(solution)/shard_map/ppermute | solution.py:980
  370.5 22.4 %collective-permute-start.14 = (bf16[2,2,2,48,1152]{4,3,2,1,0:T(8,128)(2,1)}, bf16[2,2,2,48,1152]{4,3,2,1,0:T(8,128)(2,1)}, u32[]{:S(2)}, u32[]{:S(2)}) collective-permute-start(bf16[2,2,2,48,1152]{4,3,2,1,0:T(8,128)(2,1)} %dynamic-slice_bitcast_fusion.1), channel_id=1, source_target_pairs={{0,2},{2,0},{4,6},{6,4},{8,10},{10,8},{12,14},{14,12},{16,18},{18,... | collective-permute-start | bytes 2654216 | tf_op jit(solution)/shard_map/ppermute | solution.py:1190
  371.1 51.6 %collective-permute-start.9 = (bf16[20,24,768]{2,1,0:T(8,128)(2,1)}, bf16[20,24,768]{2,1,0:T(8,128)(2,1)}, u32[]{:S(2)}, u32[]{:S(2)}) collective-permute-start(bf16[20,24,768]{2,1,0:T(8,128)(2,1)} %get-tuple-element.131), channel_id=1, source_target_pairs={{0,1},{1,0},{2,3},{3,2},{4,5},{5,4},{6,7},{7,6},{8,9},{9,8},{10,11... | collective-permute-start | bytes 2211848 | tf_op jit(solution)/shard_map/ppermute | solution.py:980
  374.2 57.0 %all-to-all-start.5 = ((bf16[4,48,3072]{2,1,0:T(8,128)(2,1)}), bf16[4,48,3072]{2,1,0:T(8,128)(2,1)}, u32[]{:S(2)}, u32[]{:S(2)}) async-start(bf16[4,48,3072]{2,1,0:T(8,128)(2,1)} %bitcast.162), calls=%async_computation.5 | async-start | bytes 2359296 | tf_op jit(solution)/shard_map/all_to_all | solution.py:1228
  379.0 39.6 %collective-permute-start.12 = (bf16[20,24,768]{2,1,0:T(8,128)(2,1)}, bf16[20,24,768]{2,1,0:T(8,128)(2,1)}, u32[]{:S(2)}, u32[]{:S(2)}) collective-permute-start(bf16[20,24,768]{2,1,0:T(8,128)(2,1)} %get-tuple-element.139), channel_id=1, source_target_pairs={{0,1},{1,0},{2,3},{3,2},{4,5},{5,4},{6,7},{7,6},{8,9},{9,8},{10,11... | collective-permute-start | bytes 2211848 | tf_op jit(solution)/shard_map/ppermute | solution.py:980
  386.0 8.3 %copy-start.7 = (bf16[2,2,2,48,1152]{4,3,2,1,0:T(8,128)(2,1)}, bf16[2,2,2,48,1152]{4,3,2,1,0:T(8,128)(2,1)S(1)}, u32[]{:S(2)}) copy-start(bf16[2,2,2,48,1152]{4,3,2,1,0:T(8,128)(2,1)S(1)} %collective-permute-done.16.refs_8_) | copy-start | bytes 2654212
  386.0 25.1 %collective-permute-start.20 = (bf16[2,2,2,48,512]{4,3,1,0,2:T(8,128)(2,1)}, bf16[2,2,2,48,512]{4,3,1,0,2:T(8,128)(2,1)}, u32[]{:S(2)}, u32[]{:S(2)}) collective-permute-start(bf16[2,2,2,48,512]{4,3,1,0,2:T(8,128)(2,1)} %bitcast.151), channel_id=1, source_target_pairs={{0,4},{2,6},{4,0},{6,2},{8,12},{10,14},{12,8},{14,10},{16,20},{18,... | collective-permute-start | bytes 1179656 | tf_op jit(solution)/shard_map/ppermute | solution.py:1190
  386.5 7.7 %copy-start.25 = (bf16[8,160,768]{2,1,0:T(8,128)(2,1)S(1)}, bf16[8,160,768]{2,1,0:T(8,128)(2,1)}, u32[]{:S(2)}) copy-start(bf16[8,160,768]{2,1,0:T(8,128)(2,1)} %get-tuple-element.132) | copy-start | bytes 5898244
  386.8 7.5 %copy-start.9 = (bf16[1280,768]{1,0:T(8,128)(2,1)S(1)}, bf16[1280,768]{1,0:T(8,128)(2,1)}, u32[]{:S(2)}) copy-start(bf16[1280,768]{1,0:T(8,128)(2,1)} %get-tuple-element.135.refs_3_) | copy-start | bytes 5898244
  398.4 4.4 copy-start.1
  400.0 1.4 collective-permute-start.22
  402.3 4.6 collective-permute-start.23
  403.0 25.8 %collective-permute-start.18 = (bf16[2,2,2,48,768]{4,3,1,0,2:T(8,128)(2,1)S(1)}, bf16[2,2,2,48,768]{4,3,1,0,2:T(8,128)(2,1)S(1)}, u32[]{:S(2)}, u32[]{:S(2)}) collective-permute-start(bf16[2,2,2,48,768]{4,3,1,0,2:T(8,128)(2,1)S(1)} %bitcast.174), channel_id=1, source_target_pairs={{0,2},{2,0},{4,6},{6,4},{8,10},{10,8},{12,14},{14,12},{16,18},{18,... | collective-permute-start | bytes 1769480 | tf_op jit(solution)/shard_map/ppermute | solution.py:1190
  406.9 4.2 collective-permute-start.24
  411.0 22.5 %collective-permute-start.17 = (bf16[2,2,48,1152]{3,2,1,0:T(8,128)(2,1)S(1)}, bf16[2,2,48,1152]{3,2,1,0:T(8,128)(2,1)S(1)}, u32[]{:S(2)}, u32[]{:S(2)}) collective-permute-start(bf16[2,2,48,1152]{3,2,1,0:T(8,128)(2,1)S(1)} %get-tuple-element.170), channel_id=1, source_target_pairs={{0,2},{2,0},{4,6},{6,4},{8,10},{10,8},{12,14},{14,12},{16,18},{18,... | collective-permute-start | bytes 1327112 | tf_op jit(solution)/shard_map/ppermute | solution.py:1190
  411.1 4.2 collective-permute-start.25
  415.3 12.9 %collective-permute-start.26 = (f32[32,384]{1,0:T(8,128)S(1)}, f32[32,384]{1,0:T(8,128)S(1)}, u32[]{:S(2)}, u32[]{:S(2)}) collective-permute-start(f32[32,384]{1,0:T(8,128)S(1)} %add.226), channel_id=1, source_target_pairs={{0,16},{2,18},{4,20},{6,22},{8,24},{10,26},{12,28},{14,30},{16,0},... | collective-permute-start | bytes 147464 | tf_op jit(solution)/shard_map/ppermute | solution.py:1190
  418.6 14.9 %collective-permute-start.15 = (bf16[2,2,48,1152]{3,2,1,0:T(8,128)(2,1)S(1)}, bf16[2,2,48,1152]{3,2,1,0:T(8,128)(2,1)S(1)}, u32[]{:S(2)}, u32[]{:S(2)}) collective-permute-start(bf16[2,2,48,1152]{3,2,1,0:T(8,128)(2,1)S(1)} %get-tuple-element.172), channel_id=1, source_target_pairs={{0,4},{2,6},{4,0},{6,2},{8,12},{10,14},{12,8},{14,10},{16,20},{18,... | collective-permute-start | bytes 1327112 | tf_op jit(solution)/shard_map/ppermute | solution.py:1190
  422.6 10.9 %collective-permute-start.21 = (bf16[2,2,48,512]{3,2,1,0:T(8,128)(2,1)S(1)}, bf16[2,2,48,512]{3,2,1,0:T(8,128)(2,1)S(1)}, u32[]{:S(2)}, u32[]{:S(2)}) collective-permute-start(bf16[2,2,48,512]{3,2,1,0:T(8,128)(2,1)S(1)} %get-tuple-element.182), channel_id=1, source_target_pairs={{0,2},{2,0},{4,6},{6,4},{8,10},{10,8},{12,14},{14,12},{16,18},{18,... | collective-permute-start | bytes 589832 | tf_op jit(solution)/shard_map/ppermute | solution.py:1190
  429.7 6.7 %collective-permute-start.19 = (bf16[2,2,48,768]{3,2,1,0:T(8,128)(2,1)S(1)}, bf16[2,2,48,768]{3,2,1,0:T(8,128)(2,1)S(1)}, u32[]{:S(2)}, u32[]{:S(2)}) collective-permute-start(bf16[2,2,48,768]{3,2,1,0:T(8,128)(2,1)S(1)} %get-tuple-element.180), channel_id=1, source_target_pairs={{0,4},{2,6},{4,0},{6,2},{8,12},{10,14},{12,8},{14,10},{16,20},{18,... | collective-permute-start | bytes 884744 | tf_op jit(solution)/shard_map/ppermute | solution.py:1190
  433.5 2.9 copy-start.12
  440.2 3.7 copy-start.11
  440.2 33.0 %all-to-all-start.6 = ((bf16[4,48,3584]{2,1,0:T(8,128)(2,1)}), bf16[4,48,3584]{2,1,0:T(8,128)(2,1)S(1)}, u32[]{:S(2)}, u32[]{:S(2)}) async-start(bf16[4,48,3584]{2,1,0:T(8,128)(2,1)} %bitcast.159), calls=%async_computation.6 | async-start | bytes 2752512 | tf_op jit(solution)/shard_map/all_to_all | solution.py:1228
  (20 other events, 35.6 us)

commit v5 on v3

--- a/solution.py
+++ b/solution.py
@@ -74,9 +74,7 @@
         compiler_params=pltpu.CompilerParams(
             dimension_semantics=("arbitrary",), vmem_limit_bytes=VMEM_LIMIT
         ),
-        cost_estimate=pl.CostEstimate(
-            flops=flops, bytes_accessed=moved, transcendentals=0
-        ),
+        cost_estimate=pl.CostEstimate(flops=flops, bytes_accessed=moved, transcendentals=0),
     )(*scalars, *[array for array, _ in ins])
 
 
@@ -862,19 +860,6 @@
         text_grad[where[base + row]] = acc[row * length : (row + 1) * length].astype(BF16)
     for at in range(8):
         sums[0, at : at + 1] = jnp.sum(part[at], axis=0, keepdims=True)
-
-
-def join_kernel(scalars, ins, outs, scratch):
-    stay_x, got_x, stay_y, got_y = ins
-    (out,) = outs
-    for start, stay, got in ((0, stay_x, got_x), (stay_x.shape[1], stay_y, got_y)):
-        for at in range(0, out.shape[0], 96):
-            rows = slice(at, at + 96)
-            out[rows, start : start + stay.shape[1]] = add_low(stay[rows], got[rows])
-
-
-def add_low(left, right):
-    return (left.astype(F32) + right.astype(F32)).astype(BF16)
 
 
 def pack_kernel(local, hidden, scalars, ins, outs, scratch):
@@ -1202,23 +1187,13 @@
         return swap(add(stay_x, got_x), bits - 2, 1) + swap(add(stay_y, got_y), bits - 2, 0)
 
     def add(stay, got):
-        return add_low(stay, got)
-
-    def last_parts(values, after):
-        count = values[0].size // values[0].shape[-1]
-        shape = (count, values[0].shape[-1] + values[2].shape[-1])
-        values = [value.reshape(count, value.shape[-1]) for value in values]
-        (joined,) = run(
-            join_kernel,
-            1,
-            [],
-            [whole(value) for value in values],
-            [(shape, BF16, whole_spec(shape))],
-            [],
-            0,
-            after,
+        return (stay.astype(F32) + got.astype(F32)).astype(BF16)
+
+    def last_parts(stay_x, got_x, stay_y, got_y):
+        parts = [add(stay_x, got_x), add(stay_y, got_y)]
+        return jnp.concatenate(
+            [part.reshape((devices // 4,) + part.shape[-2:]) for part in parts], axis=2
         )
-        return joined.reshape(devices // 4, count // (devices // 4), shape[1])
 
     def last_sum(both, first_width):
         groups = [[low + 4 * n for n in range(devices // 4)] for low in range(4)]
@@ -1311,6 +1286,8 @@
     self_part = (self_own + self_got.astype(F32)).astype(BF16)
     half_width = self_part.shape[1] // 2
     self_stage = first_swaps(self_part[:, :half_width], self_part[:, half_width:])
+    feed_parts = last_parts(*feed_stage)
+    piece, piece_mate, self_part, feed_parts = tie(piece, piece_mate, self_part, feed_parts)
 
     flat_images = own_images * patch_pad
     patch_grad_shape = (patch_count, own_images, vision)
@@ -1344,9 +1321,10 @@
             pltpu.SemaphoreType.DMA((4,)),
         ],
         2 * flat_images * width * (2 * width + 2 * vision),
-    )
-
-    up_grad, down_grad = last_sum(last_parts(feed_stage, [kv_own]), hidden)
+        [text_in],
+    )
+
+    up_grad, down_grad = last_sum(feed_parts, hidden)
     self_stage = second_swaps(*self_stage)
     kv_low = proj.reshape(flat_images, width)
     kv_away = low_tn(kv_low, kv_mate)
@@ -1358,9 +1336,9 @@
     proj_part = (proj_own + proj_got.astype(F32)).astype(BF16)
     proj_part = proj_part.reshape(width, vision * local // width)
     image_stage = first_swaps(kv_part, proj_part)
-    self_one, self_two = last_sum(last_parts(self_stage, []), half_width)
+    self_one, self_two = last_sum(last_parts(*self_stage), half_width)
     image_stage = second_swaps(*image_stage)
-    kv_grad, proj_grad = last_sum(last_parts(image_stage, []), width)
+    kv_grad, proj_grad = last_sum(last_parts(*image_stage), width)
     proj_grad = proj_grad.reshape(vision // devices, local)
 
     lines = 23 + hidden // local
@@ -1419,7 +1397,7 @@
 
     return (
         tokens_out(merged_in, [self_part], [kv_part]),
-        tokens_out(text_in, [kv_own], [kv_part, proj_part]),
+        tokens_out(text_in, [kv_away], [kv_part, proj_part]),
         jnp.transpose(patch_grad, (1, 0, 2)),
         proj_grad,
         proj_bias_grad,

time: 488 us -> 474 us (0.971)
  waiting for transfers between devices: 83.8 us -> 68.5 us
  Pallas kernels: 225 us -> 217 us
  starting transfers between devices: 71.5 us -> 79.2 us
  other arithmetic: 20.2 us -> 27.4 us
    ppermute x16, waiting for transfers between devices: 51.5 us -> 20.9 us  [partner_bits(): return lax.ppermute(value, 'dp', [(d, d ^ mask) for d in range(devices)])]
    all_to_all x5, waiting for transfers between devices: 19.7 us -> 34.8 us  [exchange(): return lax.all_to_all(value, 'dp', split_axis=0, concat_axis=0, tiled=True)]
    pallas_call x16 -> x13, Pallas kernels: 225 us -> 217 us  [run(): pl.pallas_call(kernel, grid_spec=pltpu.PrefetchScalarGridSpec(num_scalar_...]
    convert_element_type x5 -> x12, other arithmetic: 7.09 us -> 13.2 us  [add(): return (stay.astype(F32) + got.astype(F32)).astype(BF16)]
    unnamed x95 -> x99, local copies, waits for them, and re-layouts: 11.9 us -> 8.38 us
  transfers between devices with their start and end apart: 39 -> 39, of which waited for: 11 -> 11; matrix products, arithmetic and copies ran while one was open for 17% -> 18% of each run, Pallas kernels for 33% -> 33%
where the time goes in v5:
time: 474 us; the launch traced here: 472 us
  Pallas kernels  217 us (46%)
  starting transfers between devices  79.2 us (17%)
  waiting for transfers between devices  68.5 us (14%)
  matrix products  46.7 us (10%)
  local copies, waits for them, and re-layouts  31.6 us (7%)
  other arithmetic  27.4 us (6%)
    pallas_call x13, Pallas kernels, run(): pl.pallas_call(kernel, grid_spec=pltpu.PrefetchScalarGridSpec(num_scalar_...  217 us
    dot_general x14, matrix products, dot_tn(): lax.dot_general(left, right, (((0,), (0,)), ((), ())), preferred_element_...  46.7 us
    all_to_all x5, starting transfers between devices, exchange(): return lax.all_to_all(value, 'dp', split_axis=0, concat_axis=0, tiled=True)  39.6 us
    all_to_all x5, waiting for transfers between devices, exchange(): return lax.all_to_all(value, 'dp', split_axis=0, concat_axis=0, tiled=True)  34.8 us
    ppermute x16, waiting for transfers between devices, partner_bits(): return lax.ppermute(value, 'dp', [(d, d ^ mask) for d in range(devices)])  20.9 us
    ppermute x16, starting transfers between devices, partner_bits(): return lax.ppermute(value, 'dp', [(d, d ^ mask) for d in range(devices)])  19.7 us
    all_to_all x3, starting transfers between devices, last_sum(): lax.all_to_all(both, 'dp', split_axis=0, concat_axis=0, axis_index_groups...  17 us
    convert_element_type x12, other arithmetic, add(): return (stay.astype(F32) + got.astype(F32)).astype(BF16)  13.2 us
  transfers between devices with their start and end apart: 39, of which 11 were waited for; matrix products, arithmetic and copies ran while one was open for 18% of the time, Pallas kernels for 33%

profile of v5, /device:TPU:0, one launch (start us, length us, event | category | flops | bytes accessed | tf_op | source)
XLA Modules:
  0.0 472.2 jit_solution(1355818554477588862)
XLA Ops:
  3.6 7.9 %all-to-all-start = ((s32[16,2,6]{2,1,0:T(2,128)}), s32[16,2,6]{2,1,0:T(2,128)S(1)}, u32[]{:S(2)}, u32[]{:S(2)}) async-start(s32[16,2,6]{2,1,0:T(2,128)} %bitcast.4), calls=%async_computation | async-start | bytes 32768 | tf_op jit(solution)/shard_map/all_to_all | solution.py:968
  12.1 5.3 %shard_map.281 = (bf16[32,40,768]{2,1,0:T(8,128)(2,1)}, bf16[32,40,768]{2,1,0:T(8,128)(2,1)}) custom-call(s32[32]{0:T(128)} %select_reduce_fusion.1.refs_0_, bf16[48,40,768]{2,1,0:T(8,128)(2,1)} %refs_1_.1, bf16[48,40,768]{2,1,0:T(8,128)(2,1)} %refs_2_.2), custom_call_target="tpu_custom_call" | custom-call | bytes 9830400 | tf_op jit(solution)/shard_map/pallas_call | solution.py:64
  17.5 1.4 all-to-all-done
  18.8 5.9 %all-to-all-start.2 = ((bf16[32,40,768]{2,1,0:T(8,128)(2,1)}), bf16[32,40,768]{2,1,0:T(8,128)(2,1)S(1)}, u32[]{:S(2)}, u32[]{:S(2)}) async-start(bf16[32,40,768]{2,1,0:T(8,128)(2,1)} %get-tuple-element.97), calls=%async_computation.2 | async-start | bytes 3932160 | tf_op jit(solution)/shard_map/all_to_all | solution.py:968
  29.3 22.2 %shard_map.282 = (bf16[8,160,768]{2,1,0:T(8,128)(2,1)}, bf16[16,160,768]{2,1,0:T(8,128)(2,1)}, bf16[16,160,768]{2,1,0:T(8,128)(2,1)}) custom-call(s32[1]{0:T(128)} %bitcast.refs_0_, bf16[145,16,1024]{2,1,0:T(8,128)(2,1)} %bitcast.168, bf16[1024,768]{1,0:T(8,128)(2,1)} %refs_4_.5, f32[1,768]{1,0:T(1,128)} %reshape.219.refs_3_, ...), custom_call_target="tpu_custom_call" | custom-call | flops 10066329600 | bytes 23247872 | tf_op jit(solution)/shard_map/pallas_call | solution.py:64
  51.5 14.0 %all-to-all-done.2.refs_2_ = bf16[32,40,768]{2,1,0:T(8,128)(2,1)S(1)} async-done(((bf16[32,40,768]{2,1,0:T(8,128)(2,1)}), bf16[32,40,768]{2,1,0:T(8,128)(2,1)S(1)}, u32[]{:S(2)}, u32[]{:S(2)}) %all-to-all-start.2) | async-done | bytes 1966112 | tf_op jit(solution)/shard_map/all_to_all | solution.py:968
  65.6 1.3 copy-done.17
  66.9 9.7 %all-to-all-start.1 = ((bf16[32,40,768]{2,1,0:T(8,128)(2,1)}), bf16[32,40,768]{2,1,0:T(8,128)(2,1)}, u32[]{:S(2)}, u32[]{:S(2)}) async-start(bf16[32,40,768]{2,1,0:T(8,128)(2,1)} %get-tuple-element.93), calls=%async_computation.1 | async-start | bytes 3932160 | tf_op jit(solution)/shard_map/all_to_all | solution.py:968
  77.8 22.1 %shard_map.283 = (bf16[960,768]{1,0:T(8,128)(2,1)}, f32[960,768]{1,0:T(8,128)}, bf16[960,768]{1,0:T(8,128)(2,1)}, bf16[960,768]{1,0:T(8,128)(2,1)}, bf16[960,768...) custom-call(s32[24]{0:T(128)} %get-tuple-element.96.refs_0_, ...), custom_call_target="tpu_custom_call" | custom-call | flops 6417285120 | bytes 24718080 | tf_op jit(solution)/shard_map/pallas_call | solution.py:64
  100.0 12.5 %shard_map.284.refs_2_ = bf16[960,768]{1,0:T(8,128)(2,1)} custom-call(s32[24]{0:T(128)} %and_select_fusion.refs_0_, s32[96]{0:T(128)} %reshape.218.refs_1_, bf16[960,768]{1,0:T(8,128)(2,1)} %get-tuple-element.109.refs_2_, bf16[16,160,768]{2,1,0:T(8,128)(2,1)} %get-tuple-element.100.refs_3_.refs_4_, bf16[16,160,768]{2,1,0:T(8,128)(2,1)} %get-tuple-element.101.refs_4_.refs_5_), custom_call_target="tpu_custom_call" | custom-call | flops 3019898880 | bytes 10813440 | tf_op jit(solution)/shard_map/pallas_call | solution.py:64
  112.5 4.4 all-to-all-done.1.refs_1_
  116.8 63.1 %shard_map.285 = (bf16[32,40,768]{2,1,0:T(8,128)(2,1)}, bf16[960,768]{1,0:T(8,128)(2,1)}, bf16[960,768]{1,0:T(8,128)(2,1)}, bf16[960,768]{1,0:T(8,128)(2,1)}, f3...) custom-call(s32[24]{0:T(128)} %compare_select_fusion.4.refs_1_.refs_, ...), custom_call_target="tpu_custom_call" | custom-call | flops 20384317440 | bytes 42384384 | tf_op jit(solution)/shard_map/pallas_call | solution.py:64
  180.0 6.5 %convolution_convert_fusion.1 = bf16[768,1536]{1,0:T(8,128)(2,1)} fusion(bf16[960,768]{1,0:T(8,128)(2,1)} %get-tuple-element.107, bf16[960,1536]{1,0:T(8,128)(2,1)} %get-tuple-element.108), kind=kOutput, calls=%fused_computation.7 | convolution fusion | flops 2266103808 | bytes 6782976 | tf_op jit(solution)/shard_map/dot_general | solution.py:38
  186.5 4.0 convolution_convert_fusion.2
  191.6 24.3 %shard_map.286 = (bf16[2,8,160,768]{3,2,1,0:T(8,128)(2,1)}, bf16[2,8,160,768]{3,2,1,0:T(8,128)(2,1)}, bf16[960,768]{1,0:T(8,128)(2,1)}) custom-call(s32[24]{0:T(128)} %and_select_fusion.refs_0_, s32[96]{0:T(128)} %reshape.218.refs_1_, bf16[960,768]{1,0:T(8,128)(2,1)} %get-tuple-element.109.refs_2_, bf16[960,768]{1,0:T(8,128)(2,1)} %get-tuple-element.110.refs_3_, ...), custom_call_target="tpu_custom_call" | custom-call | flops 9059696640 | bytes 20152320 | tf_op jit(solution)/shard_map/pallas_call | solution.py:64
  215.9 9.2 %all-to-all-start.3 = ((bf16[32,40,768]{2,1,0:T(8,128)(2,1)}), bf16[32,40,768]{2,1,0:T(8,128)(2,1)S(1)}, u32[]{:S(2)}, u32[]{:S(2)}) async-start(bf16[32,40,768]{2,1,0:T(8,128)(2,1)} %get-tuple-element.103), calls=%async_computation.3 | async-start | bytes 3932160 | tf_op jit(solution)/shard_map/all_to_all | solution.py:968
  225.2 3.1 convolution_convert_fusion.5
  230.5 4.4 add_convert_fusion
  234.9 4.2 add_convert_fusion.1
  240.3 1.9 collective-permute-start.10
  243.4 1.5 collective-permute-start.11
  244.9 28.1 %shard_map.287 = (bf16[32,40,768]{2,1,0:T(8,128)(2,1)}, bf16[960,768]{1,0:T(8,128)(2,1)}, bf16[960,384]{1,0:T(8,128)(2,1)}, bf16[960,384]{1,0:T(8,128)(2,1)}, bf...) custom-call(s32[24]{0:T(128)} %get-tuple-element.96.refs_0_, ...), custom_call_target="tpu_custom_call" | custom-call | flops 7172259840 | bytes 30634752 | tf_op jit(solution)/shard_map/pallas_call | solution.py:64
  273.0 2.7 convolution_convert_fusion.6
  277.8 2.3 convolution_convert_fusion
  280.1 2.0 pad_maximum_fusion
  282.9 4.1 fusion.28
  287.0 2.0 fusion.29
  289.0 1.6 add_convert_fusion.4
  292.1 1.6 add_convert_fusion.3
  295.0 1.3 copy-done.3
  296.3 7.0 %all-to-all-start.4 = ((bf16[32,40,768]{2,1,0:T(8,128)(2,1)}), bf16[32,40,768]{2,1,0:T(8,128)(2,1)}, u32[]{:S(2)}, u32[]{:S(2)}) async-start(bf16[32,40,768]{2,1,0:T(8,128)(2,1)} %get-tuple-element.148), calls=%async_computation.4 | async-start | bytes 3932160 | tf_op jit(solution)/shard_map/all_to_all | solution.py:968
  303.3 2.7 fusion.31
  305.9 7.9 %collective-permute-done.12 = bf16[2,2,48,1536]{3,2,1,0:T(8,128)(2,1)} collective-permute-done((bf16[2,2,48,1536]{3,2,1,0:T(8,128)(2,1)}, bf16[2,2,48,1536]{3,2,1,0:T(8,128)(2,1)}, u32[]{:S(2)}, u32[]{:S(2)}) %collective-permute-start.12) | collective-permute-done | bytes 589856 | tf_op jit(solution)/shard_map/ppermute | solution.py:1172
  313.9 1.3 fusion.5
  315.2 1.4 fusion.4
  317.7 2.4 fusion.refs_3_
  320.4 1.4 copy-done
  324.0 4.0 shard_map.288
  328.0 15.1 %all-to-all-done.4.refs_7_.refs_2_ = bf16[32,40,768]{2,1,0:T(8,128)(2,1)} async-done(((bf16[32,40,768]{2,1,0:T(8,128)(2,1)}), bf16[32,40,768]{2,1,0:T(8,128)(2,1)}, u32[]{:S(2)}, u32[]{:S(2)}) %all-to-all-start.4) | async-done | bytes 1966112 | tf_op jit(solution)/shard_map/all_to_all | solution.py:968
  343.1 8.4 %all-to-all-start.6 = ((bf16[4,48,3072]{2,1,0:T(8,128)(2,1)}), bf16[4,48,3072]{2,1,0:T(8,128)(2,1)S(1)}, u32[]{:S(2)}, u32[]{:S(2)}) async-start(bf16[4,48,3072]{2,1,0:T(8,128)(2,1)} %pad_maximum_fusion.1), calls=%async_computation.6 | async-start | bytes 2359296 | tf_op jit(solution)/shard_map/all_to_all | solution.py:1200
  351.5 23.1 %shard_map.289 = (bf16[1280,768]{1,0:T(8,128)(2,1)}, bf16[1280,768]{1,0:T(8,128)(2,1)}, bf16[145,8,1024]{2,1,0:T(8,128)(2,1)}, f32[1024,768]{1,0:T(8,128)}, f32[8,768]{1,0:T(8,128)}) custom-call(s32[1]{0:T(128)} %bitcast.refs_0_, bf16[2,8,160,768]{3,2,1,0:T(8,128)(2,1)} %get-tuple-element.146.refs_1_, ...), custom_call_target="tpu_custom_call" | custom-call | flops 7046430720 | bytes 30744576 | tf_op jit(solution)/shard_map/pallas_call | solution.py:64
  374.6 4.3 convolution_convert_fusion.3.refs_3_
  378.9 2.4 dynamic-slice_convert_fusion
  381.9 4.1 shard_map.291
  386.0 1.4 fusion.2
  388.3 1.7 collective-permute-start.28
  389.9 1.4 fusion.1
  393.2 1.3 add_convert_fusion.5
  395.2 1.5 reshape.226.refs_4_.refs_7_
  397.9 4.5 add_convert_fusion.2.refs_3_.refs_6_
  403.3 6.2 %collective-permute-done.20 = bf16[2,2,2,48,512]{4,3,2,1,0:T(8,128)(2,1)S(1)} collective-permute-done((bf16[2,2,2,48,512]{4,3,2,1,0:T(8,128)(2,1)S(1)}, bf16[2,2,2,48,512]{4,3,2,1,0:T(8,128)(2,1)S(1)}, u32[]{:S(2)}, u32[]{:S(2)}) %collective-permute-start.20) | collective-permute-done | bytes 393248 | tf_op jit(solution)/shard_map/ppermute | solution.py:1172
  409.5 1.5 collective-permute-start.18
  413.9 1.5 shard_map.293
  417.7 1.5 collective-permute-start.23
  420.2 5.1 %all-to-all-start.7 = ((bf16[4,48,2304]{2,1,0:T(8,128)(2,1)}), bf16[4,48,2304]{2,1,0:T(8,128)(2,1)S(1)}, u32[]{:S(2)}, u32[]{:S(2)}) async-start(bf16[4,48,2304]{2,1,0:T(8,128)(2,1)} %pad_maximum_fusion.2), calls=%async_computation.7 | async-start | bytes 1769472 | tf_op jit(solution)/shard_map/all_to_all | solution.py:1200
  425.3 3.4 shard_map.292
  428.7 3.5 shard_map.290
  434.1 2.3 collective-permute-done.24
  436.4 2.1 collective-permute-start.25
  438.5 1.2 fusion.3
  440.8 4.7 collective-permute-start.26
  446.4 3.3 collective-permute-done.26
  454.3 3.5 all-to-all-start.5
  458.6 12.4 %all-to-all-done.5 = bf16[4,48,1280]{2,1,0:T(8,128)(2,1)S(1)} async-done(((bf16[4,48,1280]{2,1,0:T(8,128)(2,1)}), bf16[4,48,1280]{2,1,0:T(8,128)(2,1)S(1)}, u32[]{:S(2)}, u32[]{:S(2)}) %all-to-all-start.5) | async-done | bytes 491552 | tf_op jit(solution)/shard_map/all_to_all | solution.py:1200
  (219 shorter events, 46.8 us)
Async XLA Ops:
  0.6 28.1 %collective-permute-start.1 = (bf16[2,3,768,384]{3,2,1,0:T(8,128)(2,1)}, bf16[2,3,768,384]{3,2,1,0:T(8,128)(2,1)}, u32[]{:S(2)}, u32[]{:S(2)}) collective-permute-start(bf16[2,3,768,384]{3,2,1,0:T(8,128)(2,1)} %refs_5_.3), channel_id=1, source_target_pairs={{0,1},{1,0},{2,3},{3,2},{4,5},{5,4},{6,7},{7,6},{8,9},{9,8},{10,11... | collective-permute-start | bytes 10616840 | tf_op jit(solution)/shard_map/ppermute | solution.py:962
  3.6 15.2 %all-to-all-start = ((s32[16,2,6]{2,1,0:T(2,128)}), s32[16,2,6]{2,1,0:T(2,128)S(1)}, u32[]{:S(2)}, u32[]{:S(2)}) async-start(s32[16,2,6]{2,1,0:T(2,128)} %bitcast.4), calls=%async_computation | async-start | bytes 32768 | tf_op jit(solution)/shard_map/all_to_all | solution.py:968
  18.8 5.9 %copy-start.26 = (bf16[2,384,768]{2,1,0:T(8,128)(2,1)S(1)}, bf16[2,384,768]{2,1,0:T(8,128)(2,1)}, u32[]{:S(2)}) copy-start(bf16[2,384,768]{2,1,0:T(8,128)(2,1)} %refs_11_.5) | copy-start | bytes 3538948
  18.8 6.0 %copy-start.27 = (f32[2,2,384]{2,1,0:T(2,128)S(1)}, f32[2,2,384]{2,1,0:T(2,128)}, u32[]{:S(2)}) copy-start(f32[2,2,384]{2,1,0:T(2,128)} %refs_7_.1) | copy-start | bytes 18436
  18.8 6.5 %copy-start.25 = (s32[1,16]{1,0:T(1,128)S(1)}, s32[1,16]{1,0:T(1,128)}, u32[]{:S(2)}) copy-start(s32[1,16]{1,0:T(1,128)} %param.22) | copy-start | bytes 196
  18.8 6.8 %copy-start.24 = (f32[768]{0:T(1024)S(1)}, f32[768]{0:T(1024)}, u32[]{:S(2)}) copy-start(f32[768]{0:T(1024)} %param.26) | copy-start | bytes 9220
  18.8 46.7 %all-to-all-start.2 = ((bf16[32,40,768]{2,1,0:T(8,128)(2,1)}), bf16[32,40,768]{2,1,0:T(8,128)(2,1)S(1)}, u32[]{:S(2)}, u32[]{:S(2)}) async-start(bf16[32,40,768]{2,1,0:T(8,128)(2,1)} %get-tuple-element.97), calls=%async_computation.2 | async-start | bytes 3932160 | tf_op jit(solution)/shard_map/all_to_all | solution.py:968
  24.8 4.0 collective-permute-start
  24.9 3.9 collective-permute-start.2
  51.5 25.6 %copy-start.22 = (f32[1536]{0:T(1024)S(1)}, f32[1536]{0:T(1024)}, u32[]{:S(2)}) copy-start(f32[1536]{0:T(1024)} %param.34) | copy-start | bytes 18436
  66.9 50.0 %all-to-all-start.1 = ((bf16[32,40,768]{2,1,0:T(8,128)(2,1)}), bf16[32,40,768]{2,1,0:T(8,128)(2,1)}, u32[]{:S(2)}, u32[]{:S(2)}) async-start(bf16[32,40,768]{2,1,0:T(8,128)(2,1)} %get-tuple-element.93), calls=%async_computation.1 | async-start | bytes 3932160 | tf_op jit(solution)/shard_map/all_to_all | solution.py:968
  76.6 35.9 %collective-permute-start.3 = (bf16[768,1536]{1,0:T(8,128)(2,1)}, bf16[768,1536]{1,0:T(8,128)(2,1)}, u32[]{:S(2)}, u32[]{:S(2)}) collective-permute-start(bf16[768,1536]{1,0:T(8,128)(2,1)} %refs_6_.3), channel_id=1, source_target_pairs={{0,1},{1,0},{2,3},{3,2},{4,5},{5,4},{6,7},{7,6},{8,9},{9,8},{10,11... | collective-permute-start | bytes 7077896 | tf_op jit(solution)/shard_map/ppermute | solution.py:962
  76.7 35.8 %collective-permute-start.4 = (bf16[1536,768]{1,0:T(8,128)(2,1)}, bf16[1536,768]{1,0:T(8,128)(2,1)}, u32[]{:S(2)}, u32[]{:S(2)}) collective-permute-start(bf16[1536,768]{1,0:T(8,128)(2,1)} %refs_8_.1), channel_id=1, source_target_pairs={{0,1},{1,0},{2,3},{3,2},{4,5},{5,4},{6,7},{7,6},{8,9},{9,8},{10,11... | collective-permute-start | bytes 7077896 | tf_op jit(solution)/shard_map/ppermute | solution.py:962
  77.2 22.8 %copy-start.23 = (f32[1,1536]{1,0:T(1,128)}, f32[1,1536]{1,0:T(1,128)S(1)}, u32[]{:S(2)}) copy-start(f32[1,1536]{1,0:T(1,128)S(1)} %reshape.220.refs_13_) | copy-start | bytes 18436
  77.2 35.3 %collective-permute-start.5 = (f32[1,1536]{1,0:T(1,128)S(1)}, f32[1,1536]{1,0:T(1,128)S(1)}, u32[]{:S(2)}, u32[]{:S(2)}) collective-permute-start(f32[1,1536]{1,0:T(1,128)S(1)} %reshape.220.refs_13_), channel_id=1, source_target_pairs={{0,1},{1,0},{2,3},{3,2},{4,5},{5,4},{6,7},{7,6},{8,9},{9,8},{10,11... | collective-permute-start | bytes 18440 | tf_op jit(solution)/shard_map/ppermute | solution.py:962
  112.5 4.4 copy-start.29
  180.0 6.5 %copy-start.35 = (bf16[960,1536]{1,0:T(8,128)(2,1)S(1)}, bf16[960,1536]{1,0:T(8,128)(2,1)}, u32[]{:S(2)}) copy-start(bf16[960,1536]{1,0:T(8,128)(2,1)} %get-tuple-element.106) | copy-start | bytes 8847364
  180.0 6.5 %copy-start.38 = (bf16[960,768]{1,0:T(8,128)(2,1)S(1)}, bf16[960,768]{1,0:T(8,128)(2,1)}, u32[]{:S(2)}) copy-start(bf16[960,768]{1,0:T(8,128)(2,1)} %get-tuple-element.105) | copy-start | bytes 4423684
  190.4 38.8 %collective-permute-start.8 = (bf16[768,1536]{1,0:T(8,128)(2,1)}, bf16[768,1536]{1,0:T(8,128)(2,1)}, u32[]{:S(2)}, u32[]{:S(2)}) collective-permute-start(bf16[768,1536]{1,0:T(8,128)(2,1)} %convolution_convert_fusion.1), channel_id=1, source_target_pairs={{0,1},{1,0},{2,3},{3,2},{4,5},{5,4},{6,7},{7,6},{8,9},{9,8},{10,11... | collective-permute-start | bytes 7077896 | tf_op jit(solution)/shard_map/ppermute | solution.py:962
  190.4 44.5 %collective-permute-start.7 = (bf16[768,1536]{1,0:T(8,128)(2,1)}, bf16[768,1536]{1,0:T(8,128)(2,1)}, u32[]{:S(2)}, u32[]{:S(2)}) collective-permute-start(bf16[768,1536]{1,0:T(8,128)(2,1)} %convolution_convert_fusion.2), channel_id=1, source_target_pairs={{0,1},{1,0},{2,3},{3,2},{4,5},{5,4},{6,7},{7,6},{8,9},{9,8},{10,11... | collective-permute-start | bytes 7077896 | tf_op jit(solution)/shard_map/ppermute | solution.py:962
  215.9 108.1 %collective-permute-start.6 = (bf16[2,8,160,768]{3,2,1,0:T(8,128)(2,1)}, bf16[2,8,160,768]{3,2,1,0:T(8,128)(2,1)}, u32[]{:S(2)}, u32[]{:S(2)}) collective-permute-start(bf16[2,8,160,768]{3,2,1,0:T(8,128)(2,1)} %get-tuple-element.112), channel_id=1, source_target_pairs={{0,1},{1,0},{2,3},{3,2},{4,5},{5,4},{6,7},{7,6},{8,9},{9,8},{10,11... | collective-permute-start | bytes 11796488 | tf_op jit(solution)/shard_map/ppermute | solution.py:962
  215.9 9.2 %copy-start.32 = (bf16[960,768]{1,0:T(8,128)(2,1)S(1)}, bf16[960,768]{1,0:T(8,128)(2,1)}, u32[]{:S(2)}) copy-start(bf16[960,768]{1,0:T(8,128)(2,1)} %get-tuple-element.128) | copy-start | bytes 4423684
  215.9 79.1 %all-to-all-start.3 = ((bf16[32,40,768]{2,1,0:T(8,128)(2,1)}), bf16[32,40,768]{2,1,0:T(8,128)(2,1)S(1)}, u32[]{:S(2)}, u32[]{:S(2)}) async-start(bf16[32,40,768]{2,1,0:T(8,128)(2,1)} %get-tuple-element.103), calls=%async_computation.3 | async-start | bytes 3932160 | tf_op jit(solution)/shard_map/all_to_all | solution.py:968
  230.5 4.4 copy-start.39
  230.5 4.4 copy-start.45
  240.3 48.7 %collective-permute-start.10 = (bf16[2,2,2,48,1536]{4,3,2,1,0:T(8,128)(2,1)}, bf16[2,2,2,48,1536]{4,3,2,1,0:T(8,128)(2,1)}, u32[]{:S(2)}, u32[]{:S(2)}) collective-permute-start(bf16[2,2,2,48,1536]{4,3,2,1,0:T(8,128)(2,1)} %get-tuple-element.170), channel_id=1, source_target_pairs={{0,2},{2,0},{4,6},{6,4},{8,10},{10,8},{12,14},{14,12},{16,18},{18,... | collective-permute-start | bytes 3538952 | tf_op jit(solution)/shard_map/ppermute | solution.py:1172
  243.4 45.6 %collective-permute-start.11 = (bf16[2,2,2,48,1536]{4,3,2,1,0:T(8,128)(2,1)}, bf16[2,2,2,48,1536]{4,3,2,1,0:T(8,128)(2,1)}, u32[]{:S(2)}, u32[]{:S(2)}) collective-permute-start(bf16[2,2,2,48,1536]{4,3,2,1,0:T(8,128)(2,1)} %get-tuple-element.168), channel_id=1, source_target_pairs={{0,4},{2,6},{4,0},{6,2},{8,12},{10,14},{12,8},{14,10},{16,20},{18,... | collective-permute-start | bytes 3538952 | tf_op jit(solution)/shard_map/ppermute | solution.py:1172
  282.0 35.7 %collective-permute-start.9 = (bf16[768,2304]{1,0:T(8,128)(2,1)}, bf16[768,2304]{1,0:T(8,128)(2,1)}, u32[]{:S(2)}, u32[]{:S(2)}) collective-permute-start(bf16[768,2304]{1,0:T(8,128)(2,1)} %pad_maximum_fusion), channel_id=1, source_target_pairs={{0,1},{1,0},{2,3},{3,2},{4,5},{5,4},{6,7},{7,6},{8,9},{9,8},{10,11... | collective-permute-start | bytes 10616840 | tf_op jit(solution)/shard_map/ppermute | solution.py:962
  282.9 4.1 copy-start.34
  282.9 4.1 copy-start.36
  291.6 22.3 %collective-permute-start.12 = (bf16[2,2,48,1536]{3,2,1,0:T(8,128)(2,1)}, bf16[2,2,48,1536]{3,2,1,0:T(8,128)(2,1)}, u32[]{:S(2)}, u32[]{:S(2)}) collective-permute-start(bf16[2,2,48,1536]{3,2,1,0:T(8,128)(2,1)} %dynamic-slice_bitcast_fusion.8), channel_id=1, source_target_pairs={{0,4},{2,6},{4,0},{6,2},{8,12},{10,14},{12,8},{14,10},{16,20},{18,... | collective-permute-start | bytes 1769480 | tf_op jit(solution)/shard_map/ppermute | solution.py:1172
  294.9 20.3 %collective-permute-start.13 = (bf16[2,2,48,1536]{3,2,1,0:T(8,128)(2,1)}, bf16[2,2,48,1536]{3,2,1,0:T(8,128)(2,1)}, u32[]{:S(2)}, u32[]{:S(2)}) collective-permute-start(bf16[2,2,48,1536]{3,2,1,0:T(8,128)(2,1)} %dynamic-slice_bitcast_fusion.7), channel_id=1, source_target_pairs={{0,2},{2,0},{4,6},{6,4},{8,10},{10,8},{12,14},{14,12},{16,18},{18,... | collective-permute-start | bytes 1769480 | tf_op jit(solution)/shard_map/ppermute | solution.py:1172
  296.3 46.8 %all-to-all-start.4 = ((bf16[32,40,768]{2,1,0:T(8,128)(2,1)}), bf16[32,40,768]{2,1,0:T(8,128)(2,1)}, u32[]{:S(2)}, u32[]{:S(2)}) async-start(bf16[32,40,768]{2,1,0:T(8,128)(2,1)} %get-tuple-element.148), calls=%async_computation.4 | async-start | bytes 3932160 | tf_op jit(solution)/shard_map/all_to_all | solution.py:968
  303.3 10.6 %copy-start.7 = (bf16[2,2,2,48,1536]{4,3,2,1,0:T(8,128)(2,1)S(1)}, bf16[2,2,2,48,1536]{4,3,2,1,0:T(8,128)(2,1)}, u32[]{:S(2)}) copy-start(bf16[2,2,2,48,1536]{4,3,2,1,0:T(8,128)(2,1)} %copy-done.6) | copy-start | bytes 3538948
  305.9 9.3 %copy-start.9 = (bf16[2,2,2,48,1536]{4,3,2,1,0:T(8,128)(2,1)S(1)}, bf16[2,2,2,48,1536]{4,3,2,1,0:T(8,128)(2,1)}, u32[]{:S(2)}) copy-start(bf16[2,2,2,48,1536]{4,3,2,1,0:T(8,128)(2,1)} %copy-done.8) | copy-start | bytes 3538948
  313.9 3.9 copy-start.19
  323.0 63.0 %collective-permute-start.27 = (bf16[2,2,2,48,1152]{4,3,2,1,0:T(8,128)(2,1)}, bf16[2,2,2,48,1152]{4,3,2,1,0:T(8,128)(2,1)}, u32[]{:S(2)}, u32[]{:S(2)}) collective-permute-start(bf16[2,2,2,48,1152]{4,3,2,1,0:T(8,128)(2,1)} %dynamic-slice_bitcast_fusion.5), channel_id=1, source_target_pairs={{0,2},{2,0},{4,6},{6,4},{8,10},{10,8},{12,14},{14,12},{16,18},{18,... | collective-permute-start | bytes 2654216 | tf_op jit(solution)/shard_map/ppermute | solution.py:1172
  324.0 64.2 %collective-permute-start.29 = (bf16[2,2,2,48,1152]{4,3,2,1,0:T(8,128)(2,1)}, bf16[2,2,2,48,1152]{4,3,2,1,0:T(8,128)(2,1)}, u32[]{:S(2)}, u32[]{:S(2)}) collective-permute-start(bf16[2,2,2,48,1152]{4,3,2,1,0:T(8,128)(2,1)} %dynamic-slice_bitcast_fusion.4), channel_id=1, source_target_pairs={{0,4},{2,6},{4,0},{6,2},{8,12},{10,14},{12,8},{14,10},{16,20},{18,... | collective-permute-start | bytes 2654216 | tf_op jit(solution)/shard_map/ppermute | solution.py:1172
  328.0 100.7 %collective-permute-start.14 = (bf16[20,24,768]{2,1,0:T(8,128)(2,1)}, bf16[20,24,768]{2,1,0:T(8,128)(2,1)}, u32[]{:S(2)}, u32[]{:S(2)}) collective-permute-start(bf16[20,24,768]{2,1,0:T(8,128)(2,1)} %get-tuple-element.144), channel_id=1, source_target_pairs={{0,1},{1,0},{2,3},{3,2},{4,5},{5,4},{6,7},{7,6},{8,9},{9,8},{10,11... | collective-permute-start | bytes 2211848 | tf_op jit(solution)/shard_map/ppermute | solution.py:962
  343.1 69.8 %all-to-all-start.6 = ((bf16[4,48,3072]{2,1,0:T(8,128)(2,1)}), bf16[4,48,3072]{2,1,0:T(8,128)(2,1)S(1)}, u32[]{:S(2)}, u32[]{:S(2)}) async-start(bf16[4,48,3072]{2,1,0:T(8,128)(2,1)} %pad_maximum_fusion.1), calls=%async_computation.6 | async-start | bytes 2359296 | tf_op jit(solution)/shard_map/all_to_all | solution.py:1200
  351.5 23.1 %copy-start.30 = (bf16[8,160,768]{2,1,0:T(8,128)(2,1)S(1)}, bf16[8,160,768]{2,1,0:T(8,128)(2,1)}, u32[]{:S(2)}) copy-start(bf16[8,160,768]{2,1,0:T(8,128)(2,1)} %get-tuple-element.145) | copy-start | bytes 5898244
  378.9 17.8 %collective-permute-start.15 = (bf16[768,768]{1,0:T(8,128)(2,1)}, bf16[768,768]{1,0:T(8,128)(2,1)}, u32[]{:S(2)}, u32[]{:S(2)}) collective-permute-start(bf16[768,768]{1,0:T(8,128)(2,1)} %convolution_convert_fusion.3.refs_3_), channel_id=1, source_target_pairs={{0,1},{1,0},{2,3},{3,2},{4,5},{5,4},{6,7},{7,6},{8,9},{9,8},{10,11... | collective-permute-start | bytes 3538952 | tf_op jit(solution)/shard_map/ppermute | solution.py:962
  381.4 4.6 copy-start.5
  381.4 10.9 %collective-permute-start.17 = (bf16[1024,384]{1,0:T(8,128)(2,1)}, bf16[1024,384]{1,0:T(8,128)(2,1)}, u32[]{:S(2)}, u32[]{:S(2)}) collective-permute-start(bf16[1024,384]{1,0:T(8,128)(2,1)} %dynamic-slice_convert_fusion), channel_id=1, source_target_pairs={{0,1},{1,0},{2,3},{3,2},{4,5},{5,4},{6,7},{7,6},{8,9},{9,8},{10,11... | collective-permute-start | bytes 2359304 | tf_op jit(solution)/shard_map/ppermute | solution.py:962
  386.0 39.3 %collective-permute-start.16 = (bf16[20,24,768]{2,1,0:T(8,128)(2,1)}, bf16[20,24,768]{2,1,0:T(8,128)(2,1)}, u32[]{:S(2)}, u32[]{:S(2)}) collective-permute-start(bf16[20,24,768]{2,1,0:T(8,128)(2,1)} %get-tuple-element.152), channel_id=1, source_target_pairs={{0,1},{1,0},{2,3},{3,2},{4,5},{5,4},{6,7},{7,6},{8,9},{9,8},{10,11... | collective-permute-start | bytes 2211848 | tf_op jit(solution)/shard_map/ppermute | solution.py:962
  387.4 3.9 copy-start.13
  388.3 4.9 %copy-start.18 = (f32[1024,768]{1,0:T(8,128)S(1)}, f32[1024,768]{1,0:T(8,128)}, u32[]{:S(2)}) copy-start(f32[1024,768]{1,0:T(8,128)} %get-tuple-element.153) | copy-start | bytes 9437188
  388.3 22.9 %collective-permute-start.28 = (bf16[2,2,48,1152]{3,2,1,0:T(8,128)(2,1)}, bf16[2,2,48,1152]{3,2,1,0:T(8,128)(2,1)}, u32[]{:S(2)}, u32[]{:S(2)}) collective-permute-start(bf16[2,2,48,1152]{3,2,1,0:T(8,128)(2,1)} %dynamic-slice_bitcast_fusion.10), channel_id=1, source_target_pairs={{0,4},{2,6},{4,0},{6,2},{8,12},{10,14},{12,8},{14,10},{16,20},{18,... | collective-permute-start | bytes 1327112 | tf_op jit(solution)/shard_map/ppermute | solution.py:1172
  392.4 23.0 %collective-permute-start.30 = (bf16[2,2,48,1152]{3,2,1,0:T(8,128)(2,1)}, bf16[2,2,48,1152]{3,2,1,0:T(8,128)(2,1)}, u32[]{:S(2)}, u32[]{:S(2)}) collective-permute-start(bf16[2,2,48,1152]{3,2,1,0:T(8,128)(2,1)} %dynamic-slice_bitcast_fusion.9), channel_id=1, source_target_pairs={{0,2},{2,0},{4,6},{6,4},{8,10},{10,8},{12,14},{14,12},{16,18},{18,... | collective-permute-start | bytes 1327112 | tf_op jit(solution)/shard_map/ppermute | solution.py:1172
  396.7 12.8 %collective-permute-start.20 = (bf16[2,2,2,48,512]{4,3,2,1,0:T(8,128)(2,1)S(1)}, bf16[2,2,2,48,512]{4,3,2,1,0:T(8,128)(2,1)S(1)}, u32[]{:S(2)}, u32[]{:S(2)}) collective-permute-start(bf16[2,2,2,48,512]{4,3,2,1,0:T(8,128)(2,1)S(1)} %dynamic-slice_bitcast_fusion.11), channel_id=1, source_target_pairs={{0,4},{2,6},{4,0},{6,2},{8,12},{10,14},{12,8},{14,10},{16,20},{18,... | collective-permute-start | bytes 1179656 | tf_op jit(solution)/shard_map/ppermute | solution.py:1172
  397.9 13.1 %copy-start.16 = (bf16[2,2,2,2,48,512]{5,4,3,2,1,0:T(8,128)(2,1)S(1)}, bf16[2,2,2,2,48,512]{5,4,3,2,1,0:T(8,128)(2,1)}, u32[]{:S(2)}) copy-start(bf16[2,2,2,2,48,512]{5,4,3,2,1,0:T(8,128)(2,1)} %copy-done.15) | copy-start | bytes 2359300
  402.4 10.5 %copy-start.1 = (bf16[768,768]{1,0:T(8,128)(2,1)}, bf16[768,768]{1,0:T(8,128)(2,1)S(1)}, u32[]{:S(2)}) copy-start(bf16[768,768]{1,0:T(8,128)(2,1)S(1)} %add_convert_fusion.2.refs_3_.refs_6_) | copy-start | bytes 3538948
  402.4 9.3 %copy-start.14 = (bf16[2,2,2,48,1152]{4,3,2,1,0:T(8,128)(2,1)S(1)}, bf16[2,2,2,48,1152]{4,3,2,1,0:T(8,128)(2,1)}, u32[]{:S(2)}) copy-start(bf16[2,2,2,48,1152]{4,3,2,1,0:T(8,128)(2,1)} %copy-done.13) | copy-start | bytes 2654212
  409.5 29.0 %collective-permute-start.18 = (bf16[2,2,2,48,768]{4,3,2,1,0:T(8,128)(2,1)}, bf16[2,2,2,48,768]{4,3,2,1,0:T(8,128)(2,1)}, u32[]{:S(2)}, u32[]{:S(2)}) collective-permute-start(bf16[2,2,2,48,768]{4,3,2,1,0:T(8,128)(2,1)} %dynamic-slice_bitcast_fusion.6), channel_id=1, source_target_pairs={{0,2},{2,0},{4,6},{6,4},{8,10},{10,8},{12,14},{14,12},{16,18},{18,... | collective-permute-start | bytes 1769480 | tf_op jit(solution)/shard_map/ppermute | solution.py:1172
  411.1 22.0 %collective-permute-start.21 = (bf16[2,2,48,512]{3,2,1,0:T(8,128)(2,1)S(1)}, bf16[2,2,48,512]{3,2,1,0:T(8,128)(2,1)}, u32[]{:S(2)}, u32[]{:S(2)}) collective-permute-start(bf16[2,2,48,512]{3,2,1,0:T(8,128)(2,1)S(1)} %dynamic-slice_bitcast_fusion.13), channel_id=1, source_target_pairs={{0,2},{2,0},{4,6},{6,4},{8,10},{10,8},{12,14},{14,12},{16,18},{18,... | collective-permute-start | bytes 589832 | tf_op jit(solution)/shard_map/ppermute | solution.py:1172
  415.5 1.4 collective-permute-start.22
  417.7 14.5 %collective-permute-start.23 = (f32[32,384]{1,0:T(8,128)S(1)}, f32[32,384]{1,0:T(8,128)S(1)}, u32[]{:S(2)}, u32[]{:S(2)}) collective-permute-start(f32[32,384]{1,0:T(8,128)S(1)} %add.245), channel_id=1, source_target_pairs={{0,2},{2,0},{4,6},{6,4},{8,10},{10,8},{12,14},{14,12},{16,18},{18,... | collective-permute-start | bytes 147464 | tf_op jit(solution)/shard_map/ppermute | solution.py:1172
  420.2 34.1 %all-to-all-start.7 = ((bf16[4,48,2304]{2,1,0:T(8,128)(2,1)}), bf16[4,48,2304]{2,1,0:T(8,128)(2,1)S(1)}, u32[]{:S(2)}, u32[]{:S(2)}) async-start(bf16[4,48,2304]{2,1,0:T(8,128)(2,1)} %pad_maximum_fusion.2), calls=%async_computation.7 | async-start | bytes 1769472 | tf_op jit(solution)/shard_map/all_to_all | solution.py:1200
  428.7 9.8 %copy-start.2 = (bf16[768,768]{1,0:T(8,128)(2,1)S(1)}, bf16[768,768]{1,0:T(8,128)(2,1)}, u32[]{:S(2)}) copy-start(bf16[768,768]{1,0:T(8,128)(2,1)} %copy-done.1) | copy-start | bytes 3538948
  432.3 4.2 collective-permute-start.24
  436.4 4.4 collective-permute-start.25
  440.8 8.8 %collective-permute-start.26 = (f32[32,384]{1,0:T(8,128)S(1)}, f32[32,384]{1,0:T(8,128)S(1)}, u32[]{:S(2)}, u32[]{:S(2)}) collective-permute-start(f32[32,384]{1,0:T(8,128)S(1)} %add.248), channel_id=1, source_target_pairs={{0,16},{2,18},{4,20},{6,22},{8,24},{10,26},{12,28},{14,30},{16,0},... | collective-permute-start | bytes 147464 | tf_op jit(solution)/shard_map/ppermute | solution.py:1172
  445.5 7.8 %collective-permute-start.19 = (bf16[2,2,48,768]{3,2,1,0:T(8,128)(2,1)S(1)}, bf16[2,2,48,768]{3,2,1,0:T(8,128)(2,1)S(1)}, u32[]{:S(2)}, u32[]{:S(2)}) collective-permute-start(bf16[2,2,48,768]{3,2,1,0:T(8,128)(2,1)S(1)} %dynamic-slice_bitcast_fusion.12), channel_id=1, source_target_pairs={{0,4},{2,6},{4,0},{6,2},{8,12},{10,14},{12,8},{14,10},{16,20},{18,... | collective-permute-start | bytes 884744 | tf_op jit(solution)/shard_map/ppermute | solution.py:1172
  454.3 16.7 %all-to-all-start.5 = ((bf16[4,48,1280]{2,1,0:T(8,128)(2,1)}), bf16[4,48,1280]{2,1,0:T(8,128)(2,1)S(1)}, u32[]{:S(2)}, u32[]{:S(2)}) async-start(bf16[4,48,1280]{2,1,0:T(8,128)(2,1)} %pad_maximum_fusion.3), calls=%async_computation.5 | async-start | bytes 983040 | tf_op jit(solution)/shard_map/all_to_all | solution.py:1200
  (22 other events, 45.0 us)

commit v6 on v5

--- a/solution.py
+++ b/solution.py
@@ -51,16 +51,18 @@
 ANY = pl.BlockSpec(memory_space=pl.ANY)
 
 
-def run(body, steps, scalars, ins, outs, scratch, flops, after=()):
-    ns, ni, no = len(scalars), len(ins), len(outs)
+def run(body, steps, scalars, ins, outs, scratch, flops, after=(), through=()):
+    ns, ni, no, nt = len(scalars), len(ins), len(outs), len(through)
 
     def kernel(*refs):
-        rest = refs[ns + ni + len(after) :]
-        body(refs[:ns], refs[ns : ns + ni], rest[:no], rest[no:])
+        rest = refs[ns + ni + len(after) + nt :]
+        body(refs[:ns], refs[ns : ns + ni], rest[:no], rest[no + nt :])
 
     moved = sum(math.prod(a.shape) * a.dtype.itemsize for a, _ in ins)
-    ins = list(ins) + [(array, ANY) for array in after]
+    first = ns + ni + len(after)
+    ins = list(ins) + [(array, ANY) for array in list(after) + list(through)]
     moved += sum(math.prod(shape) * jnp.dtype(dtype).itemsize for shape, dtype, _ in outs)
+    outs = list(outs) + [(array.shape, array.dtype, ANY) for array in through]
     return pl.pallas_call(
         kernel,
         grid_spec=pltpu.PrefetchScalarGridSpec(
@@ -71,6 +73,7 @@
             scratch_shapes=scratch,
         ),
         out_shape=[jax.ShapeDtypeStruct(shape, dtype) for shape, dtype, _ in outs],
+        input_output_aliases={first + at: no + at for at in range(nt)},
         compiler_params=pltpu.CompilerParams(
             dimension_semantics=("arbitrary",), vmem_limit_bytes=VMEM_LIMIT
         ),
@@ -1262,36 +1265,9 @@
     text_out, grad_self, dq_own, dq_mate, qkv_own, qkv_mate, self_sums = result
     text_in = exchange(text_out)
 
-    self_away = jnp.concatenate(
-        [
-            low_tn(x, qkv_mate),
-            low_tn(grad_self, att_mate),
-            low_tn(grad_cross, a_mate),
-            low_tn(self_low, dq_mate),
-        ],
-        axis=1,
-    )
-    self_got = mate(self_away)
-    feed_stage = tie(self_away, *feed_stage)[1:]
-    feed_stage = second_swaps(*feed_stage)
-    self_own = jnp.concatenate(
-        [
-            dot_tn(x, qkv_own),
-            dot_tn(grad_self, att_own),
-            dot_tn(grad_cross, a_own),
-            dot_tn(self_low, dq_own),
-        ],
-        axis=1,
-    )
-    self_part = (self_own + self_got.astype(F32)).astype(BF16)
-    half_width = self_part.shape[1] // 2
-    self_stage = first_swaps(self_part[:, :half_width], self_part[:, half_width:])
-    feed_parts = last_parts(*feed_stage)
-    piece, piece_mate, self_part, feed_parts = tie(piece, piece_mate, self_part, feed_parts)
-
     flat_images = own_images * patch_pad
     patch_grad_shape = (patch_count, own_images, vision)
-    kv_own, kv_mate, patch_grad, proj_weight_sum, image_sums = run(
+    result = run(
         partial(image_kernel, images, patch_count, local),
         1,
         [core_scalar],
@@ -1321,10 +1297,40 @@
             pltpu.SemaphoreType.DMA((4,)),
         ],
         2 * flat_images * width * (2 * width + 2 * vision),
-        [text_in],
-    )
+        (),
+        [qkv_mate, qkv_own, grad_self, dq_mate, dq_own],
+    )
+    kv_own, kv_mate, patch_grad, proj_weight_sum, image_sums = result[:5]
+    qkv_mate, qkv_own, grad_self, dq_mate, dq_own = result[5:]
+
+    self_away = jnp.concatenate(
+        [
+            low_tn(x, qkv_mate),
+            low_tn(grad_self, att_mate),
+            low_tn(grad_cross, a_mate),
+            low_tn(self_low, dq_mate),
+        ],
+        axis=1,
+    )
+    self_got = mate(self_away)
+    feed_stage = tie(self_away, *feed_stage)[1:]
+    feed_stage = second_swaps(*feed_stage)
+    self_own = jnp.concatenate(
+        [
+            dot_tn(x, qkv_own),
+            dot_tn(grad_self, att_own),
+            dot_tn(grad_cross, a_own),
+            dot_tn(self_low, dq_own),
+        ],
+        axis=1,
+    )
+    self_part = (self_own + self_got.astype(F32)).astype(BF16)
+    half_width = self_part.shape[1] // 2
+    self_stage = first_swaps(self_part[:, :half_width], self_part[:, half_width:])
+    feed_parts = last_parts(*feed_stage)
 
     up_grad, down_grad = last_sum(feed_parts, hidden)
+    self_got_x, self_got_y = self_stage[1], self_stage[3]
     self_stage = second_swaps(*self_stage)
     kv_low = proj.reshape(flat_images, width)
     kv_away = low_tn(kv_low, kv_mate)
@@ -1351,7 +1357,7 @@
         [(packed_shape, F32, whole_spec(packed_shape))] * 2,
         [],
         0,
-        [up_grad, kv_part, proj_part],
+        [kv_part, proj_part, self_got_x, self_got_y],
     )
     small = small + mate(small_out)
     for bit in range(bits):
@@ -1397,7 +1403,7 @@
 
     return (
         tokens_out(merged_in, [self_part], [kv_part]),
-        tokens_out(text_in, [kv_away], [kv_part, proj_part]),
+        tokens_out(text_in, [kv_away, self_part], [kv_part, proj_part]),
         jnp.transpose(patch_grad, (1, 0, 2)),
         proj_grad,
         proj_bias_grad,

time: 474 us -> 472 us (level); the launches traced: 472 us -> 464 us
  Pallas kernels: 217 us -> 207 us
  waiting for transfers between devices: 68.5 us -> 62.2 us
    all_to_all x5, waiting for transfers between devices: 34.8 us -> 19.1 us  [exchange(): return lax.all_to_all(value, 'dp', split_axis=0, concat_axis=0, tiled=True)]
    pallas_call x13, Pallas kernels: 217 us -> 207 us  [run(): pl.pallas_call(kernel, grid_spec=pltpu.PrefetchScalarGridSpec(num_scalar_...]
    all_to_all x3, waiting for transfers between devices: 12.4 us -> 19.5 us  [last_sum(): lax.all_to_all(both, 'dp', split_axis=0, concat_axis=0, axis_index_groups...]
    ppermute x16, starting transfers between devices: 19.7 us -> 26 us  [partner_bits(): return lax.ppermute(value, 'dp', [(d, d ^ mask) for d in range(devices)])]
    unnamed x99 -> x101, local copies, waits for them, and re-layouts: 8.38 us -> 10.5 us
  transfers between devices with their start and end apart: 39 -> 39, of which waited for: 11 -> 12; matrix products, arithmetic and copies ran while one was open for 18% -> 19% of each run, Pallas kernels for 33% -> 33%
where the time goes in v6:
time: 472 us; the launch traced here: 464 us
  Pallas kernels  207 us (44%)
  starting transfers between devices  83.5 us (18%)
  waiting for transfers between devices  62.2 us (13%)
  matrix products  44.4 us (9%)
  local copies, waits for them, and re-layouts  34.6 us (7%)
  other arithmetic  31 us (7%)
    pallas_call x13, Pallas kernels, run(): pl.pallas_call(kernel, grid_spec=pltpu.PrefetchScalarGridSpec(num_scalar_...  207 us
    dot_general x14, matrix products, dot_tn(): lax.dot_general(left, right, (((0,), (0,)), ((), ())), preferred_element_...  44.4 us
    all_to_all x5, starting transfers between devices, exchange(): return lax.all_to_all(value, 'dp', split_axis=0, concat_axis=0, tiled=True)  38.9 us
    ppermute x16, starting transfers between devices, partner_bits(): return lax.ppermute(value, 'dp', [(d, d ^ mask) for d in range(devices)])  26 us
    ppermute x16, waiting for transfers between devices, partner_bits(): return lax.ppermute(value, 'dp', [(d, d ^ mask) for d in range(devices)])  23.6 us
    all_to_all x3, waiting for transfers between devices, last_sum(): lax.all_to_all(both, 'dp', split_axis=0, concat_axis=0, axis_index_groups...  19.5 us
    all_to_all x5, waiting for transfers between devices, exchange(): return lax.all_to_all(value, 'dp', split_axis=0, concat_axis=0, tiled=True)  19.1 us
    all_to_all x3, starting transfers between devices, last_sum(): lax.all_to_all(both, 'dp', split_axis=0, concat_axis=0, axis_index_groups...  15.4 us
  transfers between devices with their start and end apart: 39, of which 12 were waited for; matrix products, arithmetic and copies ran while one was open for 19% of the time, Pallas kernels for 33%

profile of v6, /device:TPU:0, one launch (start us, length us, event | category | flops | bytes accessed | tf_op | source)
XLA Modules:
  0.0 464.1 jit_solution(12915886327200031825)
XLA Ops:
  4.6 7.9 %all-to-all-start = ((s32[16,2,6]{2,1,0:T(2,128)}), s32[16,2,6]{2,1,0:T(2,128)S(1)}, u32[]{:S(2)}, u32[]{:S(2)}) async-start(s32[16,2,6]{2,1,0:T(2,128)} %bitcast.171), calls=%async_computation | async-start | bytes 32768 | tf_op jit(solution)/shard_map/all_to_all | solution.py:971
  13.8 5.5 %shard_map.281 = (bf16[32,40,768]{2,1,0:T(8,128)(2,1)}, bf16[32,40,768]{2,1,0:T(8,128)(2,1)}) custom-call(s32[32]{0:T(128)} %select_reduce_fusion.1.refs_0_, bf16[48,40,768]{2,1,0:T(8,128)(2,1)} %refs_1_.1, bf16[48,40,768]{2,1,0:T(8,128)(2,1)} %refs_2_.2), custom_call_target="tpu_custom_call" | custom-call | bytes 9830400 | tf_op jit(solution)/shard_map/pallas_call | solution.py:66
  19.8 6.4 %all-to-all-start.2 = ((bf16[32,40,768]{2,1,0:T(8,128)(2,1)}), bf16[32,40,768]{2,1,0:T(8,128)(2,1)}, u32[]{:S(2)}, u32[]{:S(2)}) async-start(bf16[32,40,768]{2,1,0:T(8,128)(2,1)} %get-tuple-element.98), calls=%async_computation.2 | async-start | bytes 3932160 | tf_op jit(solution)/shard_map/all_to_all | solution.py:971
  34.0 1.5 slice_reduce_fusion
  38.1 1.7 copy-done.13
  39.9 22.2 %shard_map.282 = (bf16[8,160,768]{2,1,0:T(8,128)(2,1)}, bf16[16,160,768]{2,1,0:T(8,128)(2,1)}, bf16[16,160,768]{2,1,0:T(8,128)(2,1)}) custom-call(s32[1]{0:T(128)} %bitcast.refs_0_, bf16[145,16,1024]{2,1,0:T(8,128)(2,1)} %bitcast.158, bf16[1024,768]{1,0:T(8,128)(2,1)} %refs_4_.5, f32[1,768]{1,0:T(1,128)} %reshape.219.refs_3_, ...), custom_call_target="tpu_custom_call" | custom-call | flops 10066329600 | bytes 23247872 | tf_op jit(solution)/shard_map/pallas_call | solution.py:66
  62.1 5.1 %all-to-all-done.2.refs_2_ = bf16[32,40,768]{2,1,0:T(8,128)(2,1)} async-done(((bf16[32,40,768]{2,1,0:T(8,128)(2,1)}), bf16[32,40,768]{2,1,0:T(8,128)(2,1)}, u32[]{:S(2)}, u32[]{:S(2)}) %all-to-all-start.2) | async-done | bytes 1966112 | tf_op jit(solution)/shard_map/all_to_all | solution.py:971
  67.2 9.7 %all-to-all-start.1 = ((bf16[32,40,768]{2,1,0:T(8,128)(2,1)}), bf16[32,40,768]{2,1,0:T(8,128)(2,1)S(1)}, u32[]{:S(2)}, u32[]{:S(2)}) async-start(bf16[32,40,768]{2,1,0:T(8,128)(2,1)} %get-tuple-element.94), calls=%async_computation.1 | async-start | bytes 3932160 | tf_op jit(solution)/shard_map/all_to_all | solution.py:971
  78.1 22.1 %shard_map.283 = (bf16[960,768]{1,0:T(8,128)(2,1)}, f32[960,768]{1,0:T(8,128)}, bf16[960,768]{1,0:T(8,128)(2,1)}, bf16[960,768]{1,0:T(8,128)(2,1)}, bf16[960,768...) custom-call(s32[24]{0:T(128)} %get-tuple-element.97.refs_0_, ...), custom_call_target="tpu_custom_call" | custom-call | flops 6417285120 | bytes 24718080 | tf_op jit(solution)/shard_map/pallas_call | solution.py:66
  100.2 12.5 %shard_map.284.refs_2_ = bf16[960,768]{1,0:T(8,128)(2,1)} custom-call(s32[24]{0:T(128)} %and_select_fusion.refs_0_, s32[96]{0:T(128)} %reshape.218.refs_1_, bf16[960,768]{1,0:T(8,128)(2,1)} %get-tuple-element.111.refs_2_, bf16[16,160,768]{2,1,0:T(8,128)(2,1)} %get-tuple-element.101.refs_3_.refs_4_, bf16[16,160,768]{2,1,0:T(8,128)(2,1)} %get-tuple-element.102.refs_4_.refs_5_), custom_call_target="tpu_custom_call" | custom-call | flops 3019898880 | bytes 10813440 | tf_op jit(solution)/shard_map/pallas_call | solution.py:66
  112.7 1.4 copy-done.31
  114.1 2.9 all-to-all-done.1.refs_1_
  118.3 52.4 %shard_map.285 = (bf16[32,40,768]{2,1,0:T(8,128)(2,1)}, bf16[960,768]{1,0:T(8,128)(2,1)}, bf16[960,768]{1,0:T(8,128)(2,1)}, bf16[960,768]{1,0:T(8,128)(2,1)}, f3...) custom-call(s32[24]{0:T(128)} %compare_select_fusion.4.refs_1_.refs_, ...), custom_call_target="tpu_custom_call" | custom-call | flops 20384317440 | bytes 42384384 | tf_op jit(solution)/shard_map/pallas_call | solution.py:66
  170.8 6.5 %convolution_convert_fusion.1 = bf16[768,1536]{1,0:T(8,128)(2,1)} fusion(bf16[960,768]{1,0:T(8,128)(2,1)} %get-tuple-element.109, bf16[960,1536]{1,0:T(8,128)(2,1)} %get-tuple-element.110), kind=kOutput, calls=%fused_computation.7 | convolution fusion | flops 2266103808 | bytes 6782976 | tf_op jit(solution)/shard_map/dot_general | solution.py:38
  177.2 2.9 convolution_convert_fusion.2
  180.8 24.2 %shard_map.286 = (bf16[2,8,160,768]{3,2,1,0:T(8,128)(2,1)}, bf16[2,8,160,768]{3,2,1,0:T(8,128)(2,1)}, bf16[960,768]{1,0:T(8,128)(2,1)}) custom-call(s32[24]{0:T(128)} %and_select_fusion.refs_0_, s32[96]{0:T(128)} %reshape.218.refs_1_, bf16[960,768]{1,0:T(8,128)(2,1)} %get-tuple-element.111.refs_2_, bf16[960,768]{1,0:T(8,128)(2,1)} %get-tuple-element.112.refs_3_, ...), custom_call_target="tpu_custom_call" | custom-call | flops 9059696640 | bytes 20152320 | tf_op jit(solution)/shard_map/pallas_call | solution.py:66
  205.8 3.4 convolution_convert_fusion.5
  209.2 2.1 fusion.30
  211.9 4.4 add_convert_fusion
  216.3 4.2 add_convert_fusion.1
  222.6 1.6 dynamic-slice_bitcast_fusion
  224.1 3.1 collective-permute-start.28
  227.3 28.2 %shard_map.287 = (bf16[32,40,768]{2,1,0:T(8,128)(2,1)}, bf16[960,768]{1,0:T(8,128)(2,1)}, bf16[960,384]{1,0:T(8,128)(2,1)}, bf16[960,384]{1,0:T(8,128)(2,1)}, bf...) custom-call(s32[24]{0:T(128)} %get-tuple-element.97.refs_0_, ...), custom_call_target="tpu_custom_call" | custom-call | flops 7172259840 | bytes 30634752 | tf_op jit(solution)/shard_map/pallas_call | solution.py:66
  255.5 6.9 %all-to-all-start.4 = ((bf16[32,40,768]{2,1,0:T(8,128)(2,1)}), bf16[32,40,768]{2,1,0:T(8,128)(2,1)S(1)}, u32[]{:S(2)}, u32[]{:S(2)}) async-start(bf16[32,40,768]{2,1,0:T(8,128)(2,1)} %get-tuple-element.147), calls=%async_computation.4 | async-start | bytes 3932160 | tf_op jit(solution)/shard_map/all_to_all | solution.py:971
  262.5 23.0 %shard_map.288 = (bf16[1280,768]{1,0:T(8,128)(2,1)}, bf16[1280,768]{1,0:T(8,128)(2,1)}, bf16[145,8,1024]{2,1,0:T(8,128)(2,1)}, f32[1024,768]{1,0:T(8,128)}, f32[...) custom-call(s32[1]{0:T(128)} %bitcast.refs_0_, ...), custom_call_target="tpu_custom_call", output_to_operand_aliasing={{5}: (7, {}), {6}: (8, {}), {7}: (9, {}), {8}: (10, {}), {9... | custom-call | flops 7046430720 | bytes 30744576 | tf_op jit(solution)/shard_map/pallas_call | solution.py:66
  285.5 2.5 convolution_convert_fusion.6
  290.1 2.3 convolution_convert_fusion
  292.3 2.1 pad_maximum_fusion
  294.5 1.7 add_convert_fusion.3
  296.3 2.0 collective-permute-start.29
  298.3 1.6 add_convert_fusion.2
  299.9 1.5 collective-permute-start.30
  301.5 2.8 convolution_convert_fusion.3.refs_3_
  304.3 4.1 fusion.28
  308.4 2.0 fusion.29
  310.4 2.0 fusion.31
  313.1 1.7 collective-permute-done.29
  319.0 1.8 collective-permute-start.16
  320.8 4.2 add_convert_fusion.4.refs_3_.refs_5_
  328.4 8.0 %all-to-all-start.3 = ((bf16[32,40,768]{2,1,0:T(8,128)(2,1)}), bf16[32,40,768]{2,1,0:T(8,128)(2,1)}, u32[]{:S(2)}, u32[]{:S(2)}) async-start(bf16[32,40,768]{2,1,0:T(8,128)(2,1)} %get-tuple-element.104), calls=%async_computation.3 | async-start | bytes 3932160 | tf_op jit(solution)/shard_map/all_to_all | solution.py:971
  336.5 2.5 pad_maximum_fusion.1
  339.0 1.5 reshape.222.refs_4_.refs_6_
  341.8 2.1 collective-permute-start.17
  345.1 1.5 collective-permute-start.15
  346.6 4.0 fusion.refs_3_.refs_4_
  350.9 1.5 copy-done
  354.1 5.6 %collective-permute-done.15 = bf16[2,2,48,768]{3,2,1,0:T(8,128)(2,1)S(1)} collective-permute-done((bf16[2,2,48,768]{3,2,1,0:T(8,128)(2,1)S(1)}, bf16[2,2,48,768]{3,2,1,0:T(8,128)(2,1)S(1)}, u32[]{:S(2)}, u32[]{:S(2)}) %collective-permute-start.15) | collective-permute-done | bytes 294944 | tf_op jit(solution)/shard_map/ppermute | solution.py:1175
  361.8 4.0 shard_map.291
  365.9 10.6 %all-to-all-done.3.refs_2_ = bf16[32,40,768]{2,1,0:T(8,128)(2,1)} async-done(((bf16[32,40,768]{2,1,0:T(8,128)(2,1)}), bf16[32,40,768]{2,1,0:T(8,128)(2,1)}, u32[]{:S(2)}, u32[]{:S(2)}) %all-to-all-start.3) | async-done | bytes 1966112 | tf_op jit(solution)/shard_map/all_to_all | solution.py:971
  376.4 8.4 %all-to-all-start.7 = ((bf16[4,48,3072]{2,1,0:T(8,128)(2,1)}), bf16[4,48,3072]{2,1,0:T(8,128)(2,1)S(1)}, u32[]{:S(2)}, u32[]{:S(2)}) async-start(bf16[4,48,3072]{2,1,0:T(8,128)(2,1)} %pad_maximum_fusion.1), calls=%async_computation.7 | async-start | bytes 2359296 | tf_op jit(solution)/shard_map/all_to_all | solution.py:1203
  384.8 4.1 shard_map.289
  390.0 1.8 collective-permute-start.25
  392.8 1.5 shard_map.293
  397.3 1.5 collective-permute-start.26
  400.5 2.7 collective-permute-done.25
  403.3 8.4 %all-to-all-done.7 = bf16[4,48,3072]{2,1,0:T(8,128)(2,1)S(1)} async-done(((bf16[4,48,3072]{2,1,0:T(8,128)(2,1)}), bf16[4,48,3072]{2,1,0:T(8,128)(2,1)S(1)}, u32[]{:S(2)}, u32[]{:S(2)}) %all-to-all-start.7) | async-done | bytes 1179680 | tf_op jit(solution)/shard_map/all_to_all | solution.py:1203
  411.7 3.5 all-to-all-start.5
  417.4 11.1 %all-to-all-done.5 = bf16[4,48,1280]{2,1,0:T(8,128)(2,1)S(1)} async-done(((bf16[4,48,1280]{2,1,0:T(8,128)(2,1)}), bf16[4,48,1280]{2,1,0:T(8,128)(2,1)S(1)}, u32[]{:S(2)}, u32[]{:S(2)}) %all-to-all-start.5) | async-done | bytes 491552 | tf_op jit(solution)/shard_map/all_to_all | solution.py:1203
  428.4 3.5 all-to-all-start.6
  432.2 2.0 collective-permute-start.23
  435.1 11.8 %collective-permute-done.23 = f32[32,384]{1,0:T(8,128)S(1)} collective-permute-done((f32[32,384]{1,0:T(8,128)S(1)}, f32[32,384]{1,0:T(8,128)S(1)}, u32[]{:S(2)}, u32[]{:S(2)}) %collective-permute-start.23) | collective-permute-done | bytes 49184 | tf_op jit(solution)/shard_map/ppermute | solution.py:1175
  446.9 4.7 %collective-permute-start.24 = (f32[32,384]{1,0:T(8,128)S(1)}, f32[32,384]{1,0:T(8,128)S(1)}, u32[]{:S(2)}, u32[]{:S(2)}) collective-permute-start(f32[32,384]{1,0:T(8,128)S(1)} %add.244), channel_id=1, source_target_pairs={{0,16},{2,18},{4,20},{6,22},{8,24},{10,26},{12,28},{14,30},{16,0},... | collective-permute-start | bytes 147464 | tf_op jit(solution)/shard_map/ppermute | solution.py:1175
  452.3 3.4 shard_map.292
  455.7 3.4 shard_map.290
  (221 shorter events, 55.2 us)
Async XLA Ops:
  0.6 37.5 %collective-permute-start.1 = (bf16[2,3,768,384]{3,2,1,0:T(8,128)(2,1)}, bf16[2,3,768,384]{3,2,1,0:T(8,128)(2,1)S(1)}, u32[]{:S(2)}, u32[]{:S(2)}) collective-permute-start(bf16[2,3,768,384]{3,2,1,0:T(8,128)(2,1)} %refs_5_.3), channel_id=1, source_target_pairs={{0,1},{1,0},{2,3},{3,2},{4,5},{5,4},{6,7},{7,6},{8,9},{9,8},{10,11... | collective-permute-start | bytes 10616840 | tf_op jit(solution)/shard_map/ppermute | solution.py:965
  4.6 15.2 %all-to-all-start = ((s32[16,2,6]{2,1,0:T(2,128)}), s32[16,2,6]{2,1,0:T(2,128)S(1)}, u32[]{:S(2)}, u32[]{:S(2)}) async-start(s32[16,2,6]{2,1,0:T(2,128)} %bitcast.171), calls=%async_computation | async-start | bytes 32768 | tf_op jit(solution)/shard_map/all_to_all | solution.py:971
  19.8 47.3 %all-to-all-start.2 = ((bf16[32,40,768]{2,1,0:T(8,128)(2,1)}), bf16[32,40,768]{2,1,0:T(8,128)(2,1)}, u32[]{:S(2)}, u32[]{:S(2)}) async-start(bf16[32,40,768]{2,1,0:T(8,128)(2,1)} %get-tuple-element.98), calls=%async_computation.2 | async-start | bytes 3932160 | tf_op jit(solution)/shard_map/all_to_all | solution.py:971
  26.3 11.8 %collective-permute-start = (bf16[2,384,768]{2,1,0:T(8,128)(2,1)}, bf16[2,384,768]{2,1,0:T(8,128)(2,1)}, u32[]{:S(2)}, u32[]{:S(2)}) collective-permute-start(bf16[2,384,768]{2,1,0:T(8,128)(2,1)} %refs_11_.5), channel_id=1, source_target_pairs={{0,1},{1,0},{2,3},{3,2},{4,5},{5,4},{6,7},{7,6},{8,9},{9,8},{10,11... | collective-permute-start | bytes 3538952 | tf_op jit(solution)/shard_map/ppermute | solution.py:965
  26.4 11.8 %collective-permute-start.2 = (f32[2,2,384]{2,1,0:T(2,128)}, f32[2,2,384]{2,1,0:T(2,128)}, u32[]{:S(2)}, u32[]{:S(2)}) collective-permute-start(f32[2,2,384]{2,1,0:T(2,128)} %refs_7_.1), channel_id=1, source_target_pairs={{0,1},{1,0},{2,3},{3,2},{4,5},{5,4},{6,7},{7,6},{8,9},{9,8},{10,11... | collective-permute-start | bytes 18440 | tf_op jit(solution)/shard_map/ppermute | solution.py:965
  62.1 15.3 %copy-start.26 = (f32[1536]{0:T(1024)S(1)}, f32[1536]{0:T(1024)}, u32[]{:S(2)}) copy-start(f32[1536]{0:T(1024)} %param.34) | copy-start | bytes 18436
  67.2 49.9 %all-to-all-start.1 = ((bf16[32,40,768]{2,1,0:T(8,128)(2,1)}), bf16[32,40,768]{2,1,0:T(8,128)(2,1)S(1)}, u32[]{:S(2)}, u32[]{:S(2)}) async-start(bf16[32,40,768]{2,1,0:T(8,128)(2,1)} %get-tuple-element.94), calls=%async_computation.1 | async-start | bytes 3932160 | tf_op jit(solution)/shard_map/all_to_all | solution.py:971
  76.8 35.9 %collective-permute-start.3 = (bf16[768,1536]{1,0:T(8,128)(2,1)}, bf16[768,1536]{1,0:T(8,128)(2,1)S(1)}, u32[]{:S(2)}, u32[]{:S(2)}) collective-permute-start(bf16[768,1536]{1,0:T(8,128)(2,1)} %refs_6_.3), channel_id=1, source_target_pairs={{0,1},{1,0},{2,3},{3,2},{4,5},{5,4},{6,7},{7,6},{8,9},{9,8},{10,11... | collective-permute-start | bytes 7077896 | tf_op jit(solution)/shard_map/ppermute | solution.py:965
  76.9 37.2 %collective-permute-start.4 = (bf16[1536,768]{1,0:T(8,128)(2,1)}, bf16[1536,768]{1,0:T(8,128)(2,1)}, u32[]{:S(2)}, u32[]{:S(2)}) collective-permute-start(bf16[1536,768]{1,0:T(8,128)(2,1)} %refs_8_.1), channel_id=1, source_target_pairs={{0,1},{1,0},{2,3},{3,2},{4,5},{5,4},{6,7},{7,6},{8,9},{9,8},{10,11... | collective-permute-start | bytes 7077896 | tf_op jit(solution)/shard_map/ppermute | solution.py:965
  77.4 22.8 %copy-start.27 = (f32[1,1536]{1,0:T(1,128)}, f32[1,1536]{1,0:T(1,128)S(1)}, u32[]{:S(2)}) copy-start(f32[1,1536]{1,0:T(1,128)S(1)} %reshape.220.refs_13_) | copy-start | bytes 18436
  77.4 35.3 %collective-permute-start.5 = (f32[1,1536]{1,0:T(1,128)S(1)}, f32[1,1536]{1,0:T(1,128)S(1)}, u32[]{:S(2)}, u32[]{:S(2)}) collective-permute-start(f32[1,1536]{1,0:T(1,128)S(1)} %reshape.220.refs_13_), channel_id=1, source_target_pairs={{0,1},{1,0},{2,3},{3,2},{4,5},{5,4},{6,7},{7,6},{8,9},{9,8},{10,11... | collective-permute-start | bytes 18440 | tf_op jit(solution)/shard_map/ppermute | solution.py:965
  112.7 4.3 copy-start.33
  170.7 6.5 %copy-start.37 = (bf16[960,1536]{1,0:T(8,128)(2,1)S(1)}, bf16[960,1536]{1,0:T(8,128)(2,1)}, u32[]{:S(2)}) copy-start(bf16[960,1536]{1,0:T(8,128)(2,1)} %get-tuple-element.108) | copy-start | bytes 8847364
  170.8 6.5 %copy-start.40 = (bf16[960,768]{1,0:T(8,128)(2,1)S(1)}, bf16[960,768]{1,0:T(8,128)(2,1)}, u32[]{:S(2)}) copy-start(bf16[960,768]{1,0:T(8,128)(2,1)} %get-tuple-element.107) | copy-start | bytes 4423684
  180.2 24.9 %copy-start.28 = (s32[48,1]{0,1:T(1,128)S(1)}, s32[48,1]{0,1:T(1,128)}, u32[]{:S(2)}) copy-start(s32[48,1]{0,1:T(1,128)} %get-tuple-element.166) | copy-start | bytes 580
  180.2 25.6 %copy-start.44 = (bf16[960,384]{1,0:T(8,128)(2,1)S(1)}, bf16[960,384]{1,0:T(8,128)(2,1)}, u32[]{:S(2)}) copy-start(bf16[960,384]{1,0:T(8,128)(2,1)} %get-tuple-element.140) | copy-start | bytes 2211844
  180.2 31.0 %collective-permute-start.8 = (bf16[768,1536]{1,0:T(8,128)(2,1)}, bf16[768,1536]{1,0:T(8,128)(2,1)}, u32[]{:S(2)}, u32[]{:S(2)}) collective-permute-start(bf16[768,1536]{1,0:T(8,128)(2,1)} %convolution_convert_fusion.1), channel_id=1, source_target_pairs={{0,1},{1,0},{2,3},{3,2},{4,5},{5,4},{6,7},{7,6},{8,9},{9,8},{10,11... | collective-permute-start | bytes 7077896 | tf_op jit(solution)/shard_map/ppermute | solution.py:965
  180.3 36.0 %collective-permute-start.7 = (bf16[768,1536]{1,0:T(8,128)(2,1)S(1)}, bf16[768,1536]{1,0:T(8,128)(2,1)}, u32[]{:S(2)}, u32[]{:S(2)}) collective-permute-start(bf16[768,1536]{1,0:T(8,128)(2,1)S(1)} %convolution_convert_fusion.2), channel_id=1, source_target_pairs={{0,1},{1,0},{2,3},{3,2},{4,5},{5,4},{6,7},{7,6},{8,9},{9,8},{10,11... | collective-permute-start | bytes 7077896 | tf_op jit(solution)/shard_map/ppermute | solution.py:965
  205.0 57.4 %collective-permute-start.6 = (bf16[2,8,160,768]{3,2,1,0:T(8,128)(2,1)}, bf16[2,8,160,768]{3,2,1,0:T(8,128)(2,1)}, u32[]{:S(2)}, u32[]{:S(2)}) collective-permute-start(bf16[2,8,160,768]{3,2,1,0:T(8,128)(2,1)} %get-tuple-element.114), channel_id=1, source_target_pairs={{0,1},{1,0},{2,3},{3,2},{4,5},{5,4},{6,7},{7,6},{8,9},{9,8},{10,11... | collective-permute-start | bytes 11796488 | tf_op jit(solution)/shard_map/ppermute | solution.py:965
  205.8 3.4 copy-start.36
  205.8 3.4 copy-start.39
  211.9 4.4 copy-start.41
  211.9 4.4 copy-start.46
  221.7 72.8 %collective-permute-start.27 = (bf16[2,2,2,48,1536]{4,3,2,1,0:T(8,128)(2,1)}, bf16[2,2,2,48,1536]{4,3,2,1,0:T(8,128)(2,1)}, u32[]{:S(2)}, u32[]{:S(2)}) collective-permute-start(bf16[2,2,2,48,1536]{4,3,2,1,0:T(8,128)(2,1)} %get-tuple-element.172), channel_id=1, source_target_pairs={{0,2},{2,0},{4,6},{6,4},{8,10},{10,8},{12,14},{14,12},{16,18},{18,... | collective-permute-start | bytes 3538952 | tf_op jit(solution)/shard_map/ppermute | solution.py:1175
  224.1 70.4 %collective-permute-start.28 = (bf16[2,2,2,48,1536]{4,3,2,1,0:T(8,128)(2,1)}, bf16[2,2,2,48,1536]{4,3,2,1,0:T(8,128)(2,1)}, u32[]{:S(2)}, u32[]{:S(2)}) collective-permute-start(bf16[2,2,2,48,1536]{4,3,2,1,0:T(8,128)(2,1)} %get-tuple-element.170), channel_id=1, source_target_pairs={{0,4},{2,6},{4,0},{6,2},{8,12},{10,14},{12,8},{14,10},{16,20},{18,... | collective-permute-start | bytes 3538952 | tf_op jit(solution)/shard_map/ppermute | solution.py:1175
  255.5 71.6 %all-to-all-start.4 = ((bf16[32,40,768]{2,1,0:T(8,128)(2,1)}), bf16[32,40,768]{2,1,0:T(8,128)(2,1)S(1)}, u32[]{:S(2)}, u32[]{:S(2)}) async-start(bf16[32,40,768]{2,1,0:T(8,128)(2,1)} %get-tuple-element.147), calls=%async_computation.4 | async-start | bytes 3932160 | tf_op jit(solution)/shard_map/all_to_all | solution.py:971
  262.4 23.0 %copy-start.43 = (bf16[960,384]{1,0:T(8,128)(2,1)S(1)}, bf16[960,384]{1,0:T(8,128)(2,1)}, u32[]{:S(2)}) copy-start(bf16[960,384]{1,0:T(8,128)(2,1)} %get-tuple-element.139) | copy-start | bytes 2211844
  294.4 52.2 %collective-permute-start.9 = (bf16[768,2304]{1,0:T(8,128)(2,1)}, bf16[768,2304]{1,0:T(8,128)(2,1)}, u32[]{:S(2)}, u32[]{:S(2)}) collective-permute-start(bf16[768,2304]{1,0:T(8,128)(2,1)} %pad_maximum_fusion), channel_id=1, source_target_pairs={{0,1},{1,0},{2,3},{3,2},{4,5},{5,4},{6,7},{7,6},{8,9},{9,8},{10,11... | collective-permute-start | bytes 10616840 | tf_op jit(solution)/shard_map/ppermute | solution.py:965
  294.5 3.7 copy-start.9
  296.3 5.2 %copy-start.32 = (bf16[1280,768]{1,0:T(8,128)(2,1)S(1)}, bf16[1280,768]{1,0:T(8,128)(2,1)}, u32[]{:S(2)}) copy-start(bf16[1280,768]{1,0:T(8,128)(2,1)} %get-tuple-element.146) | copy-start | bytes 5898244
  296.3 5.2 %copy-start.34 = (bf16[8,160,768]{2,1,0:T(8,128)(2,1)S(1)}, bf16[8,160,768]{2,1,0:T(8,128)(2,1)}, u32[]{:S(2)}) copy-start(bf16[8,160,768]{2,1,0:T(8,128)(2,1)} %get-tuple-element.144) | copy-start | bytes 5898244
  296.3 18.6 %collective-permute-start.29 = (bf16[2,2,48,1536]{3,2,1,0:T(8,128)(2,1)S(1)}, bf16[2,2,48,1536]{3,2,1,0:T(8,128)(2,1)S(1)}, u32[]{:S(2)}, u32[]{:S(2)}) collective-permute-start(bf16[2,2,48,1536]{3,2,1,0:T(8,128)(2,1)S(1)} %dynamic-slice_bitcast_fusion.7), channel_id=1, source_target_pairs={{0,4},{2,6},{4,0},{6,2},{8,12},{10,14},{12,8},{14,10},{16,20},{18,... | collective-permute-start | bytes 1769480 | tf_op jit(solution)/shard_map/ppermute | solution.py:1175
  299.9 16.4 %collective-permute-start.30 = (bf16[2,2,48,1536]{3,2,1,0:T(8,128)(2,1)S(1)}, bf16[2,2,48,1536]{3,2,1,0:T(8,128)(2,1)S(1)}, u32[]{:S(2)}, u32[]{:S(2)}) collective-permute-start(bf16[2,2,48,1536]{3,2,1,0:T(8,128)(2,1)S(1)} %dynamic-slice_bitcast_fusion.6), channel_id=1, source_target_pairs={{0,2},{2,0},{4,6},{6,4},{8,10},{10,8},{12,14},{14,12},{16,18},{18,... | collective-permute-start | bytes 1769480 | tf_op jit(solution)/shard_map/ppermute | solution.py:1175
  304.3 4.1 copy-start.20
  304.3 4.1 copy-start.38
  310.4 10.3 %collective-permute-start.11 = (bf16[768,768]{1,0:T(8,128)(2,1)}, bf16[768,768]{1,0:T(8,128)(2,1)}, u32[]{:S(2)}, u32[]{:S(2)}) collective-permute-start(bf16[768,768]{1,0:T(8,128)(2,1)} %convolution_convert_fusion.3.refs_3_), channel_id=1, source_target_pairs={{0,1},{1,0},{2,3},{3,2},{4,5},{5,4},{6,7},{7,6},{8,9},{9,8},{10,11... | collective-permute-start | bytes 3538952 | tf_op jit(solution)/shard_map/ppermute | solution.py:965
  312.6 4.8 %collective-permute-start.13 = (bf16[1024,384]{1,0:T(8,128)(2,1)S(1)}, bf16[1024,384]{1,0:T(8,128)(2,1)S(1)}, u32[]{:S(2)}, u32[]{:S(2)}) collective-permute-start(bf16[1024,384]{1,0:T(8,128)(2,1)S(1)} %dynamic-slice_convert_fusion), channel_id=1, source_target_pairs={{0,1},{1,0},{2,3},{3,2},{4,5},{5,4},{6,7},{7,6},{8,9},{9,8},{10,11... | collective-permute-start | bytes 2359304 | tf_op jit(solution)/shard_map/ppermute | solution.py:965
  317.5 3.3 copy-start.7
  319.0 21.5 %collective-permute-start.16 = (bf16[2,2,2,48,512]{4,3,2,1,0:T(8,128)(2,1)}, bf16[2,2,2,48,512]{4,3,2,1,0:T(8,128)(2,1)}, u32[]{:S(2)}, u32[]{:S(2)}) collective-permute-start(bf16[2,2,2,48,512]{4,3,2,1,0:T(8,128)(2,1)} %dynamic-slice_bitcast_fusion.11), channel_id=1, source_target_pairs={{0,4},{2,6},{4,0},{6,2},{8,12},{10,14},{12,8},{14,10},{16,20},{18,... | collective-permute-start | bytes 1179656 | tf_op jit(solution)/shard_map/ppermute | solution.py:1175
  325.0 18.9 %copy-start.1 = (bf16[768,768]{1,0:T(8,128)(2,1)}, bf16[768,768]{1,0:T(8,128)(2,1)S(1)}, u32[]{:S(2)}) copy-start(bf16[768,768]{1,0:T(8,128)(2,1)S(1)} %add_convert_fusion.4.refs_3_.refs_5_) | copy-start | bytes 3538948
  325.9 17.9 %collective-permute-start.14 = (bf16[2,2,2,48,768]{4,3,2,1,0:T(8,128)(2,1)}, bf16[2,2,2,48,768]{4,3,2,1,0:T(8,128)(2,1)}, u32[]{:S(2)}, u32[]{:S(2)}) collective-permute-start(bf16[2,2,2,48,768]{4,3,2,1,0:T(8,128)(2,1)} %dynamic-slice_bitcast_fusion.8), channel_id=1, source_target_pairs={{0,2},{2,0},{4,6},{6,4},{8,10},{10,8},{12,14},{14,12},{16,18},{18,... | collective-permute-start | bytes 1769480 | tf_op jit(solution)/shard_map/ppermute | solution.py:1175
  328.4 48.0 %all-to-all-start.3 = ((bf16[32,40,768]{2,1,0:T(8,128)(2,1)}), bf16[32,40,768]{2,1,0:T(8,128)(2,1)}, u32[]{:S(2)}, u32[]{:S(2)}) async-start(bf16[32,40,768]{2,1,0:T(8,128)(2,1)} %get-tuple-element.104), calls=%async_computation.3 | async-start | bytes 3932160 | tf_op jit(solution)/shard_map/all_to_all | solution.py:971
  336.5 4.0 copy-start.15
  340.5 6.2 %copy-start.10 = (f32[768,1152]{1,0:T(8,128)S(1)}, f32[768,1152]{1,0:T(8,128)}, u32[]{:S(2)}) copy-start(f32[768,1152]{1,0:T(8,128)} %fusion.28) | copy-start | bytes 10616836
  341.8 12.3 %collective-permute-start.17 = (bf16[2,2,48,512]{3,2,1,0:T(8,128)(2,1)S(1)}, bf16[2,2,48,512]{3,2,1,0:T(8,128)(2,1)S(1)}, u32[]{:S(2)}, u32[]{:S(2)}) collective-permute-start(bf16[2,2,48,512]{3,2,1,0:T(8,128)(2,1)S(1)} %dynamic-slice_bitcast_fusion.13), channel_id=1, source_target_pairs={{0,2},{2,0},{4,6},{6,4},{8,10},{10,8},{12,14},{14,12},{16,18},{18,... | collective-permute-start | bytes 589832 | tf_op jit(solution)/shard_map/ppermute | solution.py:1175
  345.1 14.6 %collective-permute-start.15 = (bf16[2,2,48,768]{3,2,1,0:T(8,128)(2,1)S(1)}, bf16[2,2,48,768]{3,2,1,0:T(8,128)(2,1)S(1)}, u32[]{:S(2)}, u32[]{:S(2)}) collective-permute-start(bf16[2,2,48,768]{3,2,1,0:T(8,128)(2,1)S(1)} %dynamic-slice_bitcast_fusion.12), channel_id=1, source_target_pairs={{0,4},{2,6},{4,0},{6,2},{8,12},{10,14},{12,8},{14,10},{16,20},{18,... | collective-permute-start | bytes 884744 | tf_op jit(solution)/shard_map/ppermute | solution.py:1175
  352.4 8.4 %copy-start.3 = (bf16[768,1152]{1,0:T(8,128)(2,1)}, bf16[768,1152]{1,0:T(8,128)(2,1)S(1)}, u32[]{:S(2)}) copy-start(bf16[768,1152]{1,0:T(8,128)(2,1)S(1)} %get-tuple-element.168) | copy-start | bytes 5308420
  352.4 8.4 %copy-start.5 = (bf16[768,1152]{1,0:T(8,128)(2,1)}, bf16[768,1152]{1,0:T(8,128)(2,1)S(1)}, u32[]{:S(2)}) copy-start(bf16[768,1152]{1,0:T(8,128)(2,1)S(1)} %get-tuple-element.169) | copy-start | bytes 5308420
  353.5 35.4 %collective-permute-start.18 = (bf16[2,2,2,48,1152]{4,3,2,1,0:T(8,128)(2,1)}, bf16[2,2,2,48,1152]{4,3,2,1,0:T(8,128)(2,1)S(1)}, u32[]{:S(2)}, u32[]{:S(2)}) collective-permute-start(bf16[2,2,2,48,1152]{4,3,2,1,0:T(8,128)(2,1)} %dynamic-slice_bitcast_fusion.5), channel_id=1, source_target_pairs={{0,2},{2,0},{4,6},{6,4},{8,10},{10,8},{12,14},{14,12},{16,18},{18,... | collective-permute-start | bytes 2654216 | tf_op jit(solution)/shard_map/ppermute | solution.py:1175
  360.8 31.1 %collective-permute-start.19 = (bf16[2,2,2,48,1152]{4,3,2,1,0:T(8,128)(2,1)}, bf16[2,2,2,48,1152]{4,3,2,1,0:T(8,128)(2,1)S(1)}, u32[]{:S(2)}, u32[]{:S(2)}) collective-permute-start(bf16[2,2,2,48,1152]{4,3,2,1,0:T(8,128)(2,1)} %dynamic-slice_bitcast_fusion.4), channel_id=1, source_target_pairs={{0,4},{2,6},{4,0},{6,2},{8,12},{10,14},{12,8},{14,10},{16,20},{18,... | collective-permute-start | bytes 2654216 | tf_op jit(solution)/shard_map/ppermute | solution.py:1175
  365.8 86.5 %collective-permute-start.12 = (bf16[20,24,768]{2,1,0:T(8,128)(2,1)}, bf16[20,24,768]{2,1,0:T(8,128)(2,1)}, u32[]{:S(2)}, u32[]{:S(2)}) collective-permute-start(bf16[20,24,768]{2,1,0:T(8,128)(2,1)} %get-tuple-element.149), channel_id=1, source_target_pairs={{0,1},{1,0},{2,3},{3,2},{4,5},{5,4},{6,7},{7,6},{8,9},{9,8},{10,11... | collective-permute-start | bytes 2211848 | tf_op jit(solution)/shard_map/ppermute | solution.py:965
  376.4 35.3 %all-to-all-start.7 = ((bf16[4,48,3072]{2,1,0:T(8,128)(2,1)}), bf16[4,48,3072]{2,1,0:T(8,128)(2,1)S(1)}, u32[]{:S(2)}, u32[]{:S(2)}) async-start(bf16[4,48,3072]{2,1,0:T(8,128)(2,1)} %pad_maximum_fusion.1), calls=%async_computation.7 | async-start | bytes 2359296 | tf_op jit(solution)/shard_map/all_to_all | solution.py:1203
  384.8 4.1 copy-start.6
  388.9 66.8 %collective-permute-start.10 = (bf16[20,24,768]{2,1,0:T(8,128)(2,1)}, bf16[20,24,768]{2,1,0:T(8,128)(2,1)}, u32[]{:S(2)}, u32[]{:S(2)}) collective-permute-start(bf16[20,24,768]{2,1,0:T(8,128)(2,1)} %get-tuple-element.143), channel_id=1, source_target_pairs={{0,1},{1,0},{2,3},{3,2},{4,5},{5,4},{6,7},{7,6},{8,9},{9,8},{10,11... | collective-permute-start | bytes 2211848 | tf_op jit(solution)/shard_map/ppermute | solution.py:965
  390.0 4.5 copy-start.4
  390.0 13.2 %collective-permute-start.25 = (bf16[2,2,48,1152]{3,2,1,0:T(8,128)(2,1)}, bf16[2,2,48,1152]{3,2,1,0:T(8,128)(2,1)S(1)}, u32[]{:S(2)}, u32[]{:S(2)}) collective-permute-start(bf16[2,2,48,1152]{3,2,1,0:T(8,128)(2,1)} %dynamic-slice_bitcast_fusion.10), channel_id=1, source_target_pairs={{0,4},{2,6},{4,0},{6,2},{8,12},{10,14},{12,8},{14,10},{16,20},{18,... | collective-permute-start | bytes 1327112 | tf_op jit(solution)/shard_map/ppermute | solution.py:1175
  394.3 1.6 collective-permute-start.20
  395.9 4.2 collective-permute-start.21
  397.3 17.9 %collective-permute-start.26 = (bf16[2,2,48,1152]{3,2,1,0:T(8,128)(2,1)}, bf16[2,2,48,1152]{3,2,1,0:T(8,128)(2,1)}, u32[]{:S(2)}, u32[]{:S(2)}) collective-permute-start(bf16[2,2,48,1152]{3,2,1,0:T(8,128)(2,1)} %dynamic-slice_bitcast_fusion.9), channel_id=1, source_target_pairs={{0,2},{2,0},{4,6},{6,4},{8,10},{10,8},{12,14},{14,12},{16,18},{18,... | collective-permute-start | bytes 1327112 | tf_op jit(solution)/shard_map/ppermute | solution.py:1175
  400.1 32.1 %collective-permute-start.22 = (f32[32,384]{1,0:T(8,128)S(1)}, f32[32,384]{1,0:T(8,128)S(1)}, u32[]{:S(2)}, u32[]{:S(2)}) collective-permute-start(f32[32,384]{1,0:T(8,128)S(1)} %add.242), channel_id=1, source_target_pairs={{0,4},{2,6},{4,0},{6,2},{8,12},{10,14},{12,8},{14,10},{16,20},{18,... | collective-permute-start | bytes 147464 | tf_op jit(solution)/shard_map/ppermute | solution.py:1175
  411.7 16.7 %all-to-all-start.5 = ((bf16[4,48,1280]{2,1,0:T(8,128)(2,1)}), bf16[4,48,1280]{2,1,0:T(8,128)(2,1)S(1)}, u32[]{:S(2)}, u32[]{:S(2)}) async-start(bf16[4,48,1280]{2,1,0:T(8,128)(2,1)} %pad_maximum_fusion.3), calls=%async_computation.5 | async-start | bytes 983040 | tf_op jit(solution)/shard_map/all_to_all | solution.py:1203
  428.4 34.4 %all-to-all-start.6 = ((bf16[4,48,2304]{2,1,0:T(8,128)(2,1)}), bf16[4,48,2304]{2,1,0:T(8,128)(2,1)S(1)}, u32[]{:S(2)}, u32[]{:S(2)}) async-start(bf16[4,48,2304]{2,1,0:T(8,128)(2,1)} %pad_maximum_fusion.2), calls=%async_computation.6 | async-start | bytes 1769472 | tf_op jit(solution)/shard_map/all_to_all | solution.py:1203
  432.2 14.7 %collective-permute-start.23 = (f32[32,384]{1,0:T(8,128)S(1)}, f32[32,384]{1,0:T(8,128)S(1)}, u32[]{:S(2)}, u32[]{:S(2)}) collective-permute-start(f32[32,384]{1,0:T(8,128)S(1)} %add.243), channel_id=1, source_target_pairs={{0,8},{2,10},{4,12},{6,14},{8,0},{10,2},{12,4},{14,6},{16,24},{18,... | collective-permute-start | bytes 147464 | tf_op jit(solution)/shard_map/ppermute | solution.py:1175
  446.9 12.3 %collective-permute-start.24 = (f32[32,384]{1,0:T(8,128)S(1)}, f32[32,384]{1,0:T(8,128)S(1)}, u32[]{:S(2)}, u32[]{:S(2)}) collective-permute-start(f32[32,384]{1,0:T(8,128)S(1)} %add.244), channel_id=1, source_target_pairs={{0,16},{2,18},{4,20},{6,22},{8,24},{10,26},{12,28},{14,30},{16,0},... | collective-permute-start | bytes 147464 | tf_op jit(solution)/shard_map/ppermute | solution.py:1175
  (23 other events, 42.6 us)

commit v7 on v6

--- a/solution.py
+++ b/solution.py
@@ -1232,6 +1232,37 @@
     grad_queries, up_part, down_part = tie(grad_queries, up_part, down_part)
     feed_stage = first_swaps(up_part, down_part)
 
+    token_shape = (length // 2, slots, width)
+    final_shape = (length // 2, rows, width)
+
+    def halves(value, after):
+        own, away = run(
+            partial(halve_kernel, slots, length),
+            1,
+            [core_scalar, where],
+            [whole(value)],
+            [(token_shape, BF16, whole_spec(token_shape))] * 2,
+            [slabs(all_tokens)],
+            0,
+            after,
+        )
+        return own, mate(away)
+
+    def placed(own, got, after):
+        (out,) = run(
+            place_kernel,
+            1,
+            [],
+            [whole(own), whole(got), whole(place)],
+            [(final_shape, BF16, whole_spec(final_shape))],
+            [],
+            0,
+            after,
+        )
+        return jnp.transpose(out, (1, 0, 2))
+
+    merged_own, merged_got = halves(merged_in, [])
+
     result = run(
         partial(self_grad_kernel, steps, step_rows, local, length),
         steps,
@@ -1261,6 +1292,7 @@
         + [f32_tokens(width)] * 3
         + [pltpu.VMEM((8, 8, width), F32), pltpu.SemaphoreType.DMA((10,))],
         2 * all_tokens * width * width * 5 + attention_flops * 2,
+        [merged_own],
     )
     text_out, grad_self, dq_own, dq_mate, qkv_own, qkv_mate, self_sums = result
     text_in = exchange(text_out)
@@ -1376,34 +1408,9 @@
     ).reshape(2, 3, width // devices, local)
     out_grad = jnp.stack([out_self.T, out_cross.T])
 
-    def tokens_out(value, after, after_place):
-        shape = (length // 2, slots, width)
-        own, away = run(
-            partial(halve_kernel, slots, length),
-            1,
-            [core_scalar, where],
-            [whole(value)],
-            [(shape, BF16, whole_spec(shape))] * 2,
-            [slabs(all_tokens)],
-            0,
-            after,
-        )
-        shape = (length // 2, rows, width)
-        (out,) = run(
-            place_kernel,
-            1,
-            [],
-            [whole(own), whole(mate(away)), whole(place)],
-            [(shape, BF16, whole_spec(shape))],
-            [],
-            0,
-            after_place,
-        )
-        return jnp.transpose(out, (1, 0, 2))
-
     return (
-        tokens_out(merged_in, [self_part], [kv_part]),
-        tokens_out(text_in, [kv_away, self_part], [kv_part, proj_part]),
+        placed(merged_own, merged_got, [kv_part]),
+        placed(*halves(text_in, [kv_away, self_part]), [kv_part, proj_part]),
         jnp.transpose(patch_grad, (1, 0, 2)),
         proj_grad,
         proj_bias_grad,

time: 472 us -> 455 us (0.964)
  waiting for transfers between devices: 62.2 us -> 52.1 us
    all_to_all x5, waiting for transfers between devices: 19.1 us -> 8.74 us  [exchange(): return lax.all_to_all(value, 'dp', split_axis=0, concat_axis=0, tiled=True)]
    ppermute x16, waiting for transfers between devices: 23.6 us -> 29.2 us  [partner_bits(): return lax.ppermute(value, 'dp', [(d, d ^ mask) for d in range(devices)])]
    all_to_all x3, waiting for transfers between devices: 19.5 us -> 14 us  [last_sum(): lax.all_to_all(both, 'dp', split_axis=0, concat_axis=0, axis_index_groups...]
  transfers between devices with their start and end apart: 39 -> 39, of which waited for: 12 -> 13; matrix products, arithmetic and copies ran while one was open for 19% -> 19% of each run, Pallas kernels for 33% -> 35%
where the time goes in v7:
time: 455 us; the launch traced here: 447 us
  Pallas kernels  207 us (45%)
  starting transfers between devices  80.3 us (18%)
  waiting for transfers between devices  52.1 us (11%)
  matrix products  44.3 us (10%)
  local copies, waits for them, and re-layouts  34.6 us (8%)
  other arithmetic  27.8 us (6%)
    pallas_call x13, Pallas kernels, run(): pl.pallas_call(kernel, grid_spec=pltpu.PrefetchScalarGridSpec(num_scalar_...  207 us
    dot_general x14, matrix products, dot_tn(): lax.dot_general(left, right, (((0,), (0,)), ((), ())), preferred_element_...  44.3 us
    all_to_all x5, starting transfers between devices, exchange(): return lax.all_to_all(value, 'dp', split_axis=0, concat_axis=0, tiled=True)  37.9 us
    ppermute x16, waiting for transfers between devices, partner_bits(): return lax.ppermute(value, 'dp', [(d, d ^ mask) for d in range(devices)])  29.2 us
    ppermute x16, starting transfers between devices, partner_bits(): return lax.ppermute(value, 'dp', [(d, d ^ mask) for d in range(devices)])  26.2 us
    all_to_all x3, waiting for transfers between devices, last_sum(): lax.all_to_all(both, 'dp', split_axis=0, concat_axis=0, axis_index_groups...  14 us
    all_to_all x3, starting transfers between devices, last_sum(): lax.all_to_all(both, 'dp', split_axis=0, concat_axis=0, axis_index_groups...  13.2 us
    unnamed x101, local copies, waits for them, and re-layouts  10.5 us
  transfers between devices with their start and end apart: 39, of which 13 were waited for; matrix products, arithmetic and copies ran while one was open for 19% of the time, Pallas kernels for 35%

profile of v7, /device:TPU:0, one launch (start us, length us, event | category | flops | bytes accessed | tf_op | source)
XLA Modules:
  0.0 447.4 jit_solution(2403704575447129225)
XLA Ops:
  4.6 7.9 %all-to-all-start = ((s32[16,2,6]{2,1,0:T(2,128)}), s32[16,2,6]{2,1,0:T(2,128)S(1)}, u32[]{:S(2)}, u32[]{:S(2)}) async-start(s32[16,2,6]{2,1,0:T(2,128)} %bitcast.171), calls=%async_computation | async-start | bytes 32768 | tf_op jit(solution)/shard_map/all_to_all | solution.py:971
  13.8 5.4 %shard_map.281 = (bf16[32,40,768]{2,1,0:T(8,128)(2,1)}, bf16[32,40,768]{2,1,0:T(8,128)(2,1)}) custom-call(s32[32]{0:T(128)} %select_reduce_fusion.1.refs_0_, bf16[48,40,768]{2,1,0:T(8,128)(2,1)} %refs_1_.1, bf16[48,40,768]{2,1,0:T(8,128)(2,1)} %refs_2_.2), custom_call_target="tpu_custom_call" | custom-call | bytes 9830400 | tf_op jit(solution)/shard_map/pallas_call | solution.py:66
  19.8 6.3 %all-to-all-start.2 = ((bf16[32,40,768]{2,1,0:T(8,128)(2,1)}), bf16[32,40,768]{2,1,0:T(8,128)(2,1)}, u32[]{:S(2)}, u32[]{:S(2)}) async-start(bf16[32,40,768]{2,1,0:T(8,128)(2,1)} %get-tuple-element.98), calls=%async_computation.2 | async-start | bytes 3932160 | tf_op jit(solution)/shard_map/all_to_all | solution.py:971
  33.9 1.5 slice_reduce_fusion
  38.0 1.7 copy-done.12
  39.8 22.2 %shard_map.282 = (bf16[8,160,768]{2,1,0:T(8,128)(2,1)}, bf16[16,160,768]{2,1,0:T(8,128)(2,1)}, bf16[16,160,768]{2,1,0:T(8,128)(2,1)}) custom-call(s32[1]{0:T(128)} %bitcast.refs_0_, bf16[145,16,1024]{2,1,0:T(8,128)(2,1)} %bitcast.158, bf16[1024,768]{1,0:T(8,128)(2,1)} %refs_4_.5, f32[1,768]{1,0:T(1,128)} %reshape.219.refs_3_, ...), custom_call_target="tpu_custom_call" | custom-call | flops 10066329600 | bytes 23247872 | tf_op jit(solution)/shard_map/pallas_call | solution.py:66
  62.0 5.2 %all-to-all-done.2.refs_2_ = bf16[32,40,768]{2,1,0:T(8,128)(2,1)} async-done(((bf16[32,40,768]{2,1,0:T(8,128)(2,1)}), bf16[32,40,768]{2,1,0:T(8,128)(2,1)}, u32[]{:S(2)}, u32[]{:S(2)}) %all-to-all-start.2) | async-done | bytes 1966112 | tf_op jit(solution)/shard_map/all_to_all | solution.py:971
  67.2 9.7 %all-to-all-start.1 = ((bf16[32,40,768]{2,1,0:T(8,128)(2,1)}), bf16[32,40,768]{2,1,0:T(8,128)(2,1)S(1)}, u32[]{:S(2)}, u32[]{:S(2)}) async-start(bf16[32,40,768]{2,1,0:T(8,128)(2,1)} %get-tuple-element.94), calls=%async_computation.1 | async-start | bytes 3932160 | tf_op jit(solution)/shard_map/all_to_all | solution.py:971
  78.2 22.1 %shard_map.283 = (bf16[960,768]{1,0:T(8,128)(2,1)}, f32[960,768]{1,0:T(8,128)}, bf16[960,768]{1,0:T(8,128)(2,1)}, bf16[960,768]{1,0:T(8,128)(2,1)}, bf16[960,768...) custom-call(s32[24]{0:T(128)} %get-tuple-element.97.refs_0_, ...), custom_call_target="tpu_custom_call" | custom-call | flops 6417285120 | bytes 24718080 | tf_op jit(solution)/shard_map/pallas_call | solution.py:66
  100.3 12.5 %shard_map.284.refs_2_ = bf16[960,768]{1,0:T(8,128)(2,1)} custom-call(s32[24]{0:T(128)} %and_select_fusion.refs_0_, s32[96]{0:T(128)} %reshape.218.refs_1_, bf16[960,768]{1,0:T(8,128)(2,1)} %get-tuple-element.113.refs_2_, bf16[16,160,768]{2,1,0:T(8,128)(2,1)} %get-tuple-element.101.refs_3_.refs_4_, bf16[16,160,768]{2,1,0:T(8,128)(2,1)} %get-tuple-element.102.refs_4_.refs_5_), custom_call_target="tpu_custom_call" | custom-call | flops 3019898880 | bytes 10813440 | tf_op jit(solution)/shard_map/pallas_call | solution.py:66
  112.8 1.4 copy-done.32
  114.2 3.0 all-to-all-done.1.refs_1_
  118.4 52.4 %shard_map.285 = (bf16[32,40,768]{2,1,0:T(8,128)(2,1)}, bf16[960,768]{1,0:T(8,128)(2,1)}, bf16[960,768]{1,0:T(8,128)(2,1)}, bf16[960,768]{1,0:T(8,128)(2,1)}, f3...) custom-call(s32[24]{0:T(128)} %compare_select_fusion.4.refs_1_.refs_, ...), custom_call_target="tpu_custom_call" | custom-call | flops 20384317440 | bytes 42384384 | tf_op jit(solution)/shard_map/pallas_call | solution.py:66
  170.8 6.5 %convolution_convert_fusion.1 = bf16[768,1536]{1,0:T(8,128)(2,1)} fusion(bf16[960,768]{1,0:T(8,128)(2,1)} %get-tuple-element.111, bf16[960,1536]{1,0:T(8,128)(2,1)} %get-tuple-element.112), kind=kOutput, calls=%fused_computation.7 | convolution fusion | flops 2266103808 | bytes 6782976 | tf_op jit(solution)/shard_map/dot_general | solution.py:38
  177.3 4.2 convolution_convert_fusion.2
  182.0 9.1 %all-to-all-start.3 = ((bf16[32,40,768]{2,1,0:T(8,128)(2,1)}), bf16[32,40,768]{2,1,0:T(8,128)(2,1)S(1)}, u32[]{:S(2)}, u32[]{:S(2)}) async-start(bf16[32,40,768]{2,1,0:T(8,128)(2,1)} %get-tuple-element.104), calls=%async_computation.3 | async-start | bytes 3932160 | tf_op jit(solution)/shard_map/all_to_all | solution.py:971
  191.1 24.4 %shard_map.287 = (bf16[2,8,160,768]{3,2,1,0:T(8,128)(2,1)}, bf16[2,8,160,768]{3,2,1,0:T(8,128)(2,1)}, bf16[960,768]{1,0:T(8,128)(2,1)}) custom-call(s32[24]{0:T(128)} %and_select_fusion.refs_0_, s32[96]{0:T(128)} %reshape.218.refs_1_, bf16[960,768]{1,0:T(8,128)(2,1)} %get-tuple-element.113.refs_2_, bf16[960,768]{1,0:T(8,128)(2,1)} %get-tuple-element.114.refs_3_, ...), custom_call_target="tpu_custom_call" | custom-call | flops 9059696640 | bytes 20152320 | tf_op jit(solution)/shard_map/pallas_call | solution.py:66
  216.2 3.0 convolution_convert_fusion.5
  219.2 2.1 fusion.30
  221.9 4.4 add_convert_fusion
  226.3 4.2 add_convert_fusion.1
  231.7 1.9 collective-permute-start.27
  233.6 1.5 dynamic-slice_bitcast_fusion
  235.2 1.5 collective-permute-start.28
  237.9 4.0 shard_map.286
  241.9 28.1 %shard_map.288 = (bf16[32,40,768]{2,1,0:T(8,128)(2,1)}, bf16[960,768]{1,0:T(8,128)(2,1)}, bf16[960,384]{1,0:T(8,128)(2,1)}, bf16[960,384]{1,0:T(8,128)(2,1)}, bf...) custom-call(s32[24]{0:T(128)} %get-tuple-element.97.refs_0_, ...), custom_call_target="tpu_custom_call" | custom-call | flops 7172259840 | bytes 30634752 | tf_op jit(solution)/shard_map/pallas_call | solution.py:66
  270.0 4.9 %all-to-all-start.4 = ((bf16[32,40,768]{2,1,0:T(8,128)(2,1)}), bf16[32,40,768]{2,1,0:T(8,128)(2,1)}, u32[]{:S(2)}, u32[]{:S(2)}) async-start(bf16[32,40,768]{2,1,0:T(8,128)(2,1)} %get-tuple-element.135), calls=%async_computation.4 | async-start | bytes 3932160 | tf_op jit(solution)/shard_map/all_to_all | solution.py:971
  275.0 23.0 %shard_map.289 = (bf16[1280,768]{1,0:T(8,128)(2,1)}, bf16[1280,768]{1,0:T(8,128)(2,1)}, bf16[145,8,1024]{2,1,0:T(8,128)(2,1)}, f32[1024,768]{1,0:T(8,128)}, f32[...) custom-call(s32[1]{0:T(128)} %bitcast.refs_0_, ...), custom_call_target="tpu_custom_call", output_to_operand_aliasing={{5}: (7, {}), {6}: (8, {}), {7}: (9, {}), {8}: (10, {}), {9... | custom-call | flops 7046430720 | bytes 30744576 | tf_op jit(solution)/shard_map/pallas_call | solution.py:66
  298.0 2.5 convolution_convert_fusion.6
  302.6 2.3 convolution_convert_fusion
  304.9 2.1 pad_maximum_fusion
  307.5 1.7 add_convert_fusion.3
  309.2 1.9 collective-permute-start.29
  311.1 1.6 add_convert_fusion.2
  312.8 1.5 collective-permute-start.30
  314.3 4.1 fusion.28
  318.4 1.8 convolution_convert_fusion.3.refs_3_
  320.2 2.0 fusion.29
  322.3 2.0 fusion.31
  324.4 2.8 collective-permute-done.29
  331.2 1.8 collective-permute-start.16
  333.0 4.3 add_convert_fusion.4.refs_3_.refs_5_
  340.6 1.5 reshape.222.refs_4_.refs_6_
  342.1 3.6 shard_map.290
  347.9 6.9 %collective-permute-done.14 = bf16[2,2,2,48,768]{4,3,2,1,0:T(8,128)(2,1)} collective-permute-done((bf16[2,2,2,48,768]{4,3,2,1,0:T(8,128)(2,1)}, bf16[2,2,2,48,768]{4,3,2,1,0:T(8,128)(2,1)}, u32[]{:S(2)}, u32[]{:S(2)}) %collective-permute-start.14) | collective-permute-done | bytes 589856 | tf_op jit(solution)/shard_map/ppermute | solution.py:1175
  356.4 3.0 fusion.refs_4_
  359.7 1.5 copy-done
  364.5 1.9 collective-permute-start.19
  367.2 6.2 %all-to-all-start.7 = ((bf16[4,48,3072]{2,1,0:T(8,128)(2,1)}), bf16[4,48,3072]{2,1,0:T(8,128)(2,1)S(1)}, u32[]{:S(2)}, u32[]{:S(2)}) async-start(bf16[4,48,3072]{2,1,0:T(8,128)(2,1)} %pad_maximum_fusion.1), calls=%async_computation.7 | async-start | bytes 2359296 | tf_op jit(solution)/shard_map/all_to_all | solution.py:1203
  373.5 4.1 shard_map.291
  377.6 3.8 collective-permute-done.18.refs_7_
  382.5 1.7 collective-permute-start.25
  385.5 1.5 shard_map.293
  387.0 1.4 fusion.1
  388.4 1.4 collective-permute-start.21
  392.6 1.8 collective-permute-start.22
  394.5 4.3 all-to-all-done.7
  398.8 3.5 all-to-all-start.5
  405.4 9.7 %all-to-all-done.5 = bf16[4,48,1280]{2,1,0:T(8,128)(2,1)S(1)} async-done(((bf16[4,48,1280]{2,1,0:T(8,128)(2,1)}), bf16[4,48,1280]{2,1,0:T(8,128)(2,1)S(1)}, u32[]{:S(2)}, u32[]{:S(2)}) %all-to-all-start.5) | async-done | bytes 491552 | tf_op jit(solution)/shard_map/all_to_all | solution.py:1203
  415.1 3.5 all-to-all-start.6
  418.9 2.0 collective-permute-start.23
  421.8 11.8 %collective-permute-done.23 = f32[32,384]{1,0:T(8,128)S(1)} collective-permute-done((f32[32,384]{1,0:T(8,128)S(1)}, f32[32,384]{1,0:T(8,128)S(1)}, u32[]{:S(2)}, u32[]{:S(2)}) %collective-permute-start.23) | collective-permute-done | bytes 49184 | tf_op jit(solution)/shard_map/ppermute | solution.py:1175
  433.6 4.7 %collective-permute-start.24 = (f32[32,384]{1,0:T(8,128)S(1)}, f32[32,384]{1,0:T(8,128)S(1)}, u32[]{:S(2)}, u32[]{:S(2)}) collective-permute-start(f32[32,384]{1,0:T(8,128)S(1)} %add.244), channel_id=1, source_target_pairs={{0,16},{2,18},{4,20},{6,22},{8,24},{10,26},{12,28},{14,30},{16,0},... | collective-permute-start | bytes 147464 | tf_op jit(solution)/shard_map/ppermute | solution.py:1175
  439.0 3.4 shard_map.292
  (221 shorter events, 56.3 us)
Async XLA Ops:
  0.6 37.4 %collective-permute-start.1 = (bf16[2,3,768,384]{3,2,1,0:T(8,128)(2,1)}, bf16[2,3,768,384]{3,2,1,0:T(8,128)(2,1)S(1)}, u32[]{:S(2)}, u32[]{:S(2)}) collective-permute-start(bf16[2,3,768,384]{3,2,1,0:T(8,128)(2,1)} %refs_5_.3), channel_id=1, source_target_pairs={{0,1},{1,0},{2,3},{3,2},{4,5},{5,4},{6,7},{7,6},{8,9},{9,8},{10,11... | collective-permute-start | bytes 10616840 | tf_op jit(solution)/shard_map/ppermute | solution.py:965
  4.6 15.2 %all-to-all-start = ((s32[16,2,6]{2,1,0:T(2,128)}), s32[16,2,6]{2,1,0:T(2,128)S(1)}, u32[]{:S(2)}, u32[]{:S(2)}) async-start(s32[16,2,6]{2,1,0:T(2,128)} %bitcast.171), calls=%async_computation | async-start | bytes 32768 | tf_op jit(solution)/shard_map/all_to_all | solution.py:971
  19.8 47.3 %all-to-all-start.2 = ((bf16[32,40,768]{2,1,0:T(8,128)(2,1)}), bf16[32,40,768]{2,1,0:T(8,128)(2,1)}, u32[]{:S(2)}, u32[]{:S(2)}) async-start(bf16[32,40,768]{2,1,0:T(8,128)(2,1)} %get-tuple-element.98), calls=%async_computation.2 | async-start | bytes 3932160 | tf_op jit(solution)/shard_map/all_to_all | solution.py:971
  26.2 11.8 %collective-permute-start = (bf16[2,384,768]{2,1,0:T(8,128)(2,1)}, bf16[2,384,768]{2,1,0:T(8,128)(2,1)}, u32[]{:S(2)}, u32[]{:S(2)}) collective-permute-start(bf16[2,384,768]{2,1,0:T(8,128)(2,1)} %refs_11_.5), channel_id=1, source_target_pairs={{0,1},{1,0},{2,3},{3,2},{4,5},{5,4},{6,7},{7,6},{8,9},{9,8},{10,11... | collective-permute-start | bytes 3538952 | tf_op jit(solution)/shard_map/ppermute | solution.py:965
  26.3 11.8 %collective-permute-start.2 = (f32[2,2,384]{2,1,0:T(2,128)}, f32[2,2,384]{2,1,0:T(2,128)}, u32[]{:S(2)}, u32[]{:S(2)}) collective-permute-start(f32[2,2,384]{2,1,0:T(2,128)} %refs_7_.1), channel_id=1, source_target_pairs={{0,1},{1,0},{2,3},{3,2},{4,5},{5,4},{6,7},{7,6},{8,9},{9,8},{10,11... | collective-permute-start | bytes 18440 | tf_op jit(solution)/shard_map/ppermute | solution.py:965
  62.0 15.5 %copy-start.27 = (f32[1536]{0:T(1024)S(1)}, f32[1536]{0:T(1024)}, u32[]{:S(2)}) copy-start(f32[1536]{0:T(1024)} %param.34) | copy-start | bytes 18436
  67.2 50.0 %all-to-all-start.1 = ((bf16[32,40,768]{2,1,0:T(8,128)(2,1)}), bf16[32,40,768]{2,1,0:T(8,128)(2,1)S(1)}, u32[]{:S(2)}, u32[]{:S(2)}) async-start(bf16[32,40,768]{2,1,0:T(8,128)(2,1)} %get-tuple-element.94), calls=%async_computation.1 | async-start | bytes 3932160 | tf_op jit(solution)/shard_map/all_to_all | solution.py:971
  76.9 35.9 %collective-permute-start.3 = (bf16[768,1536]{1,0:T(8,128)(2,1)}, bf16[768,1536]{1,0:T(8,128)(2,1)S(1)}, u32[]{:S(2)}, u32[]{:S(2)}) collective-permute-start(bf16[768,1536]{1,0:T(8,128)(2,1)} %refs_6_.3), channel_id=1, source_target_pairs={{0,1},{1,0},{2,3},{3,2},{4,5},{5,4},{6,7},{7,6},{8,9},{9,8},{10,11... | collective-permute-start | bytes 7077896 | tf_op jit(solution)/shard_map/ppermute | solution.py:965
  77.0 37.2 %collective-permute-start.4 = (bf16[1536,768]{1,0:T(8,128)(2,1)}, bf16[1536,768]{1,0:T(8,128)(2,1)}, u32[]{:S(2)}, u32[]{:S(2)}) collective-permute-start(bf16[1536,768]{1,0:T(8,128)(2,1)} %refs_8_.1), channel_id=1, source_target_pairs={{0,1},{1,0},{2,3},{3,2},{4,5},{5,4},{6,7},{7,6},{8,9},{9,8},{10,11... | collective-permute-start | bytes 7077896 | tf_op jit(solution)/shard_map/ppermute | solution.py:965
  77.5 22.8 %copy-start.28 = (f32[1,1536]{1,0:T(1,128)}, f32[1,1536]{1,0:T(1,128)S(1)}, u32[]{:S(2)}) copy-start(f32[1,1536]{1,0:T(1,128)S(1)} %reshape.220.refs_13_) | copy-start | bytes 18436
  77.5 35.3 %collective-permute-start.5 = (f32[1,1536]{1,0:T(1,128)S(1)}, f32[1,1536]{1,0:T(1,128)S(1)}, u32[]{:S(2)}, u32[]{:S(2)}) collective-permute-start(f32[1,1536]{1,0:T(1,128)S(1)} %reshape.220.refs_13_), channel_id=1, source_target_pairs={{0,1},{1,0},{2,3},{3,2},{4,5},{5,4},{6,7},{7,6},{8,9},{9,8},{10,11... | collective-permute-start | bytes 18440 | tf_op jit(solution)/shard_map/ppermute | solution.py:965
  112.8 4.4 copy-start.34
  170.8 6.5 %copy-start.38 = (bf16[960,1536]{1,0:T(8,128)(2,1)S(1)}, bf16[960,1536]{1,0:T(8,128)(2,1)}, u32[]{:S(2)}) copy-start(bf16[960,1536]{1,0:T(8,128)(2,1)} %get-tuple-element.110) | copy-start | bytes 8847364
  170.8 6.5 %copy-start.41 = (bf16[960,768]{1,0:T(8,128)(2,1)S(1)}, bf16[960,768]{1,0:T(8,128)(2,1)}, u32[]{:S(2)}) copy-start(bf16[960,768]{1,0:T(8,128)(2,1)} %get-tuple-element.109) | copy-start | bytes 4423684
  181.5 39.8 %collective-permute-start.9 = (bf16[768,1536]{1,0:T(8,128)(2,1)}, bf16[768,1536]{1,0:T(8,128)(2,1)}, u32[]{:S(2)}, u32[]{:S(2)}) collective-permute-start(bf16[768,1536]{1,0:T(8,128)(2,1)} %convolution_convert_fusion.1), channel_id=1, source_target_pairs={{0,1},{1,0},{2,3},{3,2},{4,5},{5,4},{6,7},{7,6},{8,9},{9,8},{10,11... | collective-permute-start | bytes 7077896 | tf_op jit(solution)/shard_map/ppermute | solution.py:965
  181.5 44.8 %collective-permute-start.8 = (bf16[768,1536]{1,0:T(8,128)(2,1)}, bf16[768,1536]{1,0:T(8,128)(2,1)}, u32[]{:S(2)}, u32[]{:S(2)}) collective-permute-start(bf16[768,1536]{1,0:T(8,128)(2,1)} %convolution_convert_fusion.2), channel_id=1, source_target_pairs={{0,1},{1,0},{2,3},{3,2},{4,5},{5,4},{6,7},{7,6},{8,9},{9,8},{10,11... | collective-permute-start | bytes 7077896 | tf_op jit(solution)/shard_map/ppermute | solution.py:965
  182.0 54.6 %all-to-all-start.3 = ((bf16[32,40,768]{2,1,0:T(8,128)(2,1)}), bf16[32,40,768]{2,1,0:T(8,128)(2,1)S(1)}, u32[]{:S(2)}, u32[]{:S(2)}) async-start(bf16[32,40,768]{2,1,0:T(8,128)(2,1)} %get-tuple-element.104), calls=%async_computation.3 | async-start | bytes 3932160 | tf_op jit(solution)/shard_map/all_to_all | solution.py:971
  191.1 24.4 %copy-start.29 = (s32[48,1]{0,1:T(1,128)S(1)}, s32[48,1]{0,1:T(1,128)}, u32[]{:S(2)}) copy-start(s32[48,1]{0,1:T(1,128)} %get-tuple-element.166) | copy-start | bytes 580
  191.1 25.1 %copy-start.37 = (bf16[960,768]{1,0:T(8,128)(2,1)S(1)}, bf16[960,768]{1,0:T(8,128)(2,1)}, u32[]{:S(2)}) copy-start(bf16[960,768]{1,0:T(8,128)(2,1)} %get-tuple-element.140) | copy-start | bytes 4423684
  215.5 59.5 %collective-permute-start.7 = (bf16[2,8,160,768]{3,2,1,0:T(8,128)(2,1)}, bf16[2,8,160,768]{3,2,1,0:T(8,128)(2,1)}, u32[]{:S(2)}, u32[]{:S(2)}) collective-permute-start(bf16[2,8,160,768]{3,2,1,0:T(8,128)(2,1)} %get-tuple-element.116), channel_id=1, source_target_pairs={{0,1},{1,0},{2,3},{3,2},{4,5},{5,4},{6,7},{7,6},{8,9},{9,8},{10,11... | collective-permute-start | bytes 11796488 | tf_op jit(solution)/shard_map/ppermute | solution.py:965
  221.9 4.4 copy-start.42
  221.9 4.4 copy-start.46
  231.7 75.8 %collective-permute-start.27 = (bf16[2,2,2,48,1536]{4,3,2,1,0:T(8,128)(2,1)}, bf16[2,2,2,48,1536]{4,3,2,1,0:T(8,128)(2,1)}, u32[]{:S(2)}, u32[]{:S(2)}) collective-permute-start(bf16[2,2,2,48,1536]{4,3,2,1,0:T(8,128)(2,1)} %get-tuple-element.172), channel_id=1, source_target_pairs={{0,2},{2,0},{4,6},{6,4},{8,10},{10,8},{12,14},{14,12},{16,18},{18,... | collective-permute-start | bytes 3538952 | tf_op jit(solution)/shard_map/ppermute | solution.py:1175
  235.2 72.3 %collective-permute-start.28 = (bf16[2,2,2,48,1536]{4,3,2,1,0:T(8,128)(2,1)}, bf16[2,2,2,48,1536]{4,3,2,1,0:T(8,128)(2,1)}, u32[]{:S(2)}, u32[]{:S(2)}) collective-permute-start(bf16[2,2,2,48,1536]{4,3,2,1,0:T(8,128)(2,1)} %get-tuple-element.170), channel_id=1, source_target_pairs={{0,4},{2,6},{4,0},{6,2},{8,12},{10,14},{12,8},{14,10},{16,20},{18,... | collective-permute-start | bytes 3538952 | tf_op jit(solution)/shard_map/ppermute | solution.py:1175
  270.0 97.2 %all-to-all-start.4 = ((bf16[32,40,768]{2,1,0:T(8,128)(2,1)}), bf16[32,40,768]{2,1,0:T(8,128)(2,1)}, u32[]{:S(2)}, u32[]{:S(2)}) async-start(bf16[32,40,768]{2,1,0:T(8,128)(2,1)} %get-tuple-element.135), calls=%async_computation.4 | async-start | bytes 3932160 | tf_op jit(solution)/shard_map/all_to_all | solution.py:971
  274.9 67.1 %collective-permute-start.6 = (bf16[20,24,768]{2,1,0:T(8,128)(2,1)}, bf16[20,24,768]{2,1,0:T(8,128)(2,1)}, u32[]{:S(2)}, u32[]{:S(2)}) collective-permute-start(bf16[20,24,768]{2,1,0:T(8,128)(2,1)} %get-tuple-element.106), channel_id=1, source_target_pairs={{0,1},{1,0},{2,3},{3,2},{4,5},{5,4},{6,7},{7,6},{8,9},{9,8},{10,11... | collective-permute-start | bytes 2211848 | tf_op jit(solution)/shard_map/ppermute | solution.py:965
  275.0 23.0 %copy-start.44 = (bf16[960,384]{1,0:T(8,128)(2,1)S(1)}, bf16[960,384]{1,0:T(8,128)(2,1)}, u32[]{:S(2)}) copy-start(bf16[960,384]{1,0:T(8,128)(2,1)} %get-tuple-element.145) | copy-start | bytes 2211844
  307.0 49.4 %collective-permute-start.11 = (bf16[768,2304]{1,0:T(8,128)(2,1)}, bf16[768,2304]{1,0:T(8,128)(2,1)}, u32[]{:S(2)}, u32[]{:S(2)}) collective-permute-start(bf16[768,2304]{1,0:T(8,128)(2,1)} %pad_maximum_fusion), channel_id=1, source_target_pairs={{0,1},{1,0},{2,3},{3,2},{4,5},{5,4},{6,7},{7,6},{8,9},{9,8},{10,11... | collective-permute-start | bytes 10616840 | tf_op jit(solution)/shard_map/ppermute | solution.py:965
  307.5 3.6 copy-start.8
  309.2 5.1 %copy-start.14 = (bf16[960,1152]{1,0:T(8,128)(2,1)S(1)}, bf16[960,1152]{1,0:T(8,128)(2,1)}, u32[]{:S(2)}) copy-start(bf16[960,1152]{1,0:T(8,128)(2,1)} %get-tuple-element.137) | copy-start | bytes 6635524
  309.2 17.9 %collective-permute-start.29 = (bf16[2,2,48,1536]{3,2,1,0:T(8,128)(2,1)S(1)}, bf16[2,2,48,1536]{3,2,1,0:T(8,128)(2,1)S(1)}, u32[]{:S(2)}, u32[]{:S(2)}) collective-permute-start(bf16[2,2,48,1536]{3,2,1,0:T(8,128)(2,1)S(1)} %dynamic-slice_bitcast_fusion.7), channel_id=1, source_target_pairs={{0,4},{2,6},{4,0},{6,2},{8,12},{10,14},{12,8},{14,10},{16,20},{18,... | collective-permute-start | bytes 1769480 | tf_op jit(solution)/shard_map/ppermute | solution.py:1175
  312.8 15.9 %collective-permute-start.30 = (bf16[2,2,48,1536]{3,2,1,0:T(8,128)(2,1)S(1)}, bf16[2,2,48,1536]{3,2,1,0:T(8,128)(2,1)S(1)}, u32[]{:S(2)}, u32[]{:S(2)}) collective-permute-start(bf16[2,2,48,1536]{3,2,1,0:T(8,128)(2,1)S(1)} %dynamic-slice_bitcast_fusion.6), channel_id=1, source_target_pairs={{0,2},{2,0},{4,6},{6,4},{8,10},{10,8},{12,14},{14,12},{16,18},{18,... | collective-permute-start | bytes 1769480 | tf_op jit(solution)/shard_map/ppermute | solution.py:1175
  314.3 4.1 copy-start.33
  314.3 4.1 copy-start.35
  322.3 10.7 %collective-permute-start.10 = (bf16[768,768]{1,0:T(8,128)(2,1)S(1)}, bf16[768,768]{1,0:T(8,128)(2,1)}, u32[]{:S(2)}, u32[]{:S(2)}) collective-permute-start(bf16[768,768]{1,0:T(8,128)(2,1)S(1)} %convolution_convert_fusion.3.refs_3_), channel_id=1, source_target_pairs={{0,1},{1,0},{2,3},{3,2},{4,5},{5,4},{6,7},{7,6},{8,9},{9,8},{10,11... | collective-permute-start | bytes 3538952 | tf_op jit(solution)/shard_map/ppermute | solution.py:965
  327.2 2.4 collective-permute-start.13
  331.2 14.4 %collective-permute-start.16 = (bf16[2,2,2,48,512]{4,3,2,1,0:T(8,128)(2,1)}, bf16[2,2,2,48,512]{4,3,2,1,0:T(8,128)(2,1)}, u32[]{:S(2)}, u32[]{:S(2)}) collective-permute-start(bf16[2,2,2,48,512]{4,3,2,1,0:T(8,128)(2,1)} %dynamic-slice_bitcast_fusion.11), channel_id=1, source_target_pairs={{0,4},{2,6},{4,0},{6,2},{8,12},{10,14},{12,8},{14,10},{16,20},{18,... | collective-permute-start | bytes 1179656 | tf_op jit(solution)/shard_map/ppermute | solution.py:1175
  333.0 6.4 %copy-start.13 = (bf16[2,2,48,1536]{3,2,1,0:T(8,128)(2,1)S(1)}, bf16[2,2,48,1536]{3,2,1,0:T(8,128)(2,1)}, u32[]{:S(2)}) copy-start(bf16[2,2,48,1536]{3,2,1,0:T(8,128)(2,1)} %fusion.3) | copy-start | bytes 1769476
  337.3 4.8 %copy-start.1 = (bf16[768,768]{1,0:T(8,128)(2,1)}, bf16[768,768]{1,0:T(8,128)(2,1)S(1)}, u32[]{:S(2)}) copy-start(bf16[768,768]{1,0:T(8,128)(2,1)S(1)} %add_convert_fusion.4.refs_3_.refs_5_) | copy-start | bytes 3538948
  338.2 16.5 %collective-permute-start.14 = (bf16[2,2,2,48,768]{4,3,2,1,0:T(8,128)(2,1)}, bf16[2,2,2,48,768]{4,3,2,1,0:T(8,128)(2,1)}, u32[]{:S(2)}, u32[]{:S(2)}) collective-permute-start(bf16[2,2,2,48,768]{4,3,2,1,0:T(8,128)(2,1)} %dynamic-slice_bitcast_fusion.8), channel_id=1, source_target_pairs={{0,2},{2,0},{4,6},{6,4},{8,10},{10,8},{12,14},{14,12},{16,18},{18,... | collective-permute-start | bytes 1769480 | tf_op jit(solution)/shard_map/ppermute | solution.py:1175
  342.1 12.7 %copy-start.2 = (bf16[768,768]{1,0:T(8,128)(2,1)S(1)}, bf16[768,768]{1,0:T(8,128)(2,1)}, u32[]{:S(2)}) copy-start(bf16[768,768]{1,0:T(8,128)(2,1)} %copy-done.1) | copy-start | bytes 3538948
  342.1 14.3 %copy-start.19 = (f32[768,384]{1,0:T(8,128)S(1)}, f32[768,384]{1,0:T(8,128)}, u32[]{:S(2)}) copy-start(f32[768,384]{1,0:T(8,128)} %fusion.30) | copy-start | bytes 3538948
  342.1 14.3 %copy-start.20 = (f32[768,384]{1,0:T(8,128)S(1)}, f32[768,384]{1,0:T(8,128)}, u32[]{:S(2)}) copy-start(f32[768,384]{1,0:T(8,128)} %fusion.29) | copy-start | bytes 3538948
  345.7 10.7 %copy-start.9 = (f32[768,1152]{1,0:T(8,128)S(1)}, f32[768,1152]{1,0:T(8,128)}, u32[]{:S(2)}) copy-start(f32[768,1152]{1,0:T(8,128)} %fusion.28) | copy-start | bytes 10616836
  346.9 16.3 %collective-permute-start.17 = (bf16[2,2,48,512]{3,2,1,0:T(8,128)(2,1)S(1)}, bf16[2,2,48,512]{3,2,1,0:T(8,128)(2,1)S(1)}, u32[]{:S(2)}, u32[]{:S(2)}) collective-permute-start(bf16[2,2,48,512]{3,2,1,0:T(8,128)(2,1)S(1)} %dynamic-slice_bitcast_fusion.13), channel_id=1, source_target_pairs={{0,2},{2,0},{4,6},{6,4},{8,10},{10,8},{12,14},{14,12},{16,18},{18,... | collective-permute-start | bytes 589832 | tf_op jit(solution)/shard_map/ppermute | solution.py:1175
  356.0 7.3 %collective-permute-start.15 = (bf16[2,2,48,768]{3,2,1,0:T(8,128)(2,1)S(1)}, bf16[2,2,48,768]{3,2,1,0:T(8,128)(2,1)S(1)}, u32[]{:S(2)}, u32[]{:S(2)}) collective-permute-start(bf16[2,2,48,768]{3,2,1,0:T(8,128)(2,1)S(1)} %dynamic-slice_bitcast_fusion.12), channel_id=1, source_target_pairs={{0,4},{2,6},{4,0},{6,2},{8,12},{10,14},{12,8},{14,10},{16,20},{18,... | collective-permute-start | bytes 884744 | tf_op jit(solution)/shard_map/ppermute | solution.py:1175
  361.1 3.3 copy-start.4
  361.1 3.3 copy-start.6
  362.2 19.2 %collective-permute-start.18 = (bf16[2,2,2,48,1152]{4,3,2,1,0:T(8,128)(2,1)}, bf16[2,2,2,48,1152]{4,3,2,1,0:T(8,128)(2,1)S(1)}, u32[]{:S(2)}, u32[]{:S(2)}) collective-permute-start(bf16[2,2,2,48,1152]{4,3,2,1,0:T(8,128)(2,1)} %dynamic-slice_bitcast_fusion.5), channel_id=1, source_target_pairs={{0,2},{2,0},{4,6},{6,4},{8,10},{10,8},{12,14},{14,12},{16,18},{18,... | collective-permute-start | bytes 2654216 | tf_op jit(solution)/shard_map/ppermute | solution.py:1175
  364.5 20.1 %collective-permute-start.19 = (bf16[2,2,2,48,1152]{4,3,2,1,0:T(8,128)(2,1)}, bf16[2,2,2,48,1152]{4,3,2,1,0:T(8,128)(2,1)S(1)}, u32[]{:S(2)}, u32[]{:S(2)}) collective-permute-start(bf16[2,2,2,48,1152]{4,3,2,1,0:T(8,128)(2,1)} %dynamic-slice_bitcast_fusion.4), channel_id=1, source_target_pairs={{0,4},{2,6},{4,0},{6,2},{8,12},{10,14},{12,8},{14,10},{16,20},{18,... | collective-permute-start | bytes 2654216 | tf_op jit(solution)/shard_map/ppermute | solution.py:1175
  367.2 31.6 %all-to-all-start.7 = ((bf16[4,48,3072]{2,1,0:T(8,128)(2,1)}), bf16[4,48,3072]{2,1,0:T(8,128)(2,1)S(1)}, u32[]{:S(2)}, u32[]{:S(2)}) async-start(bf16[4,48,3072]{2,1,0:T(8,128)(2,1)} %pad_maximum_fusion.1), calls=%async_computation.7 | async-start | bytes 2359296 | tf_op jit(solution)/shard_map/all_to_all | solution.py:1203
  373.5 7.9 %copy-start.7 = (bf16[768,1152]{1,0:T(8,128)(2,1)S(1)}, bf16[768,1152]{1,0:T(8,128)(2,1)}, u32[]{:S(2)}) copy-start(bf16[768,1152]{1,0:T(8,128)(2,1)} %copy-done.6) | copy-start | bytes 5308420
  377.6 61.4 %collective-permute-start.12 = (bf16[20,24,768]{2,1,0:T(8,128)(2,1)}, bf16[20,24,768]{2,1,0:T(8,128)(2,1)}, u32[]{:S(2)}, u32[]{:S(2)}) collective-permute-start(bf16[20,24,768]{2,1,0:T(8,128)(2,1)} %get-tuple-element.149), channel_id=1, source_target_pairs={{0,1},{1,0},{2,3},{3,2},{4,5},{5,4},{6,7},{7,6},{8,9},{9,8},{10,11... | collective-permute-start | bytes 2211848 | tf_op jit(solution)/shard_map/ppermute | solution.py:965
  381.4 3.2 copy-start.10
  382.4 4.5 %copy-start.5 = (bf16[768,1152]{1,0:T(8,128)(2,1)S(1)}, bf16[768,1152]{1,0:T(8,128)(2,1)}, u32[]{:S(2)}) copy-start(bf16[768,1152]{1,0:T(8,128)(2,1)} %copy-done.4) | copy-start | bytes 5308420
  382.5 12.0 %collective-permute-start.25 = (bf16[2,2,48,1152]{3,2,1,0:T(8,128)(2,1)}, bf16[2,2,48,1152]{3,2,1,0:T(8,128)(2,1)S(1)}, u32[]{:S(2)}, u32[]{:S(2)}) collective-permute-start(bf16[2,2,48,1152]{3,2,1,0:T(8,128)(2,1)} %dynamic-slice_bitcast_fusion.10), channel_id=1, source_target_pairs={{0,4},{2,6},{4,0},{6,2},{8,12},{10,14},{12,8},{14,10},{16,20},{18,... | collective-permute-start | bytes 1327112 | tf_op jit(solution)/shard_map/ppermute | solution.py:1175
  387.0 1.4 collective-permute-start.20
  388.4 4.2 collective-permute-start.21
  390.7 12.6 %collective-permute-start.26 = (bf16[2,2,48,1152]{3,2,1,0:T(8,128)(2,1)}, bf16[2,2,48,1152]{3,2,1,0:T(8,128)(2,1)}, u32[]{:S(2)}, u32[]{:S(2)}) collective-permute-start(bf16[2,2,48,1152]{3,2,1,0:T(8,128)(2,1)} %dynamic-slice_bitcast_fusion.9), channel_id=1, source_target_pairs={{0,2},{2,0},{4,6},{6,4},{8,10},{10,8},{12,14},{14,12},{16,18},{18,... | collective-permute-start | bytes 1327112 | tf_op jit(solution)/shard_map/ppermute | solution.py:1175
  392.6 26.2 %collective-permute-start.22 = (f32[32,384]{1,0:T(8,128)S(1)}, f32[32,384]{1,0:T(8,128)S(1)}, u32[]{:S(2)}, u32[]{:S(2)}) collective-permute-start(f32[32,384]{1,0:T(8,128)S(1)} %add.242), channel_id=1, source_target_pairs={{0,4},{2,6},{4,0},{6,2},{8,12},{10,14},{12,8},{14,10},{16,20},{18,... | collective-permute-start | bytes 147464 | tf_op jit(solution)/shard_map/ppermute | solution.py:1175
  398.8 16.3 %all-to-all-start.5 = ((bf16[4,48,1280]{2,1,0:T(8,128)(2,1)}), bf16[4,48,1280]{2,1,0:T(8,128)(2,1)S(1)}, u32[]{:S(2)}, u32[]{:S(2)}) async-start(bf16[4,48,1280]{2,1,0:T(8,128)(2,1)} %pad_maximum_fusion.3), calls=%async_computation.5 | async-start | bytes 983040 | tf_op jit(solution)/shard_map/all_to_all | solution.py:1203
  415.1 31.0 %all-to-all-start.6 = ((bf16[4,48,2304]{2,1,0:T(8,128)(2,1)}), bf16[4,48,2304]{2,1,0:T(8,128)(2,1)S(1)}, u32[]{:S(2)}, u32[]{:S(2)}) async-start(bf16[4,48,2304]{2,1,0:T(8,128)(2,1)} %pad_maximum_fusion.2), calls=%async_computation.6 | async-start | bytes 1769472 | tf_op jit(solution)/shard_map/all_to_all | solution.py:1203
  418.9 14.7 %collective-permute-start.23 = (f32[32,384]{1,0:T(8,128)S(1)}, f32[32,384]{1,0:T(8,128)S(1)}, u32[]{:S(2)}, u32[]{:S(2)}) collective-permute-start(f32[32,384]{1,0:T(8,128)S(1)} %add.243), channel_id=1, source_target_pairs={{0,8},{2,10},{4,12},{6,14},{8,0},{10,2},{12,4},{14,6},{16,24},{18,... | collective-permute-start | bytes 147464 | tf_op jit(solution)/shard_map/ppermute | solution.py:1175
  433.6 8.9 %collective-permute-start.24 = (f32[32,384]{1,0:T(8,128)S(1)}, f32[32,384]{1,0:T(8,128)S(1)}, u32[]{:S(2)}, u32[]{:S(2)}) collective-permute-start(f32[32,384]{1,0:T(8,128)S(1)} %add.244), channel_id=1, source_target_pairs={{0,16},{2,18},{4,20},{6,22},{8,24},{10,26},{12,28},{14,30},{16,0},... | collective-permute-start | bytes 147464 | tf_op jit(solution)/shard_map/ppermute | solution.py:1175
  (23 other events, 40.3 us)
